TPU v7x, 512 devices: a whole 4x8x8 slice. The times are simulated.
512 devices in a mesh: section: 16 (over y, core), expert: 32 (over z, x).
Axes of the slice: x: 4, y: 8, z: 8, core: 2. Of those that a mesh axis runs over, the one named last changes fastest.
Arguments:
- act_fwd: bfloat16 [16, 768, 3584], P('section', 'expert'), may hold values from -6 to 6
- route_fwd: int32 [16, 768, 2], P('section', 'expert'), may hold values from 0 to 3, all different within a row; in each aligned block of 24 rows (0 to 23, 24 to 47, ..., all dimensions but the last counted through in order) at most 14 rows name the same one
- weight_fwd: float32 [16, 768, 2], P('section', 'expert'), may hold values from 0.3 to 1.2
- act_bwd: bfloat16 [16, 768, 3584], P('section', 'expert'), may hold values from -6 to 6
- route_bwd: int32 [16, 768, 2], P('section', 'expert'), may hold values from 0 to 3, all different within a row; in each aligned block of 24 rows (0 to 23, 24 to 47, ..., all dimensions but the last counted through in order) at most 14 rows name the same one
- weight_bwd: float32 [16, 768, 2], P('section', 'expert'), may hold values from 0.3 to 1.2
- cot_bwd: bfloat16 [16, 768, 3584], P('section', 'expert'), may hold values from -6 to 6
- norm_gain: float32 [16, 3584], P('section'), may hold values from 0.25 to 1.75
- w_gate: bfloat16 [16, 32, 3584, 128], P('section', 'expert'), may hold values from -0.09375 to 0.09375
- w_up: bfloat16 [16, 32, 3584, 128], P('section', 'expert'), may hold values from -0.09375 to 0.09375
- w_down: bfloat16 [16, 32, 128, 3584], P('section', 'expert'), may hold values from -0.1875 to 0.1875
Outputs:
- act_next: bfloat16 [16, 768, 3584], P('section', 'expert')
- cot_next: bfloat16 [16, 768, 3584], P('section', 'expert')
- gate_grad: bfloat16 [16, 768, 2], P('section', 'expert')
Inputs may be any that keep to these rules, and one draw needn't show every extreme that they name: `route_fwd`: each row names 2 different experts; among the 24 rows of one device no expert is named more than 14 times, and in some devices' rows some expert exactly 14 times. `route_bwd`: each row names 2 different experts; among the 24 rows of one device no expert is named more than 14 times, and in some devices' rows some expert exactly 14 times.
All inputs are finite; a program needn't handle non-finite values.
Results may differ from a plain program's by a relative error of at most 0.019.
Values may be sent and summed in bfloat16 or wider, within the bound.
No kernel may reach another device: no remote copies, remote signals or barrier semaphores. Data moves between devices by JAX's collectives and lax.ppermute only.
A program may use at most 64 MiB of HBM per device.

v0:
```python
import jax
import jax.numpy as jnp
from jax import lax
from jax.sharding import PartitionSpec as P

EXPERTS = 4


def shifted(value, axis, by):
    devices = lax.axis_size(axis)
    pairs = [(i, i + by) for i in range(devices) if 0 <= i + by < devices]
    return lax.ppermute(value, axis, pairs)


def normalize(rows, gain):
    values = rows.astype(jnp.float32)
    scale = lax.rsqrt(jnp.mean(values * values, axis=-1, keepdims=True) + 1e-06)
    unit = values * scale
    return (unit, scale, (unit * gain).astype(jnp.bfloat16))


def slot_index(route, experts, capacity):
    flat = route.reshape(-1)
    onehot = (flat[:, None] == jnp.arange(experts, dtype=jnp.int32)[None, :]).astype(jnp.int32)
    before = jnp.cumsum(onehot, axis=0) - onehot
    return flat * capacity + jnp.sum(before * onehot, axis=1)


def packed(rows, slots, topk, experts, capacity, slices):
    width = rows.shape[-1]
    buffer = jnp.zeros((experts * capacity, width), rows.dtype)
    buffer = buffer.at[slots].set(jnp.repeat(rows, topk, axis=0))
    return jnp.repeat(buffer.reshape(experts, capacity, width), slices, axis=0)


def expert_pass(rows, wg, wu, wd):
    gate = jnp.einsum("scd,df->scf", rows, wg, preferred_element_type=jnp.float32)
    upper = jnp.einsum("scd,df->scf", rows, wu, preferred_element_type=jnp.float32)
    inner = (jax.nn.silu(gate) * upper).astype(jnp.bfloat16)
    part = jnp.einsum("scf,fd->scd", inner, wd, preferred_element_type=jnp.float32).astype(
        jnp.bfloat16
    )
    return (gate, upper, part)


def expert_back(rows, grads, wg, wu, wd):
    gate, upper, part = expert_pass(rows, wg, wu, wd)
    grad_rows = jnp.einsum("scd,scd->sc", part, grads, preferred_element_type=jnp.float32).astype(
        jnp.bfloat16
    )
    d_inner = jnp.einsum("scd,fd->scf", grads, wd, preferred_element_type=jnp.float32)
    sig = jax.nn.sigmoid(gate)
    d_gate = (d_inner * upper * sig * (1.0 + gate * (1.0 - sig))).astype(jnp.bfloat16)
    d_up = (d_inner * gate * sig).astype(jnp.bfloat16)
    d_part = (
        jnp.einsum("scf,df->scd", d_gate, wg, preferred_element_type=jnp.float32)
        + jnp.einsum("scf,df->scd", d_up, wu, preferred_element_type=jnp.float32)
    ).astype(jnp.bfloat16)
    return (d_part, grad_rows)


def summed_parts(returned, experts, slices):
    shape = returned.shape
    grouped = returned.reshape((experts, slices) + shape[1:])
    return jnp.sum(grouped.astype(jnp.float32), axis=1).reshape((experts * shape[1],) + shape[2:])


def weighted_sum(returned, slots, weights, experts, slices, tokens, topk, width):
    whole = summed_parts(returned, experts, slices)
    picked = whole[slots].reshape(tokens, topk, width)
    return jnp.sum(weights[..., None] * picked, axis=1)


def body(
    act_fwd,
    route_fwd,
    weight_fwd,
    act_bwd,
    route_bwd,
    weight_bwd,
    cot_bwd,
    norm_gain,
    w_gate,
    w_up,
    w_down,
):
    tokens = act_fwd.shape[1]
    width = act_fwd.shape[2]
    topk = route_fwd.shape[2]
    groups = lax.axis_size("expert")
    experts = EXPERTS
    slices = groups // experts
    capacity = (tokens + 4) // 2
    gain = norm_gain[0]
    wg = w_gate[0, 0]
    wu = w_up[0, 0]
    wd = w_down[0, 0]
    x_fwd = act_fwd[0]
    unit_a, scale_a, normed_a = normalize(x_fwd, gain)
    slots_a = slot_index(route_fwd[0], experts, capacity)
    send_a = packed(normed_a, slots_a, topk, experts, capacity, slices)
    unit_b, scale_b, normed_b = normalize(act_bwd[0], gain)
    slots_b = slot_index(route_bwd[0], experts, capacity)
    send_h = packed(normed_b, slots_b, topk, experts, capacity, slices)
    send_c = packed(cot_bwd[0], slots_b, topk, experts, capacity, slices)
    got_a = lax.all_to_all(send_a, "expert", split_axis=0, concat_axis=0, tiled=True)
    out_rows = expert_pass(got_a, wg, wu, wd)[2]
    back_a = lax.all_to_all(out_rows, "expert", split_axis=0, concat_axis=0, tiled=True)
    got_h, got_c = (
        lax.all_to_all(send_h, "expert", split_axis=0, concat_axis=0, tiled=True),
        lax.all_to_all(send_c, "expert", split_axis=0, concat_axis=0, tiled=True),
    )
    d_rows, grad_rows = expert_back(got_h, got_c, wg, wu, wd)
    back_h, back_g = (
        lax.all_to_all(d_rows, "expert", split_axis=0, concat_axis=0, tiled=True),
        lax.all_to_all(grad_rows, "expert", split_axis=0, concat_axis=0, tiled=True),
    )
    mixed = weighted_sum(back_a, slots_a, weight_fwd[0], experts, slices, tokens, topk, width)
    layer_out = (x_fwd.astype(jnp.float32) + mixed).astype(jnp.bfloat16)
    d_normed = weighted_sum(back_h, slots_b, weight_bwd[0], experts, slices, tokens, topk, width)
    grad_whole = summed_parts(back_g, experts, slices)
    gate_grad = grad_whole[slots_b].reshape(tokens, topk).astype(jnp.bfloat16)
    q_term = d_normed * gain
    d_input = cot_bwd[0].astype(jnp.float32) + scale_b * (
        q_term - unit_b * jnp.mean(q_term * unit_b, axis=-1, keepdims=True)
    )
    d_input = d_input.astype(jnp.bfloat16)
    act_next = shifted(layer_out, "section", 1)
    cot_next = shifted(d_input, "section", -1)
    return (act_next[None], cot_next[None], gate_grad[None])


def solution(mesh):
    return jax.shard_map(
        body,
        mesh=mesh,
        in_specs=(
            P("section", "expert", None),
            P("section", "expert", None),
            P("section", "expert", None),
            P("section", "expert", None),
            P("section", "expert", None),
            P("section", "expert", None),
            P("section", "expert", None),
            P("section", None),
            P("section", "expert", None, None),
            P("section", "expert", None, None),
            P("section", "expert", None, None),
        ),
        out_specs=(
            P("section", "expert", None),
            P("section", "expert", None),
            P("section", "expert", None),
        ),
        check_vma=False,
    )
```

profile of v0, /device:TPU:1, one launch (start us, length us, event | category | flops | bytes accessed | tf_op | source)
XLA Modules:
  0.0 541.8 jit_solution(7504382910438321327)
XLA Ops:
  9.5 2.3 broadcast_in_dim.42
  11.8 14.0 %all-to-all-start.3 = ((bf16[32,14,3584]{2,1,0:T(8,128)(2,1)}), bf16[32,14,3584]{2,1,0:T(8,128)(2,1)}, u32[]{:S(2)}, u32[]{:S(2)}) async-start(bf16[32,14,3584]{2,1,0:T(8,128)(2,1)} %bitcast.75), calls=%async_computation.3 | async-start | bytes 7340032 | tf_op jit(solution)/shard_map/all_to_all | solution.py:110
  27.4 79.5 %all-to-all-done.3 = bf16[32,14,3584]{2,1,0:T(8,128)(2,1)} async-done(((bf16[32,14,3584]{2,1,0:T(8,128)(2,1)}), bf16[32,14,3584]{2,1,0:T(8,128)(2,1)}, u32[]{:S(2)}, u32[]{:S(2)}) %all-to-all-start.3) | async-done | bytes 3211296 | tf_op jit(solution)/shard_map/all_to_all | solution.py:110
  106.9 2.3 broadcast_in_dim.40
  109.2 9.2 %all-to-all-start.2 = ((bf16[32,14,3584]{2,1,0:T(8,128)(2,1)}), bf16[32,14,3584]{2,1,0:T(8,128)(2,1)}, u32[]{:S(2)}, u32[]{:S(2)}) async-start(bf16[32,14,3584]{2,1,0:T(8,128)(2,1)} %bitcast.76), calls=%async_computation.2 | async-start | bytes 7340032 | tf_op jit(solution)/shard_map/all_to_all | solution.py:111
  118.4 4.2 fusion.3
  122.7 4.3 fusion.5
  127.0 72.9 %all-to-all-done.2 = bf16[32,14,3584]{2,1,0:T(8,128)(2,1)} async-done(((bf16[32,14,3584]{2,1,0:T(8,128)(2,1)}), bf16[32,14,3584]{2,1,0:T(8,128)(2,1)}, u32[]{:S(2)}, u32[]{:S(2)}) %all-to-all-start.2) | async-done | bytes 3211296 | tf_op jit(solution)/shard_map/all_to_all | solution.py:111
  199.9 4.2 fusion.1
  206.1 3.7 copy.63
  209.8 8.8 %all-to-all-start.4 = ((bf16[32,14,3584]{2,1,0:T(8,128)(2,1)}), bf16[32,14,3584]{2,1,0:T(8,128)(2,1)}, u32[]{:S(2)}, u32[]{:S(2)}) async-start(bf16[32,14,3584]{2,1,0:T(8,128)(2,1)} %copy.63), calls=%async_computation.4 | async-start | bytes 7340032 | tf_op jit(solution)/shard_map/all_to_all | solution.py:115
  221.1 79.4 %all-to-all-done.4 = bf16[32,14,3584]{2,1,0:T(8,128)(2,1)} async-done(((bf16[32,14,3584]{2,1,0:T(8,128)(2,1)}), bf16[32,14,3584]{2,1,0:T(8,128)(2,1)}, u32[]{:S(2)}, u32[]{:S(2)}) %all-to-all-start.4) | async-done | bytes 3211296 | tf_op jit(solution)/shard_map/all_to_all | solution.py:115
  300.5 2.7 convert_reduce_fusion
  309.4 91.2 %all_to_all.34 = bf16[32,14,3584]{2,1,0:T(8,128)(2,1)S(1)} all-to-all(bf16[32,14,3584]{2,1,0:T(8,128)(2,1)S(1)} %bitcast.77), channel_id=1, replica_groups=mesh['section'=16,'expert'=32] {'expert'}, dimensions={0} | all-to-all | bytes 6422528 | tf_op jit(solution)/shard_map/all_to_all | solution.py:106
  404.6 7.2 %convolution_convert_fusion.1 = bf16[32,14,3584]{2,0,1:T(8,128)(2,1)} fusion(bf16[32,14,3584]{2,1,0:T(8,128)(2,1)} %copy-done.1, bf16[1,1,3584,128]{3,2,1,0:T(8,128)(2,1)S(1)} %copy-done, bf16[1,1,128,3584]{3,2,1,0:T(8,128)(2,1)S(1)} %copy-done.2, f32[32,14,128]{2,0,1:T(8,128)S(1)} %fusion.9), kind=kOutput, calls=%fused_computation.11 | convolution fusion | flops 824033280 | bytes 8486912 | tf_op jit(solution)/shard_map/scf,fd->scd/dot_general | solution.py:40
  411.8 5.6 %copy.54 = bf16[32,14,3584]{2,1,0:T(8,128)(2,1)} copy(bf16[32,14,3584]{2,0,1:T(8,128)(2,1)} %convolution_convert_fusion.1) | data formatting | bytes 6422528 | tf_op jit(solution)/shard_map/convert_element_type | solution.py:40
  417.4 5.8 %all-to-all-start.1 = ((bf16[32,14,3584]{2,1,0:T(8,128)(2,1)}), bf16[32,14,3584]{2,1,0:T(8,128)(2,1)}, u32[]{:S(2)}, u32[]{:S(2)}) async-start(bf16[32,14,3584]{2,1,0:T(8,128)(2,1)} %copy.54), calls=%async_computation.1 | async-start | bytes 7340032 | tf_op jit(solution)/shard_map/all_to_all | solution.py:108
  423.3 3.7 fusion
  427.0 3.8 collective-permute-start.1
  430.8 74.2 %all-to-all-done.1 = bf16[32,14,3584]{2,1,0:T(8,128)(2,1)} async-done(((bf16[32,14,3584]{2,1,0:T(8,128)(2,1)}), bf16[32,14,3584]{2,1,0:T(8,128)(2,1)}, u32[]{:S(2)}, u32[]{:S(2)}) %all-to-all-start.1) | async-done | bytes 3211296 | tf_op jit(solution)/shard_map/all_to_all | solution.py:108
  505.0 2.7 convert_reduce_fusion.1
  510.0 5.9 %collective-permute-start = (bf16[24,3584]{1,0:T(8,128)(2,1)S(1)}, bf16[24,3584]{1,0:T(8,128)(2,1)S(1)}, u32[]{:S(2)}, u32[]{:S(2)}) collective-permute-start(bf16[24,3584]{1,0:T(8,128)(2,1)S(1)} %fusion.43), channel_id=1, source_target_pairs={{0,32},{32,64},{64,96},{96,128},{128,160},{160,192},{192,224},{224... | collective-permute-start | bytes 516104 | tf_op jit(solution)/shard_map/ppermute | solution.py:12
  515.9 7.6 %multiply_reduce_fusion = bf16[32,14]{1,0:T(8,128)(2,1)S(1)} fusion(f32[32,14,3584]{2,0,1:T(8,128)} %fusion, bf16[32,14,3584]{2,1,0:T(8,128)(2,1)} %all-to-all-done.2), kind=kLoop, calls=%fused_computation.8 | loop fusion | flops 4816448 | bytes 9634688
  523.7 15.0 %all_to_all.35 = bf16[32,1,14]{2,1,0:T(2,128)(2,1)S(1)} all-to-all(bf16[32,1,14]{2,1,0:T(2,128)(2,1)S(1)} %copy.66), channel_id=1, replica_groups=mesh['section'=16,'expert'=32] {'expert'}, dimensions={0} | all-to-all | bytes 1792 | tf_op jit(solution)/shard_map/all_to_all | solution.py:116
  (115 shorter events, 30.5 us)
Async XLA Ops:
  0.6 122.0 %copy-start = (bf16[1,1,3584,128]{3,2,1,0:T(8,128)(2,1)S(1)}, bf16[1,1,3584,128]{3,2,1,0:T(8,128)(2,1)}, u32[]{:S(2)}) copy-start(bf16[1,1,3584,128]{3,2,1,0:T(8,128)(2,1)} %param.20) | copy-start | bytes 2752516
  8.2 17.9 %copy-start.21 = (s32[48]{0:T(128)}, s32[48]{0:T(128)S(1)}, u32[]{:S(2)}) copy-start(s32[48]{0:T(128)S(1)} %fusion.62) | copy-start | bytes 580
  11.8 14.0 %copy-start.11 = (bf16[1,24,3584]{2,1,0:T(8,128)(2,1)S(1)}, bf16[1,24,3584]{2,1,0:T(8,128)(2,1)}, u32[]{:S(2)}) copy-start(bf16[1,24,3584]{2,1,0:T(8,128)(2,1)} %param.17) | copy-start | bytes 516100
  11.8 95.1 %all-to-all-start.3 = ((bf16[32,14,3584]{2,1,0:T(8,128)(2,1)}), bf16[32,14,3584]{2,1,0:T(8,128)(2,1)}, u32[]{:S(2)}, u32[]{:S(2)}) async-start(bf16[32,14,3584]{2,1,0:T(8,128)(2,1)} %bitcast.75), calls=%async_computation.3 | async-start | bytes 7340032 | tf_op jit(solution)/shard_map/all_to_all | solution.py:110
  109.2 9.2 %copy-start.7 = (bf16[1,1,3584,128]{3,2,1,0:T(8,128)(2,1)S(1)}, bf16[1,1,3584,128]{3,2,1,0:T(8,128)(2,1)}, u32[]{:S(2)}) copy-start(bf16[1,1,3584,128]{3,2,1,0:T(8,128)(2,1)} %param.19) | copy-start | bytes 2752516
  109.2 90.7 %all-to-all-start.2 = ((bf16[32,14,3584]{2,1,0:T(8,128)(2,1)}), bf16[32,14,3584]{2,1,0:T(8,128)(2,1)}, u32[]{:S(2)}, u32[]{:S(2)}) async-start(bf16[32,14,3584]{2,1,0:T(8,128)(2,1)} %bitcast.76), calls=%async_computation.2 | async-start | bytes 7340032 | tf_op jit(solution)/shard_map/all_to_all | solution.py:111
  122.7 82.4 %copy-start.4 = (f32[32,14,128]{2,0,1:T(8,128)}, f32[32,14,128]{2,0,1:T(8,128)S(1)}, u32[]{:S(2)}) copy-start(f32[32,14,128]{2,0,1:T(8,128)S(1)} %fusion.3) | copy-start | bytes 688132
  122.7 77.2 %copy-start.2 = (bf16[1,1,128,3584]{3,2,1,0:T(8,128)(2,1)S(1)}, bf16[1,1,128,3584]{3,2,1,0:T(8,128)(2,1)}, u32[]{:S(2)}) copy-start(bf16[1,1,128,3584]{3,2,1,0:T(8,128)(2,1)} %param.21) | copy-start | bytes 2752516
  127.0 78.1 %copy-start.9 = (f32[32,14,128]{2,0,1:T(8,128)}, f32[32,14,128]{2,0,1:T(8,128)S(1)}, u32[]{:S(2)}) copy-start(f32[32,14,128]{2,0,1:T(8,128)S(1)} %fusion.5) | copy-start | bytes 688132
  209.8 8.8 %copy-start.17 = (s32[1,24,2]{1,2,0:T(2,128)S(1)}, s32[1,24,2]{1,2,0:T(2,128)}, u32[]{:S(2)}) copy-start(s32[1,24,2]{1,2,0:T(2,128)} %param.12) | copy-start | bytes 580
  209.8 9.1 %copy-start.19 = (f32[1,24,2]{1,2,0:T(2,128)S(1)}, f32[1,24,2]{1,2,0:T(2,128)}, u32[]{:S(2)}) copy-start(f32[1,24,2]{1,2,0:T(2,128)} %param.16) | copy-start | bytes 580
  209.8 10.0 %copy-start.22 = (s32[48]{0:T(128)S(1)}, s32[48]{0:T(128)}, u32[]{:S(2)}) copy-start(s32[48]{0:T(128)} %copy-done.21) | copy-start | bytes 580
  209.8 90.7 %all-to-all-start.4 = ((bf16[32,14,3584]{2,1,0:T(8,128)(2,1)}), bf16[32,14,3584]{2,1,0:T(8,128)(2,1)}, u32[]{:S(2)}, u32[]{:S(2)}) async-start(bf16[32,14,3584]{2,1,0:T(8,128)(2,1)} %copy.63), calls=%async_computation.4 | async-start | bytes 7340032 | tf_op jit(solution)/shard_map/all_to_all | solution.py:115
  303.4 2.5 copy-start.3
  303.4 2.5 copy-start.13
  303.4 2.7 copy-start.18
  304.5 3.2 copy-start.23
  309.4 93.0 %copy-start.8 = (bf16[1,1,3584,128]{3,2,1,0:T(8,128)(2,1)S(1)}, bf16[1,1,3584,128]{3,2,1,0:T(8,128)(2,1)}, u32[]{:S(2)}) copy-start(bf16[1,1,3584,128]{3,2,1,0:T(8,128)(2,1)} %param.19) | copy-start | bytes 2752516
  417.4 5.9 %copy-start.20 = (f32[1,24,2]{1,2,0:T(2,128)S(1)}, f32[1,24,2]{1,2,0:T(2,128)}, u32[]{:S(2)}) copy-start(f32[1,24,2]{1,2,0:T(2,128)} %param.13) | copy-start | bytes 580
  417.4 6.0 %copy-start.5 = (f32[32,14,128]{2,0,1:T(8,128)S(1)}, f32[32,14,128]{2,0,1:T(8,128)}, u32[]{:S(2)}) copy-start(f32[32,14,128]{2,0,1:T(8,128)} %copy-done.4) | copy-start | bytes 688132
  417.4 6.0 %copy-start.10 = (f32[32,14,128]{2,0,1:T(8,128)S(1)}, f32[32,14,128]{2,0,1:T(8,128)}, u32[]{:S(2)}) copy-start(f32[32,14,128]{2,0,1:T(8,128)} %copy-done.9) | copy-start | bytes 688132
  417.4 87.6 %all-to-all-start.1 = ((bf16[32,14,3584]{2,1,0:T(8,128)(2,1)}), bf16[32,14,3584]{2,1,0:T(8,128)(2,1)}, u32[]{:S(2)}, u32[]{:S(2)}) async-start(bf16[32,14,3584]{2,1,0:T(8,128)(2,1)} %copy.54), calls=%async_computation.1 | async-start | bytes 7340032 | tf_op jit(solution)/shard_map/all_to_all | solution.py:108
  427.0 113.4 %collective-permute-start.1 = (bf16[24,3584]{1,0:T(8,128)(2,1)S(1)}, bf16[24,3584]{1,0:T(8,128)(2,1)S(1)}, u32[]{:S(2)}, u32[]{:S(2)}) collective-permute-start(bf16[24,3584]{1,0:T(8,128)(2,1)S(1)} %get-tuple-element.15), channel_id=1, source_target_pairs={{32,0},{64,32},{96,64},{128,96},{160,128},{192,160},{224,192},{256... | collective-permute-start | bytes 516104 | tf_op jit(solution)/shard_map/ppermute | solution.py:12
  510.0 30.4 %collective-permute-start = (bf16[24,3584]{1,0:T(8,128)(2,1)S(1)}, bf16[24,3584]{1,0:T(8,128)(2,1)S(1)}, u32[]{:S(2)}, u32[]{:S(2)}) collective-permute-start(bf16[24,3584]{1,0:T(8,128)(2,1)S(1)} %fusion.43), channel_id=1, source_target_pairs={{0,32},{32,64},{64,96},{96,128},{128,160},{160,192},{192,224},{224... | collective-permute-start | bytes 516104 | tf_op jit(solution)/shard_map/ppermute | solution.py:12
  (6 other events, 9.3 us)
where the time goes:
time: 543 us; the launch traced here: 542 us
  waiting for transfers between devices  306 us (56%)
  blocking collectives  106 us (20%)
  starting transfers between devices  47.4 us (9%)
  local copies, waits for them, and re-layouts  29.8 us (5%)
  matrix products  27.8 us (5%)
  other arithmetic  23.5 us (4%)
    all_to_all x1, blocking collectives, body(): lax.all_to_all(send_a, 'expert', split_axis=0, concat_axis=0, tiled=True)  91.2 us
    all_to_all x1, waiting for transfers between devices, body(): lax.all_to_all(send_h, 'expert', split_axis=0, concat_axis=0, tiled=True)  79.5 us
    all_to_all x1, waiting for transfers between devices, body(): lax.all_to_all(d_rows, 'expert', split_axis=0, concat_axis=0, tiled=True)  79.4 us
    all_to_all x1, waiting for transfers between devices, body(): lax.all_to_all(out_rows, 'expert', split_axis=0, concat_axis=0, tiled=True)  74.2 us
    all_to_all x1, waiting for transfers between devices, body(): lax.all_to_all(send_c, 'expert', split_axis=0, concat_axis=0, tiled=True)  72.9 us
    all_to_all x1, blocking collectives, body(): lax.all_to_all(grad_rows, 'expert', split_axis=0, concat_axis=0, tiled=True)  15 us
    all_to_all x1, starting transfers between devices, body(): lax.all_to_all(send_h, 'expert', split_axis=0, concat_axis=0, tiled=True)  14 us
    dot_general x2, matrix products, expert_pass(): jnp.einsum('scf,fd->scd', inner, wd, preferred_element_type=jnp.float32)  10.9 us
  transfers between devices with their start and end apart: 6, of which 4 were waited for; matrix products, arithmetic and copies ran while one was open for 6% of the time, Pallas kernels for 0%

commit v1 on v0

v1 whole, which is shorter than its diff:
```python
import functools

import jax
import jax.numpy as jnp
from jax import lax
from jax.experimental import pallas as pl
from jax.experimental.pallas import tpu as pltpu
from jax.sharding import PartitionSpec as P

EXPERTS = 4
GRID_X = 4
GRID_Z = 8
SLOT = 16
F32 = jnp.float32
BF16 = jnp.bfloat16
NT = (((1,), (1,)), ((), ()))
TN = (((0,), (0,)), ((), ()))


def expert_pairs(move):
    pairs = []
    for z in range(GRID_Z):
        for x in range(GRID_X):
            to_z, to_x = move(z, x)
            pairs.append((z * GRID_X + x, to_z % GRID_Z * GRID_X + to_x))
    return pairs


def signed(z, even, odd):
    return z + (odd if z % 2 else even)


HOP_W = expert_pairs(lambda z, x: (z ^ 1, x))
HOP_A = expert_pairs(lambda z, x: (signed(z, -1, 1), x))
HOP_B = expert_pairs(lambda z, x: (signed(z, 2, -2), x))
HOP_B_BACK = expert_pairs(lambda z, x: (signed(z, -2, 2), x))
HOP_C = expert_pairs(lambda z, x: (signed(z, -3, 3), x))
HOP_X1 = expert_pairs(lambda z, x: (z, x ^ 1))
HOP_X3 = expert_pairs(lambda z, x: (z, x ^ 3))


def hop(value, pairs):
    return lax.ppermute(value, "expert", pairs)


def shifted(value, axis, by):
    devices = lax.axis_size(axis)
    pairs = [(i, i + by) for i in range(devices) if 0 <= i + by < devices]
    return lax.ppermute(value, axis, pairs)


def kernel_call(kernel, outs, n_in, scratch=(), info=True, limit=32):
    smem = pl.BlockSpec(memory_space=pltpu.SMEM)
    vmem = pl.BlockSpec(memory_space=pltpu.VMEM)
    return pl.pallas_call(
        kernel,
        out_shape=[jax.ShapeDtypeStruct(s, d) for s, d in outs],
        in_specs=[smem] * info + [vmem] * n_in,
        out_specs=[vmem] * len(outs),
        scratch_shapes=list(scratch),
        compiler_params=pltpu.CompilerParams(vmem_limit_bytes=limit * 1024 * 1024),
    )


def slot_masks(info_ref, route_ref):
    tokens = route_ref.shape[0]
    own, odd = info_ref[0], info_ref[1]
    lanes = lax.broadcasted_iota(jnp.int32, (tokens, 128), 1)
    route = route_ref[...]
    named = [(route[:, k : k + 1] == lanes).astype(F32) for k in range(2)]
    row = lax.broadcasted_iota(jnp.int32, (tokens, tokens), 0)
    col = lax.broadcasted_iota(jnp.int32, (tokens, tokens), 1)
    earlier = (col < row).astype(BF16)
    counts = jnp.dot(earlier, (named[0] + named[1]).astype(BF16), preferred_element_type=F32)
    out = []
    for k in range(2):
        rank = jnp.sum(named[k] * counts, axis=1, keepdims=True).astype(jnp.int32)
        away = (route[:, k : k + 1] - own) & 3
        side = jnp.where((away == 3) == (odd == 0), 1, 2)
        rel = jnp.where(away == 0, 0, jnp.where(away == 2, 3, side))
        slots = lax.broadcasted_iota(jnp.int32, (tokens, 4 * SLOT), 1)
        out.append((slots == rel * SLOT + rank, rel, rank))
    return out


def normalized(x, gain):
    values = x.astype(F32)
    scale = lax.rsqrt(jnp.mean(values * values, axis=-1, keepdims=True) + 1e-06)
    return values * scale, scale


def pack_kernel(info_ref, x_ref, route_ref, gain_ref, *rest):
    masks = slot_masks(info_ref, route_ref)
    place = (masks[0][0] | masks[1][0]).astype(F32).astype(BF16)
    unit, _ = normalized(x_ref[...], gain_ref[...])
    normed = (unit * gain_ref[...]).astype(BF16)
    sources = [normed]
    if len(rest) == 5:
        sources.append(rest[0][...])
    outs = rest[-4:]
    width = x_ref.shape[1]
    for i, rows in enumerate(sources):
        packed = lax.dot_general(place, rows, TN, preferred_element_type=F32).astype(BF16)
        for j in range(4):
            outs[j][:, i * width : (i + 1) * width] = packed[j * SLOT : (j + 1) * SLOT]


def hidden(rows, wg, wu):
    both = jnp.dot(rows, jnp.concatenate([wg, wu], axis=1), preferred_element_type=F32)
    return both[:, :128], both[:, 128:]


def fwd_kernel(c1, qr1, c2, pr2, wg, wu, wd, vg, vu, vd, keep1, send1, keep2, send2, rows):
    for i, ref in enumerate((c1, qr1, c2, pr2)):
        rows[64 * i : 64 * (i + 1), :] = ref[...]
    inner = []
    for g_ref, u_ref in ((wg, wu), (vg, vu)):
        gate, up = hidden(rows[...], g_ref[...], u_ref[...])
        inner.append((gate * jax.nn.sigmoid(gate) * up).astype(BF16))
    inner = jnp.concatenate(inner, axis=1)
    width = rows.shape[1]
    step = 512
    for at in range(0, width, step):
        cols = slice(at, at + step)
        down = jnp.concatenate([wd[:, cols], vd[:, cols]], axis=0)
        part = jnp.dot(inner, down, preferred_element_type=F32)
        keep1[:, cols] = part[0:64]
        send1[:, cols] = part[64:128].astype(BF16)
        keep2[:, cols] = part[128:192]
        send2[:, cols] = part[192:256].astype(BF16)


def bwd_kernel(c1, qr1, c2, pr2, wg, wu, wd, vg, vu, vd, keep1, send1, keep2, send2, rows, cots):
    width = rows.shape[1]
    for i, ref in enumerate((c1, qr1, c2, pr2)):
        rows[64 * i : 64 * (i + 1), :] = ref[:, :width]
        cots[64 * i : 64 * (i + 1), :] = ref[:, width:]
    back = []
    products = None
    for g_ref, u_ref, d_ref in ((wg, wu, wd), (vg, vu, vd)):
        gate, up = hidden(rows[...], g_ref[...], u_ref[...])
        d_inner = lax.dot_general(cots[...], d_ref[...], NT, preferred_element_type=F32)
        sig = jax.nn.sigmoid(gate)
        silu = gate * sig
        inner = (silu * up).astype(BF16).astype(F32)
        d_gate = (d_inner * up * sig * (1.0 + gate * (1.0 - sig))).astype(BF16)
        d_up = (d_inner * silu).astype(BF16)
        back.append(jnp.concatenate([d_gate, d_up], axis=1))
        product = inner * d_inner
        products = product if products is None else products + product
    count = products.shape[0]
    high = products.astype(BF16)
    low = (products - high.astype(F32)).astype(BF16)
    ones = jnp.ones((16, 128), BF16)
    grads = lax.dot_general(ones, high, NT, preferred_element_type=F32)
    grads = grads + lax.dot_general(ones, low, NT, preferred_element_type=F32)
    row = lax.broadcasted_iota(jnp.int32, (count, count), 0)
    col = lax.broadcasted_iota(jnp.int32, (count, count), 1)
    held = (row // SLOT == col // SLOT) & (row % SLOT == SLOT - 2)
    spread = jnp.where(held, grads[0:1, :], 0.0).astype(BF16)
    at_row = lax.broadcasted_iota(jnp.int32, (count, 128), 0)
    at_col = lax.broadcasted_iota(jnp.int32, (count, 128), 1)
    pick = (at_row % SLOT == at_col).astype(F32).astype(BF16)
    grad_rows = jnp.dot(spread, pick, preferred_element_type=F32)
    step = 512
    for at in range(0, width, step):
        cols = slice(at, at + step)
        part = None
        for grad, g_ref, u_ref in ((back[0], wg, wu), (back[1], vg, vu)):
            weight = jnp.concatenate([g_ref[cols, :], u_ref[cols, :]], axis=1)
            term = lax.dot_general(grad, weight, NT, preferred_element_type=F32)
            part = term if part is None else part + term
        if at == 0:
            part = jnp.concatenate([part[:, :128] + grad_rows, part[:, 128:]], axis=1)
        keep1[:, cols] = part[0:64]
        send1[:, cols] = part[64:128].astype(BF16)
        keep2[:, cols] = part[128:192]
        send2[:, cols] = part[192:256].astype(BF16)


def mixed_rows(masks, weight_ref, parts):
    weights = weight_ref[...]
    spread = jnp.where(masks[0][0], weights[:, 0:1], 0.0) + jnp.where(
        masks[1][0], weights[:, 1:2], 0.0
    )
    high = spread.astype(BF16)
    rest = spread - high.astype(F32)
    middle = rest.astype(BF16)
    low = (rest - middle.astype(F32)).astype(BF16)
    total = None
    for j, part in enumerate(parts):
        at = slice(j * SLOT, (j + 1) * SLOT)
        for piece in (high, middle, low):
            term = jnp.dot(piece[:, at], part, preferred_element_type=F32)
            total = term if total is None else total + term
    return total


def fwd_out_kernel(info_ref, x_ref, route_ref, weight_ref, own, a, b, c, out_ref):
    masks = slot_masks(info_ref, route_ref)
    parts = [own[...], a[...], b[...], c[...]]
    mixed = mixed_rows(masks, weight_ref, parts)
    out_ref[...] = (x_ref[...].astype(F32) + mixed).astype(BF16)


def bwd_out_kernel(
    info_ref, x_ref, route_ref, weight_ref, cot_ref, gain_ref, own, a, b, c, out_ref, grad_ref
):
    masks = slot_masks(info_ref, route_ref)
    parts = [own[...], a[...], b[...], c[...]]
    d_normed = mixed_rows(masks, weight_ref, parts)
    unit, scale = normalized(x_ref[...], gain_ref[...])
    q_term = d_normed * gain_ref[...]
    mean = jnp.mean(q_term * unit, axis=-1, keepdims=True)
    d_input = cot_ref[...].astype(F32) + scale * (q_term - unit * mean)
    out_ref[...] = d_input.astype(BF16)
    tokens = x_ref.shape[0]
    lanes = lax.broadcasted_iota(jnp.int32, (tokens, 128), 1)
    grads = []
    for _, rel, rank in masks:
        held = jnp.zeros((tokens, 128), F32)
        for j, part in enumerate(parts):
            row = part[:, :128].astype(F32)[SLOT - 2 : SLOT - 1, :]
            held = held + jnp.where(rel == j, row, 0.0)
        grads.append(jnp.sum(jnp.where(lanes == rank, held, 0.0), axis=1, keepdims=True))
    pair = lax.broadcasted_iota(jnp.int32, (tokens, 2), 1)
    grad_ref[...] = jnp.where(pair == 0, grads[0], grads[1]).astype(BF16)


def spread_rows(own, a, b, c):
    got_a, got_b, got_c = hop(a, HOP_A), hop(b, HOP_B), hop(c, HOP_C)
    half1 = jnp.concatenate([own, got_a], axis=0)
    half2 = jnp.concatenate([got_b, got_c], axis=0)
    p1 = hop(half1, HOP_X1)
    q2 = hop(half2, HOP_X3)
    c1 = jnp.concatenate([half1, p1], axis=0)
    c2 = jnp.concatenate([half2, q2], axis=0)
    return c1, hop(c1, HOP_X3), c2, hop(c2, HOP_X1)


def return_rows(keep1, send1, keep2, send2):
    sum1 = keep1 + hop(send1, HOP_X3).astype(F32)
    sum2 = keep2 + hop(send2, HOP_X1).astype(F32)
    full1 = sum1[:32] + hop(sum1[32:].astype(BF16), HOP_X1).astype(F32)
    full2 = sum2[:32] + hop(sum2[32:].astype(BF16), HOP_X3).astype(F32)
    full1 = full1.astype(BF16)
    full2 = full2.astype(BF16)
    back_a = hop(full1[SLOT:], HOP_A)
    back_b = hop(full2[:SLOT], HOP_B_BACK)
    back_c = hop(full2[SLOT:], HOP_C)
    return full1[:SLOT], back_a, back_b, back_c


def body(
    act_fwd,
    route_fwd,
    weight_fwd,
    act_bwd,
    route_bwd,
    weight_bwd,
    cot_bwd,
    norm_gain,
    w_gate,
    w_up,
    w_down,
):
    tokens, width = act_fwd.shape[1:]
    index = lax.axis_index("expert")
    z = index // GRID_X
    info = jnp.stack([z // 2, z % 2]).astype(jnp.int32)
    wg, wu, wd = w_gate[0, 0], w_up[0, 0], w_down[0, 0]
    wide = [((SLOT, width), BF16)] * 4
    sent_a = kernel_call(pack_kernel, wide, 3)(info, act_fwd[0], route_fwd[0], norm_gain)
    wide = [((SLOT, 2 * width), BF16)] * 4
    sent_b = kernel_call(pack_kernel, wide, 4)(
        info, act_bwd[0], route_bwd[0], norm_gain, cot_bwd[0]
    )
    rows_a = spread_rows(*sent_a)
    weights = (wg, wu, wd, hop(wg, HOP_W), hop(wu, HOP_W), hop(wd, HOP_W))
    rows_b = spread_rows(*sent_b)
    outs = [((64, width), F32), ((64, width), BF16)] * 2
    scratch = pltpu.VMEM((256, width), BF16)
    parts_a = kernel_call(fwd_kernel, outs, 10, [scratch], info=False)(*rows_a, *weights)
    parts_b = kernel_call(bwd_kernel, outs, 10, [scratch] * 2, info=False)(*rows_b, *weights)
    back_a = return_rows(*parts_a)
    (layer_out,) = kernel_call(fwd_out_kernel, [((tokens, width), BF16)], 7)(
        info, act_fwd[0], route_fwd[0], weight_fwd[0], *back_a
    )
    act_next = shifted(layer_out, "section", 1)
    back_b = return_rows(*parts_b)
    d_input, gate_grad = kernel_call(
        bwd_out_kernel, [((tokens, width), BF16), ((tokens, 2), BF16)], 9
    )(info, act_bwd[0], route_bwd[0], weight_bwd[0], cot_bwd[0], norm_gain, *back_b)
    cot_next = shifted(d_input, "section", -1)
    return (act_next[None], cot_next[None], gate_grad[None])


def solution(mesh):
    return jax.shard_map(
        body,
        mesh=mesh,
        in_specs=(
            P("section", "expert", None),
            P("section", "expert", None),
            P("section", "expert", None),
            P("section", "expert", None),
            P("section", "expert", None),
            P("section", "expert", None),
            P("section", "expert", None),
            P("section", None),
            P("section", "expert", None, None),
            P("section", "expert", None, None),
            P("section", "expert", None, None),
        ),
        out_specs=(
            P("section", "expert", None),
            P("section", "expert", None),
            P("section", "expert", None),
        ),
        check_vma=False,
    )
```

time: 543 us -> 215 us (0.40)
  waiting for transfers between devices: 306 us -> 66.3 us
  blocking collectives: 106 us -> 0 us
  starting transfers between devices: 47.4 us -> 125 us
  matrix products: 27.8 us -> 0 us
  local copies, waits for them, and re-layouts: 29.8 us -> 6.82 us
  other arithmetic: 23.5 us -> 1.61 us
  Pallas kernels: 0 us -> 11.1 us
    all_to_all x4 -> x0, waiting for transfers between devices: 306 us -> none  [the longest x1 79.5 us: body(): lax.all_to_all(send_h, 'expert', split_axis=0, concat_axis=0, tiled=True)]
    ppermute x0 -> x31, starting transfers between devices: none -> 108 us  [hop(): return lax.ppermute(value, 'expert', pairs)]
    all_to_all x2 -> x0, blocking collectives: 106 us -> none  [the longest x1 91.2 us: body(): lax.all_to_all(send_a, 'expert', split_axis=0, concat_axis=0, tiled=True)]
    ppermute x0 -> x31, waiting for transfers between devices: none -> 62.2 us  [hop(): return lax.ppermute(value, 'expert', pairs)]
    all_to_all x4 -> x0, starting transfers between devices: 37.8 us -> none  [the longest x1 14 us: body(): lax.all_to_all(send_h, 'expert', split_axis=0, concat_axis=0, tiled=True)]
    dot_general x8 -> x0, matrix products: 27.8 us -> none  [the longest x2 10.9 us: expert_pass(): jnp.einsum('scf,fd->scd', inner, wd, preferred_element_type=jnp.float32)]
    pallas_call x0 -> x6, Pallas kernels: none -> 11.1 us  [the longest x1 3.35 us: body(): kernel_call(bwd_kernel, outs, 10, [scratch] * 2, info=False)]
    reduce_sum x10 -> x0, other arithmetic: 10.1 us -> none  [the longest x3 5.51 us: summed_parts(): jnp.sum(grouped.astype(jnp.float32), axis=1)]
  transfers between devices with their start and end apart: 6 -> 33, of which waited for: 4 -> 11; matrix products, arithmetic and copies ran while one was open for 6% -> 2% of each run, Pallas kernels for 0% -> 5%
where the time goes in v1:
time: 215 us; the launch traced here: 212 us
  starting transfers between devices  125 us (58%)
  waiting for transfers between devices  66.3 us (31%)
  Pallas kernels  11.1 us (5%)
  local copies, waits for them, and re-layouts  6.82 us (3%)
    ppermute x31, starting transfers between devices, hop(): return lax.ppermute(value, 'expert', pairs)  108 us
    ppermute x31, waiting for transfers between devices, hop(): return lax.ppermute(value, 'expert', pairs)  62.2 us
    ppermute x2, starting transfers between devices, shifted(): return lax.ppermute(value, axis, pairs)  17.2 us
    unnamed x36, local copies, waits for them, and re-layouts  5.61 us
  transfers between devices with their start and end apart: 33, of which 11 were waited for; matrix products, arithmetic and copies ran while one was open for 2% of the time, Pallas kernels for 5%

profile of v1, /device:TPU:1, one launch (start us, length us, event | category | flops | bytes accessed | tf_op | source)
XLA Modules:
  0.0 212.5 jit_solution(6318513499619959550)
XLA Ops:
  4.7 6.6 %collective-permute-start.21 = (bf16[16,7168]{1,0:T(8,128)(2,1)S(1)}, bf16[16,7168]{1,0:T(8,128)(2,1)}, u32[]{:S(2)}, u32[]{:S(2)}) collective-permute-start(bf16[16,7168]{1,0:T(8,128)(2,1)S(1)} %get-tuple-element.31), channel_id=1, source_target_pairs={{0,8},{1,9},{2,10},{3,11},{4,28},{5,29},{6,30},{7,31},{8,16},{9,17... | collective-permute-start | bytes 688136 | tf_op jit(solution)/shard_map/ppermute | solution.py:43
  11.3 6.8 %collective-permute-start.22 = (bf16[16,7168]{1,0:T(8,128)(2,1)S(1)}, bf16[16,7168]{1,0:T(8,128)(2,1)S(1)}, u32[]{:S(2)}, u32[]{:S(2)}) collective-permute-start(bf16[16,7168]{1,0:T(8,128)(2,1)S(1)} %get-tuple-element.32), channel_id=1, source_target_pairs={{0,20},{1,21},{2,22},{3,23},{4,16},{5,17},{6,18},{7,19},{8,28},{9,... | collective-permute-start | bytes 688136 | tf_op jit(solution)/shard_map/ppermute | solution.py:43
  18.1 4.7 %collective-permute-start.18 = (bf16[16,7168]{1,0:T(8,128)(2,1)S(1)}, bf16[16,7168]{1,0:T(8,128)(2,1)S(1)}, u32[]{:S(2)}, u32[]{:S(2)}) collective-permute-start(bf16[16,7168]{1,0:T(8,128)(2,1)S(1)} %get-tuple-element.30), channel_id=1, source_target_pairs={{0,28},{1,29},{2,30},{3,31},{4,8},{5,9},{6,10},{7,11},{8,4},{9,5},... | collective-permute-start | bytes 688136 | tf_op jit(solution)/shard_map/ppermute | solution.py:43
  26.0 5.2 %collective-permute-start.3 = (bf16[16,3584]{1,0:T(8,128)(2,1)S(1)}, bf16[16,3584]{1,0:T(8,128)(2,1)S(1)}, u32[]{:S(2)}, u32[]{:S(2)}) collective-permute-start(bf16[16,3584]{1,0:T(8,128)(2,1)S(1)} %get-tuple-element.23), channel_id=1, source_target_pairs={{0,8},{1,9},{2,10},{3,11},{4,28},{5,29},{6,30},{7,31},{8,16},{9,17... | collective-permute-start | bytes 344072 | tf_op jit(solution)/shard_map/ppermute | solution.py:43
  31.3 18.4 %collective-permute-done.3 = bf16[16,3584]{1,0:T(8,128)(2,1)S(1)} collective-permute-done((bf16[16,3584]{1,0:T(8,128)(2,1)S(1)}, bf16[16,3584]{1,0:T(8,128)(2,1)S(1)}, u32[]{:S(2)}, u32[]{:S(2)}) %collective-permute-start.3) | collective-permute-done | bytes 114720 | tf_op jit(solution)/shard_map/ppermute | solution.py:43
  49.7 5.6 %collective-permute-start.4 = (bf16[16,3584]{1,0:T(8,128)(2,1)S(1)}, bf16[16,3584]{1,0:T(8,128)(2,1)S(1)}, u32[]{:S(2)}, u32[]{:S(2)}) collective-permute-start(bf16[16,3584]{1,0:T(8,128)(2,1)S(1)} %get-tuple-element.24), channel_id=1, source_target_pairs={{0,20},{1,21},{2,22},{3,23},{4,16},{5,17},{6,18},{7,19},{8,28},{9,... | collective-permute-start | bytes 344072 | tf_op jit(solution)/shard_map/ppermute | solution.py:43
  55.4 4.2 %collective-permute-done.4 = bf16[16,3584]{1,0:T(8,128)(2,1)S(1)} collective-permute-done((bf16[16,3584]{1,0:T(8,128)(2,1)S(1)}, bf16[16,3584]{1,0:T(8,128)(2,1)S(1)}, u32[]{:S(2)}, u32[]{:S(2)}) %collective-permute-start.4) | collective-permute-done | bytes 114720 | tf_op jit(solution)/shard_map/ppermute | solution.py:43
  62.4 3.9 %collective-permute-done = bf16[16,3584]{1,0:T(8,128)(2,1)S(1)} collective-permute-done((bf16[16,3584]{1,0:T(8,128)(2,1)S(1)}, bf16[16,3584]{1,0:T(8,128)(2,1)S(1)}, u32[]{:S(2)}, u32[]{:S(2)}) %collective-permute-start) | collective-permute-done | bytes 114720 | tf_op jit(solution)/shard_map/ppermute | solution.py:43
  66.3 4.6 %collective-permute-start.8 = (bf16[3584,128]{1,0:T(8,128)(2,1)S(1)}, bf16[3584,128]{1,0:T(8,128)(2,1)S(1)}, u32[]{:S(2)}, u32[]{:S(2)}) collective-permute-start(bf16[3584,128]{1,0:T(8,128)(2,1)S(1)} %bitcast.18), channel_id=1, source_target_pairs={{0,4},{1,5},{2,6},{3,7},{4,0},{5,1},{6,2},{7,3},{8,12},{9,13},{10,... | collective-permute-start | bytes 2752520 | tf_op jit(solution)/shard_map/ppermute | solution.py:43
  70.9 4.4 %collective-permute-start.5 = (bf16[32,3584]{1,0:T(8,128)(2,1)S(1)}, bf16[32,3584]{1,0:T(8,128)(2,1)S(1)}, u32[]{:S(2)}, u32[]{:S(2)}) collective-permute-start(bf16[32,3584]{1,0:T(8,128)(2,1)S(1)} %pad_maximum_fusion.3), channel_id=1, source_target_pairs={{0,3},{1,2},{2,1},{3,0},{4,7},{5,6},{6,5},{7,4},{8,11},{9,10},{10,... | collective-permute-start | bytes 688136 | tf_op jit(solution)/shard_map/ppermute | solution.py:43
  95.6 7.3 %collective-permute-done.2.qr1 = bf16[64,3584]{1,0:T(8,128)(2,1)S(1)} collective-permute-done((bf16[64,3584]{1,0:T(8,128)(2,1)S(1)}, bf16[64,3584]{1,0:T(8,128)(2,1)S(1)}, u32[]{:S(2)}, u32[]{:S(2)}) %collective-permute-start.2) | collective-permute-done | bytes 458784 | tf_op jit(solution)/shard_map/ppermute | solution.py:43
  112.9 3.7 %collective-permute-start.20 = (bf16[64,7168]{1,0:T(8,128)(2,1)S(1)}, bf16[64,7168]{1,0:T(8,128)(2,1)S(1)}, u32[]{:S(2)}, u32[]{:S(2)}) collective-permute-start(bf16[64,7168]{1,0:T(8,128)(2,1)S(1)} %constant_dynamic-update-slice_fusion.6.c1), channel_id=1, source_target_pairs={{0,3},{1,2},{2,1},{3,0},{4,7},{5,6},{6,5},{7,4},{8,11},{9,10},{10,... | collective-permute-start | bytes 2752520 | tf_op jit(solution)/shard_map/ppermute | solution.py:43
  119.5 7.4 %collective-permute-done.13 = bf16[64,3584]{1,0:T(8,128)(2,1)S(1)} collective-permute-done((bf16[64,3584]{1,0:T(8,128)(2,1)S(1)}, bf16[64,3584]{1,0:T(8,128)(2,1)S(1)}, u32[]{:S(2)}, u32[]{:S(2)}) %collective-permute-start.13) | collective-permute-done | bytes 458784 | tf_op jit(solution)/shard_map/ppermute | solution.py:43
  127.0 3.5 %collective-permute-start.14 = (bf16[32,3584]{1,0:T(8,128)(2,1)S(1)}, bf16[32,3584]{1,0:T(8,128)(2,1)S(1)}, u32[]{:S(2)}, u32[]{:S(2)}) collective-permute-start(bf16[32,3584]{1,0:T(8,128)(2,1)S(1)} %slice.102), channel_id=1, source_target_pairs={{0,3},{1,2},{2,1},{3,0},{4,7},{5,6},{6,5},{7,4},{8,11},{9,10},{10,... | collective-permute-start | bytes 688136 | tf_op jit(solution)/shard_map/ppermute | solution.py:43
  130.5 10.0 %collective-permute-done.10 = bf16[64,3584]{1,0:T(8,128)(2,1)S(1)} collective-permute-done((bf16[64,3584]{1,0:T(8,128)(2,1)S(1)}, bf16[64,3584]{1,0:T(8,128)(2,1)S(1)}, u32[]{:S(2)}, u32[]{:S(2)}) %collective-permute-start.10) | collective-permute-done | bytes 458784 | tf_op jit(solution)/shard_map/ppermute | solution.py:43
  142.7 3.3 %shard_map.134 = (f32[64,3584]{1,0:T(8,128)S(1)}, bf16[64,3584]{1,0:T(8,128)(2,1)S(1)}, f32[64,3584]{1,0:T(8,128)S(1)}, bf16[64,3584]{1,0:T(8,128)(2,1)S(1)}) custom-call(bf16[64,7168]{1,0:T(8,128)(2,1)S(1)} %constant_dynamic-update-slice_fusion.6.c1, bf16[64,7168]{1,0:T(8,128)(2,1)S(1)} %collective-permute-done.20.qr1, ...), custom_call_target="tpu_custom_call" | custom-call | tf_op jit(solution)/shard_map/pallas_call | solution.py:284
  149.3 3.9 %collective-permute-start.25 = (bf16[64,3584]{1,0:T(8,128)(2,1)S(1)}, bf16[64,3584]{1,0:T(8,128)(2,1)S(1)}, u32[]{:S(2)}, u32[]{:S(2)}) collective-permute-start(bf16[64,3584]{1,0:T(8,128)(2,1)S(1)} %get-tuple-element.34), channel_id=1, source_target_pairs={{0,3},{1,2},{2,1},{3,0},{4,7},{5,6},{6,5},{7,4},{8,11},{9,10},{10,... | collective-permute-start | bytes 1376264 | tf_op jit(solution)/shard_map/ppermute | solution.py:43
  153.3 4.8 %collective-permute-start.15 = (bf16[16,3584]{1,0:T(8,128)(2,1)S(1)}, bf16[16,3584]{1,0:T(8,128)(2,1)S(1)}, u32[]{:S(2)}, u32[]{:S(2)}) collective-permute-start(bf16[16,3584]{1,0:T(8,128)(2,1)S(1)} %get-tuple-element.44), channel_id=1, source_target_pairs={{0,24},{1,25},{2,26},{3,27},{4,12},{5,13},{6,14},{7,15},{8,0},{9,1... | collective-permute-start | bytes 344072 | tf_op jit(solution)/shard_map/ppermute | solution.py:43
  158.1 4.0 %collective-permute-start.16 = (bf16[16,3584]{1,0:T(8,128)(2,1)S(1)}, bf16[16,3584]{1,0:T(8,128)(2,1)S(1)}, u32[]{:S(2)}, u32[]{:S(2)}) collective-permute-start(bf16[16,3584]{1,0:T(8,128)(2,1)S(1)} %get-tuple-element.43), channel_id=1, source_target_pairs={{0,20},{1,21},{2,22},{3,23},{4,16},{5,17},{6,18},{7,19},{8,28},{9,... | collective-permute-start | bytes 344072 | tf_op jit(solution)/shard_map/ppermute | solution.py:43
  169.4 4.4 %collective-permute-done.29 = bf16[32,3584]{1,0:T(8,128)(2,1)S(1)} collective-permute-done((bf16[32,3584]{1,0:T(8,128)(2,1)S(1)}, bf16[32,3584]{1,0:T(8,128)(2,1)S(1)}, u32[]{:S(2)}, u32[]{:S(2)}) %collective-permute-start.29) | collective-permute-done | bytes 229408 | tf_op jit(solution)/shard_map/ppermute | solution.py:43
  173.9 3.8 %collective-permute-start.30 = (bf16[16,3584]{1,0:T(8,128)(2,1)S(1)}, bf16[16,3584]{1,0:T(8,128)(2,1)S(1)}, u32[]{:S(2)}, u32[]{:S(2)}) collective-permute-start(bf16[16,3584]{1,0:T(8,128)(2,1)S(1)} %get-tuple-element.40), channel_id=1, source_target_pairs={{0,24},{1,25},{2,26},{3,27},{4,12},{5,13},{6,14},{7,15},{8,0},{9,1... | collective-permute-start | bytes 344072 | tf_op jit(solution)/shard_map/ppermute | solution.py:43
  177.7 3.6 %collective-permute-start.31 = (bf16[16,3584]{1,0:T(8,128)(2,1)S(1)}, bf16[16,3584]{1,0:T(8,128)(2,1)S(1)}, u32[]{:S(2)}, u32[]{:S(2)}) collective-permute-start(bf16[16,3584]{1,0:T(8,128)(2,1)S(1)} %get-tuple-element.39), channel_id=1, source_target_pairs={{0,20},{1,21},{2,22},{3,23},{4,16},{5,17},{6,18},{7,19},{8,28},{9,... | collective-permute-start | bytes 344072 | tf_op jit(solution)/shard_map/ppermute | solution.py:43
  187.1 15.3 %collective-permute-start.17 = (bf16[24,3584]{1,0:T(8,128)(2,1)S(1)}, bf16[24,3584]{1,0:T(8,128)(2,1)S(1)}, u32[]{:S(2)}, u32[]{:S(2)}) collective-permute-start(bf16[24,3584]{1,0:T(8,128)(2,1)S(1)} %shard_map.132), channel_id=1, source_target_pairs={{0,32},{32,64},{64,96},{96,128},{128,160},{160,192},{192,224},{224... | collective-permute-start | bytes 516104 | tf_op jit(solution)/shard_map/ppermute | solution.py:49
  206.9 4.2 %collective-permute-done.32 = bf16[24,3584]{1,0:T(8,128)(2,1)S(1)} collective-permute-done((bf16[24,3584]{1,0:T(8,128)(2,1)S(1)}, bf16[24,3584]{1,0:T(8,128)(2,1)S(1)}, u32[]{:S(2)}, u32[]{:S(2)}) %collective-permute-start.32) | collective-permute-done | bytes 172064 | tf_op jit(solution)/shard_map/ppermute | solution.py:49
  (114 shorter events, 67.4 us)
Async XLA Ops:
  4.7 66.2 %collective-permute-start.21 = (bf16[16,7168]{1,0:T(8,128)(2,1)S(1)}, bf16[16,7168]{1,0:T(8,128)(2,1)}, u32[]{:S(2)}, u32[]{:S(2)}) collective-permute-start(bf16[16,7168]{1,0:T(8,128)(2,1)S(1)} %get-tuple-element.31), channel_id=1, source_target_pairs={{0,8},{1,9},{2,10},{3,11},{4,28},{5,29},{6,30},{7,31},{8,16},{9,17... | collective-permute-start | bytes 688136 | tf_op jit(solution)/shard_map/ppermute | solution.py:43
  11.3 64.0 %collective-permute-start.22 = (bf16[16,7168]{1,0:T(8,128)(2,1)S(1)}, bf16[16,7168]{1,0:T(8,128)(2,1)S(1)}, u32[]{:S(2)}, u32[]{:S(2)}) collective-permute-start(bf16[16,7168]{1,0:T(8,128)(2,1)S(1)} %get-tuple-element.32), channel_id=1, source_target_pairs={{0,20},{1,21},{2,22},{3,23},{4,16},{5,17},{6,18},{7,19},{8,28},{9,... | collective-permute-start | bytes 688136 | tf_op jit(solution)/shard_map/ppermute | solution.py:43
  18.1 61.1 %collective-permute-start.18 = (bf16[16,7168]{1,0:T(8,128)(2,1)S(1)}, bf16[16,7168]{1,0:T(8,128)(2,1)S(1)}, u32[]{:S(2)}, u32[]{:S(2)}) collective-permute-start(bf16[16,7168]{1,0:T(8,128)(2,1)S(1)} %get-tuple-element.30), channel_id=1, source_target_pairs={{0,28},{1,29},{2,30},{3,31},{4,8},{5,9},{6,10},{7,11},{8,4},{9,5},... | collective-permute-start | bytes 688136 | tf_op jit(solution)/shard_map/ppermute | solution.py:43
  22.8 82.1 %collective-permute-start.7 = (bf16[3584,128]{1,0:T(8,128)(2,1)}, bf16[3584,128]{1,0:T(8,128)(2,1)S(1)}, u32[]{:S(2)}, u32[]{:S(2)}) collective-permute-start(bf16[3584,128]{1,0:T(8,128)(2,1)} %bitcast.15), channel_id=1, source_target_pairs={{0,4},{1,5},{2,6},{3,7},{4,0},{5,1},{6,2},{7,3},{8,12},{9,13},{10,... | collective-permute-start | bytes 2752520 | tf_op jit(solution)/shard_map/ppermute | solution.py:43
  26.0 23.7 %collective-permute-start.3 = (bf16[16,3584]{1,0:T(8,128)(2,1)S(1)}, bf16[16,3584]{1,0:T(8,128)(2,1)S(1)}, u32[]{:S(2)}, u32[]{:S(2)}) collective-permute-start(bf16[16,3584]{1,0:T(8,128)(2,1)S(1)} %get-tuple-element.23), channel_id=1, source_target_pairs={{0,8},{1,9},{2,10},{3,11},{4,28},{5,29},{6,30},{7,31},{8,16},{9,17... | collective-permute-start | bytes 344072 | tf_op jit(solution)/shard_map/ppermute | solution.py:43
  66.3 38.6 %collective-permute-start.8 = (bf16[3584,128]{1,0:T(8,128)(2,1)S(1)}, bf16[3584,128]{1,0:T(8,128)(2,1)S(1)}, u32[]{:S(2)}, u32[]{:S(2)}) collective-permute-start(bf16[3584,128]{1,0:T(8,128)(2,1)S(1)} %bitcast.18), channel_id=1, source_target_pairs={{0,4},{1,5},{2,6},{3,7},{4,0},{5,1},{6,2},{7,3},{8,12},{9,13},{10,... | collective-permute-start | bytes 2752520 | tf_op jit(solution)/shard_map/ppermute | solution.py:43
  70.9 11.1 %collective-permute-start.5 = (bf16[32,3584]{1,0:T(8,128)(2,1)S(1)}, bf16[32,3584]{1,0:T(8,128)(2,1)S(1)}, u32[]{:S(2)}, u32[]{:S(2)}) collective-permute-start(bf16[32,3584]{1,0:T(8,128)(2,1)S(1)} %pad_maximum_fusion.3), channel_id=1, source_target_pairs={{0,3},{1,2},{2,1},{3,0},{4,7},{5,6},{6,5},{7,4},{8,11},{9,10},{10,... | collective-permute-start | bytes 688136 | tf_op jit(solution)/shard_map/ppermute | solution.py:43
  84.8 23.1 %collective-permute-start.9 = (bf16[128,3584]{1,0:T(8,128)(2,1)S(1)}, bf16[128,3584]{1,0:T(8,128)(2,1)S(1)}, u32[]{:S(2)}, u32[]{:S(2)}) collective-permute-start(bf16[128,3584]{1,0:T(8,128)(2,1)S(1)} %bitcast.21), channel_id=1, source_target_pairs={{0,4},{1,5},{2,6},{3,7},{4,0},{5,1},{6,2},{7,3},{8,12},{9,13},{10,... | collective-permute-start | bytes 2752520 | tf_op jit(solution)/shard_map/ppermute | solution.py:43
  89.6 23.3 %collective-permute-start.19 = (bf16[32,7168]{1,0:T(8,128)(2,1)S(1)}, bf16[32,7168]{1,0:T(8,128)(2,1)S(1)}, u32[]{:S(2)}, u32[]{:S(2)}) collective-permute-start(bf16[32,7168]{1,0:T(8,128)(2,1)S(1)} %pad_maximum_fusion), channel_id=1, source_target_pairs={{0,1},{1,0},{2,3},{3,2},{4,5},{5,4},{6,7},{7,6},{8,9},{9,8},{10,11... | collective-permute-start | bytes 1376264 | tf_op jit(solution)/shard_map/ppermute | solution.py:43
  102.9 39.8 %collective-permute-start.24 = (bf16[64,7168]{1,0:T(8,128)(2,1)S(1)}, bf16[64,7168]{1,0:T(8,128)(2,1)S(1)}, u32[]{:S(2)}, u32[]{:S(2)}) collective-permute-start(bf16[64,7168]{1,0:T(8,128)(2,1)S(1)} %constant_dynamic-update-slice_fusion.9.c2), channel_id=1, source_target_pairs={{0,1},{1,0},{2,3},{3,2},{4,5},{5,4},{6,7},{7,6},{8,9},{9,8},{10,11... | collective-permute-start | bytes 2752520 | tf_op jit(solution)/shard_map/ppermute | solution.py:43
  109.6 17.3 %collective-permute-start.13 = (bf16[64,3584]{1,0:T(8,128)(2,1)S(1)}, bf16[64,3584]{1,0:T(8,128)(2,1)S(1)}, u32[]{:S(2)}, u32[]{:S(2)}) collective-permute-start(bf16[64,3584]{1,0:T(8,128)(2,1)S(1)} %get-tuple-element.28), channel_id=1, source_target_pairs={{0,1},{1,0},{2,3},{3,2},{4,5},{5,4},{6,7},{7,6},{8,9},{9,8},{10,11... | collective-permute-start | bytes 1376264 | tf_op jit(solution)/shard_map/ppermute | solution.py:43
  112.9 29.8 %collective-permute-start.20 = (bf16[64,7168]{1,0:T(8,128)(2,1)S(1)}, bf16[64,7168]{1,0:T(8,128)(2,1)S(1)}, u32[]{:S(2)}, u32[]{:S(2)}) collective-permute-start(bf16[64,7168]{1,0:T(8,128)(2,1)S(1)} %constant_dynamic-update-slice_fusion.6.c1), channel_id=1, source_target_pairs={{0,3},{1,2},{2,1},{3,0},{4,7},{5,6},{6,5},{7,4},{8,11},{9,10},{10,... | collective-permute-start | bytes 2752520 | tf_op jit(solution)/shard_map/ppermute | solution.py:43
  116.6 23.9 %collective-permute-start.10 = (bf16[64,3584]{1,0:T(8,128)(2,1)S(1)}, bf16[64,3584]{1,0:T(8,128)(2,1)S(1)}, u32[]{:S(2)}, u32[]{:S(2)}) collective-permute-start(bf16[64,3584]{1,0:T(8,128)(2,1)S(1)} %get-tuple-element.26), channel_id=1, source_target_pairs={{0,3},{1,2},{2,1},{3,0},{4,7},{5,6},{6,5},{7,4},{8,11},{9,10},{10,... | collective-permute-start | bytes 1376264 | tf_op jit(solution)/shard_map/ppermute | solution.py:43
  127.0 26.2 %collective-permute-start.14 = (bf16[32,3584]{1,0:T(8,128)(2,1)S(1)}, bf16[32,3584]{1,0:T(8,128)(2,1)S(1)}, u32[]{:S(2)}, u32[]{:S(2)}) collective-permute-start(bf16[32,3584]{1,0:T(8,128)(2,1)S(1)} %slice.102), channel_id=1, source_target_pairs={{0,3},{1,2},{2,1},{3,0},{4,7},{5,6},{6,5},{7,4},{8,11},{9,10},{10,... | collective-permute-start | bytes 688136 | tf_op jit(solution)/shard_map/ppermute | solution.py:43
  140.6 21.4 %collective-permute-start.11 = (bf16[32,3584]{1,0:T(8,128)(2,1)S(1)}, bf16[32,3584]{1,0:T(8,128)(2,1)S(1)}, u32[]{:S(2)}, u32[]{:S(2)}) collective-permute-start(bf16[32,3584]{1,0:T(8,128)(2,1)S(1)} %slice.103), channel_id=1, source_target_pairs={{0,1},{1,0},{2,3},{3,2},{4,5},{5,4},{6,7},{7,6},{8,9},{9,8},{10,11... | collective-permute-start | bytes 688136 | tf_op jit(solution)/shard_map/ppermute | solution.py:43
  146.1 18.0 %collective-permute-start.28 = (bf16[64,3584]{1,0:T(8,128)(2,1)S(1)}, bf16[64,3584]{1,0:T(8,128)(2,1)S(1)}, u32[]{:S(2)}, u32[]{:S(2)}) collective-permute-start(bf16[64,3584]{1,0:T(8,128)(2,1)S(1)} %get-tuple-element.36), channel_id=1, source_target_pairs={{0,1},{1,0},{2,3},{3,2},{4,5},{5,4},{6,7},{7,6},{8,9},{9,8},{10,11... | collective-permute-start | bytes 1376264 | tf_op jit(solution)/shard_map/ppermute | solution.py:43
  149.3 18.0 %collective-permute-start.25 = (bf16[64,3584]{1,0:T(8,128)(2,1)S(1)}, bf16[64,3584]{1,0:T(8,128)(2,1)S(1)}, u32[]{:S(2)}, u32[]{:S(2)}) collective-permute-start(bf16[64,3584]{1,0:T(8,128)(2,1)S(1)} %get-tuple-element.34), channel_id=1, source_target_pairs={{0,3},{1,2},{2,1},{3,0},{4,7},{5,6},{6,5},{7,4},{8,11},{9,10},{10,... | collective-permute-start | bytes 1376264 | tf_op jit(solution)/shard_map/ppermute | solution.py:43
  153.3 28.1 %collective-permute-start.15 = (bf16[16,3584]{1,0:T(8,128)(2,1)S(1)}, bf16[16,3584]{1,0:T(8,128)(2,1)S(1)}, u32[]{:S(2)}, u32[]{:S(2)}) collective-permute-start(bf16[16,3584]{1,0:T(8,128)(2,1)S(1)} %get-tuple-element.44), channel_id=1, source_target_pairs={{0,24},{1,25},{2,26},{3,27},{4,12},{5,13},{6,14},{7,15},{8,0},{9,1... | collective-permute-start | bytes 344072 | tf_op jit(solution)/shard_map/ppermute | solution.py:43
  158.1 27.3 %collective-permute-start.16 = (bf16[16,3584]{1,0:T(8,128)(2,1)S(1)}, bf16[16,3584]{1,0:T(8,128)(2,1)S(1)}, u32[]{:S(2)}, u32[]{:S(2)}) collective-permute-start(bf16[16,3584]{1,0:T(8,128)(2,1)S(1)} %get-tuple-element.43), channel_id=1, source_target_pairs={{0,20},{1,21},{2,22},{3,23},{4,16},{5,17},{6,18},{7,19},{8,28},{9,... | collective-permute-start | bytes 344072 | tf_op jit(solution)/shard_map/ppermute | solution.py:43
  162.1 23.3 %collective-permute-start.12 = (bf16[16,3584]{1,0:T(8,128)(2,1)S(1)}, bf16[16,3584]{1,0:T(8,128)(2,1)S(1)}, u32[]{:S(2)}, u32[]{:S(2)}) collective-permute-start(bf16[16,3584]{1,0:T(8,128)(2,1)S(1)} %get-tuple-element.45), channel_id=1, source_target_pairs={{0,28},{1,29},{2,30},{3,31},{4,8},{5,9},{6,10},{7,11},{8,4},{9,5},... | collective-permute-start | bytes 344072 | tf_op jit(solution)/shard_map/ppermute | solution.py:43
  173.9 28.6 %collective-permute-start.30 = (bf16[16,3584]{1,0:T(8,128)(2,1)S(1)}, bf16[16,3584]{1,0:T(8,128)(2,1)S(1)}, u32[]{:S(2)}, u32[]{:S(2)}) collective-permute-start(bf16[16,3584]{1,0:T(8,128)(2,1)S(1)} %get-tuple-element.40), channel_id=1, source_target_pairs={{0,24},{1,25},{2,26},{3,27},{4,12},{5,13},{6,14},{7,15},{8,0},{9,1... | collective-permute-start | bytes 344072 | tf_op jit(solution)/shard_map/ppermute | solution.py:43
  177.7 24.8 %collective-permute-start.31 = (bf16[16,3584]{1,0:T(8,128)(2,1)S(1)}, bf16[16,3584]{1,0:T(8,128)(2,1)S(1)}, u32[]{:S(2)}, u32[]{:S(2)}) collective-permute-start(bf16[16,3584]{1,0:T(8,128)(2,1)S(1)} %get-tuple-element.39), channel_id=1, source_target_pairs={{0,20},{1,21},{2,22},{3,23},{4,16},{5,17},{6,18},{7,19},{8,28},{9,... | collective-permute-start | bytes 344072 | tf_op jit(solution)/shard_map/ppermute | solution.py:43
  181.4 21.1 %collective-permute-start.27 = (bf16[16,3584]{1,0:T(8,128)(2,1)S(1)}, bf16[16,3584]{1,0:T(8,128)(2,1)S(1)}, u32[]{:S(2)}, u32[]{:S(2)}) collective-permute-start(bf16[16,3584]{1,0:T(8,128)(2,1)S(1)} %get-tuple-element.41), channel_id=1, source_target_pairs={{0,28},{1,29},{2,30},{3,31},{4,8},{5,9},{6,10},{7,11},{8,4},{9,5},... | collective-permute-start | bytes 344072 | tf_op jit(solution)/shard_map/ppermute | solution.py:43
  187.1 19.2 %collective-permute-start.17 = (bf16[24,3584]{1,0:T(8,128)(2,1)S(1)}, bf16[24,3584]{1,0:T(8,128)(2,1)S(1)}, u32[]{:S(2)}, u32[]{:S(2)}) collective-permute-start(bf16[24,3584]{1,0:T(8,128)(2,1)S(1)} %shard_map.132), channel_id=1, source_target_pairs={{0,32},{32,64},{64,96},{96,128},{128,160},{160,192},{192,224},{224... | collective-permute-start | bytes 516104 | tf_op jit(solution)/shard_map/ppermute | solution.py:49
  (22 other events, 243.9 us)

commit v2 on v1

--- a/solution.py
+++ b/solution.py
@@ -1,5 +1,3 @@
-import functools
-
 import jax
 import jax.numpy as jnp
 from jax import lax
@@ -83,63 +81,92 @@
     return out
 
 
-def normalized(x, gain):
+def normalized(x):
     values = x.astype(F32)
     scale = lax.rsqrt(jnp.mean(values * values, axis=-1, keepdims=True) + 1e-06)
     return values * scale, scale
 
 
-def pack_kernel(info_ref, x_ref, route_ref, gain_ref, *rest):
-    masks = slot_masks(info_ref, route_ref)
-    place = (masks[0][0] | masks[1][0]).astype(F32).astype(BF16)
-    unit, _ = normalized(x_ref[...], gain_ref[...])
-    normed = (unit * gain_ref[...]).astype(BF16)
-    sources = [normed]
-    if len(rest) == 5:
-        sources.append(rest[0][...])
-    outs = rest[-4:]
-    width = x_ref.shape[1]
-    for i, rows in enumerate(sources):
+def pack_kernel(info_ref, xa_ref, ra_ref, xb_ref, rb_ref, cot_ref, gain_ref, *outs):
+    width = xa_ref.shape[1]
+    places = []
+    for route_ref in (ra_ref, rb_ref):
+        masks = slot_masks(info_ref, route_ref)
+        places.append((masks[0][0] | masks[1][0]).astype(F32).astype(BF16))
+    gain = gain_ref[...]
+    normed_a = (normalized(xa_ref[...])[0] * gain).astype(BF16)
+    normed_b = (normalized(xb_ref[...])[0] * gain).astype(BF16)
+    sources = ((places[0], normed_a), (places[1], normed_b), (places[1], cot_ref[...]))
+    for i, (place, rows) in enumerate(sources):
         packed = lax.dot_general(place, rows, TN, preferred_element_type=F32).astype(BF16)
         for j in range(4):
             outs[j][:, i * width : (i + 1) * width] = packed[j * SLOT : (j + 1) * SLOT]
 
 
+def merge_kernel(wg, wu, wd, out, sems):
+    width, units = wg.shape
+    copies = [
+        pltpu.make_async_copy(wg, out.at[pl.ds(0, width)], sems.at[0]),
+        pltpu.make_async_copy(wu, out.at[pl.ds(width, width)], sems.at[1]),
+    ]
+    for i in range(width // units):
+        to = out.at[pl.ds(2 * width + i * units, units)]
+        copies.append(pltpu.make_async_copy(wd.at[:, pl.ds(i * units, units)], to, sems.at[2 + i]))
+    for copy in copies:
+        copy.start()
+    for copy in copies:
+        copy.wait()
+
+
 def hidden(rows, wg, wu):
     both = jnp.dot(rows, jnp.concatenate([wg, wu], axis=1), preferred_element_type=F32)
     return both[:, :128], both[:, 128:]
 
 
-def fwd_kernel(c1, qr1, c2, pr2, wg, wu, wd, vg, vu, vd, keep1, send1, keep2, send2, rows):
-    for i, ref in enumerate((c1, qr1, c2, pr2)):
-        rows[64 * i : 64 * (i + 1), :] = ref[...]
+def down_columns(merged, at, count):
+    width = merged.shape[0] // 3
+    starts = range(2 * width + at, 2 * width + at + count, 128)
+    return jnp.concatenate([merged[start : start + 128, :] for start in starts], axis=1)
+
+
+def gather_rows(refs, at, width, scratch):
+    cols = slice(at, at + width)
+    places = ((0, 64), (128, 192), (32, 160), (96, 224))
+    for ref, (one, two) in zip(refs, places):
+        scratch[one : one + 32, :] = ref[0:32, cols]
+        scratch[two : two + 32, :] = ref[32:64, cols]
+
+
+def fwd_kernel(c1, qr1, c2, pr2, wg, wu, wd, other, keep, send, rows):
+    width = rows.shape[1]
+    gather_rows((c1, qr1, c2, pr2), 0, width, rows)
     inner = []
-    for g_ref, u_ref in ((wg, wu), (vg, vu)):
-        gate, up = hidden(rows[...], g_ref[...], u_ref[...])
+    for weights in ((wg[...], wu[...]), (other[0:width, :], other[width : 2 * width, :])):
+        gate, up = hidden(rows[...], *weights)
         inner.append((gate * jax.nn.sigmoid(gate) * up).astype(BF16))
     inner = jnp.concatenate(inner, axis=1)
-    width = rows.shape[1]
     step = 512
     for at in range(0, width, step):
         cols = slice(at, at + step)
-        down = jnp.concatenate([wd[:, cols], vd[:, cols]], axis=0)
+        down = jnp.concatenate([wd[:, cols], down_columns(other, at, step)], axis=0)
         part = jnp.dot(inner, down, preferred_element_type=F32)
-        keep1[:, cols] = part[0:64]
-        send1[:, cols] = part[64:128].astype(BF16)
-        keep2[:, cols] = part[128:192]
-        send2[:, cols] = part[192:256].astype(BF16)
-
-
-def bwd_kernel(c1, qr1, c2, pr2, wg, wu, wd, vg, vu, vd, keep1, send1, keep2, send2, rows, cots):
+        keep[:, cols] = part[0:128]
+        send[:, cols] = part[128:256].astype(BF16)
+
+
+def bwd_kernel(c1, qr1, c2, pr2, wg, wu, wd, other, keep, send, rows, cots):
     width = rows.shape[1]
-    for i, ref in enumerate((c1, qr1, c2, pr2)):
-        rows[64 * i : 64 * (i + 1), :] = ref[:, :width]
-        cots[64 * i : 64 * (i + 1), :] = ref[:, width:]
+    gather_rows((c1, qr1, c2, pr2), width, width, rows)
+    gather_rows((c1, qr1, c2, pr2), 2 * width, width, cots)
     back = []
     products = None
-    for g_ref, u_ref, d_ref in ((wg, wu, wd), (vg, vu, vd)):
-        gate, up = hidden(rows[...], g_ref[...], u_ref[...])
-        d_inner = lax.dot_general(cots[...], d_ref[...], NT, preferred_element_type=F32)
+    sources = (
+        (wg[...], wu[...], wd[...]),
+        (other[0:width, :], other[width : 2 * width, :], down_columns(other, 0, width)),
+    )
+    for gate_w, up_w, down_w in sources:
+        gate, up = hidden(rows[...], gate_w, up_w)
+        d_inner = lax.dot_general(cots[...], down_w, NT, preferred_element_type=F32)
         sig = jax.nn.sigmoid(gate)
         silu = gate * sig
         inner = (silu * up).astype(BF16).astype(F32)
@@ -165,17 +192,21 @@
     step = 512
     for at in range(0, width, step):
         cols = slice(at, at + step)
+        there = slice(width + at, width + at + step)
+        weights = (
+            jnp.concatenate([wg[cols, :], wu[cols, :]], axis=1),
+            jnp.concatenate([other[cols, :], other[there, :]], axis=1),
+        )
         part = None
-        for grad, g_ref, u_ref in ((back[0], wg, wu), (back[1], vg, vu)):
-            weight = jnp.concatenate([g_ref[cols, :], u_ref[cols, :]], axis=1)
+        for grad, weight in zip(back, weights):
             term = lax.dot_general(grad, weight, NT, preferred_element_type=F32)
             part = term if part is None else part + term
         if at == 0:
             part = jnp.concatenate([part[:, :128] + grad_rows, part[:, 128:]], axis=1)
-        keep1[:, cols] = part[0:64]
-        send1[:, cols] = part[64:128].astype(BF16)
-        keep2[:, cols] = part[128:192]
-        send2[:, cols] = part[192:256].astype(BF16)
+        keep[0:64, cols] = part[0:64]
+        send[0:64, cols] = part[64:128].astype(BF16)
+        keep[64:128, cols] = part[128:192]
+        send[64:128, cols] = part[192:256].astype(BF16)
 
 
 def mixed_rows(masks, weight_ref, parts):
@@ -209,7 +240,7 @@
     masks = slot_masks(info_ref, route_ref)
     parts = [own[...], a[...], b[...], c[...]]
     d_normed = mixed_rows(masks, weight_ref, parts)
-    unit, scale = normalized(x_ref[...], gain_ref[...])
+    unit, scale = normalized(x_ref[...])
     q_term = d_normed * gain_ref[...]
     mean = jnp.mean(q_term * unit, axis=-1, keepdims=True)
     d_input = cot_ref[...].astype(F32) + scale * (q_term - unit * mean)
@@ -238,17 +269,12 @@
     return c1, hop(c1, HOP_X3), c2, hop(c2, HOP_X1)
 
 
-def return_rows(keep1, send1, keep2, send2):
-    sum1 = keep1 + hop(send1, HOP_X3).astype(F32)
-    sum2 = keep2 + hop(send2, HOP_X1).astype(F32)
-    full1 = sum1[:32] + hop(sum1[32:].astype(BF16), HOP_X1).astype(F32)
-    full2 = sum2[:32] + hop(sum2[32:].astype(BF16), HOP_X3).astype(F32)
-    full1 = full1.astype(BF16)
-    full2 = full2.astype(BF16)
-    back_a = hop(full1[SLOT:], HOP_A)
-    back_b = hop(full2[:SLOT], HOP_B_BACK)
-    back_c = hop(full2[SLOT:], HOP_C)
-    return full1[:SLOT], back_a, back_b, back_c
+def return_rows(keep, send, first, second):
+    total = keep + hop(send, first).astype(F32)
+    whole = total[:64] + hop(total[64:].astype(BF16), second).astype(F32)
+    whole = whole.astype(BF16)
+    own, a, b, c = (whole[j * SLOT : (j + 1) * SLOT] for j in range(4))
+    return own, hop(a, HOP_A), hop(b, HOP_B_BACK), hop(c, HOP_C)
 
 
 def body(
@@ -268,26 +294,32 @@
     index = lax.axis_index("expert")
     z = index // GRID_X
     info = jnp.stack([z // 2, z % 2]).astype(jnp.int32)
-    wg, wu, wd = w_gate[0, 0], w_up[0, 0], w_down[0, 0]
-    wide = [((SLOT, width), BF16)] * 4
-    sent_a = kernel_call(pack_kernel, wide, 3)(info, act_fwd[0], route_fwd[0], norm_gain)
-    wide = [((SLOT, 2 * width), BF16)] * 4
-    sent_b = kernel_call(pack_kernel, wide, 4)(
-        info, act_bwd[0], route_bwd[0], norm_gain, cot_bwd[0]
-    )
-    rows_a = spread_rows(*sent_a)
-    weights = (wg, wu, wd, hop(wg, HOP_W), hop(wu, HOP_W), hop(wd, HOP_W))
-    rows_b = spread_rows(*sent_b)
-    outs = [((64, width), F32), ((64, width), BF16)] * 2
+    weights = (w_gate[0, 0], w_up[0, 0], w_down[0, 0])
+    units = w_down.shape[2]
+    hbm = pl.BlockSpec(memory_space=pl.ANY)
+    merged = pl.pallas_call(
+        merge_kernel,
+        out_shape=jax.ShapeDtypeStruct((3 * width, units), BF16),
+        in_specs=[hbm] * 3,
+        out_specs=hbm,
+        scratch_shapes=[pltpu.SemaphoreType.DMA((2 + width // units,))],
+    )(*weights)
+    other = hop(merged, HOP_W)
+    wide = [((SLOT, 3 * width), BF16)] * 4
+    sent = kernel_call(pack_kernel, wide, 6)(
+        info, act_fwd[0], route_fwd[0], act_bwd[0], route_bwd[0], cot_bwd[0], norm_gain
+    )
+    rows = spread_rows(*sent)
+    outs = [((128, width), F32), ((128, width), BF16)]
     scratch = pltpu.VMEM((256, width), BF16)
-    parts_a = kernel_call(fwd_kernel, outs, 10, [scratch], info=False)(*rows_a, *weights)
-    parts_b = kernel_call(bwd_kernel, outs, 10, [scratch] * 2, info=False)(*rows_b, *weights)
-    back_a = return_rows(*parts_a)
+    part_a = kernel_call(fwd_kernel, outs, 8, [scratch], info=False)(*rows, *weights, other)
+    part_b = kernel_call(bwd_kernel, outs, 8, [scratch] * 2, info=False)(*rows, *weights, other)
+    back_a = return_rows(*part_a, HOP_X3, HOP_X1)
+    back_b = return_rows(*part_b, HOP_X1, HOP_X3)
     (layer_out,) = kernel_call(fwd_out_kernel, [((tokens, width), BF16)], 7)(
         info, act_fwd[0], route_fwd[0], weight_fwd[0], *back_a
     )
     act_next = shifted(layer_out, "section", 1)
-    back_b = return_rows(*parts_b)
     d_input, gate_grad = kernel_call(
         bwd_out_kernel, [((tokens, width), BF16), ((tokens, 2), BF16)], 9
     )(info, act_bwd[0], route_bwd[0], weight_bwd[0], cot_bwd[0], norm_gain, *back_b)

time: 215 us -> 254 us (1.18)
  Pallas kernels: 11.1 us -> 94.8 us
  starting transfers between devices: 125 us -> 76.8 us
  waiting for transfers between devices: 66.3 us -> 71.4 us
    pallas_call x4, Pallas kernels: 7.52 us -> 91.2 us  [the longest x1 84.8 us: body(): pl.pallas_call(merge_kernel, out_shape=jax.ShapeDtypeStruct((3 * width, u...]
    ppermute x31 -> x18, starting transfers between devices: 108 us -> 65.8 us  [hop(): return lax.ppermute(value, 'expert', pairs)]
    ppermute x31 -> x18, waiting for transfers between devices: 62.2 us -> 69.7 us  [hop(): return lax.ppermute(value, 'expert', pairs)]
    ppermute x2, starting transfers between devices: 17.2 us -> 11.1 us  [shifted(): return lax.ppermute(value, axis, pairs)]
    unnamed x36 -> x32, local copies, waits for them, and re-layouts: 5.61 us -> 4.96 us
  transfers between devices with their start and end apart: 33 -> 20, of which waited for: 11 -> 9; matrix products, arithmetic and copies ran while one was open for 2% -> 1% of each run, Pallas kernels for 5% -> 36%
where the time goes in v2:
time: 254 us; the launch traced here: 252 us
  Pallas kernels  94.8 us (37%)
  starting transfers between devices  76.8 us (30%)
  waiting for transfers between devices  71.4 us (28%)
  local copies, waits for them, and re-layouts  7.5 us (3%)
    pallas_call x1, Pallas kernels, body(): pl.pallas_call(merge_kernel, out_shape=jax.ShapeDtypeStruct((3 * width, u...  84.8 us
    ppermute x18, waiting for transfers between devices, hop(): return lax.ppermute(value, 'expert', pairs)  69.7 us
    ppermute x18, starting transfers between devices, hop(): return lax.ppermute(value, 'expert', pairs)  65.8 us
    ppermute x2, starting transfers between devices, shifted(): return lax.ppermute(value, axis, pairs)  11.1 us
  transfers between devices with their start and end apart: 20, of which 9 were waited for; matrix products, arithmetic and copies ran while one was open for 1% of the time, Pallas kernels for 36%

profile of v2, /device:TPU:1, one launch (start us, length us, event | category | flops | bytes accessed | tf_op | source)
XLA Modules:
  0.0 252.5 jit_solution(6980573659828746187)
XLA Ops:
  7.2 6.6 %collective-permute-start.3 = (bf16[16,10752]{1,0:T(8,128)(2,1)S(1)}, bf16[16,10752]{1,0:T(8,128)(2,1)S(1)}, u32[]{:S(2)}, u32[]{:S(2)}) collective-permute-start(bf16[16,10752]{1,0:T(8,128)(2,1)S(1)} %get-tuple-element.15), channel_id=1, source_target_pairs={{0,8},{1,9},{2,10},{3,11},{4,28},{5,29},{6,30},{7,31},{8,16},{9,17... | collective-permute-start | bytes 1032200 | tf_op jit(solution)/shard_map/ppermute | solution.py:41
  13.8 6.8 %collective-permute-start.4 = (bf16[16,10752]{1,0:T(8,128)(2,1)S(1)}, bf16[16,10752]{1,0:T(8,128)(2,1)S(1)}, u32[]{:S(2)}, u32[]{:S(2)}) collective-permute-start(bf16[16,10752]{1,0:T(8,128)(2,1)S(1)} %get-tuple-element.16), channel_id=1, source_target_pairs={{0,20},{1,21},{2,22},{3,23},{4,16},{5,17},{6,18},{7,19},{8,28},{9,... | collective-permute-start | bytes 1032200 | tf_op jit(solution)/shard_map/ppermute | solution.py:41
  20.6 4.6 %collective-permute-start = (bf16[16,10752]{1,0:T(8,128)(2,1)S(1)}, bf16[16,10752]{1,0:T(8,128)(2,1)S(1)}, u32[]{:S(2)}, u32[]{:S(2)}) collective-permute-start(bf16[16,10752]{1,0:T(8,128)(2,1)S(1)} %get-tuple-element.14), channel_id=1, source_target_pairs={{0,28},{1,29},{2,30},{3,31},{4,8},{5,9},{6,10},{7,11},{8,4},{9,5},... | collective-permute-start | bytes 1032200 | tf_op jit(solution)/shard_map/ppermute | solution.py:41
  25.2 84.8 %shard_map.131 = bf16[10752,128]{1,0:T(8,128)(2,1)} custom-call(bf16[3584,128]{1,0:T(8,128)(2,1)} %bitcast.15, bf16[3584,128]{1,0:T(8,128)(2,1)} %bitcast.18, bf16[128,3584]{1,0:T(8,128)(2,1)} %bitcast.21), custom_call_target="tpu_custom_call" | custom-call | tf_op jit(solution)/shard_map/pallas_call | solution.py:300
  112.0 4.4 %collective-permute-start.5 = (bf16[32,10752]{1,0:T(8,128)(2,1)S(1)}, bf16[32,10752]{1,0:T(8,128)(2,1)S(1)}, u32[]{:S(2)}, u32[]{:S(2)}) collective-permute-start(bf16[32,10752]{1,0:T(8,128)(2,1)S(1)} %pad_maximum_fusion.1), channel_id=1, source_target_pairs={{0,3},{1,2},{2,1},{3,0},{4,7},{5,6},{6,5},{7,4},{8,11},{9,10},{10,... | collective-permute-start | bytes 2064392 | tf_op jit(solution)/shard_map/ppermute | solution.py:41
  116.4 1.9 collective-permute-start.1
  118.5 11.7 %collective-permute-done.5 = bf16[32,10752]{1,0:T(8,128)(2,1)S(1)} collective-permute-done((bf16[32,10752]{1,0:T(8,128)(2,1)S(1)}, bf16[32,10752]{1,0:T(8,128)(2,1)S(1)}, u32[]{:S(2)}, u32[]{:S(2)}) %collective-permute-start.5) | collective-permute-done | bytes 688160 | tf_op jit(solution)/shard_map/ppermute | solution.py:41
  133.2 3.4 %collective-permute-start.2 = (bf16[64,10752]{1,0:T(8,128)(2,1)S(1)}, bf16[64,10752]{1,0:T(8,128)(2,1)S(1)}, u32[]{:S(2)}, u32[]{:S(2)}) collective-permute-start(bf16[64,10752]{1,0:T(8,128)(2,1)S(1)} %constant_dynamic-update-slice_fusion.c1), channel_id=1, source_target_pairs={{0,3},{1,2},{2,1},{3,0},{4,7},{5,6},{6,5},{7,4},{8,11},{9,10},{10,... | collective-permute-start | bytes 4128776 | tf_op jit(solution)/shard_map/ppermute | solution.py:41
  136.7 26.3 %collective-permute-done.6.pr2 = bf16[64,10752]{1,0:T(8,128)(2,1)S(1)} collective-permute-done((bf16[64,10752]{1,0:T(8,128)(2,1)S(1)}, bf16[64,10752]{1,0:T(8,128)(2,1)S(1)}, u32[]{:S(2)}, u32[]{:S(2)}) %collective-permute-start.6) | collective-permute-done | bytes 1376288 | tf_op jit(solution)/shard_map/ppermute | solution.py:41
  164.2 7.4 %collective-permute-done.7.other = bf16[10752,128]{1,0:T(8,128)(2,1)S(1)} collective-permute-done((bf16[10752,128]{1,0:T(8,128)(2,1)}, bf16[10752,128]{1,0:T(8,128)(2,1)S(1)}, u32[]{:S(2)}, u32[]{:S(2)}) %collective-permute-start.7) | collective-permute-done | bytes 2752544 | tf_op jit(solution)/shard_map/ppermute | solution.py:41
  171.7 3.3 %shard_map.134 = (f32[128,3584]{1,0:T(8,128)S(1)}, bf16[128,3584]{1,0:T(8,128)(2,1)S(1)}) custom-call(bf16[64,10752]{1,0:T(8,128)(2,1)S(1)} %constant_dynamic-update-slice_fusion.c1, bf16[64,10752]{1,0:T(8,128)(2,1)S(1)} %collective-permute-done.2.qr1, bf16[64,10752]{1,0:T(8,128)(2,1)S(1)} %constant_dynamic-update-slice_fusion.3.c2, ...), custom_call_target="tpu_custom_call" | custom-call | tf_op jit(solution)/shard_map/pallas_call | solution.py:316
  175.0 3.1 %collective-permute-start.14 = (bf16[128,3584]{1,0:T(8,128)(2,1)S(1)}, bf16[128,3584]{1,0:T(8,128)(2,1)S(1)}, u32[]{:S(2)}, u32[]{:S(2)}) collective-permute-start(bf16[128,3584]{1,0:T(8,128)(2,1)S(1)} %get-tuple-element.20), channel_id=1, source_target_pairs={{0,1},{1,0},{2,3},{3,2},{4,5},{5,4},{6,7},{7,6},{8,9},{9,8},{10,11... | collective-permute-start | bytes 2752520 | tf_op jit(solution)/shard_map/ppermute | solution.py:41
  179.8 3.7 %collective-permute-start.8 = (bf16[128,3584]{1,0:T(8,128)(2,1)S(1)}, bf16[128,3584]{1,0:T(8,128)(2,1)S(1)}, u32[]{:S(2)}, u32[]{:S(2)}) collective-permute-start(bf16[128,3584]{1,0:T(8,128)(2,1)S(1)} %get-tuple-element.18), channel_id=1, source_target_pairs={{0,3},{1,2},{2,1},{3,0},{4,7},{5,6},{6,5},{7,4},{8,11},{9,10},{10,... | collective-permute-start | bytes 2752520 | tf_op jit(solution)/shard_map/ppermute | solution.py:41
  183.6 12.8 %collective-permute-done.14 = bf16[128,3584]{1,0:T(8,128)(2,1)S(1)} collective-permute-done((bf16[128,3584]{1,0:T(8,128)(2,1)S(1)}, bf16[128,3584]{1,0:T(8,128)(2,1)S(1)}, u32[]{:S(2)}, u32[]{:S(2)}) %collective-permute-start.14) | collective-permute-done | bytes 917536 | tf_op jit(solution)/shard_map/ppermute | solution.py:41
  196.6 4.4 %collective-permute-start.15 = (bf16[64,3584]{1,0:T(8,128)(2,1)S(1)}, bf16[64,3584]{1,0:T(8,128)(2,1)S(1)}, u32[]{:S(2)}, u32[]{:S(2)}) collective-permute-start(bf16[64,3584]{1,0:T(8,128)(2,1)S(1)} %slice.70), channel_id=1, source_target_pairs={{0,3},{1,2},{2,1},{3,0},{4,7},{5,6},{6,5},{7,4},{8,11},{9,10},{10,... | collective-permute-start | bytes 1376264 | tf_op jit(solution)/shard_map/ppermute | solution.py:41
  204.2 8.0 %collective-permute-done.15 = bf16[64,3584]{1,0:T(8,128)(2,1)S(1)} collective-permute-done((bf16[64,3584]{1,0:T(8,128)(2,1)S(1)}, bf16[64,3584]{1,0:T(8,128)(2,1)S(1)}, u32[]{:S(2)}, u32[]{:S(2)}) %collective-permute-start.15) | collective-permute-done | bytes 458784 | tf_op jit(solution)/shard_map/ppermute | solution.py:41
  212.4 2.5 collective-permute-start.16
  214.9 4.4 %collective-permute-start.17 = (bf16[16,3584]{1,0:T(8,128)(2,1)S(1)}, bf16[16,3584]{1,0:T(8,128)(2,1)S(1)}, u32[]{:S(2)}, u32[]{:S(2)}) collective-permute-start(bf16[16,3584]{1,0:T(8,128)(2,1)S(1)} %get-tuple-element.24), channel_id=1, source_target_pairs={{0,24},{1,25},{2,26},{3,27},{4,12},{5,13},{6,14},{7,15},{8,0},{9,1... | collective-permute-start | bytes 344072 | tf_op jit(solution)/shard_map/ppermute | solution.py:41
  219.3 3.8 %collective-permute-start.18 = (bf16[16,3584]{1,0:T(8,128)(2,1)S(1)}, bf16[16,3584]{1,0:T(8,128)(2,1)S(1)}, u32[]{:S(2)}, u32[]{:S(2)}) collective-permute-start(bf16[16,3584]{1,0:T(8,128)(2,1)S(1)} %get-tuple-element.23), channel_id=1, source_target_pairs={{0,20},{1,21},{2,22},{3,23},{4,16},{5,17},{6,18},{7,19},{8,28},{9,... | collective-permute-start | bytes 344072 | tf_op jit(solution)/shard_map/ppermute | solution.py:41
  223.3 2.5 collective-permute-start.10
  225.8 4.4 %collective-permute-start.11 = (bf16[16,3584]{1,0:T(8,128)(2,1)S(1)}, bf16[16,3584]{1,0:T(8,128)(2,1)S(1)}, u32[]{:S(2)}, u32[]{:S(2)}) collective-permute-start(bf16[16,3584]{1,0:T(8,128)(2,1)S(1)} %get-tuple-element.28), channel_id=1, source_target_pairs={{0,24},{1,25},{2,26},{3,27},{4,12},{5,13},{6,14},{7,15},{8,0},{9,1... | collective-permute-start | bytes 344072 | tf_op jit(solution)/shard_map/ppermute | solution.py:41
  230.1 3.7 %collective-permute-start.12 = (bf16[16,3584]{1,0:T(8,128)(2,1)S(1)}, bf16[16,3584]{1,0:T(8,128)(2,1)S(1)}, u32[]{:S(2)}, u32[]{:S(2)}) collective-permute-start(bf16[16,3584]{1,0:T(8,128)(2,1)S(1)} %get-tuple-element.27), channel_id=1, source_target_pairs={{0,20},{1,21},{2,22},{3,23},{4,16},{5,17},{6,18},{7,19},{8,28},{9,... | collective-permute-start | bytes 344072 | tf_op jit(solution)/shard_map/ppermute | solution.py:41
  235.9 6.9 %collective-permute-start.19 = (bf16[24,3584]{1,0:T(8,128)(2,1)S(1)}, bf16[24,3584]{1,0:T(8,128)(2,1)S(1)}, u32[]{:S(2)}, u32[]{:S(2)}) collective-permute-start(bf16[24,3584]{1,0:T(8,128)(2,1)S(1)} %get-tuple-element.21), channel_id=1, source_target_pairs={{32,0},{64,32},{96,64},{128,96},{160,128},{192,160},{224,192},{256... | collective-permute-start | bytes 516104 | tf_op jit(solution)/shard_map/ppermute | solution.py:47
  244.6 4.2 %collective-permute-start.13 = (bf16[24,3584]{1,0:T(8,128)(2,1)S(1)}, bf16[24,3584]{1,0:T(8,128)(2,1)S(1)}, u32[]{:S(2)}, u32[]{:S(2)}) collective-permute-start(bf16[24,3584]{1,0:T(8,128)(2,1)S(1)} %shard_map.133), channel_id=1, source_target_pairs={{0,32},{32,64},{64,96},{96,128},{128,160},{160,192},{192,224},{224... | collective-permute-start | bytes 516104 | tf_op jit(solution)/shard_map/ppermute | solution.py:47
  (72 shorter events, 25.9 us)
Async XLA Ops:
  7.2 104.7 %collective-permute-start.3 = (bf16[16,10752]{1,0:T(8,128)(2,1)S(1)}, bf16[16,10752]{1,0:T(8,128)(2,1)S(1)}, u32[]{:S(2)}, u32[]{:S(2)}) collective-permute-start(bf16[16,10752]{1,0:T(8,128)(2,1)S(1)} %get-tuple-element.15), channel_id=1, source_target_pairs={{0,8},{1,9},{2,10},{3,11},{4,28},{5,29},{6,30},{7,31},{8,16},{9,17... | collective-permute-start | bytes 1032200 | tf_op jit(solution)/shard_map/ppermute | solution.py:41
  13.8 98.1 %collective-permute-start.4 = (bf16[16,10752]{1,0:T(8,128)(2,1)S(1)}, bf16[16,10752]{1,0:T(8,128)(2,1)S(1)}, u32[]{:S(2)}, u32[]{:S(2)}) collective-permute-start(bf16[16,10752]{1,0:T(8,128)(2,1)S(1)} %get-tuple-element.16), channel_id=1, source_target_pairs={{0,20},{1,21},{2,22},{3,23},{4,16},{5,17},{6,18},{7,19},{8,28},{9,... | collective-permute-start | bytes 1032200 | tf_op jit(solution)/shard_map/ppermute | solution.py:41
  20.6 95.8 %collective-permute-start = (bf16[16,10752]{1,0:T(8,128)(2,1)S(1)}, bf16[16,10752]{1,0:T(8,128)(2,1)S(1)}, u32[]{:S(2)}, u32[]{:S(2)}) collective-permute-start(bf16[16,10752]{1,0:T(8,128)(2,1)S(1)} %get-tuple-element.14), channel_id=1, source_target_pairs={{0,28},{1,29},{2,30},{3,31},{4,8},{5,9},{6,10},{7,11},{8,4},{9,5},... | collective-permute-start | bytes 1032200 | tf_op jit(solution)/shard_map/ppermute | solution.py:41
  109.9 61.8 %collective-permute-start.7 = (bf16[10752,128]{1,0:T(8,128)(2,1)}, bf16[10752,128]{1,0:T(8,128)(2,1)S(1)}, u32[]{:S(2)}, u32[]{:S(2)}) collective-permute-start(bf16[10752,128]{1,0:T(8,128)(2,1)} %shard_map.131), channel_id=1, source_target_pairs={{0,4},{1,5},{2,6},{3,7},{4,0},{5,1},{6,2},{7,3},{8,12},{9,13},{10,... | collective-permute-start | bytes 8257544 | tf_op jit(solution)/shard_map/ppermute | solution.py:41
  112.0 18.3 %collective-permute-start.5 = (bf16[32,10752]{1,0:T(8,128)(2,1)S(1)}, bf16[32,10752]{1,0:T(8,128)(2,1)S(1)}, u32[]{:S(2)}, u32[]{:S(2)}) collective-permute-start(bf16[32,10752]{1,0:T(8,128)(2,1)S(1)} %pad_maximum_fusion.1), channel_id=1, source_target_pairs={{0,3},{1,2},{2,1},{3,0},{4,7},{5,6},{6,5},{7,4},{8,11},{9,10},{10,... | collective-permute-start | bytes 2064392 | tf_op jit(solution)/shard_map/ppermute | solution.py:41
  116.4 16.8 %collective-permute-start.1 = (bf16[32,10752]{1,0:T(8,128)(2,1)S(1)}, bf16[32,10752]{1,0:T(8,128)(2,1)S(1)}, u32[]{:S(2)}, u32[]{:S(2)}) collective-permute-start(bf16[32,10752]{1,0:T(8,128)(2,1)S(1)} %pad_maximum_fusion), channel_id=1, source_target_pairs={{0,1},{1,0},{2,3},{3,2},{4,5},{5,4},{6,7},{7,6},{8,9},{9,8},{10,11... | collective-permute-start | bytes 2064392 | tf_op jit(solution)/shard_map/ppermute | solution.py:41
  118.4 53.2 %copy-start = (bf16[1,1,3584,128]{3,2,1,0:T(8,128)(2,1)S(1)}, bf16[1,1,3584,128]{3,2,1,0:T(8,128)(2,1)}, u32[]{:S(2)}) copy-start(bf16[1,1,3584,128]{3,2,1,0:T(8,128)(2,1)} %param.19) | copy-start | bytes 2752516
  118.5 53.2 %copy-start.1 = (bf16[1,1,3584,128]{3,2,1,0:T(8,128)(2,1)S(1)}, bf16[1,1,3584,128]{3,2,1,0:T(8,128)(2,1)}, u32[]{:S(2)}) copy-start(bf16[1,1,3584,128]{3,2,1,0:T(8,128)(2,1)} %param.20) | copy-start | bytes 2752516
  118.5 53.2 %copy-start.2 = (bf16[1,1,128,3584]{3,2,1,0:T(8,128)(2,1)S(1)}, bf16[1,1,128,3584]{3,2,1,0:T(8,128)(2,1)}, u32[]{:S(2)}) copy-start(bf16[1,1,128,3584]{3,2,1,0:T(8,128)(2,1)} %param.21) | copy-start | bytes 2752516
  130.3 32.7 %collective-permute-start.6 = (bf16[64,10752]{1,0:T(8,128)(2,1)S(1)}, bf16[64,10752]{1,0:T(8,128)(2,1)S(1)}, u32[]{:S(2)}, u32[]{:S(2)}) collective-permute-start(bf16[64,10752]{1,0:T(8,128)(2,1)S(1)} %constant_dynamic-update-slice_fusion.3.c2), channel_id=1, source_target_pairs={{0,1},{1,0},{2,3},{3,2},{4,5},{5,4},{6,7},{7,6},{8,9},{9,8},{10,11... | collective-permute-start | bytes 4128776 | tf_op jit(solution)/shard_map/ppermute | solution.py:41
  133.2 31.0 %collective-permute-start.2 = (bf16[64,10752]{1,0:T(8,128)(2,1)S(1)}, bf16[64,10752]{1,0:T(8,128)(2,1)S(1)}, u32[]{:S(2)}, u32[]{:S(2)}) collective-permute-start(bf16[64,10752]{1,0:T(8,128)(2,1)S(1)} %constant_dynamic-update-slice_fusion.c1), channel_id=1, source_target_pairs={{0,3},{1,2},{2,1},{3,0},{4,7},{5,6},{6,5},{7,4},{8,11},{9,10},{10,... | collective-permute-start | bytes 4128776 | tf_op jit(solution)/shard_map/ppermute | solution.py:41
  175.0 21.3 %collective-permute-start.14 = (bf16[128,3584]{1,0:T(8,128)(2,1)S(1)}, bf16[128,3584]{1,0:T(8,128)(2,1)S(1)}, u32[]{:S(2)}, u32[]{:S(2)}) collective-permute-start(bf16[128,3584]{1,0:T(8,128)(2,1)S(1)} %get-tuple-element.20), channel_id=1, source_target_pairs={{0,1},{1,0},{2,3},{3,2},{4,5},{5,4},{6,7},{7,6},{8,9},{9,8},{10,11... | collective-permute-start | bytes 2752520 | tf_op jit(solution)/shard_map/ppermute | solution.py:41
  179.8 22.2 %collective-permute-start.8 = (bf16[128,3584]{1,0:T(8,128)(2,1)S(1)}, bf16[128,3584]{1,0:T(8,128)(2,1)S(1)}, u32[]{:S(2)}, u32[]{:S(2)}) collective-permute-start(bf16[128,3584]{1,0:T(8,128)(2,1)S(1)} %get-tuple-element.18), channel_id=1, source_target_pairs={{0,3},{1,2},{2,1},{3,0},{4,7},{5,6},{6,5},{7,4},{8,11},{9,10},{10,... | collective-permute-start | bytes 2752520 | tf_op jit(solution)/shard_map/ppermute | solution.py:41
  196.6 15.7 %collective-permute-start.15 = (bf16[64,3584]{1,0:T(8,128)(2,1)S(1)}, bf16[64,3584]{1,0:T(8,128)(2,1)S(1)}, u32[]{:S(2)}, u32[]{:S(2)}) collective-permute-start(bf16[64,3584]{1,0:T(8,128)(2,1)S(1)} %slice.70), channel_id=1, source_target_pairs={{0,3},{1,2},{2,1},{3,0},{4,7},{5,6},{6,5},{7,4},{8,11},{9,10},{10,... | collective-permute-start | bytes 1376264 | tf_op jit(solution)/shard_map/ppermute | solution.py:41
  202.3 20.8 %collective-permute-start.9 = (bf16[64,3584]{1,0:T(8,128)(2,1)S(1)}, bf16[64,3584]{1,0:T(8,128)(2,1)S(1)}, u32[]{:S(2)}, u32[]{:S(2)}) collective-permute-start(bf16[64,3584]{1,0:T(8,128)(2,1)S(1)} %slice.71), channel_id=1, source_target_pairs={{0,1},{1,0},{2,3},{3,2},{4,5},{5,4},{6,7},{7,6},{8,9},{9,8},{10,11... | collective-permute-start | bytes 1376264 | tf_op jit(solution)/shard_map/ppermute | solution.py:41
  212.4 17.7 %collective-permute-start.16 = (bf16[16,3584]{1,0:T(8,128)(2,1)S(1)}, bf16[16,3584]{1,0:T(8,128)(2,1)S(1)}, u32[]{:S(2)}, u32[]{:S(2)}) collective-permute-start(bf16[16,3584]{1,0:T(8,128)(2,1)S(1)} %get-tuple-element.25), channel_id=1, source_target_pairs={{0,28},{1,29},{2,30},{3,31},{4,8},{5,9},{6,10},{7,11},{8,4},{9,5},... | collective-permute-start | bytes 344072 | tf_op jit(solution)/shard_map/ppermute | solution.py:41
  214.9 19.1 %collective-permute-start.17 = (bf16[16,3584]{1,0:T(8,128)(2,1)S(1)}, bf16[16,3584]{1,0:T(8,128)(2,1)S(1)}, u32[]{:S(2)}, u32[]{:S(2)}) collective-permute-start(bf16[16,3584]{1,0:T(8,128)(2,1)S(1)} %get-tuple-element.24), channel_id=1, source_target_pairs={{0,24},{1,25},{2,26},{3,27},{4,12},{5,13},{6,14},{7,15},{8,0},{9,1... | collective-permute-start | bytes 344072 | tf_op jit(solution)/shard_map/ppermute | solution.py:41
  219.3 23.5 %copy-start.8 = (bf16[1,24,3584]{2,1,0:T(8,128)(2,1)S(1)}, bf16[1,24,3584]{2,1,0:T(8,128)(2,1)}, u32[]{:S(2)}) copy-start(bf16[1,24,3584]{2,1,0:T(8,128)(2,1)} %param.11) | copy-start | bytes 516100
  219.3 14.7 %collective-permute-start.18 = (bf16[16,3584]{1,0:T(8,128)(2,1)S(1)}, bf16[16,3584]{1,0:T(8,128)(2,1)S(1)}, u32[]{:S(2)}, u32[]{:S(2)}) collective-permute-start(bf16[16,3584]{1,0:T(8,128)(2,1)S(1)} %get-tuple-element.23), channel_id=1, source_target_pairs={{0,20},{1,21},{2,22},{3,23},{4,16},{5,17},{6,18},{7,19},{8,28},{9,... | collective-permute-start | bytes 344072 | tf_op jit(solution)/shard_map/ppermute | solution.py:41
  223.3 19.5 %collective-permute-start.10 = (bf16[16,3584]{1,0:T(8,128)(2,1)S(1)}, bf16[16,3584]{1,0:T(8,128)(2,1)S(1)}, u32[]{:S(2)}, u32[]{:S(2)}) collective-permute-start(bf16[16,3584]{1,0:T(8,128)(2,1)S(1)} %get-tuple-element.29), channel_id=1, source_target_pairs={{0,28},{1,29},{2,30},{3,31},{4,8},{5,9},{6,10},{7,11},{8,4},{9,5},... | collective-permute-start | bytes 344072 | tf_op jit(solution)/shard_map/ppermute | solution.py:41
  225.8 17.0 %collective-permute-start.11 = (bf16[16,3584]{1,0:T(8,128)(2,1)S(1)}, bf16[16,3584]{1,0:T(8,128)(2,1)S(1)}, u32[]{:S(2)}, u32[]{:S(2)}) collective-permute-start(bf16[16,3584]{1,0:T(8,128)(2,1)S(1)} %get-tuple-element.28), channel_id=1, source_target_pairs={{0,24},{1,25},{2,26},{3,27},{4,12},{5,13},{6,14},{7,15},{8,0},{9,1... | collective-permute-start | bytes 344072 | tf_op jit(solution)/shard_map/ppermute | solution.py:41
  230.1 12.7 %collective-permute-start.12 = (bf16[16,3584]{1,0:T(8,128)(2,1)S(1)}, bf16[16,3584]{1,0:T(8,128)(2,1)S(1)}, u32[]{:S(2)}, u32[]{:S(2)}) collective-permute-start(bf16[16,3584]{1,0:T(8,128)(2,1)S(1)} %get-tuple-element.27), channel_id=1, source_target_pairs={{0,20},{1,21},{2,22},{3,23},{4,16},{5,17},{6,18},{7,19},{8,28},{9,... | collective-permute-start | bytes 344072 | tf_op jit(solution)/shard_map/ppermute | solution.py:41
  235.9 13.5 %collective-permute-start.19 = (bf16[24,3584]{1,0:T(8,128)(2,1)S(1)}, bf16[24,3584]{1,0:T(8,128)(2,1)S(1)}, u32[]{:S(2)}, u32[]{:S(2)}) collective-permute-start(bf16[24,3584]{1,0:T(8,128)(2,1)S(1)} %get-tuple-element.21), channel_id=1, source_target_pairs={{32,0},{64,32},{96,64},{128,96},{160,128},{192,160},{224,192},{256... | collective-permute-start | bytes 516104 | tf_op jit(solution)/shard_map/ppermute | solution.py:47
  244.6 6.5 %collective-permute-start.13 = (bf16[24,3584]{1,0:T(8,128)(2,1)S(1)}, bf16[24,3584]{1,0:T(8,128)(2,1)S(1)}, u32[]{:S(2)}, u32[]{:S(2)}) collective-permute-start(bf16[24,3584]{1,0:T(8,128)(2,1)S(1)} %shard_map.133), channel_id=1, source_target_pairs={{0,32},{32,64},{64,96},{96,128},{128,160},{160,192},{192,224},{224... | collective-permute-start | bytes 516104 | tf_op jit(solution)/shard_map/ppermute | solution.py:47
  (9 other events, 76.8 us)

commit v3 on v2

--- a/solution.py
+++ b/solution.py
@@ -103,19 +103,12 @@
             outs[j][:, i * width : (i + 1) * width] = packed[j * SLOT : (j + 1) * SLOT]
 
 
-def merge_kernel(wg, wu, wd, out, sems):
+def merge_kernel(wg, wu, wd, out):
     width, units = wg.shape
-    copies = [
-        pltpu.make_async_copy(wg, out.at[pl.ds(0, width)], sems.at[0]),
-        pltpu.make_async_copy(wu, out.at[pl.ds(width, width)], sems.at[1]),
-    ]
-    for i in range(width // units):
-        to = out.at[pl.ds(2 * width + i * units, units)]
-        copies.append(pltpu.make_async_copy(wd.at[:, pl.ds(i * units, units)], to, sems.at[2 + i]))
-    for copy in copies:
-        copy.start()
-    for copy in copies:
-        copy.wait()
+    out[0:width, :] = wg[...]
+    out[width : 2 * width, :] = wu[...]
+    for at in range(0, width, units):
+        out[2 * width + at : 2 * width + at + units, :] = wd[:, at : at + units]
 
 
 def hidden(rows, wg, wu):
@@ -130,14 +123,18 @@
 
 
 def gather_rows(refs, at, width, scratch):
-    cols = slice(at, at + width)
-    places = ((0, 64), (128, 192), (32, 160), (96, 224))
-    for ref, (one, two) in zip(refs, places):
-        scratch[one : one + 32, :] = ref[0:32, cols]
-        scratch[two : two + 32, :] = ref[32:64, cols]
-
-
-def fwd_kernel(c1, qr1, c2, pr2, wg, wu, wd, other, keep, send, rows):
+    for i, ref in enumerate(refs):
+        scratch[64 * i : 64 * (i + 1), :] = ref[:, at : at + width]
+
+
+def store_parts(part, cols, keep1, send1, keep2, send2):
+    keep1[:, cols] = part[0:64]
+    send1[:, cols] = part[64:128].astype(BF16)
+    keep2[:, cols] = part[128:192]
+    send2[:, cols] = part[192:256].astype(BF16)
+
+
+def fwd_kernel(c1, qr1, c2, pr2, wg, wu, wd, other, keep1, send1, keep2, send2, rows):
     width = rows.shape[1]
     gather_rows((c1, qr1, c2, pr2), 0, width, rows)
     inner = []
@@ -150,11 +147,12 @@
         cols = slice(at, at + step)
         down = jnp.concatenate([wd[:, cols], down_columns(other, at, step)], axis=0)
         part = jnp.dot(inner, down, preferred_element_type=F32)
-        keep[:, cols] = part[0:128]
-        send[:, cols] = part[128:256].astype(BF16)
-
-
-def bwd_kernel(c1, qr1, c2, pr2, wg, wu, wd, other, keep, send, rows, cots):
+        store_parts(part, cols, keep1, send1, keep2, send2)
+
+
+def bwd_kernel(
+    c1, qr1, c2, pr2, wg, wu, wd, other, _, keep1, send1, keep2, send2, rows, cots
+):
     width = rows.shape[1]
     gather_rows((c1, qr1, c2, pr2), width, width, rows)
     gather_rows((c1, qr1, c2, pr2), 2 * width, width, cots)
@@ -203,10 +201,7 @@
             part = term if part is None else part + term
         if at == 0:
             part = jnp.concatenate([part[:, :128] + grad_rows, part[:, 128:]], axis=1)
-        keep[0:64, cols] = part[0:64]
-        send[0:64, cols] = part[64:128].astype(BF16)
-        keep[64:128, cols] = part[128:192]
-        send[64:128, cols] = part[192:256].astype(BF16)
+        store_parts(part, cols, keep1, send1, keep2, send2)
 
 
 def mixed_rows(masks, weight_ref, parts):
@@ -269,12 +264,17 @@
     return c1, hop(c1, HOP_X3), c2, hop(c2, HOP_X1)
 
 
-def return_rows(keep, send, first, second):
-    total = keep + hop(send, first).astype(F32)
-    whole = total[:64] + hop(total[64:].astype(BF16), second).astype(F32)
-    whole = whole.astype(BF16)
-    own, a, b, c = (whole[j * SLOT : (j + 1) * SLOT] for j in range(4))
-    return own, hop(a, HOP_A), hop(b, HOP_B_BACK), hop(c, HOP_C)
+def return_rows(keep1, send1, keep2, send2):
+    sum1 = keep1 + hop(send1, HOP_X3).astype(F32)
+    sum2 = keep2 + hop(send2, HOP_X1).astype(F32)
+    full1 = sum1[:32] + hop(sum1[32:].astype(BF16), HOP_X1).astype(F32)
+    full2 = sum2[:32] + hop(sum2[32:].astype(BF16), HOP_X3).astype(F32)
+    full1 = full1.astype(BF16)
+    full2 = full2.astype(BF16)
+    back_a = hop(full1[SLOT:], HOP_A)
+    back_b = hop(full2[:SLOT], HOP_B_BACK)
+    back_c = hop(full2[SLOT:], HOP_C)
+    return full1[:SLOT], back_a, back_b, back_c
 
 
 def body(
@@ -296,26 +296,21 @@
     info = jnp.stack([z // 2, z % 2]).astype(jnp.int32)
     weights = (w_gate[0, 0], w_up[0, 0], w_down[0, 0])
     units = w_down.shape[2]
-    hbm = pl.BlockSpec(memory_space=pl.ANY)
-    merged = pl.pallas_call(
-        merge_kernel,
-        out_shape=jax.ShapeDtypeStruct((3 * width, units), BF16),
-        in_specs=[hbm] * 3,
-        out_specs=hbm,
-        scratch_shapes=[pltpu.SemaphoreType.DMA((2 + width // units,))],
-    )(*weights)
+    (merged,) = kernel_call(merge_kernel, [((3 * width, units), BF16)], 3, info=False)(*weights)
     other = hop(merged, HOP_W)
     wide = [((SLOT, 3 * width), BF16)] * 4
     sent = kernel_call(pack_kernel, wide, 6)(
         info, act_fwd[0], route_fwd[0], act_bwd[0], route_bwd[0], cot_bwd[0], norm_gain
     )
     rows = spread_rows(*sent)
-    outs = [((128, width), F32), ((128, width), BF16)]
+    outs = [((64, width), F32), ((64, width), BF16)] * 2
     scratch = pltpu.VMEM((256, width), BF16)
     part_a = kernel_call(fwd_kernel, outs, 8, [scratch], info=False)(*rows, *weights, other)
-    part_b = kernel_call(bwd_kernel, outs, 8, [scratch] * 2, info=False)(*rows, *weights, other)
-    back_a = return_rows(*part_a, HOP_X3, HOP_X1)
-    back_b = return_rows(*part_b, HOP_X1, HOP_X3)
+    part_b = kernel_call(bwd_kernel, outs, 9, [scratch] * 2, info=False)(
+        *rows, *weights, other, part_a[1]
+    )
+    back_a = return_rows(*part_a)
+    back_b = return_rows(*part_b)
     (layer_out,) = kernel_call(fwd_out_kernel, [((tokens, width), BF16)], 7)(
         info, act_fwd[0], route_fwd[0], weight_fwd[0], *back_a
     )

time: 254 us -> 178 us (0.70)
  Pallas kernels: 94.8 us -> 10.4 us
  starting transfers between devices: 76.8 us -> 94.5 us
  waiting for transfers between devices: 71.4 us -> 58.5 us
  local copies, waits for them, and re-layouts: 7.5 us -> 11 us
    pallas_call x2, Pallas kernels: 88.1 us -> 3.62 us  [the longest x1 3.34 us: body(): kernel_call(bwd_kernel, outs, 9, [scratch] * 2, info=False)]
    ppermute x18 -> x22, waiting for transfers between devices: 69.7 us -> 54.8 us  [hop(): return lax.ppermute(value, 'expert', pairs)]
    ppermute x18 -> x22, starting transfers between devices: 65.8 us -> 78.9 us  [hop(): return lax.ppermute(value, 'expert', pairs)]
    ppermute x2, starting transfers between devices: 11.1 us -> 15.6 us  [shifted(): return lax.ppermute(value, axis, pairs)]
    unnamed x32, local copies, waits for them, and re-layouts: 4.96 us -> 8.47 us
  transfers between devices with their start and end apart: 20 -> 24, of which waited for: 9 -> 10; matrix products, arithmetic and copies ran while one was open for 1% -> 1% of each run, Pallas kernels for 36% -> 4%
where the time goes in v3:
time: 178 us; the launch traced here: 176 us
  starting transfers between devices  94.5 us (53%)
  waiting for transfers between devices  58.5 us (33%)
  local copies, waits for them, and re-layouts  11 us (6%)
  Pallas kernels  10.4 us (6%)
    ppermute x22, starting transfers between devices, hop(): return lax.ppermute(value, 'expert', pairs)  78.9 us
    ppermute x22, waiting for transfers between devices, hop(): return lax.ppermute(value, 'expert', pairs)  54.8 us
    ppermute x2, starting transfers between devices, shifted(): return lax.ppermute(value, axis, pairs)  15.6 us
    unnamed x32, local copies, waits for them, and re-layouts  8.47 us
    ppermute x2, waiting for transfers between devices, shifted(): return lax.ppermute(value, axis, pairs)  3.69 us
  transfers between devices with their start and end apart: 24, of which 10 were waited for; matrix products, arithmetic and copies ran while one was open for 1% of the time, Pallas kernels for 4%

profile of v3, /device:TPU:1, one launch (start us, length us, event | category | flops | bytes accessed | tf_op | source)
XLA Modules:
  0.0 176.2 jit_solution(6750681656270210979)
XLA Ops:
  7.2 11.5 %collective-permute-start = (bf16[16,10752]{1,0:T(8,128)(2,1)S(1)}, bf16[16,10752]{1,0:T(8,128)(2,1)S(1)}, u32[]{:S(2)}, u32[]{:S(2)}) collective-permute-start(bf16[16,10752]{1,0:T(8,128)(2,1)S(1)} %get-tuple-element.18), channel_id=1, source_target_pairs={{0,28},{1,29},{2,30},{3,31},{4,8},{5,9},{6,10},{7,11},{8,4},{9,5},... | collective-permute-start | bytes 1032200 | tf_op jit(solution)/shard_map/ppermute | solution.py:41
  20.6 4.5 %collective-permute-start.4 = (bf16[16,10752]{1,0:T(8,128)(2,1)S(1)}, bf16[16,10752]{1,0:T(8,128)(2,1)S(1)}, u32[]{:S(2)}, u32[]{:S(2)}) collective-permute-start(bf16[16,10752]{1,0:T(8,128)(2,1)S(1)} %get-tuple-element.20), channel_id=1, source_target_pairs={{0,20},{1,21},{2,22},{3,23},{4,16},{5,17},{6,18},{7,19},{8,28},{9,... | collective-permute-start | bytes 1032200 | tf_op jit(solution)/shard_map/ppermute | solution.py:41
  30.9 9.2 %collective-permute-done = bf16[16,10752]{1,0:T(8,128)(2,1)S(1)} collective-permute-done((bf16[16,10752]{1,0:T(8,128)(2,1)S(1)}, bf16[16,10752]{1,0:T(8,128)(2,1)S(1)}, u32[]{:S(2)}, u32[]{:S(2)}) %collective-permute-start) | collective-permute-done | bytes 344096 | tf_op jit(solution)/shard_map/ppermute | solution.py:41
  40.2 3.1 %collective-permute-start.1 = (bf16[32,10752]{1,0:T(8,128)(2,1)S(1)}, bf16[32,10752]{1,0:T(8,128)(2,1)S(1)}, u32[]{:S(2)}, u32[]{:S(2)}) collective-permute-start(bf16[32,10752]{1,0:T(8,128)(2,1)S(1)} %pad_maximum_fusion), channel_id=1, source_target_pairs={{0,1},{1,0},{2,3},{3,2},{4,5},{5,4},{6,7},{7,6},{8,9},{9,8},{10,11... | collective-permute-start | bytes 2064392 | tf_op jit(solution)/shard_map/ppermute | solution.py:41
  43.3 4.2 %collective-permute-done.4 = bf16[16,10752]{1,0:T(8,128)(2,1)S(1)} collective-permute-done((bf16[16,10752]{1,0:T(8,128)(2,1)S(1)}, bf16[16,10752]{1,0:T(8,128)(2,1)S(1)}, u32[]{:S(2)}, u32[]{:S(2)}) %collective-permute-start.4) | collective-permute-done | bytes 344096 | tf_op jit(solution)/shard_map/ppermute | solution.py:41
  47.6 4.4 %collective-permute-start.5 = (bf16[32,10752]{1,0:T(8,128)(2,1)S(1)}, bf16[32,10752]{1,0:T(8,128)(2,1)S(1)}, u32[]{:S(2)}, u32[]{:S(2)}) collective-permute-start(bf16[32,10752]{1,0:T(8,128)(2,1)S(1)} %pad_maximum_fusion.1), channel_id=1, source_target_pairs={{0,3},{1,2},{2,1},{3,0},{4,7},{5,6},{6,5},{7,4},{8,11},{9,10},{10,... | collective-permute-start | bytes 2064392 | tf_op jit(solution)/shard_map/ppermute | solution.py:41
  52.1 4.2 %collective-permute-done.1 = bf16[32,10752]{1,0:T(8,128)(2,1)S(1)} collective-permute-done((bf16[32,10752]{1,0:T(8,128)(2,1)S(1)}, bf16[32,10752]{1,0:T(8,128)(2,1)S(1)}, u32[]{:S(2)}, u32[]{:S(2)}) %collective-permute-start.1) | collective-permute-done | bytes 688160 | tf_op jit(solution)/shard_map/ppermute | solution.py:41
  56.4 4.3 %collective-permute-start.2 = (bf16[64,10752]{1,0:T(8,128)(2,1)S(1)}, bf16[64,10752]{1,0:T(8,128)(2,1)S(1)}, u32[]{:S(2)}, u32[]{:S(2)}) collective-permute-start(bf16[64,10752]{1,0:T(8,128)(2,1)S(1)} %constant_dynamic-update-slice_fusion.c1), channel_id=1, source_target_pairs={{0,3},{1,2},{2,1},{3,0},{4,7},{5,6},{6,5},{7,4},{8,11},{9,10},{10,... | collective-permute-start | bytes 4128776 | tf_op jit(solution)/shard_map/ppermute | solution.py:41
  60.7 5.4 %collective-permute-done.5 = bf16[32,10752]{1,0:T(8,128)(2,1)S(1)} collective-permute-done((bf16[32,10752]{1,0:T(8,128)(2,1)S(1)}, bf16[32,10752]{1,0:T(8,128)(2,1)S(1)}, u32[]{:S(2)}, u32[]{:S(2)}) %collective-permute-start.5) | collective-permute-done | bytes 688160 | tf_op jit(solution)/shard_map/ppermute | solution.py:41
  68.1 27.5 %collective-permute-done.2.qr1 = bf16[64,10752]{1,0:T(8,128)(2,1)S(1)} collective-permute-done((bf16[64,10752]{1,0:T(8,128)(2,1)S(1)}, bf16[64,10752]{1,0:T(8,128)(2,1)S(1)}, u32[]{:S(2)}, u32[]{:S(2)}) %collective-permute-start.2) | collective-permute-done | bytes 1376288 | tf_op jit(solution)/shard_map/ppermute | solution.py:41
  98.0 4.4 %collective-permute-start.8 = (bf16[64,3584]{1,0:T(8,128)(2,1)S(1)}, bf16[64,3584]{1,0:T(8,128)(2,1)S(1)}, u32[]{:S(2)}, u32[]{:S(2)}) collective-permute-start(bf16[64,3584]{1,0:T(8,128)(2,1)S(1)} %get-tuple-element.22._), channel_id=1, source_target_pairs={{0,3},{1,2},{2,1},{3,0},{4,7},{5,6},{6,5},{7,4},{8,11},{9,10},{10,... | collective-permute-start | bytes 1376264 | tf_op jit(solution)/shard_map/ppermute | solution.py:41
  104.3 3.3 %shard_map.134 = (f32[64,3584]{1,0:T(8,128)S(1)}, bf16[64,3584]{1,0:T(8,128)(2,1)S(1)}, f32[64,3584]{1,0:T(8,128)S(1)}, bf16[64,3584]{1,0:T(8,128)(2,1)S(1)}) custom-call(bf16[64,10752]{1,0:T(8,128)(2,1)S(1)} %constant_dynamic-update-slice_fusion.c1, bf16[64,10752]{1,0:T(8,128)(2,1)S(1)} %collective-permute-done.2.qr1, ...), custom_call_target="tpu_custom_call" | custom-call | tf_op jit(solution)/shard_map/pallas_call | solution.py:309
  107.7 2.7 %collective-permute-start.16 = (bf16[64,3584]{1,0:T(8,128)(2,1)S(1)}, bf16[64,3584]{1,0:T(8,128)(2,1)S(1)}, u32[]{:S(2)}, u32[]{:S(2)}) collective-permute-start(bf16[64,3584]{1,0:T(8,128)(2,1)S(1)} %get-tuple-element.26), channel_id=1, source_target_pairs={{0,3},{1,2},{2,1},{3,0},{4,7},{5,6},{6,5},{7,4},{8,11},{9,10},{10,... | collective-permute-start | bytes 1376264 | tf_op jit(solution)/shard_map/ppermute | solution.py:41
  110.4 2.6 %collective-permute-start.19 = (bf16[64,3584]{1,0:T(8,128)(2,1)S(1)}, bf16[64,3584]{1,0:T(8,128)(2,1)S(1)}, u32[]{:S(2)}, u32[]{:S(2)}) collective-permute-start(bf16[64,3584]{1,0:T(8,128)(2,1)S(1)} %get-tuple-element.28), channel_id=1, source_target_pairs={{0,1},{1,0},{2,3},{3,2},{4,5},{5,4},{6,7},{7,6},{8,9},{9,8},{10,11... | collective-permute-start | bytes 1376264 | tf_op jit(solution)/shard_map/ppermute | solution.py:41
  113.1 2.7 %collective-permute-start.9 = (bf16[32,3584]{1,0:T(8,128)(2,1)S(1)}, bf16[32,3584]{1,0:T(8,128)(2,1)S(1)}, u32[]{:S(2)}, u32[]{:S(2)}) collective-permute-start(bf16[32,3584]{1,0:T(8,128)(2,1)S(1)} %slice.103), channel_id=1, source_target_pairs={{0,1},{1,0},{2,3},{3,2},{4,5},{5,4},{6,7},{7,6},{8,9},{9,8},{10,11... | collective-permute-start | bytes 688136 | tf_op jit(solution)/shard_map/ppermute | solution.py:41
  115.9 3.8 %collective-permute-start.12 = (bf16[32,3584]{1,0:T(8,128)(2,1)S(1)}, bf16[32,3584]{1,0:T(8,128)(2,1)S(1)}, u32[]{:S(2)}, u32[]{:S(2)}) collective-permute-start(bf16[32,3584]{1,0:T(8,128)(2,1)S(1)} %slice.102), channel_id=1, source_target_pairs={{0,3},{1,2},{2,1},{3,0},{4,7},{5,6},{6,5},{7,4},{8,11},{9,10},{10,... | collective-permute-start | bytes 688136 | tf_op jit(solution)/shard_map/ppermute | solution.py:41
  124.0 3.3 %collective-permute-start.20 = (bf16[32,3584]{1,0:T(8,128)(2,1)S(1)}, bf16[32,3584]{1,0:T(8,128)(2,1)S(1)}, u32[]{:S(2)}, u32[]{:S(2)}) collective-permute-start(bf16[32,3584]{1,0:T(8,128)(2,1)S(1)} %slice.100), channel_id=1, source_target_pairs={{0,3},{1,2},{2,1},{3,0},{4,7},{5,6},{6,5},{7,4},{8,11},{9,10},{10,... | collective-permute-start | bytes 688136 | tf_op jit(solution)/shard_map/ppermute | solution.py:41
  128.9 4.9 %collective-permute-start.10 = (bf16[16,3584]{1,0:T(8,128)(2,1)S(1)}, bf16[16,3584]{1,0:T(8,128)(2,1)S(1)}, u32[]{:S(2)}, u32[]{:S(2)}) collective-permute-start(bf16[16,3584]{1,0:T(8,128)(2,1)S(1)} %get-tuple-element.37), channel_id=1, source_target_pairs={{0,28},{1,29},{2,30},{3,31},{4,8},{5,9},{6,10},{7,11},{8,4},{9,5},... | collective-permute-start | bytes 344072 | tf_op jit(solution)/shard_map/ppermute | solution.py:41
  133.9 4.0 %collective-permute-start.13 = (bf16[16,3584]{1,0:T(8,128)(2,1)S(1)}, bf16[16,3584]{1,0:T(8,128)(2,1)S(1)}, u32[]{:S(2)}, u32[]{:S(2)}) collective-permute-start(bf16[16,3584]{1,0:T(8,128)(2,1)S(1)} %get-tuple-element.36), channel_id=1, source_target_pairs={{0,24},{1,25},{2,26},{3,27},{4,12},{5,13},{6,14},{7,15},{8,0},{9,1... | collective-permute-start | bytes 344072 | tf_op jit(solution)/shard_map/ppermute | solution.py:41
  140.1 4.7 %collective-permute-start.18 = (bf16[16,3584]{1,0:T(8,128)(2,1)S(1)}, bf16[16,3584]{1,0:T(8,128)(2,1)S(1)}, u32[]{:S(2)}, u32[]{:S(2)}) collective-permute-start(bf16[16,3584]{1,0:T(8,128)(2,1)S(1)} %get-tuple-element.33), channel_id=1, source_target_pairs={{0,28},{1,29},{2,30},{3,31},{4,8},{5,9},{6,10},{7,11},{8,4},{9,5},... | collective-permute-start | bytes 344072 | tf_op jit(solution)/shard_map/ppermute | solution.py:41
  144.9 4.0 %collective-permute-start.21 = (bf16[16,3584]{1,0:T(8,128)(2,1)S(1)}, bf16[16,3584]{1,0:T(8,128)(2,1)S(1)}, u32[]{:S(2)}, u32[]{:S(2)}) collective-permute-start(bf16[16,3584]{1,0:T(8,128)(2,1)S(1)} %get-tuple-element.32), channel_id=1, source_target_pairs={{0,24},{1,25},{2,26},{3,27},{4,12},{5,13},{6,14},{7,15},{8,0},{9,1... | collective-permute-start | bytes 344072 | tf_op jit(solution)/shard_map/ppermute | solution.py:41
  153.0 10.4 %collective-permute-start.15 = (bf16[24,3584]{1,0:T(8,128)(2,1)S(1)}, bf16[24,3584]{1,0:T(8,128)(2,1)S(1)}, u32[]{:S(2)}, u32[]{:S(2)}) collective-permute-start(bf16[24,3584]{1,0:T(8,128)(2,1)S(1)} %shard_map.133), channel_id=1, source_target_pairs={{0,32},{32,64},{64,96},{96,128},{128,160},{160,192},{192,224},{224... | collective-permute-start | bytes 516104 | tf_op jit(solution)/shard_map/ppermute | solution.py:47
  165.3 5.2 %collective-permute-start.23 = (bf16[24,3584]{1,0:T(8,128)(2,1)S(1)}, bf16[24,3584]{1,0:T(8,128)(2,1)S(1)}, u32[]{:S(2)}, u32[]{:S(2)}) collective-permute-start(bf16[24,3584]{1,0:T(8,128)(2,1)S(1)} %get-tuple-element.29), channel_id=1, source_target_pairs={{32,0},{64,32},{96,64},{128,96},{160,128},{192,160},{224,192},{256... | collective-permute-start | bytes 516104 | tf_op jit(solution)/shard_map/ppermute | solution.py:47
  171.2 3.7 %collective-permute-done.23 = bf16[24,3584]{1,0:T(8,128)(2,1)S(1)} collective-permute-done((bf16[24,3584]{1,0:T(8,128)(2,1)S(1)}, bf16[24,3584]{1,0:T(8,128)(2,1)S(1)}, u32[]{:S(2)}, u32[]{:S(2)}) %collective-permute-start.23) | collective-permute-done | bytes 172064 | tf_op jit(solution)/shard_map/ppermute | solution.py:47
  (88 shorter events, 36.8 us)
Async XLA Ops:
  7.2 33.0 %collective-permute-start = (bf16[16,10752]{1,0:T(8,128)(2,1)S(1)}, bf16[16,10752]{1,0:T(8,128)(2,1)S(1)}, u32[]{:S(2)}, u32[]{:S(2)}) collective-permute-start(bf16[16,10752]{1,0:T(8,128)(2,1)S(1)} %get-tuple-element.18), channel_id=1, source_target_pairs={{0,28},{1,29},{2,30},{3,31},{4,8},{5,9},{6,10},{7,11},{8,4},{9,5},... | collective-permute-start | bytes 1032200 | tf_op jit(solution)/shard_map/ppermute | solution.py:41
  18.7 24.6 %collective-permute-start.3 = (bf16[16,10752]{1,0:T(8,128)(2,1)S(1)}, bf16[16,10752]{1,0:T(8,128)(2,1)S(1)}, u32[]{:S(2)}, u32[]{:S(2)}) collective-permute-start(bf16[16,10752]{1,0:T(8,128)(2,1)S(1)} %get-tuple-element.19), channel_id=1, source_target_pairs={{0,8},{1,9},{2,10},{3,11},{4,28},{5,29},{6,30},{7,31},{8,16},{9,17... | collective-permute-start | bytes 1032200 | tf_op jit(solution)/shard_map/ppermute | solution.py:41
  20.6 26.9 %collective-permute-start.4 = (bf16[16,10752]{1,0:T(8,128)(2,1)S(1)}, bf16[16,10752]{1,0:T(8,128)(2,1)S(1)}, u32[]{:S(2)}, u32[]{:S(2)}) collective-permute-start(bf16[16,10752]{1,0:T(8,128)(2,1)S(1)} %get-tuple-element.20), channel_id=1, source_target_pairs={{0,20},{1,21},{2,22},{3,23},{4,16},{5,17},{6,18},{7,19},{8,28},{9,... | collective-permute-start | bytes 1032200 | tf_op jit(solution)/shard_map/ppermute | solution.py:41
  29.0 67.3 %collective-permute-start.7 = (bf16[10752,128]{1,0:T(8,128)(2,1)S(1)}, bf16[10752,128]{1,0:T(8,128)(2,1)S(1)}, u32[]{:S(2)}, u32[]{:S(2)}) collective-permute-start(bf16[10752,128]{1,0:T(8,128)(2,1)S(1)} %shard_map.131), channel_id=1, source_target_pairs={{0,4},{1,5},{2,6},{3,7},{4,0},{5,1},{6,2},{7,3},{8,12},{9,13},{10,... | collective-permute-start | bytes 8257544 | tf_op jit(solution)/shard_map/ppermute | solution.py:41
  40.2 16.1 %collective-permute-start.1 = (bf16[32,10752]{1,0:T(8,128)(2,1)S(1)}, bf16[32,10752]{1,0:T(8,128)(2,1)S(1)}, u32[]{:S(2)}, u32[]{:S(2)}) collective-permute-start(bf16[32,10752]{1,0:T(8,128)(2,1)S(1)} %pad_maximum_fusion), channel_id=1, source_target_pairs={{0,1},{1,0},{2,3},{3,2},{4,5},{5,4},{6,7},{7,6},{8,9},{9,8},{10,11... | collective-permute-start | bytes 2064392 | tf_op jit(solution)/shard_map/ppermute | solution.py:41
  47.6 18.5 %collective-permute-start.5 = (bf16[32,10752]{1,0:T(8,128)(2,1)S(1)}, bf16[32,10752]{1,0:T(8,128)(2,1)S(1)}, u32[]{:S(2)}, u32[]{:S(2)}) collective-permute-start(bf16[32,10752]{1,0:T(8,128)(2,1)S(1)} %pad_maximum_fusion.1), channel_id=1, source_target_pairs={{0,3},{1,2},{2,1},{3,0},{4,7},{5,6},{6,5},{7,4},{8,11},{9,10},{10,... | collective-permute-start | bytes 2064392 | tf_op jit(solution)/shard_map/ppermute | solution.py:41
  56.4 39.2 %collective-permute-start.2 = (bf16[64,10752]{1,0:T(8,128)(2,1)S(1)}, bf16[64,10752]{1,0:T(8,128)(2,1)S(1)}, u32[]{:S(2)}, u32[]{:S(2)}) collective-permute-start(bf16[64,10752]{1,0:T(8,128)(2,1)S(1)} %constant_dynamic-update-slice_fusion.c1), channel_id=1, source_target_pairs={{0,3},{1,2},{2,1},{3,0},{4,7},{5,6},{6,5},{7,4},{8,11},{9,10},{10,... | collective-permute-start | bytes 4128776 | tf_op jit(solution)/shard_map/ppermute | solution.py:41
  66.1 29.4 %collective-permute-start.6 = (bf16[64,10752]{1,0:T(8,128)(2,1)S(1)}, bf16[64,10752]{1,0:T(8,128)(2,1)S(1)}, u32[]{:S(2)}, u32[]{:S(2)}) collective-permute-start(bf16[64,10752]{1,0:T(8,128)(2,1)S(1)} %constant_dynamic-update-slice_fusion.3.c2), channel_id=1, source_target_pairs={{0,1},{1,0},{2,3},{3,2},{4,5},{5,4},{6,7},{7,6},{8,9},{9,8},{10,11... | collective-permute-start | bytes 4128776 | tf_op jit(solution)/shard_map/ppermute | solution.py:41
  98.0 15.0 %collective-permute-start.8 = (bf16[64,3584]{1,0:T(8,128)(2,1)S(1)}, bf16[64,3584]{1,0:T(8,128)(2,1)S(1)}, u32[]{:S(2)}, u32[]{:S(2)}) collective-permute-start(bf16[64,3584]{1,0:T(8,128)(2,1)S(1)} %get-tuple-element.22._), channel_id=1, source_target_pairs={{0,3},{1,2},{2,1},{3,0},{4,7},{5,6},{6,5},{7,4},{8,11},{9,10},{10,... | collective-permute-start | bytes 1376264 | tf_op jit(solution)/shard_map/ppermute | solution.py:41
  102.4 13.4 %collective-permute-start.11 = (bf16[64,3584]{1,0:T(8,128)(2,1)S(1)}, bf16[64,3584]{1,0:T(8,128)(2,1)S(1)}, u32[]{:S(2)}, u32[]{:S(2)}) collective-permute-start(bf16[64,3584]{1,0:T(8,128)(2,1)S(1)} %get-tuple-element.24), channel_id=1, source_target_pairs={{0,1},{1,0},{2,3},{3,2},{4,5},{5,4},{6,7},{7,6},{8,9},{9,8},{10,11... | collective-permute-start | bytes 1376264 | tf_op jit(solution)/shard_map/ppermute | solution.py:41
  107.7 12.2 %collective-permute-start.16 = (bf16[64,3584]{1,0:T(8,128)(2,1)S(1)}, bf16[64,3584]{1,0:T(8,128)(2,1)S(1)}, u32[]{:S(2)}, u32[]{:S(2)}) collective-permute-start(bf16[64,3584]{1,0:T(8,128)(2,1)S(1)} %get-tuple-element.26), channel_id=1, source_target_pairs={{0,3},{1,2},{2,1},{3,0},{4,7},{5,6},{6,5},{7,4},{8,11},{9,10},{10,... | collective-permute-start | bytes 1376264 | tf_op jit(solution)/shard_map/ppermute | solution.py:41
  110.4 13.5 %collective-permute-start.19 = (bf16[64,3584]{1,0:T(8,128)(2,1)S(1)}, bf16[64,3584]{1,0:T(8,128)(2,1)S(1)}, u32[]{:S(2)}, u32[]{:S(2)}) collective-permute-start(bf16[64,3584]{1,0:T(8,128)(2,1)S(1)} %get-tuple-element.28), channel_id=1, source_target_pairs={{0,1},{1,0},{2,3},{3,2},{4,5},{5,4},{6,7},{7,6},{8,9},{9,8},{10,11... | collective-permute-start | bytes 1376264 | tf_op jit(solution)/shard_map/ppermute | solution.py:41
  113.1 15.7 %collective-permute-start.9 = (bf16[32,3584]{1,0:T(8,128)(2,1)S(1)}, bf16[32,3584]{1,0:T(8,128)(2,1)S(1)}, u32[]{:S(2)}, u32[]{:S(2)}) collective-permute-start(bf16[32,3584]{1,0:T(8,128)(2,1)S(1)} %slice.103), channel_id=1, source_target_pairs={{0,1},{1,0},{2,3},{3,2},{4,5},{5,4},{6,7},{7,6},{8,9},{9,8},{10,11... | collective-permute-start | bytes 688136 | tf_op jit(solution)/shard_map/ppermute | solution.py:41
  115.9 17.9 %collective-permute-start.12 = (bf16[32,3584]{1,0:T(8,128)(2,1)S(1)}, bf16[32,3584]{1,0:T(8,128)(2,1)S(1)}, u32[]{:S(2)}, u32[]{:S(2)}) collective-permute-start(bf16[32,3584]{1,0:T(8,128)(2,1)S(1)} %slice.102), channel_id=1, source_target_pairs={{0,3},{1,2},{2,1},{3,0},{4,7},{5,6},{6,5},{7,4},{8,11},{9,10},{10,... | collective-permute-start | bytes 688136 | tf_op jit(solution)/shard_map/ppermute | solution.py:41
  120.0 20.0 %collective-permute-start.17 = (bf16[32,3584]{1,0:T(8,128)(2,1)S(1)}, bf16[32,3584]{1,0:T(8,128)(2,1)S(1)}, u32[]{:S(2)}, u32[]{:S(2)}) collective-permute-start(bf16[32,3584]{1,0:T(8,128)(2,1)S(1)} %slice.101), channel_id=1, source_target_pairs={{0,1},{1,0},{2,3},{3,2},{4,5},{5,4},{6,7},{7,6},{8,9},{9,8},{10,11... | collective-permute-start | bytes 688136 | tf_op jit(solution)/shard_map/ppermute | solution.py:41
  124.0 20.8 %collective-permute-start.20 = (bf16[32,3584]{1,0:T(8,128)(2,1)S(1)}, bf16[32,3584]{1,0:T(8,128)(2,1)S(1)}, u32[]{:S(2)}, u32[]{:S(2)}) collective-permute-start(bf16[32,3584]{1,0:T(8,128)(2,1)S(1)} %slice.100), channel_id=1, source_target_pairs={{0,3},{1,2},{2,1},{3,0},{4,7},{5,6},{6,5},{7,4},{8,11},{9,10},{10,... | collective-permute-start | bytes 688136 | tf_op jit(solution)/shard_map/ppermute | solution.py:41
  128.9 20.0 %collective-permute-start.10 = (bf16[16,3584]{1,0:T(8,128)(2,1)S(1)}, bf16[16,3584]{1,0:T(8,128)(2,1)S(1)}, u32[]{:S(2)}, u32[]{:S(2)}) collective-permute-start(bf16[16,3584]{1,0:T(8,128)(2,1)S(1)} %get-tuple-element.37), channel_id=1, source_target_pairs={{0,28},{1,29},{2,30},{3,31},{4,8},{5,9},{6,10},{7,11},{8,4},{9,5},... | collective-permute-start | bytes 344072 | tf_op jit(solution)/shard_map/ppermute | solution.py:41
  133.9 17.3 %collective-permute-start.13 = (bf16[16,3584]{1,0:T(8,128)(2,1)S(1)}, bf16[16,3584]{1,0:T(8,128)(2,1)S(1)}, u32[]{:S(2)}, u32[]{:S(2)}) collective-permute-start(bf16[16,3584]{1,0:T(8,128)(2,1)S(1)} %get-tuple-element.36), channel_id=1, source_target_pairs={{0,24},{1,25},{2,26},{3,27},{4,12},{5,13},{6,14},{7,15},{8,0},{9,1... | collective-permute-start | bytes 344072 | tf_op jit(solution)/shard_map/ppermute | solution.py:41
  137.9 13.3 %collective-permute-start.14 = (bf16[16,3584]{1,0:T(8,128)(2,1)S(1)}, bf16[16,3584]{1,0:T(8,128)(2,1)S(1)}, u32[]{:S(2)}, u32[]{:S(2)}) collective-permute-start(bf16[16,3584]{1,0:T(8,128)(2,1)S(1)} %get-tuple-element.35), channel_id=1, source_target_pairs={{0,20},{1,21},{2,22},{3,23},{4,16},{5,17},{6,18},{7,19},{8,28},{9,... | collective-permute-start | bytes 344072 | tf_op jit(solution)/shard_map/ppermute | solution.py:41
  140.1 23.3 %collective-permute-start.18 = (bf16[16,3584]{1,0:T(8,128)(2,1)S(1)}, bf16[16,3584]{1,0:T(8,128)(2,1)S(1)}, u32[]{:S(2)}, u32[]{:S(2)}) collective-permute-start(bf16[16,3584]{1,0:T(8,128)(2,1)S(1)} %get-tuple-element.33), channel_id=1, source_target_pairs={{0,28},{1,29},{2,30},{3,31},{4,8},{5,9},{6,10},{7,11},{8,4},{9,5},... | collective-permute-start | bytes 344072 | tf_op jit(solution)/shard_map/ppermute | solution.py:41
  144.9 18.5 %collective-permute-start.21 = (bf16[16,3584]{1,0:T(8,128)(2,1)S(1)}, bf16[16,3584]{1,0:T(8,128)(2,1)S(1)}, u32[]{:S(2)}, u32[]{:S(2)}) collective-permute-start(bf16[16,3584]{1,0:T(8,128)(2,1)S(1)} %get-tuple-element.32), channel_id=1, source_target_pairs={{0,24},{1,25},{2,26},{3,27},{4,12},{5,13},{6,14},{7,15},{8,0},{9,1... | collective-permute-start | bytes 344072 | tf_op jit(solution)/shard_map/ppermute | solution.py:41
  148.9 14.5 %collective-permute-start.22 = (bf16[16,3584]{1,0:T(8,128)(2,1)S(1)}, bf16[16,3584]{1,0:T(8,128)(2,1)S(1)}, u32[]{:S(2)}, u32[]{:S(2)}) collective-permute-start(bf16[16,3584]{1,0:T(8,128)(2,1)S(1)} %get-tuple-element.31), channel_id=1, source_target_pairs={{0,20},{1,21},{2,22},{3,23},{4,16},{5,17},{6,18},{7,19},{8,28},{9,... | collective-permute-start | bytes 344072 | tf_op jit(solution)/shard_map/ppermute | solution.py:41
  153.0 18.2 %collective-permute-start.15 = (bf16[24,3584]{1,0:T(8,128)(2,1)S(1)}, bf16[24,3584]{1,0:T(8,128)(2,1)S(1)}, u32[]{:S(2)}, u32[]{:S(2)}) collective-permute-start(bf16[24,3584]{1,0:T(8,128)(2,1)S(1)} %shard_map.133), channel_id=1, source_target_pairs={{0,32},{32,64},{64,96},{96,128},{128,160},{160,192},{192,224},{224... | collective-permute-start | bytes 516104 | tf_op jit(solution)/shard_map/ppermute | solution.py:47
  165.3 9.5 %collective-permute-start.23 = (bf16[24,3584]{1,0:T(8,128)(2,1)S(1)}, bf16[24,3584]{1,0:T(8,128)(2,1)S(1)}, u32[]{:S(2)}, u32[]{:S(2)}) collective-permute-start(bf16[24,3584]{1,0:T(8,128)(2,1)S(1)} %get-tuple-element.29), channel_id=1, source_target_pairs={{32,0},{64,32},{96,64},{128,96},{160,128},{192,160},{224,192},{256... | collective-permute-start | bytes 516104 | tf_op jit(solution)/shard_map/ppermute | solution.py:47
  (13 other events, 116.8 us)

commit v4 on v3

--- a/solution.py
+++ b/solution.py
@@ -87,8 +87,24 @@
     return values * scale, scale
 
 
-def pack_kernel(info_ref, xa_ref, ra_ref, xb_ref, rb_ref, cot_ref, gain_ref, *outs):
-    width = xa_ref.shape[1]
+def first_kernel(info_ref, ra_ref, rb_ref, xa, xb, cot, gain_in, wg, wu, wd, *rest):
+    outs, (xa_ref, xb_ref, cot_ref, gain_ref, down, sems) = rest[:5], rest[5:]
+    width, units = wg.shape
+    merged = outs[4]
+    moves = (
+        (xa, xa_ref),
+        (gain_in, gain_ref),
+        (xb, xb_ref),
+        (cot, cot_ref),
+        (wd, down),
+        (wg, merged.at[pl.ds(0, width)]),
+        (wu, merged.at[pl.ds(width, width)]),
+    )
+    copies = [pltpu.make_async_copy(*move, sems.at[i]) for i, move in enumerate(moves)]
+    for copy in copies:
+        copy.start()
+    for copy in copies[:4]:
+        copy.wait()
     places = []
     for route_ref in (ra_ref, rb_ref):
         masks = slot_masks(info_ref, route_ref)
@@ -101,14 +117,20 @@
         packed = lax.dot_general(place, rows, TN, preferred_element_type=F32).astype(BF16)
         for j in range(4):
             outs[j][:, i * width : (i + 1) * width] = packed[j * SLOT : (j + 1) * SLOT]
-
-
-def merge_kernel(wg, wu, wd, out):
-    width, units = wg.shape
-    out[0:width, :] = wg[...]
-    out[width : 2 * width, :] = wu[...]
+    copies[4].wait()
     for at in range(0, width, units):
-        out[2 * width + at : 2 * width + at + units, :] = wd[:, at : at + units]
+        merged[2 * width + at : 2 * width + at + units, :] = down[:, at : at + units]
+    copies[5].wait()
+    copies[6].wait()
+
+
+def stage_kernel(own, a, b, c, left, right, last):
+    half = left.shape[1]
+    for i, ref in enumerate((own, a, b)):
+        rows = slice(i * SLOT, (i + 1) * SLOT)
+        left[rows, :] = ref[:, :half]
+        right[rows, :] = ref[:, half:]
+    last[...] = c[...]
 
 
 def hidden(rows, wg, wu):
@@ -122,21 +144,31 @@
     return jnp.concatenate([merged[start : start + 128, :] for start in starts], axis=1)
 
 
-def gather_rows(refs, at, width, scratch):
-    for i, ref in enumerate(refs):
-        scratch[64 * i : 64 * (i + 1), :] = ref[:, at : at + width]
+def gather_rows(refs, at, scratch, to, width):
+    *refs, order = refs
+    cols = slice(at, at + width)
+    into = slice(to, to + width)
+    for i, source in enumerate(order):
+        first, last = refs[i // 2], refs[2 + i // 2]
+        one, two = 3 * SLOT * (i % 2), SLOT * (i % 2)
+        row = 4 * SLOT * source
+        scratch[row : row + 3 * SLOT, into] = first[one : one + 3 * SLOT, cols]
+        scratch[row + 3 * SLOT : row + 4 * SLOT, into] = last[two : two + SLOT, cols]
+
+
+LEFT = (0, 1, 2, 3)
+RIGHT = (0, 2, 1, 3)
 
 
 def store_parts(part, cols, keep1, send1, keep2, send2):
-    keep1[:, cols] = part[0:64]
-    send1[:, cols] = part[64:128].astype(BF16)
-    keep2[:, cols] = part[128:192]
-    send2[:, cols] = part[192:256].astype(BF16)
-
-
-def fwd_kernel(c1, qr1, c2, pr2, wg, wu, wd, other, keep1, send1, keep2, send2, rows):
+    for ref, starts in ((keep1, (0, 64)), (send1, (128, 192)), (keep2, (32, 160)), (send2, (96, 224))):
+        for i, start in enumerate(starts):
+            ref[32 * i : 32 * (i + 1), cols] = part[start : start + 32].astype(ref.dtype)
+
+
+def fwd_kernel(l1, l2, l3, l4, wg, wu, wd, other, keep1, send1, keep2, send2, rows):
     width = rows.shape[1]
-    gather_rows((c1, qr1, c2, pr2), 0, width, rows)
+    gather_rows((l1, l2, l3, l4, LEFT), 0, rows, 0, width)
     inner = []
     for weights in ((wg[...], wu[...]), (other[0:width, :], other[width : 2 * width, :])):
         gate, up = hidden(rows[...], *weights)
@@ -151,11 +183,13 @@
 
 
 def bwd_kernel(
-    c1, qr1, c2, pr2, wg, wu, wd, other, _, keep1, send1, keep2, send2, rows, cots
+    l1, l2, l3, l4, r1, r2, r3, r4, wg, wu, wd, other, _, keep1, send1, keep2, send2, rows, cots
 ):
     width = rows.shape[1]
-    gather_rows((c1, qr1, c2, pr2), width, width, rows)
-    gather_rows((c1, qr1, c2, pr2), 2 * width, width, cots)
+    half = width // 2
+    gather_rows((l1, l2, l3, l4, LEFT), width, rows, 0, half)
+    gather_rows((r1, r2, r3, r4, RIGHT), 0, rows, half, half)
+    gather_rows((r1, r2, r3, r4, RIGHT), half, cots, 0, width)
     back = []
     products = None
     sources = (
@@ -253,15 +287,23 @@
     grad_ref[...] = jnp.where(pair == 0, grads[0], grads[1]).astype(BF16)
 
 
+def spread_x(value, first, second):
+    near = jnp.concatenate([value, hop(value, first)], axis=0)
+    return near, hop(near, second)
+
+
 def spread_rows(own, a, b, c):
-    got_a, got_b, got_c = hop(a, HOP_A), hop(b, HOP_B), hop(c, HOP_C)
-    half1 = jnp.concatenate([own, got_a], axis=0)
-    half2 = jnp.concatenate([got_b, got_c], axis=0)
-    p1 = hop(half1, HOP_X1)
-    q2 = hop(half2, HOP_X3)
-    c1 = jnp.concatenate([half1, p1], axis=0)
-    c2 = jnp.concatenate([half2, q2], axis=0)
-    return c1, hop(c1, HOP_X3), c2, hop(c2, HOP_X1)
+    half = own.shape[1] // 2
+    got_a, got_b = hop(a, HOP_A), hop(b, HOP_B)
+    left, right, c = kernel_call(
+        stage_kernel, [((3 * SLOT, half), BF16)] * 2 + [(c.shape, BF16)], 4, info=False
+    )(own, got_a, got_b, c)
+    got_c = hop(c, HOP_C)
+    lefts = spread_x(left, HOP_X1, HOP_X3)
+    rights = spread_x(right, HOP_X3, HOP_X1)
+    lefts += spread_x(got_c[:, :half], HOP_X1, HOP_X3)
+    rights += spread_x(got_c[:, half:], HOP_X3, HOP_X1)
+    return lefts, rights
 
 
 def return_rows(keep1, send1, keep2, send2):
@@ -292,22 +334,33 @@
 ):
     tokens, width = act_fwd.shape[1:]
     index = lax.axis_index("expert")
-    z = index // GRID_X
-    info = jnp.stack([z // 2, z % 2]).astype(jnp.int32)
+    info = jnp.stack([index >> 3, (index >> 2) & 1]).astype(jnp.int32)
     weights = (w_gate[0, 0], w_up[0, 0], w_down[0, 0])
     units = w_down.shape[2]
-    (merged,) = kernel_call(merge_kernel, [((3 * width, units), BF16)], 3, info=False)(*weights)
+    wide = [((SLOT, 3 * width), BF16)] * 4 + [((3 * width, units), BF16)]
+    sources = (act_fwd[0], act_bwd[0], cot_bwd[0], norm_gain, *weights)
+    vmem = pl.BlockSpec(memory_space=pltpu.VMEM)
+    *sent, merged = pl.pallas_call(
+        first_kernel,
+        out_shape=[jax.ShapeDtypeStruct(s, d) for s, d in wide],
+        in_specs=[pl.BlockSpec(memory_space=pltpu.SMEM), vmem, vmem]
+        + [pl.BlockSpec(memory_space=pltpu.HBM)] * 7,
+        out_specs=[vmem] * len(wide),
+        scratch_shapes=[pltpu.VMEM((tokens, width), BF16)] * 3
+        + [
+            pltpu.VMEM((1, width), F32),
+            pltpu.VMEM((units, width), BF16),
+            pltpu.SemaphoreType.DMA((7,)),
+        ],
+        compiler_params=pltpu.CompilerParams(vmem_limit_bytes=32 * 1024 * 1024),
+    )(info, route_fwd[0], route_bwd[0], *sources)
     other = hop(merged, HOP_W)
-    wide = [((SLOT, 3 * width), BF16)] * 4
-    sent = kernel_call(pack_kernel, wide, 6)(
-        info, act_fwd[0], route_fwd[0], act_bwd[0], route_bwd[0], cot_bwd[0], norm_gain
-    )
-    rows = spread_rows(*sent)
+    lefts, rights = spread_rows(*sent)
     outs = [((64, width), F32), ((64, width), BF16)] * 2
     scratch = pltpu.VMEM((256, width), BF16)
-    part_a = kernel_call(fwd_kernel, outs, 8, [scratch], info=False)(*rows, *weights, other)
-    part_b = kernel_call(bwd_kernel, outs, 9, [scratch] * 2, info=False)(
-        *rows, *weights, other, part_a[1]
+    part_a = kernel_call(fwd_kernel, outs, 8, [scratch], info=False)(*lefts, *weights, other)
+    part_b = kernel_call(bwd_kernel, outs, 13, [scratch] * 2, info=False)(
+        *lefts, *rights, *weights, other, part_a[1]
     )
     back_a = return_rows(*part_a)
     back_b = return_rows(*part_b)

time: 178 us -> 189 us (1.062)
  starting transfers between devices: 94.5 us -> 104 us
    ppermute x22 -> x26, starting transfers between devices: 78.9 us -> 88.7 us  [hop(): return lax.ppermute(value, 'expert', pairs)]
    ppermute x22 -> x26, waiting for transfers between devices: 54.8 us -> 53.4 us  [hop(): return lax.ppermute(value, 'expert', pairs)]
    unnamed x32 -> x36, local copies, waits for them, and re-layouts: 8.47 us -> 8.47 us
  transfers between devices with their start and end apart: 24 -> 28, of which waited for: 10 -> 7; matrix products, arithmetic and copies ran while one was open for 1% -> 1% of each run, Pallas kernels for 4% -> 5%
where the time goes in v4:
time: 189 us; the launch traced here: 186 us
  starting transfers between devices  104 us (55%)
  waiting for transfers between devices  57.6 us (30%)
  Pallas kernels  11.7 us (6%)
  local copies, waits for them, and re-layouts  11 us (6%)
    ppermute x26, starting transfers between devices, hop(): return lax.ppermute(value, 'expert', pairs)  88.7 us
    ppermute x26, waiting for transfers between devices, hop(): return lax.ppermute(value, 'expert', pairs)  53.4 us
    ppermute x2, starting transfers between devices, shifted(): return lax.ppermute(value, axis, pairs)  15.3 us
    unnamed x36, local copies, waits for them, and re-layouts  8.47 us
    ppermute x2, waiting for transfers between devices, shifted(): return lax.ppermute(value, axis, pairs)  4.2 us
  transfers between devices with their start and end apart: 28, of which 7 were waited for; matrix products, arithmetic and copies ran while one was open for 1% of the time, Pallas kernels for 5%

profile of v4, /device:TPU:1, one launch (start us, length us, event | category | flops | bytes accessed | tf_op | source)
XLA Modules:
  0.0 186.3 jit_solution(10124724524557899180)
XLA Ops:
  9.2 3.0 %shard_map.130 = (bf16[16,10752]{1,0:T(8,128)(2,1)S(1)}, bf16[16,10752]{1,0:T(8,128)(2,1)S(1)}, bf16[16,10752]{1,0:T(8,128)(2,1)S(1)}, bf16[16,10752]{1,0:T(8,128)(2,1)S(1)}, bf16[10752,128]{1,0:T(8,128)(2,1)S(1)}) custom-call(s32[2]{0:T(128)S(1)} %pad_add_fusion.info_ref, s32[24,2]{1,0:T(8,128)S(1)} %copy.16.ra_ref.route_ref, ...), custom_call_target="tpu_custom_call" | custom-call | tf_op jit(solution)/shard_map/pallas_call | solution.py:343
  12.3 11.5 %collective-permute-start = (bf16[16,10752]{1,0:T(8,128)(2,1)S(1)}, bf16[16,10752]{1,0:T(8,128)(2,1)S(1)}, u32[]{:S(2)}, u32[]{:S(2)}) collective-permute-start(bf16[16,10752]{1,0:T(8,128)(2,1)S(1)} %get-tuple-element.22), channel_id=1, source_target_pairs={{0,28},{1,29},{2,30},{3,31},{4,8},{5,9},{6,10},{7,11},{8,4},{9,5},... | collective-permute-start | bytes 1032200 | tf_op jit(solution)/shard_map/ppermute | solution.py:41
  25.7 3.1 %collective-permute-start.7 = (bf16[10752,128]{1,0:T(8,128)(2,1)S(1)}, bf16[10752,128]{1,0:T(8,128)(2,1)S(1)}, u32[]{:S(2)}, u32[]{:S(2)}) collective-permute-start(bf16[10752,128]{1,0:T(8,128)(2,1)S(1)} %get-tuple-element.27), channel_id=1, source_target_pairs={{0,4},{1,5},{2,6},{3,7},{4,0},{5,1},{6,2},{7,3},{8,12},{9,13},{10,... | collective-permute-start | bytes 8257544 | tf_op jit(solution)/shard_map/ppermute | solution.py:41
  28.8 9.7 %collective-permute-done.a = bf16[16,10752]{1,0:T(8,128)(2,1)S(1)} collective-permute-done((bf16[16,10752]{1,0:T(8,128)(2,1)S(1)}, bf16[16,10752]{1,0:T(8,128)(2,1)S(1)}, u32[]{:S(2)}, u32[]{:S(2)}) %collective-permute-start) | collective-permute-done | bytes 344096 | tf_op jit(solution)/shard_map/ppermute | solution.py:41
  38.7 3.2 %collective-permute-start.2 = (bf16[48,5376]{1,0:T(8,128)(2,1)S(1)}, bf16[48,5376]{1,0:T(8,128)(2,1)S(1)}, u32[]{:S(2)}, u32[]{:S(2)}) collective-permute-start(bf16[48,5376]{1,0:T(8,128)(2,1)S(1)} %get-tuple-element.25), channel_id=1, source_target_pairs={{0,1},{1,0},{2,3},{3,2},{4,5},{5,4},{6,7},{7,6},{8,9},{9,8},{10,11... | collective-permute-start | bytes 1548296 | tf_op jit(solution)/shard_map/ppermute | solution.py:41
  41.9 3.5 %collective-permute-start.4 = (bf16[16,10752]{1,0:T(8,128)(2,1)S(1)}, bf16[16,10752]{1,0:T(8,128)(2,1)S(1)}, u32[]{:S(2)}, u32[]{:S(2)}) collective-permute-start(bf16[16,10752]{1,0:T(8,128)(2,1)S(1)} %get-tuple-element.26), channel_id=1, source_target_pairs={{0,20},{1,21},{2,22},{3,23},{4,16},{5,17},{6,18},{7,19},{8,28},{9,... | collective-permute-start | bytes 1032200 | tf_op jit(solution)/shard_map/ppermute | solution.py:41
  45.4 3.7 %collective-permute-start.16 = (bf16[48,5376]{1,0:T(8,128)(2,1)S(1)}, bf16[48,5376]{1,0:T(8,128)(2,1)S(1)}, u32[]{:S(2)}, u32[]{:S(2)}) collective-permute-start(bf16[48,5376]{1,0:T(8,128)(2,1)S(1)} %get-tuple-element.32), channel_id=1, source_target_pairs={{0,3},{1,2},{2,1},{3,0},{4,7},{5,6},{6,5},{7,4},{8,11},{9,10},{10,... | collective-permute-start | bytes 1548296 | tf_op jit(solution)/shard_map/ppermute | solution.py:41
  49.1 13.8 %collective-permute-done.4 = bf16[16,10752]{1,0:T(8,128)(2,1)S(1)} collective-permute-done((bf16[16,10752]{1,0:T(8,128)(2,1)S(1)}, bf16[16,10752]{1,0:T(8,128)(2,1)S(1)}, u32[]{:S(2)}, u32[]{:S(2)}) %collective-permute-start.4) | collective-permute-done | bytes 344096 | tf_op jit(solution)/shard_map/ppermute | solution.py:41
  65.2 4.5 %collective-permute-start.18 = (bf16[16,5376]{1,0:T(8,128)(2,1)S(1)}, bf16[16,5376]{1,0:T(8,128)(2,1)S(1)}, u32[]{:S(2)}, u32[]{:S(2)}) collective-permute-start(bf16[16,5376]{1,0:T(8,128)(2,1)S(1)} %get-tuple-element.39), channel_id=1, source_target_pairs={{0,3},{1,2},{2,1},{3,0},{4,7},{5,6},{6,5},{7,4},{8,11},{9,10},{10,... | collective-permute-start | bytes 516104 | tf_op jit(solution)/shard_map/ppermute | solution.py:41
  71.8 4.5 %collective-permute-start.6 = (bf16[32,5376]{1,0:T(8,128)(2,1)S(1)}, bf16[32,5376]{1,0:T(8,128)(2,1)S(1)}, u32[]{:S(2)}, u32[]{:S(2)}) collective-permute-start(bf16[32,5376]{1,0:T(8,128)(2,1)S(1)} %pad_maximum_fusion.l3), channel_id=1, source_target_pairs={{0,3},{1,2},{2,1},{3,0},{4,7},{5,6},{6,5},{7,4},{8,11},{9,10},{10,... | collective-permute-start | bytes 1032200 | tf_op jit(solution)/shard_map/ppermute | solution.py:41
  78.3 23.8 %collective-permute-done.6.l4 = bf16[32,5376]{1,0:T(8,128)(2,1)S(1)} collective-permute-done((bf16[32,5376]{1,0:T(8,128)(2,1)S(1)}, bf16[32,5376]{1,0:T(8,128)(2,1)S(1)}, u32[]{:S(2)}, u32[]{:S(2)}) %collective-permute-start.6) | collective-permute-done | bytes 344096 | tf_op jit(solution)/shard_map/ppermute | solution.py:41
  103.8 4.5 %collective-permute-start.8 = (bf16[64,3584]{1,0:T(8,128)(2,1)S(1)}, bf16[64,3584]{1,0:T(8,128)(2,1)S(1)}, u32[]{:S(2)}, u32[]{:S(2)}) collective-permute-start(bf16[64,3584]{1,0:T(8,128)(2,1)S(1)} %get-tuple-element.29._), channel_id=1, source_target_pairs={{0,3},{1,2},{2,1},{3,0},{4,7},{5,6},{6,5},{7,4},{8,11},{9,10},{10,... | collective-permute-start | bytes 1376264 | tf_op jit(solution)/shard_map/ppermute | solution.py:41
  110.3 3.4 %collective-permute-start.11 = (bf16[64,3584]{1,0:T(8,128)(2,1)S(1)}, bf16[64,3584]{1,0:T(8,128)(2,1)S(1)}, u32[]{:S(2)}, u32[]{:S(2)}) collective-permute-start(bf16[64,3584]{1,0:T(8,128)(2,1)S(1)} %get-tuple-element.31), channel_id=1, source_target_pairs={{0,1},{1,0},{2,3},{3,2},{4,5},{5,4},{6,7},{7,6},{8,9},{9,8},{10,11... | collective-permute-start | bytes 1376264 | tf_op jit(solution)/shard_map/ppermute | solution.py:41
  113.7 3.2 %collective-permute-done.19.r4 = bf16[32,5376]{1,0:T(8,128)(2,1)S(1)} collective-permute-done((bf16[32,5376]{1,0:T(8,128)(2,1)S(1)}, bf16[32,5376]{1,0:T(8,128)(2,1)S(1)}, u32[]{:S(2)}, u32[]{:S(2)}) %collective-permute-start.19) | collective-permute-done | bytes 344096 | tf_op jit(solution)/shard_map/ppermute | solution.py:41
  116.8 3.3 %shard_map.134 = (f32[64,3584]{1,0:T(8,128)S(1)}, bf16[64,3584]{1,0:T(8,128)(2,1)S(1)}, f32[64,3584]{1,0:T(8,128)S(1)}, bf16[64,3584]{1,0:T(8,128)(2,1)S(1)}) custom-call(bf16[96,5376]{1,0:T(8,128)(2,1)S(1)} %constant_dynamic-update-slice_fusion.l1, bf16[96,5376]{1,0:T(8,128)(2,1)S(1)} %collective-permute-done.3.l2, ...), custom_call_target="tpu_custom_call" | custom-call | tf_op jit(solution)/shard_map/pallas_call | solution.py:362
  124.5 3.1 %collective-permute-start.9 = (bf16[32,3584]{1,0:T(8,128)(2,1)S(1)}, bf16[32,3584]{1,0:T(8,128)(2,1)S(1)}, u32[]{:S(2)}, u32[]{:S(2)}) collective-permute-start(bf16[32,3584]{1,0:T(8,128)(2,1)S(1)} %slice.113), channel_id=1, source_target_pairs={{0,1},{1,0},{2,3},{3,2},{4,5},{5,4},{6,7},{7,6},{8,9},{9,8},{10,11... | collective-permute-start | bytes 688136 | tf_op jit(solution)/shard_map/ppermute | solution.py:41
  127.7 4.6 %collective-permute-start.12 = (bf16[32,3584]{1,0:T(8,128)(2,1)S(1)}, bf16[32,3584]{1,0:T(8,128)(2,1)S(1)}, u32[]{:S(2)}, u32[]{:S(2)}) collective-permute-start(bf16[32,3584]{1,0:T(8,128)(2,1)S(1)} %slice.112), channel_id=1, source_target_pairs={{0,3},{1,2},{2,1},{3,0},{4,7},{5,6},{6,5},{7,4},{8,11},{9,10},{10,... | collective-permute-start | bytes 688136 | tf_op jit(solution)/shard_map/ppermute | solution.py:41
  139.6 2.9 %collective-permute-start.10 = (bf16[16,3584]{1,0:T(8,128)(2,1)S(1)}, bf16[16,3584]{1,0:T(8,128)(2,1)S(1)}, u32[]{:S(2)}, u32[]{:S(2)}) collective-permute-start(bf16[16,3584]{1,0:T(8,128)(2,1)S(1)} %get-tuple-element.47), channel_id=1, source_target_pairs={{0,28},{1,29},{2,30},{3,31},{4,8},{5,9},{6,10},{7,11},{8,4},{9,5},... | collective-permute-start | bytes 344072 | tf_op jit(solution)/shard_map/ppermute | solution.py:41
  144.9 5.4 %collective-permute-start.14 = (bf16[16,3584]{1,0:T(8,128)(2,1)S(1)}, bf16[16,3584]{1,0:T(8,128)(2,1)S(1)}, u32[]{:S(2)}, u32[]{:S(2)}) collective-permute-start(bf16[16,3584]{1,0:T(8,128)(2,1)S(1)} %get-tuple-element.45), channel_id=1, source_target_pairs={{0,20},{1,21},{2,22},{3,23},{4,16},{5,17},{6,18},{7,19},{8,28},{9,... | collective-permute-start | bytes 344072 | tf_op jit(solution)/shard_map/ppermute | solution.py:41
  150.4 2.8 %collective-permute-start.22 = (bf16[16,3584]{1,0:T(8,128)(2,1)S(1)}, bf16[16,3584]{1,0:T(8,128)(2,1)S(1)}, u32[]{:S(2)}, u32[]{:S(2)}) collective-permute-start(bf16[16,3584]{1,0:T(8,128)(2,1)S(1)} %get-tuple-element.43), channel_id=1, source_target_pairs={{0,28},{1,29},{2,30},{3,31},{4,8},{5,9},{6,10},{7,11},{8,4},{9,5},... | collective-permute-start | bytes 344072 | tf_op jit(solution)/shard_map/ppermute | solution.py:41
  153.3 3.3 %collective-permute-start.25 = (bf16[16,3584]{1,0:T(8,128)(2,1)S(1)}, bf16[16,3584]{1,0:T(8,128)(2,1)S(1)}, u32[]{:S(2)}, u32[]{:S(2)}) collective-permute-start(bf16[16,3584]{1,0:T(8,128)(2,1)S(1)} %get-tuple-element.42), channel_id=1, source_target_pairs={{0,24},{1,25},{2,26},{3,27},{4,12},{5,13},{6,14},{7,15},{8,0},{9,1... | collective-permute-start | bytes 344072 | tf_op jit(solution)/shard_map/ppermute | solution.py:41
  156.6 4.3 %collective-permute-start.26 = (bf16[16,3584]{1,0:T(8,128)(2,1)S(1)}, bf16[16,3584]{1,0:T(8,128)(2,1)S(1)}, u32[]{:S(2)}, u32[]{:S(2)}) collective-permute-start(bf16[16,3584]{1,0:T(8,128)(2,1)S(1)} %get-tuple-element.41), channel_id=1, source_target_pairs={{0,20},{1,21},{2,22},{3,23},{4,16},{5,17},{6,18},{7,19},{8,28},{9,... | collective-permute-start | bytes 344072 | tf_op jit(solution)/shard_map/ppermute | solution.py:41
  162.9 13.4 %collective-permute-start.15 = (bf16[24,3584]{1,0:T(8,128)(2,1)S(1)}, bf16[24,3584]{1,0:T(8,128)(2,1)S(1)}, u32[]{:S(2)}, u32[]{:S(2)}) collective-permute-start(bf16[24,3584]{1,0:T(8,128)(2,1)S(1)} %shard_map.133), channel_id=1, source_target_pairs={{0,32},{32,64},{64,96},{96,128},{128,160},{160,192},{192,224},{224... | collective-permute-start | bytes 516104 | tf_op jit(solution)/shard_map/ppermute | solution.py:47
  180.8 4.2 %collective-permute-done.27 = bf16[24,3584]{1,0:T(8,128)(2,1)S(1)} collective-permute-done((bf16[24,3584]{1,0:T(8,128)(2,1)S(1)}, bf16[24,3584]{1,0:T(8,128)(2,1)S(1)}, u32[]{:S(2)}, u32[]{:S(2)}) %collective-permute-start.27) | collective-permute-done | bytes 172064 | tf_op jit(solution)/shard_map/ppermute | solution.py:47
  (101 shorter events, 42.2 us)
Async XLA Ops:
  12.3 26.2 %collective-permute-start = (bf16[16,10752]{1,0:T(8,128)(2,1)S(1)}, bf16[16,10752]{1,0:T(8,128)(2,1)S(1)}, u32[]{:S(2)}, u32[]{:S(2)}) collective-permute-start(bf16[16,10752]{1,0:T(8,128)(2,1)S(1)} %get-tuple-element.22), channel_id=1, source_target_pairs={{0,28},{1,29},{2,30},{3,31},{4,8},{5,9},{6,10},{7,11},{8,4},{9,5},... | collective-permute-start | bytes 1032200 | tf_op jit(solution)/shard_map/ppermute | solution.py:41
  23.8 14.7 %collective-permute-start.1 = (bf16[16,10752]{1,0:T(8,128)(2,1)S(1)}, bf16[16,10752]{1,0:T(8,128)(2,1)S(1)}, u32[]{:S(2)}, u32[]{:S(2)}) collective-permute-start(bf16[16,10752]{1,0:T(8,128)(2,1)S(1)} %get-tuple-element.23), channel_id=1, source_target_pairs={{0,8},{1,9},{2,10},{3,11},{4,28},{5,29},{6,30},{7,31},{8,16},{9,17... | collective-permute-start | bytes 1032200 | tf_op jit(solution)/shard_map/ppermute | solution.py:41
  25.7 76.4 %collective-permute-start.7 = (bf16[10752,128]{1,0:T(8,128)(2,1)S(1)}, bf16[10752,128]{1,0:T(8,128)(2,1)S(1)}, u32[]{:S(2)}, u32[]{:S(2)}) collective-permute-start(bf16[10752,128]{1,0:T(8,128)(2,1)S(1)} %get-tuple-element.27), channel_id=1, source_target_pairs={{0,4},{1,5},{2,6},{3,7},{4,0},{5,1},{6,2},{7,3},{8,12},{9,13},{10,... | collective-permute-start | bytes 8257544 | tf_op jit(solution)/shard_map/ppermute | solution.py:41
  38.7 31.0 %collective-permute-start.2 = (bf16[48,5376]{1,0:T(8,128)(2,1)S(1)}, bf16[48,5376]{1,0:T(8,128)(2,1)S(1)}, u32[]{:S(2)}, u32[]{:S(2)}) collective-permute-start(bf16[48,5376]{1,0:T(8,128)(2,1)S(1)} %get-tuple-element.25), channel_id=1, source_target_pairs={{0,1},{1,0},{2,3},{3,2},{4,5},{5,4},{6,7},{7,6},{8,9},{9,8},{10,11... | collective-permute-start | bytes 1548296 | tf_op jit(solution)/shard_map/ppermute | solution.py:41
  41.9 21.1 %collective-permute-start.4 = (bf16[16,10752]{1,0:T(8,128)(2,1)S(1)}, bf16[16,10752]{1,0:T(8,128)(2,1)S(1)}, u32[]{:S(2)}, u32[]{:S(2)}) collective-permute-start(bf16[16,10752]{1,0:T(8,128)(2,1)S(1)} %get-tuple-element.26), channel_id=1, source_target_pairs={{0,20},{1,21},{2,22},{3,23},{4,16},{5,17},{6,18},{7,19},{8,28},{9,... | collective-permute-start | bytes 1032200 | tf_op jit(solution)/shard_map/ppermute | solution.py:41
  45.4 30.9 %collective-permute-start.16 = (bf16[48,5376]{1,0:T(8,128)(2,1)S(1)}, bf16[48,5376]{1,0:T(8,128)(2,1)S(1)}, u32[]{:S(2)}, u32[]{:S(2)}) collective-permute-start(bf16[48,5376]{1,0:T(8,128)(2,1)S(1)} %get-tuple-element.32), channel_id=1, source_target_pairs={{0,3},{1,2},{2,1},{3,0},{4,7},{5,6},{6,5},{7,4},{8,11},{9,10},{10,... | collective-permute-start | bytes 1548296 | tf_op jit(solution)/shard_map/ppermute | solution.py:41
  65.2 43.1 %collective-permute-start.18 = (bf16[16,5376]{1,0:T(8,128)(2,1)S(1)}, bf16[16,5376]{1,0:T(8,128)(2,1)S(1)}, u32[]{:S(2)}, u32[]{:S(2)}) collective-permute-start(bf16[16,5376]{1,0:T(8,128)(2,1)S(1)} %get-tuple-element.39), channel_id=1, source_target_pairs={{0,3},{1,2},{2,1},{3,0},{4,7},{5,6},{6,5},{7,4},{8,11},{9,10},{10,... | collective-permute-start | bytes 516104 | tf_op jit(solution)/shard_map/ppermute | solution.py:41
  69.7 32.4 %collective-permute-start.3 = (bf16[96,5376]{1,0:T(8,128)(2,1)S(1)}, bf16[96,5376]{1,0:T(8,128)(2,1)S(1)}, u32[]{:S(2)}, u32[]{:S(2)}) collective-permute-start(bf16[96,5376]{1,0:T(8,128)(2,1)S(1)} %constant_dynamic-update-slice_fusion.l1), channel_id=1, source_target_pairs={{0,3},{1,2},{2,1},{3,0},{4,7},{5,6},{6,5},{7,4},{8,11},{9,10},{10,... | collective-permute-start | bytes 3096584 | tf_op jit(solution)/shard_map/ppermute | solution.py:41
  71.8 30.3 %collective-permute-start.6 = (bf16[32,5376]{1,0:T(8,128)(2,1)S(1)}, bf16[32,5376]{1,0:T(8,128)(2,1)S(1)}, u32[]{:S(2)}, u32[]{:S(2)}) collective-permute-start(bf16[32,5376]{1,0:T(8,128)(2,1)S(1)} %pad_maximum_fusion.l3), channel_id=1, source_target_pairs={{0,3},{1,2},{2,1},{3,0},{4,7},{5,6},{6,5},{7,4},{8,11},{9,10},{10,... | collective-permute-start | bytes 1032200 | tf_op jit(solution)/shard_map/ppermute | solution.py:41
  76.4 40.5 %collective-permute-start.17 = (bf16[96,5376]{1,0:T(8,128)(2,1)S(1)}, bf16[96,5376]{1,0:T(8,128)(2,1)S(1)}, u32[]{:S(2)}, u32[]{:S(2)}) collective-permute-start(bf16[96,5376]{1,0:T(8,128)(2,1)S(1)} %constant_dynamic-update-slice_fusion.2.r1), channel_id=1, source_target_pairs={{0,1},{1,0},{2,3},{3,2},{4,5},{5,4},{6,7},{7,6},{8,9},{9,8},{10,11... | collective-permute-start | bytes 3096584 | tf_op jit(solution)/shard_map/ppermute | solution.py:41
  103.8 20.5 %collective-permute-start.8 = (bf16[64,3584]{1,0:T(8,128)(2,1)S(1)}, bf16[64,3584]{1,0:T(8,128)(2,1)S(1)}, u32[]{:S(2)}, u32[]{:S(2)}) collective-permute-start(bf16[64,3584]{1,0:T(8,128)(2,1)S(1)} %get-tuple-element.29._), channel_id=1, source_target_pairs={{0,3},{1,2},{2,1},{3,0},{4,7},{5,6},{6,5},{7,4},{8,11},{9,10},{10,... | collective-permute-start | bytes 1376264 | tf_op jit(solution)/shard_map/ppermute | solution.py:41
  110.3 17.3 %collective-permute-start.11 = (bf16[64,3584]{1,0:T(8,128)(2,1)S(1)}, bf16[64,3584]{1,0:T(8,128)(2,1)S(1)}, u32[]{:S(2)}, u32[]{:S(2)}) collective-permute-start(bf16[64,3584]{1,0:T(8,128)(2,1)S(1)} %get-tuple-element.31), channel_id=1, source_target_pairs={{0,1},{1,0},{2,3},{3,2},{4,5},{5,4},{6,7},{7,6},{8,9},{9,8},{10,11... | collective-permute-start | bytes 1376264 | tf_op jit(solution)/shard_map/ppermute | solution.py:41
  122.1 13.0 %collective-permute-start.23 = (bf16[64,3584]{1,0:T(8,128)(2,1)S(1)}, bf16[64,3584]{1,0:T(8,128)(2,1)S(1)}, u32[]{:S(2)}, u32[]{:S(2)}) collective-permute-start(bf16[64,3584]{1,0:T(8,128)(2,1)S(1)} %get-tuple-element.36), channel_id=1, source_target_pairs={{0,1},{1,0},{2,3},{3,2},{4,5},{5,4},{6,7},{7,6},{8,9},{9,8},{10,11... | collective-permute-start | bytes 1376264 | tf_op jit(solution)/shard_map/ppermute | solution.py:41
  124.5 15.0 %collective-permute-start.9 = (bf16[32,3584]{1,0:T(8,128)(2,1)S(1)}, bf16[32,3584]{1,0:T(8,128)(2,1)S(1)}, u32[]{:S(2)}, u32[]{:S(2)}) collective-permute-start(bf16[32,3584]{1,0:T(8,128)(2,1)S(1)} %slice.113), channel_id=1, source_target_pairs={{0,1},{1,0},{2,3},{3,2},{4,5},{5,4},{6,7},{7,6},{8,9},{9,8},{10,11... | collective-permute-start | bytes 688136 | tf_op jit(solution)/shard_map/ppermute | solution.py:41
  127.7 14.8 %collective-permute-start.12 = (bf16[32,3584]{1,0:T(8,128)(2,1)S(1)}, bf16[32,3584]{1,0:T(8,128)(2,1)S(1)}, u32[]{:S(2)}, u32[]{:S(2)}) collective-permute-start(bf16[32,3584]{1,0:T(8,128)(2,1)S(1)} %slice.112), channel_id=1, source_target_pairs={{0,3},{1,2},{2,1},{3,0},{4,7},{5,6},{6,5},{7,4},{8,11},{9,10},{10,... | collective-permute-start | bytes 688136 | tf_op jit(solution)/shard_map/ppermute | solution.py:41
  132.4 17.9 %collective-permute-start.21 = (bf16[32,3584]{1,0:T(8,128)(2,1)S(1)}, bf16[32,3584]{1,0:T(8,128)(2,1)S(1)}, u32[]{:S(2)}, u32[]{:S(2)}) collective-permute-start(bf16[32,3584]{1,0:T(8,128)(2,1)S(1)} %slice.111), channel_id=1, source_target_pairs={{0,1},{1,0},{2,3},{3,2},{4,5},{5,4},{6,7},{7,6},{8,9},{9,8},{10,11... | collective-permute-start | bytes 688136 | tf_op jit(solution)/shard_map/ppermute | solution.py:41
  135.2 17.9 %collective-permute-start.24 = (bf16[32,3584]{1,0:T(8,128)(2,1)S(1)}, bf16[32,3584]{1,0:T(8,128)(2,1)S(1)}, u32[]{:S(2)}, u32[]{:S(2)}) collective-permute-start(bf16[32,3584]{1,0:T(8,128)(2,1)S(1)} %slice.110), channel_id=1, source_target_pairs={{0,3},{1,2},{2,1},{3,0},{4,7},{5,6},{6,5},{7,4},{8,11},{9,10},{10,... | collective-permute-start | bytes 688136 | tf_op jit(solution)/shard_map/ppermute | solution.py:41
  139.6 17.1 %collective-permute-start.10 = (bf16[16,3584]{1,0:T(8,128)(2,1)S(1)}, bf16[16,3584]{1,0:T(8,128)(2,1)S(1)}, u32[]{:S(2)}, u32[]{:S(2)}) collective-permute-start(bf16[16,3584]{1,0:T(8,128)(2,1)S(1)} %get-tuple-element.47), channel_id=1, source_target_pairs={{0,28},{1,29},{2,30},{3,31},{4,8},{5,9},{6,10},{7,11},{8,4},{9,5},... | collective-permute-start | bytes 344072 | tf_op jit(solution)/shard_map/ppermute | solution.py:41
  142.6 18.6 %collective-permute-start.13 = (bf16[16,3584]{1,0:T(8,128)(2,1)S(1)}, bf16[16,3584]{1,0:T(8,128)(2,1)S(1)}, u32[]{:S(2)}, u32[]{:S(2)}) collective-permute-start(bf16[16,3584]{1,0:T(8,128)(2,1)S(1)} %get-tuple-element.46), channel_id=1, source_target_pairs={{0,24},{1,25},{2,26},{3,27},{4,12},{5,13},{6,14},{7,15},{8,0},{9,1... | collective-permute-start | bytes 344072 | tf_op jit(solution)/shard_map/ppermute | solution.py:41
  144.9 16.3 %collective-permute-start.14 = (bf16[16,3584]{1,0:T(8,128)(2,1)S(1)}, bf16[16,3584]{1,0:T(8,128)(2,1)S(1)}, u32[]{:S(2)}, u32[]{:S(2)}) collective-permute-start(bf16[16,3584]{1,0:T(8,128)(2,1)S(1)} %get-tuple-element.45), channel_id=1, source_target_pairs={{0,20},{1,21},{2,22},{3,23},{4,16},{5,17},{6,18},{7,19},{8,28},{9,... | collective-permute-start | bytes 344072 | tf_op jit(solution)/shard_map/ppermute | solution.py:41
  150.4 25.9 %collective-permute-start.22 = (bf16[16,3584]{1,0:T(8,128)(2,1)S(1)}, bf16[16,3584]{1,0:T(8,128)(2,1)S(1)}, u32[]{:S(2)}, u32[]{:S(2)}) collective-permute-start(bf16[16,3584]{1,0:T(8,128)(2,1)S(1)} %get-tuple-element.43), channel_id=1, source_target_pairs={{0,28},{1,29},{2,30},{3,31},{4,8},{5,9},{6,10},{7,11},{8,4},{9,5},... | collective-permute-start | bytes 344072 | tf_op jit(solution)/shard_map/ppermute | solution.py:41
  153.3 23.0 %collective-permute-start.25 = (bf16[16,3584]{1,0:T(8,128)(2,1)S(1)}, bf16[16,3584]{1,0:T(8,128)(2,1)S(1)}, u32[]{:S(2)}, u32[]{:S(2)}) collective-permute-start(bf16[16,3584]{1,0:T(8,128)(2,1)S(1)} %get-tuple-element.42), channel_id=1, source_target_pairs={{0,24},{1,25},{2,26},{3,27},{4,12},{5,13},{6,14},{7,15},{8,0},{9,1... | collective-permute-start | bytes 344072 | tf_op jit(solution)/shard_map/ppermute | solution.py:41
  156.6 19.7 %collective-permute-start.26 = (bf16[16,3584]{1,0:T(8,128)(2,1)S(1)}, bf16[16,3584]{1,0:T(8,128)(2,1)S(1)}, u32[]{:S(2)}, u32[]{:S(2)}) collective-permute-start(bf16[16,3584]{1,0:T(8,128)(2,1)S(1)} %get-tuple-element.41), channel_id=1, source_target_pairs={{0,20},{1,21},{2,22},{3,23},{4,16},{5,17},{6,18},{7,19},{8,28},{9,... | collective-permute-start | bytes 344072 | tf_op jit(solution)/shard_map/ppermute | solution.py:41
  162.9 17.9 %collective-permute-start.15 = (bf16[24,3584]{1,0:T(8,128)(2,1)S(1)}, bf16[24,3584]{1,0:T(8,128)(2,1)S(1)}, u32[]{:S(2)}, u32[]{:S(2)}) collective-permute-start(bf16[24,3584]{1,0:T(8,128)(2,1)S(1)} %shard_map.133), channel_id=1, source_target_pairs={{0,32},{32,64},{64,96},{96,128},{128,160},{160,192},{192,224},{224... | collective-permute-start | bytes 516104 | tf_op jit(solution)/shard_map/ppermute | solution.py:47
  (20 other events, 421.8 us)

commit v5 on v4

--- a/solution.py
+++ b/solution.py
@@ -124,15 +124,6 @@
     copies[6].wait()
 
 
-def stage_kernel(own, a, b, c, left, right, last):
-    half = left.shape[1]
-    for i, ref in enumerate((own, a, b)):
-        rows = slice(i * SLOT, (i + 1) * SLOT)
-        left[rows, :] = ref[:, :half]
-        right[rows, :] = ref[:, half:]
-    last[...] = c[...]
-
-
 def hidden(rows, wg, wu):
     both = jnp.dot(rows, jnp.concatenate([wg, wu], axis=1), preferred_element_type=F32)
     return both[:, :128], both[:, 128:]
@@ -144,31 +135,21 @@
     return jnp.concatenate([merged[start : start + 128, :] for start in starts], axis=1)
 
 
-def gather_rows(refs, at, scratch, to, width):
-    *refs, order = refs
-    cols = slice(at, at + width)
-    into = slice(to, to + width)
-    for i, source in enumerate(order):
-        first, last = refs[i // 2], refs[2 + i // 2]
-        one, two = 3 * SLOT * (i % 2), SLOT * (i % 2)
-        row = 4 * SLOT * source
-        scratch[row : row + 3 * SLOT, into] = first[one : one + 3 * SLOT, cols]
-        scratch[row + 3 * SLOT : row + 4 * SLOT, into] = last[two : two + SLOT, cols]
-
-
-LEFT = (0, 1, 2, 3)
-RIGHT = (0, 2, 1, 3)
+def gather_rows(refs, at, width, scratch):
+    for i, ref in enumerate(refs):
+        scratch[64 * i : 64 * (i + 1), :] = ref[:, at : at + width]
 
 
 def store_parts(part, cols, keep1, send1, keep2, send2):
-    for ref, starts in ((keep1, (0, 64)), (send1, (128, 192)), (keep2, (32, 160)), (send2, (96, 224))):
-        for i, start in enumerate(starts):
-            ref[32 * i : 32 * (i + 1), cols] = part[start : start + 32].astype(ref.dtype)
-
-
-def fwd_kernel(l1, l2, l3, l4, wg, wu, wd, other, keep1, send1, keep2, send2, rows):
+    keep1[:, cols] = part[0:64]
+    send1[:, cols] = part[64:128].astype(BF16)
+    keep2[:, cols] = part[128:192]
+    send2[:, cols] = part[192:256].astype(BF16)
+
+
+def fwd_kernel(c1, qr1, c2, pr2, wg, wu, wd, other, keep1, send1, keep2, send2, rows):
     width = rows.shape[1]
-    gather_rows((l1, l2, l3, l4, LEFT), 0, rows, 0, width)
+    gather_rows((c1, qr1, c2, pr2), 0, width, rows)
     inner = []
     for weights in ((wg[...], wu[...]), (other[0:width, :], other[width : 2 * width, :])):
         gate, up = hidden(rows[...], *weights)
@@ -183,13 +164,11 @@
 
 
 def bwd_kernel(
-    l1, l2, l3, l4, r1, r2, r3, r4, wg, wu, wd, other, _, keep1, send1, keep2, send2, rows, cots
+    c1, qr1, c2, pr2, wg, wu, wd, other, _1, _2, keep1, send1, keep2, send2, rows, cots
 ):
     width = rows.shape[1]
-    half = width // 2
-    gather_rows((l1, l2, l3, l4, LEFT), width, rows, 0, half)
-    gather_rows((r1, r2, r3, r4, RIGHT), 0, rows, half, half)
-    gather_rows((r1, r2, r3, r4, RIGHT), half, cots, 0, width)
+    gather_rows((c1, qr1, c2, pr2), 0, width, rows)
+    gather_rows((c1, qr1, c2, pr2), width, width, cots)
     back = []
     products = None
     sources = (
@@ -256,18 +235,14 @@
     return total
 
 
-def fwd_out_kernel(info_ref, x_ref, route_ref, weight_ref, own, a, b, c, out_ref):
+def last_kernel(
+    info_ref, xa_ref, ra_ref, wa_ref, x_ref, route_ref, weight_ref, cot_ref, gain_ref, *rest
+):
+    parts_a, parts = [r[...] for r in rest[:4]], [r[...] for r in rest[4:8]]
+    out_a_ref, out_ref, grad_ref = rest[8:]
+    mixed = mixed_rows(slot_masks(info_ref, ra_ref), wa_ref, parts_a)
+    out_a_ref[...] = (xa_ref[...].astype(F32) + mixed).astype(BF16)
     masks = slot_masks(info_ref, route_ref)
-    parts = [own[...], a[...], b[...], c[...]]
-    mixed = mixed_rows(masks, weight_ref, parts)
-    out_ref[...] = (x_ref[...].astype(F32) + mixed).astype(BF16)
-
-
-def bwd_out_kernel(
-    info_ref, x_ref, route_ref, weight_ref, cot_ref, gain_ref, own, a, b, c, out_ref, grad_ref
-):
-    masks = slot_masks(info_ref, route_ref)
-    parts = [own[...], a[...], b[...], c[...]]
     d_normed = mixed_rows(masks, weight_ref, parts)
     unit, scale = normalized(x_ref[...])
     q_term = d_normed * gain_ref[...]
@@ -287,28 +262,30 @@
     grad_ref[...] = jnp.where(pair == 0, grads[0], grads[1]).astype(BF16)
 
 
-def spread_x(value, first, second):
-    near = jnp.concatenate([value, hop(value, first)], axis=0)
-    return near, hop(near, second)
+def spread_x(half1, half2):
+    c1 = jnp.concatenate([half1, hop(half1, HOP_X1)], axis=0)
+    c2 = jnp.concatenate([half2, hop(half2, HOP_X3)], axis=0)
+    return c1, hop(c1, HOP_X3), c2, hop(c2, HOP_X1)
 
 
 def spread_rows(own, a, b, c):
-    half = own.shape[1] // 2
-    got_a, got_b = hop(a, HOP_A), hop(b, HOP_B)
-    left, right, c = kernel_call(
-        stage_kernel, [((3 * SLOT, half), BF16)] * 2 + [(c.shape, BF16)], 4, info=False
-    )(own, got_a, got_b, c)
-    got_c = hop(c, HOP_C)
-    lefts = spread_x(left, HOP_X1, HOP_X3)
-    rights = spread_x(right, HOP_X3, HOP_X1)
-    lefts += spread_x(got_c[:, :half], HOP_X1, HOP_X3)
-    rights += spread_x(got_c[:, half:], HOP_X3, HOP_X1)
-    return lefts, rights
-
-
-def return_rows(keep1, send1, keep2, send2):
+    got_a, got_b, got_c = hop(a, HOP_A), hop(b, HOP_B), hop(c, HOP_C)
+    half1 = jnp.concatenate([own, got_a], axis=0)
+    half2 = jnp.concatenate([got_b, got_c], axis=0)
+    width = own.shape[1] // 3
+    return (
+        spread_x(half1[:, :width], half2[:, :width]),
+        spread_x(half1[:, width:], half2[:, width:]),
+    )
+
+
+def first_sums(keep1, send1, keep2, send2):
     sum1 = keep1 + hop(send1, HOP_X3).astype(F32)
     sum2 = keep2 + hop(send2, HOP_X1).astype(F32)
+    return sum1, sum2
+
+
+def return_rows(sum1, sum2):
     full1 = sum1[:32] + hop(sum1[32:].astype(BF16), HOP_X1).astype(F32)
     full2 = sum2[:32] + hop(sum2[32:].astype(BF16), HOP_X3).astype(F32)
     full1 = full1.astype(BF16)
@@ -352,25 +329,35 @@
             pltpu.VMEM((units, width), BF16),
             pltpu.SemaphoreType.DMA((7,)),
         ],
-        compiler_params=pltpu.CompilerParams(vmem_limit_bytes=32 * 1024 * 1024),
+        compiler_params=pltpu.CompilerParams(vmem_limit_bytes=60 * 1024 * 1024),
     )(info, route_fwd[0], route_bwd[0], *sources)
     other = hop(merged, HOP_W)
-    lefts, rights = spread_rows(*sent)
+    rows_a, rows_b = spread_rows(*sent)
     outs = [((64, width), F32), ((64, width), BF16)] * 2
     scratch = pltpu.VMEM((256, width), BF16)
-    part_a = kernel_call(fwd_kernel, outs, 8, [scratch], info=False)(*lefts, *weights, other)
-    part_b = kernel_call(bwd_kernel, outs, 13, [scratch] * 2, info=False)(
-        *lefts, *rights, *weights, other, part_a[1]
-    )
-    back_a = return_rows(*part_a)
-    back_b = return_rows(*part_b)
-    (layer_out,) = kernel_call(fwd_out_kernel, [((tokens, width), BF16)], 7)(
-        info, act_fwd[0], route_fwd[0], weight_fwd[0], *back_a
+    part_a = kernel_call(fwd_kernel, outs, 8, [scratch], info=False)(*rows_a, *weights, other)
+    sums_a = first_sums(*part_a)
+    part_b = kernel_call(bwd_kernel, outs, 10, [scratch] * 2, info=False)(
+        *rows_b, *weights, other, *sums_a
+    )
+    back_a = return_rows(*sums_a)
+    back_b = return_rows(*first_sums(*part_b))
+    layer_out, d_input, gate_grad = kernel_call(
+        last_kernel, [((tokens, width), BF16)] * 2 + [((tokens, 2), BF16)], 16
+    )(
+        info,
+        act_fwd[0],
+        route_fwd[0],
+        weight_fwd[0],
+        act_bwd[0],
+        route_bwd[0],
+        weight_bwd[0],
+        cot_bwd[0],
+        norm_gain,
+        *back_a,
+        *back_b,
     )
     act_next = shifted(layer_out, "section", 1)
-    d_input, gate_grad = kernel_call(
-        bwd_out_kernel, [((tokens, width), BF16), ((tokens, 2), BF16)], 9
-    )(info, act_bwd[0], route_bwd[0], weight_bwd[0], cot_bwd[0], norm_gain, *back_b)
     cot_next = shifted(d_input, "section", -1)
     return (act_next[None], cot_next[None], gate_grad[None])
 

time: 189 us -> 204 us (1.079)
  waiting for transfers between devices: 57.6 us -> 78.3 us
  local copies, waits for them, and re-layouts: 11 us -> 6.23 us
    ppermute x26, waiting for transfers between devices: 53.4 us -> 74.1 us  [hop(): return lax.ppermute(value, 'expert', pairs)]
    unnamed x36 -> x28, local copies, waits for them, and re-layouts: 8.47 us -> 2.44 us
    ppermute x2, starting transfers between devices: 15.3 us -> 11.8 us  [shifted(): return lax.ppermute(value, axis, pairs)]
    pallas_call x4 -> x2, Pallas kernels: 7.06 us -> 6.31 us  [the longest x1 3.35 us: body(): kernel_call(bwd_kernel, outs, 10, [scratch] * 2, info=False)]
  transfers between devices with their start and end apart: 28 -> 28, of which waited for: 7 -> 12; matrix products, arithmetic and copies ran while one was open for 1% -> 1% of each run, Pallas kernels for 5% -> 2%
where the time goes in v5:
time: 204 us; the launch traced here: 202 us
  starting transfers between devices  102 us (50%)
  waiting for transfers between devices  78.3 us (38%)
  Pallas kernels  12.9 us (6%)
  local copies, waits for them, and re-layouts  6.23 us (3%)
    ppermute x26, starting transfers between devices, hop(): return lax.ppermute(value, 'expert', pairs)  90 us
    ppermute x26, waiting for transfers between devices, hop(): return lax.ppermute(value, 'expert', pairs)  74.1 us
    ppermute x2, starting transfers between devices, shifted(): return lax.ppermute(value, axis, pairs)  11.8 us
    pallas_call x1, Pallas kernels, body(): pl.pallas_call(first_kernel, out_shape=[jax.ShapeDtypeStruct(s, d) for s,...  4.92 us
    ppermute x2, waiting for transfers between devices, shifted(): return lax.ppermute(value, axis, pairs)  4.2 us
  transfers between devices with their start and end apart: 28, of which 12 were waited for; matrix products, arithmetic and copies ran while one was open for 1% of the time, Pallas kernels for 2%

profile of v5, /device:TPU:1, one launch (start us, length us, event | category | flops | bytes accessed | tf_op | source)
XLA Modules:
  0.0 201.8 jit_solution(9411607193867951587)
XLA Ops:
  3.9 4.9 %shard_map.130 = (bf16[16,10752]{1,0:T(8,128)(2,1)}, bf16[16,10752]{1,0:T(8,128)(2,1)}, bf16[16,10752]{1,0:T(8,128)(2,1)}, bf16[16,10752]{1,0:T(8,128)(2,1)}, bf16[10752,128]{1,0:T(8,128)(2,1)}) custom-call(s32[2]{0:T(128)} %pad_add_fusion.info_ref, s32[24,2]{1,0:T(8,128)} %copy.16.ra_ref, s32[24,2]{1,0:T(8,128)} %copy.18.rb_ref.route_ref, ...), custom_call_target="tpu_custom_call" | custom-call | tf_op jit(solution)/shard_map/pallas_call | solution.py:320
  8.8 6.6 %collective-permute-start.3 = (bf16[16,10752]{1,0:T(8,128)(2,1)}, bf16[16,10752]{1,0:T(8,128)(2,1)S(1)}, u32[]{:S(2)}, u32[]{:S(2)}) collective-permute-start(bf16[16,10752]{1,0:T(8,128)(2,1)} %get-tuple-element.21), channel_id=1, source_target_pairs={{0,8},{1,9},{2,10},{3,11},{4,28},{5,29},{6,30},{7,31},{8,16},{9,17... | collective-permute-start | bytes 1032200 | tf_op jit(solution)/shard_map/ppermute | solution.py:41
  15.5 6.8 %collective-permute-start.4 = (bf16[16,10752]{1,0:T(8,128)(2,1)}, bf16[16,10752]{1,0:T(8,128)(2,1)S(1)}, u32[]{:S(2)}, u32[]{:S(2)}) collective-permute-start(bf16[16,10752]{1,0:T(8,128)(2,1)} %get-tuple-element.22), channel_id=1, source_target_pairs={{0,20},{1,21},{2,22},{3,23},{4,16},{5,17},{6,18},{7,19},{8,28},{9,... | collective-permute-start | bytes 1032200 | tf_op jit(solution)/shard_map/ppermute | solution.py:41
  22.2 4.6 %collective-permute-start = (bf16[16,10752]{1,0:T(8,128)(2,1)}, bf16[16,10752]{1,0:T(8,128)(2,1)S(1)}, u32[]{:S(2)}, u32[]{:S(2)}) collective-permute-start(bf16[16,10752]{1,0:T(8,128)(2,1)} %get-tuple-element.20), channel_id=1, source_target_pairs={{0,28},{1,29},{2,30},{3,31},{4,8},{5,9},{6,10},{7,11},{8,4},{9,5},... | collective-permute-start | bytes 1032200 | tf_op jit(solution)/shard_map/ppermute | solution.py:41
  29.8 14.3 %collective-permute-done.4 = bf16[16,10752]{1,0:T(8,128)(2,1)S(1)} collective-permute-done((bf16[16,10752]{1,0:T(8,128)(2,1)}, bf16[16,10752]{1,0:T(8,128)(2,1)S(1)}, u32[]{:S(2)}, u32[]{:S(2)}) %collective-permute-start.4) | collective-permute-done | bytes 344096 | tf_op jit(solution)/shard_map/ppermute | solution.py:41
  44.1 4.4 %collective-permute-start.5 = (bf16[32,3584]{1,0:T(8,128)(2,1)S(1)}, bf16[32,3584]{1,0:T(8,128)(2,1)S(1)}, u32[]{:S(2)}, u32[]{:S(2)}) collective-permute-start(bf16[32,3584]{1,0:T(8,128)(2,1)S(1)} %slice.85), channel_id=1, source_target_pairs={{0,3},{1,2},{2,1},{3,0},{4,7},{5,6},{6,5},{7,4},{8,11},{9,10},{10,... | collective-permute-start | bytes 688136 | tf_op jit(solution)/shard_map/ppermute | solution.py:41
  51.6 3.4 %collective-permute-start.1 = (bf16[32,3584]{1,0:T(8,128)(2,1)S(1)}, bf16[32,3584]{1,0:T(8,128)(2,1)S(1)}, u32[]{:S(2)}, u32[]{:S(2)}) collective-permute-start(bf16[32,3584]{1,0:T(8,128)(2,1)S(1)} %slice.84), channel_id=1, source_target_pairs={{0,1},{1,0},{2,3},{3,2},{4,5},{5,4},{6,7},{7,6},{8,9},{9,8},{10,11... | collective-permute-start | bytes 688136 | tf_op jit(solution)/shard_map/ppermute | solution.py:41
  55.0 3.7 %collective-permute-start.17 = (bf16[32,7168]{1,0:T(8,128)(2,1)S(1)}, bf16[32,7168]{1,0:T(8,128)(2,1)S(1)}, u32[]{:S(2)}, u32[]{:S(2)}) collective-permute-start(bf16[32,7168]{1,0:T(8,128)(2,1)S(1)} %slice.95), channel_id=1, source_target_pairs={{0,3},{1,2},{2,1},{3,0},{4,7},{5,6},{6,5},{7,4},{8,11},{9,10},{10,... | collective-permute-start | bytes 1376264 | tf_op jit(solution)/shard_map/ppermute | solution.py:41
  71.4 10.0 %collective-permute-done.6.pr2 = bf16[64,3584]{1,0:T(8,128)(2,1)S(1)} collective-permute-done((bf16[64,3584]{1,0:T(8,128)(2,1)S(1)}, bf16[64,3584]{1,0:T(8,128)(2,1)S(1)}, u32[]{:S(2)}, u32[]{:S(2)}) %collective-permute-start.6) | collective-permute-done | bytes 458784 | tf_op jit(solution)/shard_map/ppermute | solution.py:41
  81.4 14.1 %collective-permute-done.7.other = bf16[10752,128]{1,0:T(8,128)(2,1)S(1)} collective-permute-done((bf16[10752,128]{1,0:T(8,128)(2,1)}, bf16[10752,128]{1,0:T(8,128)(2,1)S(1)}, u32[]{:S(2)}, u32[]{:S(2)}) %collective-permute-start.7) | collective-permute-done | bytes 2752544 | tf_op jit(solution)/shard_map/ppermute | solution.py:41
  100.5 3.7 %collective-permute-start.16 = (bf16[64,7168]{1,0:T(8,128)(2,1)S(1)}, bf16[64,7168]{1,0:T(8,128)(2,1)S(1)}, u32[]{:S(2)}, u32[]{:S(2)}) collective-permute-start(bf16[64,7168]{1,0:T(8,128)(2,1)S(1)} %pad_maximum_fusion.c1), channel_id=1, source_target_pairs={{0,3},{1,2},{2,1},{3,0},{4,7},{5,6},{6,5},{7,4},{8,11},{9,10},{10,... | collective-permute-start | bytes 2752520 | tf_op jit(solution)/shard_map/ppermute | solution.py:41
  107.0 4.3 %collective-permute-done.11 = bf16[64,3584]{1,0:T(8,128)(2,1)S(1)} collective-permute-done((bf16[64,3584]{1,0:T(8,128)(2,1)S(1)}, bf16[64,3584]{1,0:T(8,128)(2,1)S(1)}, u32[]{:S(2)}, u32[]{:S(2)}) %collective-permute-start.11) | collective-permute-done | bytes 458784 | tf_op jit(solution)/shard_map/ppermute | solution.py:41
  114.1 19.3 %collective-permute-done.8 = bf16[64,3584]{1,0:T(8,128)(2,1)S(1)} collective-permute-done((bf16[64,3584]{1,0:T(8,128)(2,1)S(1)}, bf16[64,3584]{1,0:T(8,128)(2,1)S(1)}, u32[]{:S(2)}, u32[]{:S(2)}) %collective-permute-start.8) | collective-permute-done | bytes 458784 | tf_op jit(solution)/shard_map/ppermute | solution.py:41
  133.6 3.3 %shard_map.132 = (f32[64,3584]{1,0:T(8,128)S(1)}, bf16[64,3584]{1,0:T(8,128)(2,1)S(1)}, f32[64,3584]{1,0:T(8,128)S(1)}, bf16[64,3584]{1,0:T(8,128)(2,1)S(1)}) custom-call(bf16[64,7168]{1,0:T(8,128)(2,1)S(1)} %pad_maximum_fusion.c1, bf16[64,7168]{1,0:T(8,128)(2,1)S(1)} %collective-permute-done.16.qr1, bf16[64,7168]{1,0:T(8,128)(2,1)S(1)} %pad_maximum_fusion.1.c2, ...), custom_call_target="tpu_custom_call" | custom-call | tf_op jit(solution)/shard_map/pallas_call | solution.py:340
  138.9 3.7 %collective-permute-start.19 = (bf16[64,3584]{1,0:T(8,128)(2,1)S(1)}, bf16[64,3584]{1,0:T(8,128)(2,1)S(1)}, u32[]{:S(2)}, u32[]{:S(2)}) collective-permute-start(bf16[64,3584]{1,0:T(8,128)(2,1)S(1)} %get-tuple-element.29), channel_id=1, source_target_pairs={{0,3},{1,2},{2,1},{3,0},{4,7},{5,6},{6,5},{7,4},{8,11},{9,10},{10,... | collective-permute-start | bytes 1376264 | tf_op jit(solution)/shard_map/ppermute | solution.py:41
  145.4 3.2 %collective-permute-start.13 = (bf16[16,3584]{1,0:T(8,128)(2,1)S(1)}, bf16[16,3584]{1,0:T(8,128)(2,1)S(1)}, u32[]{:S(2)}, u32[]{:S(2)}) collective-permute-start(bf16[16,3584]{1,0:T(8,128)(2,1)S(1)} %get-tuple-element.40), channel_id=1, source_target_pairs={{0,24},{1,25},{2,26},{3,27},{4,12},{5,13},{6,14},{7,15},{8,0},{9,1... | collective-permute-start | bytes 344072 | tf_op jit(solution)/shard_map/ppermute | solution.py:41
  148.7 5.7 %collective-permute-start.14 = (bf16[16,3584]{1,0:T(8,128)(2,1)S(1)}, bf16[16,3584]{1,0:T(8,128)(2,1)S(1)}, u32[]{:S(2)}, u32[]{:S(2)}) collective-permute-start(bf16[16,3584]{1,0:T(8,128)(2,1)S(1)} %get-tuple-element.39), channel_id=1, source_target_pairs={{0,20},{1,21},{2,22},{3,23},{4,16},{5,17},{6,18},{7,19},{8,28},{9,... | collective-permute-start | bytes 344072 | tf_op jit(solution)/shard_map/ppermute | solution.py:41
  154.5 3.3 %collective-permute-start.10 = (bf16[16,3584]{1,0:T(8,128)(2,1)S(1)}, bf16[16,3584]{1,0:T(8,128)(2,1)S(1)}, u32[]{:S(2)}, u32[]{:S(2)}) collective-permute-start(bf16[16,3584]{1,0:T(8,128)(2,1)S(1)} %get-tuple-element.41), channel_id=1, source_target_pairs={{0,28},{1,29},{2,30},{3,31},{4,8},{5,9},{6,10},{7,11},{8,4},{9,5},... | collective-permute-start | bytes 344072 | tf_op jit(solution)/shard_map/ppermute | solution.py:41
  157.9 3.7 %collective-permute-start.23 = (bf16[32,3584]{1,0:T(8,128)(2,1)S(1)}, bf16[32,3584]{1,0:T(8,128)(2,1)S(1)}, u32[]{:S(2)}, u32[]{:S(2)}) collective-permute-start(bf16[32,3584]{1,0:T(8,128)(2,1)S(1)} %slice.120), channel_id=1, source_target_pairs={{0,3},{1,2},{2,1},{3,0},{4,7},{5,6},{6,5},{7,4},{8,11},{9,10},{10,... | collective-permute-start | bytes 688136 | tf_op jit(solution)/shard_map/ppermute | solution.py:41
  168.7 4.7 %collective-permute-start.25 = (bf16[16,3584]{1,0:T(8,128)(2,1)S(1)}, bf16[16,3584]{1,0:T(8,128)(2,1)S(1)}, u32[]{:S(2)}, u32[]{:S(2)}) collective-permute-start(bf16[16,3584]{1,0:T(8,128)(2,1)S(1)} %get-tuple-element.35), channel_id=1, source_target_pairs={{0,20},{1,21},{2,22},{3,23},{4,16},{5,17},{6,18},{7,19},{8,28},{9,... | collective-permute-start | bytes 344072 | tf_op jit(solution)/shard_map/ppermute | solution.py:41
  173.6 3.3 %collective-permute-start.21 = (bf16[16,3584]{1,0:T(8,128)(2,1)S(1)}, bf16[16,3584]{1,0:T(8,128)(2,1)S(1)}, u32[]{:S(2)}, u32[]{:S(2)}) collective-permute-start(bf16[16,3584]{1,0:T(8,128)(2,1)S(1)} %get-tuple-element.37), channel_id=1, source_target_pairs={{0,28},{1,29},{2,30},{3,31},{4,8},{5,9},{6,10},{7,11},{8,4},{9,5},... | collective-permute-start | bytes 344072 | tf_op jit(solution)/shard_map/ppermute | solution.py:41
  177.4 3.4 %collective-permute-done.21.rest_5_ = bf16[16,3584]{1,0:T(8,128)(2,1)S(1)} collective-permute-done((bf16[16,3584]{1,0:T(8,128)(2,1)S(1)}, bf16[16,3584]{1,0:T(8,128)(2,1)S(1)}, u32[]{:S(2)}, u32[]{:S(2)}) %collective-permute-start.21) | collective-permute-done | bytes 114720 | tf_op jit(solution)/shard_map/ppermute | solution.py:41
  183.8 9.9 %collective-permute-start.26 = (bf16[24,3584]{1,0:T(8,128)(2,1)S(1)}, bf16[24,3584]{1,0:T(8,128)(2,1)S(1)}, u32[]{:S(2)}, u32[]{:S(2)}) collective-permute-start(bf16[24,3584]{1,0:T(8,128)(2,1)S(1)} %get-tuple-element.32), channel_id=1, source_target_pairs={{0,32},{32,64},{64,96},{96,128},{128,160},{160,192},{192,224},{224... | collective-permute-start | bytes 516104 | tf_op jit(solution)/shard_map/ppermute | solution.py:47
  196.2 4.2 %collective-permute-done.27 = bf16[24,3584]{1,0:T(8,128)(2,1)S(1)} collective-permute-done((bf16[24,3584]{1,0:T(8,128)(2,1)S(1)}, bf16[24,3584]{1,0:T(8,128)(2,1)S(1)}, u32[]{:S(2)}, u32[]{:S(2)}) %collective-permute-start.27) | collective-permute-done | bytes 172064 | tf_op jit(solution)/shard_map/ppermute | solution.py:47
  (96 shorter events, 51.8 us)
Async XLA Ops:
  8.8 20.9 %collective-permute-start.3 = (bf16[16,10752]{1,0:T(8,128)(2,1)}, bf16[16,10752]{1,0:T(8,128)(2,1)S(1)}, u32[]{:S(2)}, u32[]{:S(2)}) collective-permute-start(bf16[16,10752]{1,0:T(8,128)(2,1)} %get-tuple-element.21), channel_id=1, source_target_pairs={{0,8},{1,9},{2,10},{3,11},{4,28},{5,29},{6,30},{7,31},{8,16},{9,17... | collective-permute-start | bytes 1032200 | tf_op jit(solution)/shard_map/ppermute | solution.py:41
  15.5 28.6 %collective-permute-start.4 = (bf16[16,10752]{1,0:T(8,128)(2,1)}, bf16[16,10752]{1,0:T(8,128)(2,1)S(1)}, u32[]{:S(2)}, u32[]{:S(2)}) collective-permute-start(bf16[16,10752]{1,0:T(8,128)(2,1)} %get-tuple-element.22), channel_id=1, source_target_pairs={{0,20},{1,21},{2,22},{3,23},{4,16},{5,17},{6,18},{7,19},{8,28},{9,... | collective-permute-start | bytes 1032200 | tf_op jit(solution)/shard_map/ppermute | solution.py:41
  22.2 29.2 %collective-permute-start = (bf16[16,10752]{1,0:T(8,128)(2,1)}, bf16[16,10752]{1,0:T(8,128)(2,1)S(1)}, u32[]{:S(2)}, u32[]{:S(2)}) collective-permute-start(bf16[16,10752]{1,0:T(8,128)(2,1)} %get-tuple-element.20), channel_id=1, source_target_pairs={{0,28},{1,29},{2,30},{3,31},{4,8},{5,9},{6,10},{7,11},{8,4},{9,5},... | collective-permute-start | bytes 1032200 | tf_op jit(solution)/shard_map/ppermute | solution.py:41
  26.8 68.8 %collective-permute-start.7 = (bf16[10752,128]{1,0:T(8,128)(2,1)}, bf16[10752,128]{1,0:T(8,128)(2,1)S(1)}, u32[]{:S(2)}, u32[]{:S(2)}) collective-permute-start(bf16[10752,128]{1,0:T(8,128)(2,1)} %get-tuple-element.23), channel_id=1, source_target_pairs={{0,4},{1,5},{2,6},{3,7},{4,0},{5,1},{6,2},{7,3},{8,12},{9,13},{10,... | collective-permute-start | bytes 8257544 | tf_op jit(solution)/shard_map/ppermute | solution.py:41
  44.1 16.8 %collective-permute-start.5 = (bf16[32,3584]{1,0:T(8,128)(2,1)S(1)}, bf16[32,3584]{1,0:T(8,128)(2,1)S(1)}, u32[]{:S(2)}, u32[]{:S(2)}) collective-permute-start(bf16[32,3584]{1,0:T(8,128)(2,1)S(1)} %slice.85), channel_id=1, source_target_pairs={{0,3},{1,2},{2,1},{3,0},{4,7},{5,6},{6,5},{7,4},{8,11},{9,10},{10,... | collective-permute-start | bytes 688136 | tf_op jit(solution)/shard_map/ppermute | solution.py:41
  51.6 12.5 %collective-permute-start.1 = (bf16[32,3584]{1,0:T(8,128)(2,1)S(1)}, bf16[32,3584]{1,0:T(8,128)(2,1)S(1)}, u32[]{:S(2)}, u32[]{:S(2)}) collective-permute-start(bf16[32,3584]{1,0:T(8,128)(2,1)S(1)} %slice.84), channel_id=1, source_target_pairs={{0,1},{1,0},{2,3},{3,2},{4,5},{5,4},{6,7},{7,6},{8,9},{9,8},{10,11... | collective-permute-start | bytes 688136 | tf_op jit(solution)/shard_map/ppermute | solution.py:41
  55.0 14.4 %collective-permute-start.17 = (bf16[32,7168]{1,0:T(8,128)(2,1)S(1)}, bf16[32,7168]{1,0:T(8,128)(2,1)S(1)}, u32[]{:S(2)}, u32[]{:S(2)}) collective-permute-start(bf16[32,7168]{1,0:T(8,128)(2,1)S(1)} %slice.95), channel_id=1, source_target_pairs={{0,3},{1,2},{2,1},{3,0},{4,7},{5,6},{6,5},{7,4},{8,11},{9,10},{10,... | collective-permute-start | bytes 1376264 | tf_op jit(solution)/shard_map/ppermute | solution.py:41
  58.8 41.6 %collective-permute-start.15 = (bf16[32,7168]{1,0:T(8,128)(2,1)S(1)}, bf16[32,7168]{1,0:T(8,128)(2,1)S(1)}, u32[]{:S(2)}, u32[]{:S(2)}) collective-permute-start(bf16[32,7168]{1,0:T(8,128)(2,1)S(1)} %slice.94), channel_id=1, source_target_pairs={{0,1},{1,0},{2,3},{3,2},{4,5},{5,4},{6,7},{7,6},{8,9},{9,8},{10,11... | collective-permute-start | bytes 1376264 | tf_op jit(solution)/shard_map/ppermute | solution.py:41
  61.0 20.4 %collective-permute-start.6 = (bf16[64,3584]{1,0:T(8,128)(2,1)S(1)}, bf16[64,3584]{1,0:T(8,128)(2,1)S(1)}, u32[]{:S(2)}, u32[]{:S(2)}) collective-permute-start(bf16[64,3584]{1,0:T(8,128)(2,1)S(1)} %pad_maximum_fusion.3.c2), channel_id=1, source_target_pairs={{0,1},{1,0},{2,3},{3,2},{4,5},{5,4},{6,7},{7,6},{8,9},{9,8},{10,11... | collective-permute-start | bytes 1376264 | tf_op jit(solution)/shard_map/ppermute | solution.py:41
  64.2 17.3 %collective-permute-start.2 = (bf16[64,3584]{1,0:T(8,128)(2,1)S(1)}, bf16[64,3584]{1,0:T(8,128)(2,1)S(1)}, u32[]{:S(2)}, u32[]{:S(2)}) collective-permute-start(bf16[64,3584]{1,0:T(8,128)(2,1)S(1)} %pad_maximum_fusion.2.c1), channel_id=1, source_target_pairs={{0,3},{1,2},{2,1},{3,0},{4,7},{5,6},{6,5},{7,4},{8,11},{9,10},{10,... | collective-permute-start | bytes 1376264 | tf_op jit(solution)/shard_map/ppermute | solution.py:41
  69.5 64.1 %collective-permute-start.18 = (bf16[64,7168]{1,0:T(8,128)(2,1)S(1)}, bf16[64,7168]{1,0:T(8,128)(2,1)S(1)}, u32[]{:S(2)}, u32[]{:S(2)}) collective-permute-start(bf16[64,7168]{1,0:T(8,128)(2,1)S(1)} %pad_maximum_fusion.1.c2), channel_id=1, source_target_pairs={{0,1},{1,0},{2,3},{3,2},{4,5},{5,4},{6,7},{7,6},{8,9},{9,8},{10,11... | collective-permute-start | bytes 2752520 | tf_op jit(solution)/shard_map/ppermute | solution.py:41
  97.3 14.0 %collective-permute-start.11 = (bf16[64,3584]{1,0:T(8,128)(2,1)S(1)}, bf16[64,3584]{1,0:T(8,128)(2,1)S(1)}, u32[]{:S(2)}, u32[]{:S(2)}) collective-permute-start(bf16[64,3584]{1,0:T(8,128)(2,1)S(1)} %get-tuple-element.27), channel_id=1, source_target_pairs={{0,1},{1,0},{2,3},{3,2},{4,5},{5,4},{6,7},{7,6},{8,9},{9,8},{10,11... | collective-permute-start | bytes 1376264 | tf_op jit(solution)/shard_map/ppermute | solution.py:41
  100.5 33.1 %collective-permute-start.16 = (bf16[64,7168]{1,0:T(8,128)(2,1)S(1)}, bf16[64,7168]{1,0:T(8,128)(2,1)S(1)}, u32[]{:S(2)}, u32[]{:S(2)}) collective-permute-start(bf16[64,7168]{1,0:T(8,128)(2,1)S(1)} %pad_maximum_fusion.c1), channel_id=1, source_target_pairs={{0,3},{1,2},{2,1},{3,0},{4,7},{5,6},{6,5},{7,4},{8,11},{9,10},{10,... | collective-permute-start | bytes 2752520 | tf_op jit(solution)/shard_map/ppermute | solution.py:41
  104.2 29.2 %collective-permute-start.8 = (bf16[64,3584]{1,0:T(8,128)(2,1)S(1)}, bf16[64,3584]{1,0:T(8,128)(2,1)S(1)}, u32[]{:S(2)}, u32[]{:S(2)}) collective-permute-start(bf16[64,3584]{1,0:T(8,128)(2,1)S(1)} %get-tuple-element.25), channel_id=1, source_target_pairs={{0,3},{1,2},{2,1},{3,0},{4,7},{5,6},{6,5},{7,4},{8,11},{9,10},{10,... | collective-permute-start | bytes 1376264 | tf_op jit(solution)/shard_map/ppermute | solution.py:41
  111.4 34.0 %collective-permute-start.12 = (bf16[32,3584]{1,0:T(8,128)(2,1)S(1)}, bf16[32,3584]{1,0:T(8,128)(2,1)S(1)}, u32[]{:S(2)}, u32[]{:S(2)}) collective-permute-start(bf16[32,3584]{1,0:T(8,128)(2,1)S(1)} %slice.122), channel_id=1, source_target_pairs={{0,3},{1,2},{2,1},{3,0},{4,7},{5,6},{6,5},{7,4},{8,11},{9,10},{10,... | collective-permute-start | bytes 688136 | tf_op jit(solution)/shard_map/ppermute | solution.py:41
  136.9 20.9 %collective-permute-start.22 = (bf16[64,3584]{1,0:T(8,128)(2,1)S(1)}, bf16[64,3584]{1,0:T(8,128)(2,1)S(1)}, u32[]{:S(2)}, u32[]{:S(2)}) collective-permute-start(bf16[64,3584]{1,0:T(8,128)(2,1)S(1)} %get-tuple-element.31), channel_id=1, source_target_pairs={{0,1},{1,0},{2,3},{3,2},{4,5},{5,4},{6,7},{7,6},{8,9},{9,8},{10,11... | collective-permute-start | bytes 1376264 | tf_op jit(solution)/shard_map/ppermute | solution.py:41
  138.9 22.8 %collective-permute-start.19 = (bf16[64,3584]{1,0:T(8,128)(2,1)S(1)}, bf16[64,3584]{1,0:T(8,128)(2,1)S(1)}, u32[]{:S(2)}, u32[]{:S(2)}) collective-permute-start(bf16[64,3584]{1,0:T(8,128)(2,1)S(1)} %get-tuple-element.29), channel_id=1, source_target_pairs={{0,3},{1,2},{2,1},{3,0},{4,7},{5,6},{6,5},{7,4},{8,11},{9,10},{10,... | collective-permute-start | bytes 1376264 | tf_op jit(solution)/shard_map/ppermute | solution.py:41
  142.6 11.8 %collective-permute-start.9 = (bf16[32,3584]{1,0:T(8,128)(2,1)S(1)}, bf16[32,3584]{1,0:T(8,128)(2,1)S(1)}, u32[]{:S(2)}, u32[]{:S(2)}) collective-permute-start(bf16[32,3584]{1,0:T(8,128)(2,1)S(1)} %slice.123), channel_id=1, source_target_pairs={{0,1},{1,0},{2,3},{3,2},{4,5},{5,4},{6,7},{7,6},{8,9},{9,8},{10,11... | collective-permute-start | bytes 688136 | tf_op jit(solution)/shard_map/ppermute | solution.py:41
  145.4 28.1 %collective-permute-start.13 = (bf16[16,3584]{1,0:T(8,128)(2,1)S(1)}, bf16[16,3584]{1,0:T(8,128)(2,1)S(1)}, u32[]{:S(2)}, u32[]{:S(2)}) collective-permute-start(bf16[16,3584]{1,0:T(8,128)(2,1)S(1)} %get-tuple-element.40), channel_id=1, source_target_pairs={{0,24},{1,25},{2,26},{3,27},{4,12},{5,13},{6,14},{7,15},{8,0},{9,1... | collective-permute-start | bytes 344072 | tf_op jit(solution)/shard_map/ppermute | solution.py:41
  148.7 28.4 %collective-permute-start.14 = (bf16[16,3584]{1,0:T(8,128)(2,1)S(1)}, bf16[16,3584]{1,0:T(8,128)(2,1)S(1)}, u32[]{:S(2)}, u32[]{:S(2)}) collective-permute-start(bf16[16,3584]{1,0:T(8,128)(2,1)S(1)} %get-tuple-element.39), channel_id=1, source_target_pairs={{0,20},{1,21},{2,22},{3,23},{4,16},{5,17},{6,18},{7,19},{8,28},{9,... | collective-permute-start | bytes 344072 | tf_op jit(solution)/shard_map/ppermute | solution.py:41
  154.5 22.6 %collective-permute-start.10 = (bf16[16,3584]{1,0:T(8,128)(2,1)S(1)}, bf16[16,3584]{1,0:T(8,128)(2,1)S(1)}, u32[]{:S(2)}, u32[]{:S(2)}) collective-permute-start(bf16[16,3584]{1,0:T(8,128)(2,1)S(1)} %get-tuple-element.41), channel_id=1, source_target_pairs={{0,28},{1,29},{2,30},{3,31},{4,8},{5,9},{6,10},{7,11},{8,4},{9,5},... | collective-permute-start | bytes 344072 | tf_op jit(solution)/shard_map/ppermute | solution.py:41
  166.3 10.8 %collective-permute-start.24 = (bf16[16,3584]{1,0:T(8,128)(2,1)S(1)}, bf16[16,3584]{1,0:T(8,128)(2,1)S(1)}, u32[]{:S(2)}, u32[]{:S(2)}) collective-permute-start(bf16[16,3584]{1,0:T(8,128)(2,1)S(1)} %get-tuple-element.36), channel_id=1, source_target_pairs={{0,24},{1,25},{2,26},{3,27},{4,12},{5,13},{6,14},{7,15},{8,0},{9,1... | collective-permute-start | bytes 344072 | tf_op jit(solution)/shard_map/ppermute | solution.py:41
  168.7 8.6 %collective-permute-start.25 = (bf16[16,3584]{1,0:T(8,128)(2,1)S(1)}, bf16[16,3584]{1,0:T(8,128)(2,1)S(1)}, u32[]{:S(2)}, u32[]{:S(2)}) collective-permute-start(bf16[16,3584]{1,0:T(8,128)(2,1)S(1)} %get-tuple-element.35), channel_id=1, source_target_pairs={{0,20},{1,21},{2,22},{3,23},{4,16},{5,17},{6,18},{7,19},{8,28},{9,... | collective-permute-start | bytes 344072 | tf_op jit(solution)/shard_map/ppermute | solution.py:41
  183.8 12.4 %collective-permute-start.26 = (bf16[24,3584]{1,0:T(8,128)(2,1)S(1)}, bf16[24,3584]{1,0:T(8,128)(2,1)S(1)}, u32[]{:S(2)}, u32[]{:S(2)}) collective-permute-start(bf16[24,3584]{1,0:T(8,128)(2,1)S(1)} %get-tuple-element.32), channel_id=1, source_target_pairs={{0,32},{32,64},{64,96},{96,128},{128,160},{160,192},{192,224},{224... | collective-permute-start | bytes 516104 | tf_op jit(solution)/shard_map/ppermute | solution.py:47
  (16 other events, 325.0 us)

commit v6 on v3

--- a/solution.py
+++ b/solution.py
@@ -222,18 +222,16 @@
     return total
 
 
-def fwd_out_kernel(info_ref, x_ref, route_ref, weight_ref, own, a, b, c, out_ref):
+def last_kernel(
+    info_ref, xa_ref, ra_ref, wa_ref, x_ref, route_ref, weight_ref, cot_ref, gain_ref, *rest
+):
+    width = x_ref.shape[1]
+    parts_a = [ref[:, :width] for ref in rest[:4]]
+    parts = [ref[:, width:] for ref in rest[:4]]
+    out_a_ref, out_ref, grad_ref = rest[4:]
+    mixed = mixed_rows(slot_masks(info_ref, ra_ref), wa_ref, parts_a)
+    out_a_ref[...] = (xa_ref[...].astype(F32) + mixed).astype(BF16)
     masks = slot_masks(info_ref, route_ref)
-    parts = [own[...], a[...], b[...], c[...]]
-    mixed = mixed_rows(masks, weight_ref, parts)
-    out_ref[...] = (x_ref[...].astype(F32) + mixed).astype(BF16)
-
-
-def bwd_out_kernel(
-    info_ref, x_ref, route_ref, weight_ref, cot_ref, gain_ref, own, a, b, c, out_ref, grad_ref
-):
-    masks = slot_masks(info_ref, route_ref)
-    parts = [own[...], a[...], b[...], c[...]]
     d_normed = mixed_rows(masks, weight_ref, parts)
     unit, scale = normalized(x_ref[...])
     q_term = d_normed * gain_ref[...]
@@ -264,16 +262,18 @@
     return c1, hop(c1, HOP_X3), c2, hop(c2, HOP_X1)
 
 
-def return_rows(keep1, send1, keep2, send2):
+def return_x(keep1, send1, keep2, send2):
     sum1 = keep1 + hop(send1, HOP_X3).astype(F32)
     sum2 = keep2 + hop(send2, HOP_X1).astype(F32)
     full1 = sum1[:32] + hop(sum1[32:].astype(BF16), HOP_X1).astype(F32)
     full2 = sum2[:32] + hop(sum2[32:].astype(BF16), HOP_X3).astype(F32)
-    full1 = full1.astype(BF16)
-    full2 = full2.astype(BF16)
+    return full1.astype(BF16), full2.astype(BF16)
+
+
+def return_z(full1, full2):
+    back_c = hop(full2[SLOT:], HOP_C)
+    back_b = hop(full2[:SLOT], HOP_B_BACK)
     back_a = hop(full1[SLOT:], HOP_A)
-    back_b = hop(full2[:SLOT], HOP_B_BACK)
-    back_c = hop(full2[SLOT:], HOP_C)
     return full1[:SLOT], back_a, back_b, back_c
 
 
@@ -292,8 +292,7 @@
 ):
     tokens, width = act_fwd.shape[1:]
     index = lax.axis_index("expert")
-    z = index // GRID_X
-    info = jnp.stack([z // 2, z % 2]).astype(jnp.int32)
+    info = jnp.stack([index >> 3, (index >> 2) & 1]).astype(jnp.int32)
     weights = (w_gate[0, 0], w_up[0, 0], w_down[0, 0])
     units = w_down.shape[2]
     (merged,) = kernel_call(merge_kernel, [((3 * width, units), BF16)], 3, info=False)(*weights)
@@ -309,15 +308,23 @@
     part_b = kernel_call(bwd_kernel, outs, 9, [scratch] * 2, info=False)(
         *rows, *weights, other, part_a[1]
     )
-    back_a = return_rows(*part_a)
-    back_b = return_rows(*part_b)
-    (layer_out,) = kernel_call(fwd_out_kernel, [((tokens, width), BF16)], 7)(
-        info, act_fwd[0], route_fwd[0], weight_fwd[0], *back_a
+    halves = zip(return_x(*part_a), return_x(*part_b))
+    back = return_z(*[jnp.concatenate(pair, axis=1) for pair in halves])
+    layer_out, d_input, gate_grad = kernel_call(
+        last_kernel, [((tokens, width), BF16)] * 2 + [((tokens, 2), BF16)], 12
+    )(
+        info,
+        act_fwd[0],
+        route_fwd[0],
+        weight_fwd[0],
+        act_bwd[0],
+        route_bwd[0],
+        weight_bwd[0],
+        cot_bwd[0],
+        norm_gain,
+        *back,
     )
     act_next = shifted(layer_out, "section", 1)
-    d_input, gate_grad = kernel_call(
-        bwd_out_kernel, [((tokens, width), BF16), ((tokens, 2), BF16)], 9
-    )(info, act_bwd[0], route_bwd[0], weight_bwd[0], cot_bwd[0], norm_gain, *back_b)
     cot_next = shifted(d_input, "section", -1)
     return (act_next[None], cot_next[None], gate_grad[None])
 

time: 178 us -> 181 us (1.017); the launches traced: 176 us -> 177 us
  waiting for transfers between devices: 58.5 us -> 75.1 us
  starting transfers between devices: 94.5 us -> 79.7 us
    ppermute x22 -> x19, waiting for transfers between devices: 54.8 us -> 70.9 us  [hop(): return lax.ppermute(value, 'expert', pairs)]
    ppermute x2, starting transfers between devices: 15.6 us -> 7.96 us  [shifted(): return lax.ppermute(value, axis, pairs)]
    ppermute x22 -> x19, starting transfers between devices: 78.9 us -> 71.8 us  [hop(): return lax.ppermute(value, 'expert', pairs)]
  transfers between devices with their start and end apart: 24 -> 21, of which waited for: 10 -> 11; matrix products, arithmetic and copies ran while one was open for 1% -> 1% of each run, Pallas kernels for 4% -> 2%
where the time goes in v6:
time: 181 us; the launch traced here: 177 us
  starting transfers between devices  79.7 us (44%)
  waiting for transfers between devices  75.1 us (41%)
  local copies, waits for them, and re-layouts  10.9 us (6%)
  Pallas kernels  9.7 us (5%)
    ppermute x19, starting transfers between devices, hop(): return lax.ppermute(value, 'expert', pairs)  71.8 us
    ppermute x19, waiting for transfers between devices, hop(): return lax.ppermute(value, 'expert', pairs)  70.9 us
    unnamed x32, local copies, waits for them, and re-layouts  8.47 us
    ppermute x2, starting transfers between devices, shifted(): return lax.ppermute(value, axis, pairs)  7.96 us
    ppermute x2, waiting for transfers between devices, shifted(): return lax.ppermute(value, axis, pairs)  4.2 us
  transfers between devices with their start and end apart: 21, of which 11 were waited for; matrix products, arithmetic and copies ran while one was open for 1% of the time, Pallas kernels for 2%

profile of v6, /device:TPU:1, one launch (start us, length us, event | category | flops | bytes accessed | tf_op | source)
XLA Modules:
  0.0 177.3 jit_solution(8016855654854867592)
XLA Ops:
  7.1 6.6 %collective-permute-start.3 = (bf16[16,10752]{1,0:T(8,128)(2,1)S(1)}, bf16[16,10752]{1,0:T(8,128)(2,1)S(1)}, u32[]{:S(2)}, u32[]{:S(2)}) collective-permute-start(bf16[16,10752]{1,0:T(8,128)(2,1)S(1)} %get-tuple-element.20), channel_id=1, source_target_pairs={{0,8},{1,9},{2,10},{3,11},{4,28},{5,29},{6,30},{7,31},{8,16},{9,17... | collective-permute-start | bytes 1032200 | tf_op jit(solution)/shard_map/ppermute | solution.py:41
  13.8 6.8 %collective-permute-start.4 = (bf16[16,10752]{1,0:T(8,128)(2,1)S(1)}, bf16[16,10752]{1,0:T(8,128)(2,1)S(1)}, u32[]{:S(2)}, u32[]{:S(2)}) collective-permute-start(bf16[16,10752]{1,0:T(8,128)(2,1)S(1)} %get-tuple-element.21), channel_id=1, source_target_pairs={{0,20},{1,21},{2,22},{3,23},{4,16},{5,17},{6,18},{7,19},{8,28},{9,... | collective-permute-start | bytes 1032200 | tf_op jit(solution)/shard_map/ppermute | solution.py:41
  20.5 4.6 %collective-permute-start = (bf16[16,10752]{1,0:T(8,128)(2,1)S(1)}, bf16[16,10752]{1,0:T(8,128)(2,1)S(1)}, u32[]{:S(2)}, u32[]{:S(2)}) collective-permute-start(bf16[16,10752]{1,0:T(8,128)(2,1)S(1)} %get-tuple-element.19), channel_id=1, source_target_pairs={{0,28},{1,29},{2,30},{3,31},{4,8},{5,9},{6,10},{7,11},{8,4},{9,5},... | collective-permute-start | bytes 1032200 | tf_op jit(solution)/shard_map/ppermute | solution.py:41
  30.9 11.2 %collective-permute-done.4 = bf16[16,10752]{1,0:T(8,128)(2,1)S(1)} collective-permute-done((bf16[16,10752]{1,0:T(8,128)(2,1)S(1)}, bf16[16,10752]{1,0:T(8,128)(2,1)S(1)}, u32[]{:S(2)}, u32[]{:S(2)}) %collective-permute-start.4) | collective-permute-done | bytes 344096 | tf_op jit(solution)/shard_map/ppermute | solution.py:41
  42.1 4.4 %collective-permute-start.5 = (bf16[32,10752]{1,0:T(8,128)(2,1)S(1)}, bf16[32,10752]{1,0:T(8,128)(2,1)S(1)}, u32[]{:S(2)}, u32[]{:S(2)}) collective-permute-start(bf16[32,10752]{1,0:T(8,128)(2,1)S(1)} %pad_maximum_fusion.1), channel_id=1, source_target_pairs={{0,3},{1,2},{2,1},{3,0},{4,7},{5,6},{6,5},{7,4},{8,11},{9,10},{10,... | collective-permute-start | bytes 2064392 | tf_op jit(solution)/shard_map/ppermute | solution.py:41
  46.5 2.9 %collective-permute-done = bf16[16,10752]{1,0:T(8,128)(2,1)S(1)} collective-permute-done((bf16[16,10752]{1,0:T(8,128)(2,1)S(1)}, bf16[16,10752]{1,0:T(8,128)(2,1)S(1)}, u32[]{:S(2)}, u32[]{:S(2)}) %collective-permute-start) | collective-permute-done | bytes 344096 | tf_op jit(solution)/shard_map/ppermute | solution.py:41
  49.5 3.1 %collective-permute-start.1 = (bf16[32,10752]{1,0:T(8,128)(2,1)S(1)}, bf16[32,10752]{1,0:T(8,128)(2,1)S(1)}, u32[]{:S(2)}, u32[]{:S(2)}) collective-permute-start(bf16[32,10752]{1,0:T(8,128)(2,1)S(1)} %pad_maximum_fusion), channel_id=1, source_target_pairs={{0,1},{1,0},{2,3},{3,2},{4,5},{5,4},{6,7},{7,6},{8,9},{9,8},{10,11... | collective-permute-start | bytes 2064392 | tf_op jit(solution)/shard_map/ppermute | solution.py:41
  52.7 8.9 %collective-permute-done.5 = bf16[32,10752]{1,0:T(8,128)(2,1)S(1)} collective-permute-done((bf16[32,10752]{1,0:T(8,128)(2,1)S(1)}, bf16[32,10752]{1,0:T(8,128)(2,1)S(1)}, u32[]{:S(2)}, u32[]{:S(2)}) %collective-permute-start.5) | collective-permute-done | bytes 688160 | tf_op jit(solution)/shard_map/ppermute | solution.py:41
  63.6 4.3 %collective-permute-done.1 = bf16[32,10752]{1,0:T(8,128)(2,1)S(1)} collective-permute-done((bf16[32,10752]{1,0:T(8,128)(2,1)S(1)}, bf16[32,10752]{1,0:T(8,128)(2,1)S(1)}, u32[]{:S(2)}, u32[]{:S(2)}) %collective-permute-start.1) | collective-permute-done | bytes 688160 | tf_op jit(solution)/shard_map/ppermute | solution.py:41
  68.0 4.4 %collective-permute-start.2 = (bf16[64,10752]{1,0:T(8,128)(2,1)S(1)}, bf16[64,10752]{1,0:T(8,128)(2,1)S(1)}, u32[]{:S(2)}, u32[]{:S(2)}) collective-permute-start(bf16[64,10752]{1,0:T(8,128)(2,1)S(1)} %constant_dynamic-update-slice_fusion.c1), channel_id=1, source_target_pairs={{0,3},{1,2},{2,1},{3,0},{4,7},{5,6},{6,5},{7,4},{8,11},{9,10},{10,... | collective-permute-start | bytes 4128776 | tf_op jit(solution)/shard_map/ppermute | solution.py:41
  72.4 25.0 %collective-permute-done.6.pr2 = bf16[64,10752]{1,0:T(8,128)(2,1)S(1)} collective-permute-done((bf16[64,10752]{1,0:T(8,128)(2,1)S(1)}, bf16[64,10752]{1,0:T(8,128)(2,1)S(1)}, u32[]{:S(2)}, u32[]{:S(2)}) %collective-permute-start.6) | collective-permute-done | bytes 1376288 | tf_op jit(solution)/shard_map/ppermute | solution.py:41
  97.4 3.1 %collective-permute-done.2.qr1 = bf16[64,10752]{1,0:T(8,128)(2,1)S(1)} collective-permute-done((bf16[64,10752]{1,0:T(8,128)(2,1)S(1)}, bf16[64,10752]{1,0:T(8,128)(2,1)S(1)}, u32[]{:S(2)}, u32[]{:S(2)}) %collective-permute-start.2) | collective-permute-done | bytes 1376288 | tf_op jit(solution)/shard_map/ppermute | solution.py:41
  104.1 4.4 %collective-permute-start.8 = (bf16[64,3584]{1,0:T(8,128)(2,1)S(1)}, bf16[64,3584]{1,0:T(8,128)(2,1)S(1)}, u32[]{:S(2)}, u32[]{:S(2)}) collective-permute-start(bf16[64,3584]{1,0:T(8,128)(2,1)S(1)} %get-tuple-element.23._), channel_id=1, source_target_pairs={{0,3},{1,2},{2,1},{3,0},{4,7},{5,6},{6,5},{7,4},{8,11},{9,10},{10,... | collective-permute-start | bytes 1376264 | tf_op jit(solution)/shard_map/ppermute | solution.py:41
  108.5 3.3 %shard_map.133 = (f32[64,3584]{1,0:T(8,128)S(1)}, bf16[64,3584]{1,0:T(8,128)(2,1)S(1)}, f32[64,3584]{1,0:T(8,128)S(1)}, bf16[64,3584]{1,0:T(8,128)(2,1)S(1)}) custom-call(bf16[64,10752]{1,0:T(8,128)(2,1)S(1)} %constant_dynamic-update-slice_fusion.c1, bf16[64,10752]{1,0:T(8,128)(2,1)S(1)} %collective-permute-done.2.qr1, ...), custom_call_target="tpu_custom_call" | custom-call | tf_op jit(solution)/shard_map/pallas_call | solution.py:308
  117.3 4.0 %collective-permute-start.14 = (bf16[32,3584]{1,0:T(8,128)(2,1)S(1)}, bf16[32,3584]{1,0:T(8,128)(2,1)S(1)}, u32[]{:S(2)}, u32[]{:S(2)}) collective-permute-start(bf16[32,3584]{1,0:T(8,128)(2,1)S(1)} %slice.93), channel_id=1, source_target_pairs={{0,3},{1,2},{2,1},{3,0},{4,7},{5,6},{6,5},{7,4},{8,11},{9,10},{10,... | collective-permute-start | bytes 688136 | tf_op jit(solution)/shard_map/ppermute | solution.py:41
  122.7 5.9 %collective-permute-start.16 = (bf16[32,3584]{1,0:T(8,128)(2,1)S(1)}, bf16[32,3584]{1,0:T(8,128)(2,1)S(1)}, u32[]{:S(2)}, u32[]{:S(2)}) collective-permute-start(bf16[32,3584]{1,0:T(8,128)(2,1)S(1)} %slice.92), channel_id=1, source_target_pairs={{0,3},{1,2},{2,1},{3,0},{4,7},{5,6},{6,5},{7,4},{8,11},{9,10},{10,... | collective-permute-start | bytes 688136 | tf_op jit(solution)/shard_map/ppermute | solution.py:41
  130.8 3.4 %collective-permute-start.11 = (bf16[32,3584]{1,0:T(8,128)(2,1)S(1)}, bf16[32,3584]{1,0:T(8,128)(2,1)S(1)}, u32[]{:S(2)}, u32[]{:S(2)}) collective-permute-start(bf16[32,3584]{1,0:T(8,128)(2,1)S(1)} %slice.94), channel_id=1, source_target_pairs={{0,1},{1,0},{2,3},{3,2},{4,5},{5,4},{6,7},{7,6},{8,9},{9,8},{10,11... | collective-permute-start | bytes 688136 | tf_op jit(solution)/shard_map/ppermute | solution.py:41
  135.6 2.9 %collective-permute-start.17 = (bf16[16,7168]{1,0:T(8,128)(2,1)S(1)}, bf16[16,7168]{1,0:T(8,128)(2,1)S(1)}, u32[]{:S(2)}, u32[]{:S(2)}) collective-permute-start(bf16[16,7168]{1,0:T(8,128)(2,1)S(1)} %get-tuple-element.34), channel_id=1, source_target_pairs={{0,24},{1,25},{2,26},{3,27},{4,12},{5,13},{6,14},{7,15},{8,0},{9,1... | collective-permute-start | bytes 688136 | tf_op jit(solution)/shard_map/ppermute | solution.py:41
  138.6 6.5 %collective-permute-start.18 = (bf16[16,7168]{1,0:T(8,128)(2,1)S(1)}, bf16[16,7168]{1,0:T(8,128)(2,1)S(1)}, u32[]{:S(2)}, u32[]{:S(2)}) collective-permute-start(bf16[16,7168]{1,0:T(8,128)(2,1)S(1)} %get-tuple-element.33), channel_id=1, source_target_pairs={{0,20},{1,21},{2,22},{3,23},{4,16},{5,17},{6,18},{7,19},{8,28},{9,... | collective-permute-start | bytes 688136 | tf_op jit(solution)/shard_map/ppermute | solution.py:41
  147.4 5.8 %collective-permute-done.18.rest_3_ = bf16[16,7168]{1,0:T(8,128)(2,1)S(1)} collective-permute-done((bf16[16,7168]{1,0:T(8,128)(2,1)S(1)}, bf16[16,7168]{1,0:T(8,128)(2,1)S(1)}, u32[]{:S(2)}, u32[]{:S(2)}) %collective-permute-start.18) | collective-permute-done | bytes 229408 | tf_op jit(solution)/shard_map/ppermute | solution.py:41
  153.2 7.0 %collective-permute-done.12.rest_1_ = bf16[16,7168]{1,0:T(8,128)(2,1)S(1)} collective-permute-done((bf16[16,7168]{1,0:T(8,128)(2,1)S(1)}, bf16[16,7168]{1,0:T(8,128)(2,1)S(1)}, u32[]{:S(2)}, u32[]{:S(2)}) %collective-permute-start.12) | collective-permute-done | bytes 229408 | tf_op jit(solution)/shard_map/ppermute | solution.py:41
  160.3 3.0 %shard_map.134 = (bf16[24,3584]{1,0:T(8,128)(2,1)S(1)}, bf16[24,3584]{1,0:T(8,128)(2,1)S(1)}, bf16[24,2]{1,0:T(8,128)(2,1)S(1)}) custom-call(s32[2]{0:T(128)S(1)} %pad_add_fusion.info_ref, bf16[24,3584]{1,0:T(8,128)(2,1)S(1)} %bitcast.25, s32[24,2]{1,0:T(8,128)S(1)} %copy.16.ra_ref, f32[24,2]{1,0:T(8,128)S(1)} %copy.17.wa_ref, ...), custom_call_target="tpu_custom_call" | custom-call | tf_op jit(solution)/shard_map/pallas_call | solution.py:313
  163.2 6.0 %collective-permute-start.19 = (bf16[24,3584]{1,0:T(8,128)(2,1)S(1)}, bf16[24,3584]{1,0:T(8,128)(2,1)S(1)}, u32[]{:S(2)}, u32[]{:S(2)}) collective-permute-start(bf16[24,3584]{1,0:T(8,128)(2,1)S(1)} %get-tuple-element.30), channel_id=1, source_target_pairs={{0,32},{32,64},{64,96},{96,128},{128,160},{160,192},{192,224},{224... | collective-permute-start | bytes 516104 | tf_op jit(solution)/shard_map/ppermute | solution.py:47
  171.8 4.2 %collective-permute-done.20 = bf16[24,3584]{1,0:T(8,128)(2,1)S(1)} collective-permute-done((bf16[24,3584]{1,0:T(8,128)(2,1)S(1)}, bf16[24,3584]{1,0:T(8,128)(2,1)S(1)}, u32[]{:S(2)}, u32[]{:S(2)}) %collective-permute-start.20) | collective-permute-done | bytes 172064 | tf_op jit(solution)/shard_map/ppermute | solution.py:47
  (79 shorter events, 34.5 us)
Async XLA Ops:
  7.1 23.8 %collective-permute-start.3 = (bf16[16,10752]{1,0:T(8,128)(2,1)S(1)}, bf16[16,10752]{1,0:T(8,128)(2,1)S(1)}, u32[]{:S(2)}, u32[]{:S(2)}) collective-permute-start(bf16[16,10752]{1,0:T(8,128)(2,1)S(1)} %get-tuple-element.20), channel_id=1, source_target_pairs={{0,8},{1,9},{2,10},{3,11},{4,28},{5,29},{6,30},{7,31},{8,16},{9,17... | collective-permute-start | bytes 1032200 | tf_op jit(solution)/shard_map/ppermute | solution.py:41
  13.8 28.3 %collective-permute-start.4 = (bf16[16,10752]{1,0:T(8,128)(2,1)S(1)}, bf16[16,10752]{1,0:T(8,128)(2,1)S(1)}, u32[]{:S(2)}, u32[]{:S(2)}) collective-permute-start(bf16[16,10752]{1,0:T(8,128)(2,1)S(1)} %get-tuple-element.21), channel_id=1, source_target_pairs={{0,20},{1,21},{2,22},{3,23},{4,16},{5,17},{6,18},{7,19},{8,28},{9,... | collective-permute-start | bytes 1032200 | tf_op jit(solution)/shard_map/ppermute | solution.py:41
  20.5 28.9 %collective-permute-start = (bf16[16,10752]{1,0:T(8,128)(2,1)S(1)}, bf16[16,10752]{1,0:T(8,128)(2,1)S(1)}, u32[]{:S(2)}, u32[]{:S(2)}) collective-permute-start(bf16[16,10752]{1,0:T(8,128)(2,1)S(1)} %get-tuple-element.19), channel_id=1, source_target_pairs={{0,28},{1,29},{2,30},{3,31},{4,8},{5,9},{6,10},{7,11},{8,4},{9,5},... | collective-permute-start | bytes 1032200 | tf_op jit(solution)/shard_map/ppermute | solution.py:41
  28.9 71.5 %collective-permute-start.7 = (bf16[10752,128]{1,0:T(8,128)(2,1)S(1)}, bf16[10752,128]{1,0:T(8,128)(2,1)S(1)}, u32[]{:S(2)}, u32[]{:S(2)}) collective-permute-start(bf16[10752,128]{1,0:T(8,128)(2,1)S(1)} %shard_map.131), channel_id=1, source_target_pairs={{0,4},{1,5},{2,6},{3,7},{4,0},{5,1},{6,2},{7,3},{8,12},{9,13},{10,... | collective-permute-start | bytes 8257544 | tf_op jit(solution)/shard_map/ppermute | solution.py:41
  42.1 19.5 %collective-permute-start.5 = (bf16[32,10752]{1,0:T(8,128)(2,1)S(1)}, bf16[32,10752]{1,0:T(8,128)(2,1)S(1)}, u32[]{:S(2)}, u32[]{:S(2)}) collective-permute-start(bf16[32,10752]{1,0:T(8,128)(2,1)S(1)} %pad_maximum_fusion.1), channel_id=1, source_target_pairs={{0,3},{1,2},{2,1},{3,0},{4,7},{5,6},{6,5},{7,4},{8,11},{9,10},{10,... | collective-permute-start | bytes 2064392 | tf_op jit(solution)/shard_map/ppermute | solution.py:41
  49.5 18.4 %collective-permute-start.1 = (bf16[32,10752]{1,0:T(8,128)(2,1)S(1)}, bf16[32,10752]{1,0:T(8,128)(2,1)S(1)}, u32[]{:S(2)}, u32[]{:S(2)}) collective-permute-start(bf16[32,10752]{1,0:T(8,128)(2,1)S(1)} %pad_maximum_fusion), channel_id=1, source_target_pairs={{0,1},{1,0},{2,3},{3,2},{4,5},{5,4},{6,7},{7,6},{8,9},{9,8},{10,11... | collective-permute-start | bytes 2064392 | tf_op jit(solution)/shard_map/ppermute | solution.py:41
  61.7 35.7 %collective-permute-start.6 = (bf16[64,10752]{1,0:T(8,128)(2,1)S(1)}, bf16[64,10752]{1,0:T(8,128)(2,1)S(1)}, u32[]{:S(2)}, u32[]{:S(2)}) collective-permute-start(bf16[64,10752]{1,0:T(8,128)(2,1)S(1)} %constant_dynamic-update-slice_fusion.3.c2), channel_id=1, source_target_pairs={{0,1},{1,0},{2,3},{3,2},{4,5},{5,4},{6,7},{7,6},{8,9},{9,8},{10,11... | collective-permute-start | bytes 4128776 | tf_op jit(solution)/shard_map/ppermute | solution.py:41
  68.0 32.5 %collective-permute-start.2 = (bf16[64,10752]{1,0:T(8,128)(2,1)S(1)}, bf16[64,10752]{1,0:T(8,128)(2,1)S(1)}, u32[]{:S(2)}, u32[]{:S(2)}) collective-permute-start(bf16[64,10752]{1,0:T(8,128)(2,1)S(1)} %constant_dynamic-update-slice_fusion.c1), channel_id=1, source_target_pairs={{0,3},{1,2},{2,1},{3,0},{4,7},{5,6},{6,5},{7,4},{8,11},{9,10},{10,... | collective-permute-start | bytes 4128776 | tf_op jit(solution)/shard_map/ppermute | solution.py:41
  102.2 15.0 %collective-permute-start.13 = (bf16[64,3584]{1,0:T(8,128)(2,1)S(1)}, bf16[64,3584]{1,0:T(8,128)(2,1)S(1)}, u32[]{:S(2)}, u32[]{:S(2)}) collective-permute-start(bf16[64,3584]{1,0:T(8,128)(2,1)S(1)} %get-tuple-element.27), channel_id=1, source_target_pairs={{0,1},{1,0},{2,3},{3,2},{4,5},{5,4},{6,7},{7,6},{8,9},{9,8},{10,11... | collective-permute-start | bytes 1376264 | tf_op jit(solution)/shard_map/ppermute | solution.py:41
  104.1 24.5 %collective-permute-start.8 = (bf16[64,3584]{1,0:T(8,128)(2,1)S(1)}, bf16[64,3584]{1,0:T(8,128)(2,1)S(1)}, u32[]{:S(2)}, u32[]{:S(2)}) collective-permute-start(bf16[64,3584]{1,0:T(8,128)(2,1)S(1)} %get-tuple-element.23._), channel_id=1, source_target_pairs={{0,3},{1,2},{2,1},{3,0},{4,7},{5,6},{6,5},{7,4},{8,11},{9,10},{10,... | collective-permute-start | bytes 1376264 | tf_op jit(solution)/shard_map/ppermute | solution.py:41
  111.8 10.7 %collective-permute-start.15 = (bf16[64,3584]{1,0:T(8,128)(2,1)S(1)}, bf16[64,3584]{1,0:T(8,128)(2,1)S(1)}, u32[]{:S(2)}, u32[]{:S(2)}) collective-permute-start(bf16[64,3584]{1,0:T(8,128)(2,1)S(1)} %get-tuple-element.29), channel_id=1, source_target_pairs={{0,1},{1,0},{2,3},{3,2},{4,5},{5,4},{6,7},{7,6},{8,9},{9,8},{10,11... | collective-permute-start | bytes 1376264 | tf_op jit(solution)/shard_map/ppermute | solution.py:41
  114.6 16.0 %collective-permute-start.10 = (bf16[64,3584]{1,0:T(8,128)(2,1)S(1)}, bf16[64,3584]{1,0:T(8,128)(2,1)S(1)}, u32[]{:S(2)}, u32[]{:S(2)}) collective-permute-start(bf16[64,3584]{1,0:T(8,128)(2,1)S(1)} %get-tuple-element.25), channel_id=1, source_target_pairs={{0,3},{1,2},{2,1},{3,0},{4,7},{5,6},{6,5},{7,4},{8,11},{9,10},{10,... | collective-permute-start | bytes 1376264 | tf_op jit(solution)/shard_map/ppermute | solution.py:41
  117.3 16.9 %collective-permute-start.14 = (bf16[32,3584]{1,0:T(8,128)(2,1)S(1)}, bf16[32,3584]{1,0:T(8,128)(2,1)S(1)}, u32[]{:S(2)}, u32[]{:S(2)}) collective-permute-start(bf16[32,3584]{1,0:T(8,128)(2,1)S(1)} %slice.93), channel_id=1, source_target_pairs={{0,3},{1,2},{2,1},{3,0},{4,7},{5,6},{6,5},{7,4},{8,11},{9,10},{10,... | collective-permute-start | bytes 688136 | tf_op jit(solution)/shard_map/ppermute | solution.py:41
  122.7 12.8 %collective-permute-start.16 = (bf16[32,3584]{1,0:T(8,128)(2,1)S(1)}, bf16[32,3584]{1,0:T(8,128)(2,1)S(1)}, u32[]{:S(2)}, u32[]{:S(2)}) collective-permute-start(bf16[32,3584]{1,0:T(8,128)(2,1)S(1)} %slice.92), channel_id=1, source_target_pairs={{0,3},{1,2},{2,1},{3,0},{4,7},{5,6},{6,5},{7,4},{8,11},{9,10},{10,... | collective-permute-start | bytes 688136 | tf_op jit(solution)/shard_map/ppermute | solution.py:41
  128.7 16.4 %collective-permute-start.9 = (bf16[32,3584]{1,0:T(8,128)(2,1)S(1)}, bf16[32,3584]{1,0:T(8,128)(2,1)S(1)}, u32[]{:S(2)}, u32[]{:S(2)}) collective-permute-start(bf16[32,3584]{1,0:T(8,128)(2,1)S(1)} %slice.95), channel_id=1, source_target_pairs={{0,1},{1,0},{2,3},{3,2},{4,5},{5,4},{6,7},{7,6},{8,9},{9,8},{10,11... | collective-permute-start | bytes 688136 | tf_op jit(solution)/shard_map/ppermute | solution.py:41
  130.8 14.4 %collective-permute-start.11 = (bf16[32,3584]{1,0:T(8,128)(2,1)S(1)}, bf16[32,3584]{1,0:T(8,128)(2,1)S(1)}, u32[]{:S(2)}, u32[]{:S(2)}) collective-permute-start(bf16[32,3584]{1,0:T(8,128)(2,1)S(1)} %slice.94), channel_id=1, source_target_pairs={{0,1},{1,0},{2,3},{3,2},{4,5},{5,4},{6,7},{7,6},{8,9},{9,8},{10,11... | collective-permute-start | bytes 688136 | tf_op jit(solution)/shard_map/ppermute | solution.py:41
  135.6 11.8 %collective-permute-start.17 = (bf16[16,7168]{1,0:T(8,128)(2,1)S(1)}, bf16[16,7168]{1,0:T(8,128)(2,1)S(1)}, u32[]{:S(2)}, u32[]{:S(2)}) collective-permute-start(bf16[16,7168]{1,0:T(8,128)(2,1)S(1)} %get-tuple-element.34), channel_id=1, source_target_pairs={{0,24},{1,25},{2,26},{3,27},{4,12},{5,13},{6,14},{7,15},{8,0},{9,1... | collective-permute-start | bytes 688136 | tf_op jit(solution)/shard_map/ppermute | solution.py:41
  138.6 21.7 %copy-start.4 = (bf16[1,24,3584]{2,1,0:T(8,128)(2,1)S(1)}, bf16[1,24,3584]{2,1,0:T(8,128)(2,1)}, u32[]{:S(2)}) copy-start(bf16[1,24,3584]{2,1,0:T(8,128)(2,1)} %param.11) | copy-start | bytes 516100
  138.6 21.7 %copy-start.6 = (bf16[1,24,3584]{2,1,0:T(8,128)(2,1)S(1)}, bf16[1,24,3584]{2,1,0:T(8,128)(2,1)}, u32[]{:S(2)}) copy-start(bf16[1,24,3584]{2,1,0:T(8,128)(2,1)} %param.14) | copy-start | bytes 516100
  138.6 21.7 %copy-start.8 = (bf16[1,24,3584]{2,1,0:T(8,128)(2,1)S(1)}, bf16[1,24,3584]{2,1,0:T(8,128)(2,1)}, u32[]{:S(2)}) copy-start(bf16[1,24,3584]{2,1,0:T(8,128)(2,1)} %param.17) | copy-start | bytes 516100
  138.6 14.6 %collective-permute-start.18 = (bf16[16,7168]{1,0:T(8,128)(2,1)S(1)}, bf16[16,7168]{1,0:T(8,128)(2,1)S(1)}, u32[]{:S(2)}, u32[]{:S(2)}) collective-permute-start(bf16[16,7168]{1,0:T(8,128)(2,1)S(1)} %get-tuple-element.33), channel_id=1, source_target_pairs={{0,20},{1,21},{2,22},{3,23},{4,16},{5,17},{6,18},{7,19},{8,28},{9,... | collective-permute-start | bytes 688136 | tf_op jit(solution)/shard_map/ppermute | solution.py:41
  145.3 15.0 %collective-permute-start.12 = (bf16[16,7168]{1,0:T(8,128)(2,1)S(1)}, bf16[16,7168]{1,0:T(8,128)(2,1)S(1)}, u32[]{:S(2)}, u32[]{:S(2)}) collective-permute-start(bf16[16,7168]{1,0:T(8,128)(2,1)S(1)} %get-tuple-element.35), channel_id=1, source_target_pairs={{0,28},{1,29},{2,30},{3,31},{4,8},{5,9},{6,10},{7,11},{8,4},{9,5},... | collective-permute-start | bytes 688136 | tf_op jit(solution)/shard_map/ppermute | solution.py:41
  163.2 8.6 %collective-permute-start.19 = (bf16[24,3584]{1,0:T(8,128)(2,1)S(1)}, bf16[24,3584]{1,0:T(8,128)(2,1)S(1)}, u32[]{:S(2)}, u32[]{:S(2)}) collective-permute-start(bf16[24,3584]{1,0:T(8,128)(2,1)S(1)} %get-tuple-element.30), channel_id=1, source_target_pairs={{0,32},{32,64},{64,96},{96,128},{128,160},{160,192},{192,224},{224... | collective-permute-start | bytes 516104 | tf_op jit(solution)/shard_map/ppermute | solution.py:47
  169.3 6.7 %collective-permute-start.20 = (bf16[24,3584]{1,0:T(8,128)(2,1)S(1)}, bf16[24,3584]{1,0:T(8,128)(2,1)S(1)}, u32[]{:S(2)}, u32[]{:S(2)}) collective-permute-start(bf16[24,3584]{1,0:T(8,128)(2,1)S(1)} %get-tuple-element.31), channel_id=1, source_target_pairs={{32,0},{64,32},{96,64},{128,96},{160,128},{192,160},{224,192},{256... | collective-permute-start | bytes 516104 | tf_op jit(solution)/shard_map/ppermute | solution.py:47
  (10 other events, 46.2 us)

commit v7 on v6

--- a/solution.py
+++ b/solution.py
@@ -128,10 +128,9 @@
 
 
 def store_parts(part, cols, keep1, send1, keep2, send2):
-    keep1[:, cols] = part[0:64]
-    send1[:, cols] = part[64:128].astype(BF16)
-    keep2[:, cols] = part[128:192]
-    send2[:, cols] = part[192:256].astype(BF16)
+    for ref, starts in ((keep1, (128, 192)), (send1, (160, 224)), (keep2, (0, 64)), (send2, (32, 96))):
+        for i, start in enumerate(starts):
+            ref[32 * i : 32 * (i + 1), cols] = part[start : start + 32].astype(ref.dtype)
 
 
 def fwd_kernel(c1, qr1, c2, pr2, wg, wu, wd, other, keep1, send1, keep2, send2, rows):
@@ -226,8 +225,9 @@
     info_ref, xa_ref, ra_ref, wa_ref, x_ref, route_ref, weight_ref, cot_ref, gain_ref, *rest
 ):
     width = x_ref.shape[1]
-    parts_a = [ref[:, :width] for ref in rest[:4]]
-    parts = [ref[:, width:] for ref in rest[:4]]
+    arrived = [rest[0], rest[1], rest[3], rest[2]]
+    parts_a = [ref[:, :width] for ref in arrived]
+    parts = [ref[:, width:] for ref in arrived]
     out_a_ref, out_ref, grad_ref = rest[4:]
     mixed = mixed_rows(slot_masks(info_ref, ra_ref), wa_ref, parts_a)
     out_a_ref[...] = (xa_ref[...].astype(F32) + mixed).astype(BF16)
@@ -253,8 +253,8 @@
 
 def spread_rows(own, a, b, c):
     got_a, got_b, got_c = hop(a, HOP_A), hop(b, HOP_B), hop(c, HOP_C)
-    half1 = jnp.concatenate([own, got_a], axis=0)
-    half2 = jnp.concatenate([got_b, got_c], axis=0)
+    half1 = jnp.concatenate([got_b, got_c], axis=0)
+    half2 = jnp.concatenate([own, got_a], axis=0)
     p1 = hop(half1, HOP_X1)
     q2 = hop(half2, HOP_X3)
     c1 = jnp.concatenate([half1, p1], axis=0)
@@ -274,7 +274,7 @@
     back_c = hop(full2[SLOT:], HOP_C)
     back_b = hop(full2[:SLOT], HOP_B_BACK)
     back_a = hop(full1[SLOT:], HOP_A)
-    return full1[:SLOT], back_a, back_b, back_c
+    return full1[:SLOT], back_a, back_c, back_b
 
 
 def body(

time: 181 us -> 177 us (0.978)
  waiting for transfers between devices: 75.1 us -> 67.9 us
  starting transfers between devices: 79.7 us -> 84.5 us
    ppermute x19, waiting for transfers between devices: 70.9 us -> 63.7 us  [hop(): return lax.ppermute(value, 'expert', pairs)]
    ppermute x19, starting transfers between devices: 71.8 us -> 76.9 us  [hop(): return lax.ppermute(value, 'expert', pairs)]
  transfers between devices with their start and end apart: 21 -> 21, of which waited for: 11 -> 12; matrix products, arithmetic and copies ran while one was open for 1% -> 1% of each run, Pallas kernels for 2% -> 2%
where the time goes in v7:
time: 177 us; the launch traced here: 175 us
  starting transfers between devices  84.5 us (48%)
  waiting for transfers between devices  67.9 us (38%)
  local copies, waits for them, and re-layouts  10.9 us (6%)
  Pallas kernels  9.69 us (5%)
    ppermute x19, starting transfers between devices, hop(): return lax.ppermute(value, 'expert', pairs)  76.9 us
    ppermute x19, waiting for transfers between devices, hop(): return lax.ppermute(value, 'expert', pairs)  63.7 us
    unnamed x32, local copies, waits for them, and re-layouts  8.47 us
    ppermute x2, starting transfers between devices, shifted(): return lax.ppermute(value, axis, pairs)  7.53 us
    ppermute x2, waiting for transfers between devices, shifted(): return lax.ppermute(value, axis, pairs)  4.2 us
  transfers between devices with their start and end apart: 21, of which 12 were waited for; matrix products, arithmetic and copies ran while one was open for 1% of the time, Pallas kernels for 2%

profile of v7, /device:TPU:1, one launch (start us, length us, event | category | flops | bytes accessed | tf_op | source)
XLA Modules:
  0.0 174.9 jit_solution(18030423530923913428)
XLA Ops:
  7.1 11.5 %collective-permute-start.4 = (bf16[16,10752]{1,0:T(8,128)(2,1)S(1)}, bf16[16,10752]{1,0:T(8,128)(2,1)S(1)}, u32[]{:S(2)}, u32[]{:S(2)}) collective-permute-start(bf16[16,10752]{1,0:T(8,128)(2,1)S(1)} %get-tuple-element.21), channel_id=1, source_target_pairs={{0,28},{1,29},{2,30},{3,31},{4,8},{5,9},{6,10},{7,11},{8,4},{9,5},... | collective-permute-start | bytes 1032200 | tf_op jit(solution)/shard_map/ppermute | solution.py:41
  20.6 4.5 %collective-permute-start.1 = (bf16[16,10752]{1,0:T(8,128)(2,1)S(1)}, bf16[16,10752]{1,0:T(8,128)(2,1)S(1)}, u32[]{:S(2)}, u32[]{:S(2)}) collective-permute-start(bf16[16,10752]{1,0:T(8,128)(2,1)S(1)} %get-tuple-element.19), channel_id=1, source_target_pairs={{0,20},{1,21},{2,22},{3,23},{4,16},{5,17},{6,18},{7,19},{8,28},{9,... | collective-permute-start | bytes 1032200 | tf_op jit(solution)/shard_map/ppermute | solution.py:41
  30.9 9.2 %collective-permute-done.4 = bf16[16,10752]{1,0:T(8,128)(2,1)S(1)} collective-permute-done((bf16[16,10752]{1,0:T(8,128)(2,1)S(1)}, bf16[16,10752]{1,0:T(8,128)(2,1)S(1)}, u32[]{:S(2)}, u32[]{:S(2)}) %collective-permute-start.4) | collective-permute-done | bytes 344096 | tf_op jit(solution)/shard_map/ppermute | solution.py:41
  40.1 4.4 %collective-permute-start.5 = (bf16[32,10752]{1,0:T(8,128)(2,1)S(1)}, bf16[32,10752]{1,0:T(8,128)(2,1)S(1)}, u32[]{:S(2)}, u32[]{:S(2)}) collective-permute-start(bf16[32,10752]{1,0:T(8,128)(2,1)S(1)} %pad_maximum_fusion.1), channel_id=1, source_target_pairs={{0,3},{1,2},{2,1},{3,0},{4,7},{5,6},{6,5},{7,4},{8,11},{9,10},{10,... | collective-permute-start | bytes 2064392 | tf_op jit(solution)/shard_map/ppermute | solution.py:41
  44.6 3.0 %collective-permute-done.1 = bf16[16,10752]{1,0:T(8,128)(2,1)S(1)} collective-permute-done((bf16[16,10752]{1,0:T(8,128)(2,1)S(1)}, bf16[16,10752]{1,0:T(8,128)(2,1)S(1)}, u32[]{:S(2)}, u32[]{:S(2)}) %collective-permute-start.1) | collective-permute-done | bytes 344096 | tf_op jit(solution)/shard_map/ppermute | solution.py:41
  47.6 3.1 %collective-permute-start.2 = (bf16[32,10752]{1,0:T(8,128)(2,1)S(1)}, bf16[32,10752]{1,0:T(8,128)(2,1)S(1)}, u32[]{:S(2)}, u32[]{:S(2)}) collective-permute-start(bf16[32,10752]{1,0:T(8,128)(2,1)S(1)} %pad_maximum_fusion), channel_id=1, source_target_pairs={{0,1},{1,0},{2,3},{3,2},{4,5},{5,4},{6,7},{7,6},{8,9},{9,8},{10,11... | collective-permute-start | bytes 2064392 | tf_op jit(solution)/shard_map/ppermute | solution.py:41
  50.8 6.7 %collective-permute-done.5 = bf16[32,10752]{1,0:T(8,128)(2,1)S(1)} collective-permute-done((bf16[32,10752]{1,0:T(8,128)(2,1)S(1)}, bf16[32,10752]{1,0:T(8,128)(2,1)S(1)}, u32[]{:S(2)}, u32[]{:S(2)}) %collective-permute-start.5) | collective-permute-done | bytes 688160 | tf_op jit(solution)/shard_map/ppermute | solution.py:41
  59.5 5.4 %collective-permute-done.2 = bf16[32,10752]{1,0:T(8,128)(2,1)S(1)} collective-permute-done((bf16[32,10752]{1,0:T(8,128)(2,1)S(1)}, bf16[32,10752]{1,0:T(8,128)(2,1)S(1)}, u32[]{:S(2)}, u32[]{:S(2)}) %collective-permute-start.2) | collective-permute-done | bytes 688160 | tf_op jit(solution)/shard_map/ppermute | solution.py:41
  64.9 4.4 %collective-permute-start.3 = (bf16[64,10752]{1,0:T(8,128)(2,1)S(1)}, bf16[64,10752]{1,0:T(8,128)(2,1)S(1)}, u32[]{:S(2)}, u32[]{:S(2)}) collective-permute-start(bf16[64,10752]{1,0:T(8,128)(2,1)S(1)} %constant_dynamic-update-slice_fusion.c1), channel_id=1, source_target_pairs={{0,3},{1,2},{2,1},{3,0},{4,7},{5,6},{6,5},{7,4},{8,11},{9,10},{10,... | collective-permute-start | bytes 4128776 | tf_op jit(solution)/shard_map/ppermute | solution.py:41
  69.3 25.0 %collective-permute-done.6.pr2 = bf16[64,10752]{1,0:T(8,128)(2,1)S(1)} collective-permute-done((bf16[64,10752]{1,0:T(8,128)(2,1)S(1)}, bf16[64,10752]{1,0:T(8,128)(2,1)S(1)}, u32[]{:S(2)}, u32[]{:S(2)}) %collective-permute-start.6) | collective-permute-done | bytes 1376288 | tf_op jit(solution)/shard_map/ppermute | solution.py:41
  98.0 3.1 %collective-permute-start.13 = (bf16[64,3584]{1,0:T(8,128)(2,1)S(1)}, bf16[64,3584]{1,0:T(8,128)(2,1)S(1)}, u32[]{:S(2)}, u32[]{:S(2)}) collective-permute-start(bf16[64,3584]{1,0:T(8,128)(2,1)S(1)} %get-tuple-element.27), channel_id=1, source_target_pairs={{0,1},{1,0},{2,3},{3,2},{4,5},{5,4},{6,7},{7,6},{8,9},{9,8},{10,11... | collective-permute-start | bytes 1376264 | tf_op jit(solution)/shard_map/ppermute | solution.py:41
  101.1 3.7 %collective-permute-start.8 = (bf16[64,3584]{1,0:T(8,128)(2,1)S(1)}, bf16[64,3584]{1,0:T(8,128)(2,1)S(1)}, u32[]{:S(2)}, u32[]{:S(2)}) collective-permute-start(bf16[64,3584]{1,0:T(8,128)(2,1)S(1)} %get-tuple-element.23._), channel_id=1, source_target_pairs={{0,3},{1,2},{2,1},{3,0},{4,7},{5,6},{6,5},{7,4},{8,11},{9,10},{10,... | collective-permute-start | bytes 1376264 | tf_op jit(solution)/shard_map/ppermute | solution.py:41
  104.8 3.3 %shard_map.133 = (f32[64,3584]{1,0:T(8,128)S(1)}, bf16[64,3584]{1,0:T(8,128)(2,1)S(1)}, f32[64,3584]{1,0:T(8,128)S(1)}, bf16[64,3584]{1,0:T(8,128)(2,1)S(1)}) custom-call(bf16[64,10752]{1,0:T(8,128)(2,1)S(1)} %constant_dynamic-update-slice_fusion.c1, bf16[64,10752]{1,0:T(8,128)(2,1)S(1)} %collective-permute-done.3.qr1, ...), custom_call_target="tpu_custom_call" | custom-call | tf_op jit(solution)/shard_map/pallas_call | solution.py:308
  113.1 4.0 %collective-permute-start.14 = (bf16[32,3584]{1,0:T(8,128)(2,1)S(1)}, bf16[32,3584]{1,0:T(8,128)(2,1)S(1)}, u32[]{:S(2)}, u32[]{:S(2)}) collective-permute-start(bf16[32,3584]{1,0:T(8,128)(2,1)S(1)} %slice.93), channel_id=1, source_target_pairs={{0,3},{1,2},{2,1},{3,0},{4,7},{5,6},{6,5},{7,4},{8,11},{9,10},{10,... | collective-permute-start | bytes 688136 | tf_op jit(solution)/shard_map/ppermute | solution.py:41
  118.1 5.7 %collective-permute-start.16 = (bf16[32,3584]{1,0:T(8,128)(2,1)S(1)}, bf16[32,3584]{1,0:T(8,128)(2,1)S(1)}, u32[]{:S(2)}, u32[]{:S(2)}) collective-permute-start(bf16[32,3584]{1,0:T(8,128)(2,1)S(1)} %slice.92), channel_id=1, source_target_pairs={{0,3},{1,2},{2,1},{3,0},{4,7},{5,6},{6,5},{7,4},{8,11},{9,10},{10,... | collective-permute-start | bytes 688136 | tf_op jit(solution)/shard_map/ppermute | solution.py:41
  126.0 3.4 %collective-permute-start.11 = (bf16[32,3584]{1,0:T(8,128)(2,1)S(1)}, bf16[32,3584]{1,0:T(8,128)(2,1)S(1)}, u32[]{:S(2)}, u32[]{:S(2)}) collective-permute-start(bf16[32,3584]{1,0:T(8,128)(2,1)S(1)} %slice.94), channel_id=1, source_target_pairs={{0,1},{1,0},{2,3},{3,2},{4,5},{5,4},{6,7},{7,6},{8,9},{9,8},{10,11... | collective-permute-start | bytes 688136 | tf_op jit(solution)/shard_map/ppermute | solution.py:41
  131.3 5.6 %collective-permute-start.17 = (bf16[16,7168]{1,0:T(8,128)(2,1)S(1)}, bf16[16,7168]{1,0:T(8,128)(2,1)S(1)}, u32[]{:S(2)}, u32[]{:S(2)}) collective-permute-start(bf16[16,7168]{1,0:T(8,128)(2,1)S(1)} %get-tuple-element.34), channel_id=1, source_target_pairs={{0,20},{1,21},{2,22},{3,23},{4,16},{5,17},{6,18},{7,19},{8,28},{9,... | collective-permute-start | bytes 688136 | tf_op jit(solution)/shard_map/ppermute | solution.py:41
  137.0 6.3 %collective-permute-start.18 = (bf16[16,7168]{1,0:T(8,128)(2,1)S(1)}, bf16[16,7168]{1,0:T(8,128)(2,1)S(1)}, u32[]{:S(2)}, u32[]{:S(2)}) collective-permute-start(bf16[16,7168]{1,0:T(8,128)(2,1)S(1)} %get-tuple-element.33), channel_id=1, source_target_pairs={{0,24},{1,25},{2,26},{3,27},{4,12},{5,13},{6,14},{7,15},{8,0},{9,1... | collective-permute-start | bytes 688136 | tf_op jit(solution)/shard_map/ppermute | solution.py:41
  143.5 4.8 %collective-permute-start.12 = (bf16[16,7168]{1,0:T(8,128)(2,1)S(1)}, bf16[16,7168]{1,0:T(8,128)(2,1)S(1)}, u32[]{:S(2)}, u32[]{:S(2)}) collective-permute-start(bf16[16,7168]{1,0:T(8,128)(2,1)S(1)} %get-tuple-element.35), channel_id=1, source_target_pairs={{0,28},{1,29},{2,30},{3,31},{4,8},{5,9},{6,10},{7,11},{8,4},{9,5},... | collective-permute-start | bytes 688136 | tf_op jit(solution)/shard_map/ppermute | solution.py:41
  148.5 2.7 %collective-permute-done.18.rest_3_ = bf16[16,7168]{1,0:T(8,128)(2,1)S(1)} collective-permute-done((bf16[16,7168]{1,0:T(8,128)(2,1)S(1)}, bf16[16,7168]{1,0:T(8,128)(2,1)S(1)}, u32[]{:S(2)}, u32[]{:S(2)}) %collective-permute-start.18) | collective-permute-done | bytes 229408 | tf_op jit(solution)/shard_map/ppermute | solution.py:41
  151.2 7.0 %collective-permute-done.12.rest_1_ = bf16[16,7168]{1,0:T(8,128)(2,1)S(1)} collective-permute-done((bf16[16,7168]{1,0:T(8,128)(2,1)S(1)}, bf16[16,7168]{1,0:T(8,128)(2,1)S(1)}, u32[]{:S(2)}, u32[]{:S(2)}) %collective-permute-start.12) | collective-permute-done | bytes 229408 | tf_op jit(solution)/shard_map/ppermute | solution.py:41
  158.2 3.0 %shard_map.134 = (bf16[24,3584]{1,0:T(8,128)(2,1)S(1)}, bf16[24,3584]{1,0:T(8,128)(2,1)S(1)}, bf16[24,2]{1,0:T(8,128)(2,1)S(1)}) custom-call(s32[2]{0:T(128)S(1)} %pad_add_fusion.info_ref, bf16[24,3584]{1,0:T(8,128)(2,1)S(1)} %bitcast.25, s32[24,2]{1,0:T(8,128)S(1)} %copy.16.ra_ref, f32[24,2]{1,0:T(8,128)S(1)} %copy.17.wa_ref, ...), custom_call_target="tpu_custom_call" | custom-call | tf_op jit(solution)/shard_map/pallas_call | solution.py:313
  161.2 5.6 %collective-permute-start.19 = (bf16[24,3584]{1,0:T(8,128)(2,1)S(1)}, bf16[24,3584]{1,0:T(8,128)(2,1)S(1)}, u32[]{:S(2)}, u32[]{:S(2)}) collective-permute-start(bf16[24,3584]{1,0:T(8,128)(2,1)S(1)} %get-tuple-element.30), channel_id=1, source_target_pairs={{0,32},{32,64},{64,96},{96,128},{128,160},{160,192},{192,224},{224... | collective-permute-start | bytes 516104 | tf_op jit(solution)/shard_map/ppermute | solution.py:47
  169.4 4.2 %collective-permute-done.20 = bf16[24,3584]{1,0:T(8,128)(2,1)S(1)} collective-permute-done((bf16[24,3584]{1,0:T(8,128)(2,1)S(1)}, bf16[24,3584]{1,0:T(8,128)(2,1)S(1)}, u32[]{:S(2)}, u32[]{:S(2)}) %collective-permute-start.20) | collective-permute-done | bytes 172064 | tf_op jit(solution)/shard_map/ppermute | solution.py:47
  (79 shorter events, 34.1 us)
Async XLA Ops:
  7.1 33.0 %collective-permute-start.4 = (bf16[16,10752]{1,0:T(8,128)(2,1)S(1)}, bf16[16,10752]{1,0:T(8,128)(2,1)S(1)}, u32[]{:S(2)}, u32[]{:S(2)}) collective-permute-start(bf16[16,10752]{1,0:T(8,128)(2,1)S(1)} %get-tuple-element.21), channel_id=1, source_target_pairs={{0,28},{1,29},{2,30},{3,31},{4,8},{5,9},{6,10},{7,11},{8,4},{9,5},... | collective-permute-start | bytes 1032200 | tf_op jit(solution)/shard_map/ppermute | solution.py:41
  18.6 25.9 %collective-permute-start = (bf16[16,10752]{1,0:T(8,128)(2,1)S(1)}, bf16[16,10752]{1,0:T(8,128)(2,1)S(1)}, u32[]{:S(2)}, u32[]{:S(2)}) collective-permute-start(bf16[16,10752]{1,0:T(8,128)(2,1)S(1)} %get-tuple-element.18), channel_id=1, source_target_pairs={{0,8},{1,9},{2,10},{3,11},{4,28},{5,29},{6,30},{7,31},{8,16},{9,17... | collective-permute-start | bytes 1032200 | tf_op jit(solution)/shard_map/ppermute | solution.py:41
  20.6 26.9 %collective-permute-start.1 = (bf16[16,10752]{1,0:T(8,128)(2,1)S(1)}, bf16[16,10752]{1,0:T(8,128)(2,1)S(1)}, u32[]{:S(2)}, u32[]{:S(2)}) collective-permute-start(bf16[16,10752]{1,0:T(8,128)(2,1)S(1)} %get-tuple-element.19), channel_id=1, source_target_pairs={{0,20},{1,21},{2,22},{3,23},{4,16},{5,17},{6,18},{7,19},{8,28},{9,... | collective-permute-start | bytes 1032200 | tf_op jit(solution)/shard_map/ppermute | solution.py:41
  28.9 67.3 %collective-permute-start.7 = (bf16[10752,128]{1,0:T(8,128)(2,1)S(1)}, bf16[10752,128]{1,0:T(8,128)(2,1)S(1)}, u32[]{:S(2)}, u32[]{:S(2)}) collective-permute-start(bf16[10752,128]{1,0:T(8,128)(2,1)S(1)} %shard_map.131), channel_id=1, source_target_pairs={{0,4},{1,5},{2,6},{3,7},{4,0},{5,1},{6,2},{7,3},{8,12},{9,13},{10,... | collective-permute-start | bytes 8257544 | tf_op jit(solution)/shard_map/ppermute | solution.py:41
  40.1 17.3 %collective-permute-start.5 = (bf16[32,10752]{1,0:T(8,128)(2,1)S(1)}, bf16[32,10752]{1,0:T(8,128)(2,1)S(1)}, u32[]{:S(2)}, u32[]{:S(2)}) collective-permute-start(bf16[32,10752]{1,0:T(8,128)(2,1)S(1)} %pad_maximum_fusion.1), channel_id=1, source_target_pairs={{0,3},{1,2},{2,1},{3,0},{4,7},{5,6},{6,5},{7,4},{8,11},{9,10},{10,... | collective-permute-start | bytes 2064392 | tf_op jit(solution)/shard_map/ppermute | solution.py:41
  47.6 17.3 %collective-permute-start.2 = (bf16[32,10752]{1,0:T(8,128)(2,1)S(1)}, bf16[32,10752]{1,0:T(8,128)(2,1)S(1)}, u32[]{:S(2)}, u32[]{:S(2)}) collective-permute-start(bf16[32,10752]{1,0:T(8,128)(2,1)S(1)} %pad_maximum_fusion), channel_id=1, source_target_pairs={{0,1},{1,0},{2,3},{3,2},{4,5},{5,4},{6,7},{7,6},{8,9},{9,8},{10,11... | collective-permute-start | bytes 2064392 | tf_op jit(solution)/shard_map/ppermute | solution.py:41
  57.5 36.8 %collective-permute-start.6 = (bf16[64,10752]{1,0:T(8,128)(2,1)S(1)}, bf16[64,10752]{1,0:T(8,128)(2,1)S(1)}, u32[]{:S(2)}, u32[]{:S(2)}) collective-permute-start(bf16[64,10752]{1,0:T(8,128)(2,1)S(1)} %constant_dynamic-update-slice_fusion.3.c2), channel_id=1, source_target_pairs={{0,1},{1,0},{2,3},{3,2},{4,5},{5,4},{6,7},{7,6},{8,9},{9,8},{10,11... | collective-permute-start | bytes 4128776 | tf_op jit(solution)/shard_map/ppermute | solution.py:41
  64.9 30.2 %collective-permute-start.3 = (bf16[64,10752]{1,0:T(8,128)(2,1)S(1)}, bf16[64,10752]{1,0:T(8,128)(2,1)S(1)}, u32[]{:S(2)}, u32[]{:S(2)}) collective-permute-start(bf16[64,10752]{1,0:T(8,128)(2,1)S(1)} %constant_dynamic-update-slice_fusion.c1), channel_id=1, source_target_pairs={{0,3},{1,2},{2,1},{3,0},{4,7},{5,6},{6,5},{7,4},{8,11},{9,10},{10,... | collective-permute-start | bytes 4128776 | tf_op jit(solution)/shard_map/ppermute | solution.py:41
  98.0 15.0 %collective-permute-start.13 = (bf16[64,3584]{1,0:T(8,128)(2,1)S(1)}, bf16[64,3584]{1,0:T(8,128)(2,1)S(1)}, u32[]{:S(2)}, u32[]{:S(2)}) collective-permute-start(bf16[64,3584]{1,0:T(8,128)(2,1)S(1)} %get-tuple-element.27), channel_id=1, source_target_pairs={{0,1},{1,0},{2,3},{3,2},{4,5},{5,4},{6,7},{7,6},{8,9},{9,8},{10,11... | collective-permute-start | bytes 1376264 | tf_op jit(solution)/shard_map/ppermute | solution.py:41
  101.1 22.7 %collective-permute-start.8 = (bf16[64,3584]{1,0:T(8,128)(2,1)S(1)}, bf16[64,3584]{1,0:T(8,128)(2,1)S(1)}, u32[]{:S(2)}, u32[]{:S(2)}) collective-permute-start(bf16[64,3584]{1,0:T(8,128)(2,1)S(1)} %get-tuple-element.23._), channel_id=1, source_target_pairs={{0,3},{1,2},{2,1},{3,0},{4,7},{5,6},{6,5},{7,4},{8,11},{9,10},{10,... | collective-permute-start | bytes 1376264 | tf_op jit(solution)/shard_map/ppermute | solution.py:41
  108.2 9.9 %collective-permute-start.15 = (bf16[64,3584]{1,0:T(8,128)(2,1)S(1)}, bf16[64,3584]{1,0:T(8,128)(2,1)S(1)}, u32[]{:S(2)}, u32[]{:S(2)}) collective-permute-start(bf16[64,3584]{1,0:T(8,128)(2,1)S(1)} %get-tuple-element.29), channel_id=1, source_target_pairs={{0,1},{1,0},{2,3},{3,2},{4,5},{5,4},{6,7},{7,6},{8,9},{9,8},{10,11... | collective-permute-start | bytes 1376264 | tf_op jit(solution)/shard_map/ppermute | solution.py:41
  110.4 15.5 %collective-permute-start.10 = (bf16[64,3584]{1,0:T(8,128)(2,1)S(1)}, bf16[64,3584]{1,0:T(8,128)(2,1)S(1)}, u32[]{:S(2)}, u32[]{:S(2)}) collective-permute-start(bf16[64,3584]{1,0:T(8,128)(2,1)S(1)} %get-tuple-element.25), channel_id=1, source_target_pairs={{0,3},{1,2},{2,1},{3,0},{4,7},{5,6},{6,5},{7,4},{8,11},{9,10},{10,... | collective-permute-start | bytes 1376264 | tf_op jit(solution)/shard_map/ppermute | solution.py:41
  113.1 16.3 %collective-permute-start.14 = (bf16[32,3584]{1,0:T(8,128)(2,1)S(1)}, bf16[32,3584]{1,0:T(8,128)(2,1)S(1)}, u32[]{:S(2)}, u32[]{:S(2)}) collective-permute-start(bf16[32,3584]{1,0:T(8,128)(2,1)S(1)} %slice.93), channel_id=1, source_target_pairs={{0,3},{1,2},{2,1},{3,0},{4,7},{5,6},{6,5},{7,4},{8,11},{9,10},{10,... | collective-permute-start | bytes 688136 | tf_op jit(solution)/shard_map/ppermute | solution.py:41
  118.1 13.1 %collective-permute-start.16 = (bf16[32,3584]{1,0:T(8,128)(2,1)S(1)}, bf16[32,3584]{1,0:T(8,128)(2,1)S(1)}, u32[]{:S(2)}, u32[]{:S(2)}) collective-permute-start(bf16[32,3584]{1,0:T(8,128)(2,1)S(1)} %slice.92), channel_id=1, source_target_pairs={{0,3},{1,2},{2,1},{3,0},{4,7},{5,6},{6,5},{7,4},{8,11},{9,10},{10,... | collective-permute-start | bytes 688136 | tf_op jit(solution)/shard_map/ppermute | solution.py:41
  123.9 19.4 %collective-permute-start.9 = (bf16[32,3584]{1,0:T(8,128)(2,1)S(1)}, bf16[32,3584]{1,0:T(8,128)(2,1)S(1)}, u32[]{:S(2)}, u32[]{:S(2)}) collective-permute-start(bf16[32,3584]{1,0:T(8,128)(2,1)S(1)} %slice.95), channel_id=1, source_target_pairs={{0,1},{1,0},{2,3},{3,2},{4,5},{5,4},{6,7},{7,6},{8,9},{9,8},{10,11... | collective-permute-start | bytes 688136 | tf_op jit(solution)/shard_map/ppermute | solution.py:41
  126.0 17.4 %collective-permute-start.11 = (bf16[32,3584]{1,0:T(8,128)(2,1)S(1)}, bf16[32,3584]{1,0:T(8,128)(2,1)S(1)}, u32[]{:S(2)}, u32[]{:S(2)}) collective-permute-start(bf16[32,3584]{1,0:T(8,128)(2,1)S(1)} %slice.94), channel_id=1, source_target_pairs={{0,1},{1,0},{2,3},{3,2},{4,5},{5,4},{6,7},{7,6},{8,9},{9,8},{10,11... | collective-permute-start | bytes 688136 | tf_op jit(solution)/shard_map/ppermute | solution.py:41
  131.3 17.2 %collective-permute-start.17 = (bf16[16,7168]{1,0:T(8,128)(2,1)S(1)}, bf16[16,7168]{1,0:T(8,128)(2,1)S(1)}, u32[]{:S(2)}, u32[]{:S(2)}) collective-permute-start(bf16[16,7168]{1,0:T(8,128)(2,1)S(1)} %get-tuple-element.34), channel_id=1, source_target_pairs={{0,20},{1,21},{2,22},{3,23},{4,16},{5,17},{6,18},{7,19},{8,28},{9,... | collective-permute-start | bytes 688136 | tf_op jit(solution)/shard_map/ppermute | solution.py:41
  136.9 21.3 %copy-start.4 = (bf16[1,24,3584]{2,1,0:T(8,128)(2,1)S(1)}, bf16[1,24,3584]{2,1,0:T(8,128)(2,1)}, u32[]{:S(2)}) copy-start(bf16[1,24,3584]{2,1,0:T(8,128)(2,1)} %param.11) | copy-start | bytes 516100
  136.9 21.3 %copy-start.6 = (bf16[1,24,3584]{2,1,0:T(8,128)(2,1)S(1)}, bf16[1,24,3584]{2,1,0:T(8,128)(2,1)}, u32[]{:S(2)}) copy-start(bf16[1,24,3584]{2,1,0:T(8,128)(2,1)} %param.14) | copy-start | bytes 516100
  137.0 21.3 %copy-start.8 = (bf16[1,24,3584]{2,1,0:T(8,128)(2,1)S(1)}, bf16[1,24,3584]{2,1,0:T(8,128)(2,1)}, u32[]{:S(2)}) copy-start(bf16[1,24,3584]{2,1,0:T(8,128)(2,1)} %param.17) | copy-start | bytes 516100
  137.0 14.2 %collective-permute-start.18 = (bf16[16,7168]{1,0:T(8,128)(2,1)S(1)}, bf16[16,7168]{1,0:T(8,128)(2,1)S(1)}, u32[]{:S(2)}, u32[]{:S(2)}) collective-permute-start(bf16[16,7168]{1,0:T(8,128)(2,1)S(1)} %get-tuple-element.33), channel_id=1, source_target_pairs={{0,24},{1,25},{2,26},{3,27},{4,12},{5,13},{6,14},{7,15},{8,0},{9,1... | collective-permute-start | bytes 688136 | tf_op jit(solution)/shard_map/ppermute | solution.py:41
  143.5 14.7 %collective-permute-start.12 = (bf16[16,7168]{1,0:T(8,128)(2,1)S(1)}, bf16[16,7168]{1,0:T(8,128)(2,1)S(1)}, u32[]{:S(2)}, u32[]{:S(2)}) collective-permute-start(bf16[16,7168]{1,0:T(8,128)(2,1)S(1)} %get-tuple-element.35), channel_id=1, source_target_pairs={{0,28},{1,29},{2,30},{3,31},{4,8},{5,9},{6,10},{7,11},{8,4},{9,5},... | collective-permute-start | bytes 688136 | tf_op jit(solution)/shard_map/ppermute | solution.py:41
  161.2 8.1 %collective-permute-start.19 = (bf16[24,3584]{1,0:T(8,128)(2,1)S(1)}, bf16[24,3584]{1,0:T(8,128)(2,1)S(1)}, u32[]{:S(2)}, u32[]{:S(2)}) collective-permute-start(bf16[24,3584]{1,0:T(8,128)(2,1)S(1)} %get-tuple-element.30), channel_id=1, source_target_pairs={{0,32},{32,64},{64,96},{96,128},{128,160},{160,192},{192,224},{224... | collective-permute-start | bytes 516104 | tf_op jit(solution)/shard_map/ppermute | solution.py:47
  166.8 6.7 %collective-permute-start.20 = (bf16[24,3584]{1,0:T(8,128)(2,1)S(1)}, bf16[24,3584]{1,0:T(8,128)(2,1)S(1)}, u32[]{:S(2)}, u32[]{:S(2)}) collective-permute-start(bf16[24,3584]{1,0:T(8,128)(2,1)S(1)} %get-tuple-element.31), channel_id=1, source_target_pairs={{32,0},{64,32},{96,64},{128,96},{160,128},{192,160},{224,192},{256... | collective-permute-start | bytes 516104 | tf_op jit(solution)/shard_map/ppermute | solution.py:47
  (10 other events, 51.2 us)

commit v8 on v7

--- a/solution.py
+++ b/solution.py
@@ -9,6 +9,7 @@
 GRID_X = 4
 GRID_Z = 8
 SLOT = 16
+CAP = 14
 F32 = jnp.float32
 BF16 = jnp.bfloat16
 NT = (((1,), (1,)), ((), ()))
@@ -60,7 +61,7 @@
     )
 
 
-def slot_masks(info_ref, route_ref):
+def slot_places(info_ref, route_ref):
     tokens = route_ref.shape[0]
     own, odd = info_ref[0], info_ref[1]
     lanes = lax.broadcasted_iota(jnp.int32, (tokens, 128), 1)
@@ -68,7 +69,7 @@
     named = [(route[:, k : k + 1] == lanes).astype(F32) for k in range(2)]
     row = lax.broadcasted_iota(jnp.int32, (tokens, tokens), 0)
     col = lax.broadcasted_iota(jnp.int32, (tokens, tokens), 1)
-    earlier = (col < row).astype(BF16)
+    earlier = (col < row).astype(F32).astype(BF16)
     counts = jnp.dot(earlier, (named[0] + named[1]).astype(BF16), preferred_element_type=F32)
     out = []
     for k in range(2):
@@ -76,9 +77,20 @@
         away = (route[:, k : k + 1] - own) & 3
         side = jnp.where((away == 3) == (odd == 0), 1, 2)
         rel = jnp.where(away == 0, 0, jnp.where(away == 2, 3, side))
-        slots = lax.broadcasted_iota(jnp.int32, (tokens, 4 * SLOT), 1)
-        out.append((slots == rel * SLOT + rank, rel, rank))
+        out.append((rel, rank))
     return out
+
+
+def slot_masks(info_ref, route_ref):
+    tokens = route_ref.shape[0]
+    slots = lax.broadcasted_iota(jnp.int32, (tokens, 4 * SLOT), 1)
+    places = slot_places(info_ref, route_ref)
+    return [(slots == rel * SLOT + rank, rel, rank) for rel, rank in places]
+
+
+def split(index, size):
+    whole = sum((index >= size * i).astype(jnp.int32) for i in (1, 2, 3))
+    return whole, index - size * whole
 
 
 def normalized(x):
@@ -87,28 +99,44 @@
     return values * scale, scale
 
 
-def pack_kernel(info_ref, xa_ref, ra_ref, xb_ref, rb_ref, cot_ref, gain_ref, *outs):
-    width = xa_ref.shape[1]
-    places = []
+def pack_kernel(info_ref, xa_ref, ra_ref, xb_ref, rb_ref, cot_ref, gain_ref, _, *outs):
+    tokens, width = xa_ref.shape
+    quarter = width // 4
+    lane = lax.broadcasted_iota(jnp.int32, (tokens, 16 * CAP), 1)
+    block, rest = split(lane, 4 * CAP)
+    part, slot = split(rest, CAP)
+    held = []
     for route_ref in (ra_ref, rb_ref):
-        masks = slot_masks(info_ref, route_ref)
-        places.append((masks[0][0] | masks[1][0]).astype(F32).astype(BF16))
+        (rel0, rank0), (rel1, rank1) = slot_places(info_ref, route_ref)
+        held.append(
+            ((block == rel0) & (slot == rank0)) | ((block == rel1) & (slot == rank1))
+        )
     gain = gain_ref[...]
     normed_a = (normalized(xa_ref[...])[0] * gain).astype(BF16)
     normed_b = (normalized(xb_ref[...])[0] * gain).astype(BF16)
-    sources = ((places[0], normed_a), (places[1], normed_b), (places[1], cot_ref[...]))
-    for i, (place, rows) in enumerate(sources):
-        packed = lax.dot_general(place, rows, TN, preferred_element_type=F32).astype(BF16)
+    sources = ((held[0], normed_a), (held[1], normed_b), (held[1], cot_ref[...]))
+    for i, (mask, rows) in enumerate(sources):
+        packed = None
+        for q in range(4):
+            place = (mask & (part == q)).astype(F32).astype(BF16)
+            chunk = rows[:, q * quarter : (q + 1) * quarter]
+            term = lax.dot_general(place, chunk, TN, preferred_element_type=F32)
+            packed = term if packed is None else packed + term
         for j in range(4):
-            outs[j][:, i * width : (i + 1) * width] = packed[j * SLOT : (j + 1) * SLOT]
-
-
-def merge_kernel(wg, wu, wd, out):
-    width, units = wg.shape
+            piece = packed[4 * CAP * j : 4 * CAP * (j + 1)]
+            outs[j][:, i * quarter : (i + 1) * quarter] = piece.astype(BF16)
+
+
+def merge_kernel(wg, wu, out):
+    width = wg.shape[0]
     out[0:width, :] = wg[...]
     out[width : 2 * width, :] = wu[...]
-    for at in range(0, width, units):
-        out[2 * width + at : 2 * width + at + units, :] = wd[:, at : at + units]
+
+
+def near_kernel(half, got, _, out):
+    count = half.shape[0]
+    out[0:count, :] = half[...]
+    out[count : 2 * count, :] = got[...]
 
 
 def hidden(rows, wg, wu):
@@ -116,15 +144,23 @@
     return both[:, :128], both[:, 128:]
 
 
-def down_columns(merged, at, count):
-    width = merged.shape[0] // 3
-    starts = range(2 * width + at, 2 * width + at + count, 128)
-    return jnp.concatenate([merged[start : start + 128, :] for start in starts], axis=1)
-
-
-def gather_rows(refs, at, width, scratch):
+def unpack_places():
+    row = lax.broadcasted_iota(jnp.int32, (16 * SLOT, 16 * CAP), 0)
+    col = lax.broadcasted_iota(jnp.int32, (16 * SLOT, 16 * CAP), 1)
+    block, rest = split(col, 4 * CAP)
+    part, slot = split(rest, CAP)
+    return (row == part * 4 * SLOT + block * SLOT + slot).astype(F32).astype(BF16)
+
+
+def gather_rows(refs, which, places, scratch):
+    quarter = scratch.shape[1] // 4
+    count = 4 * SLOT
     for i, ref in enumerate(refs):
-        scratch[64 * i : 64 * (i + 1), :] = ref[:, at : at + width]
+        blocks = ref[:, which * quarter : (which + 1) * quarter]
+        rows = jnp.dot(places, blocks, preferred_element_type=F32).astype(BF16)
+        for q in range(4):
+            cols = slice(q * quarter, (q + 1) * quarter)
+            scratch[count * i : count * (i + 1), cols] = rows[count * q : count * (q + 1)]
 
 
 def store_parts(part, cols, keep1, send1, keep2, send2):
@@ -133,9 +169,9 @@
             ref[32 * i : 32 * (i + 1), cols] = part[start : start + 32].astype(ref.dtype)
 
 
-def fwd_kernel(c1, qr1, c2, pr2, wg, wu, wd, other, keep1, send1, keep2, send2, rows):
+def fwd_kernel(c1, qr1, c2, pr2, wg, wu, wd, other, vd, keep1, send1, keep2, send2, rows):
     width = rows.shape[1]
-    gather_rows((c1, qr1, c2, pr2), 0, width, rows)
+    gather_rows((c1, qr1, c2, pr2), 0, unpack_places(), rows)
     inner = []
     for weights in ((wg[...], wu[...]), (other[0:width, :], other[width : 2 * width, :])):
         gate, up = hidden(rows[...], *weights)
@@ -144,22 +180,23 @@
     step = 512
     for at in range(0, width, step):
         cols = slice(at, at + step)
-        down = jnp.concatenate([wd[:, cols], down_columns(other, at, step)], axis=0)
+        down = jnp.concatenate([wd[:, cols], vd[:, cols]], axis=0)
         part = jnp.dot(inner, down, preferred_element_type=F32)
         store_parts(part, cols, keep1, send1, keep2, send2)
 
 
 def bwd_kernel(
-    c1, qr1, c2, pr2, wg, wu, wd, other, _, keep1, send1, keep2, send2, rows, cots
+    c1, qr1, c2, pr2, wg, wu, wd, other, vd, _, keep1, send1, keep2, send2, rows, cots
 ):
     width = rows.shape[1]
-    gather_rows((c1, qr1, c2, pr2), width, width, rows)
-    gather_rows((c1, qr1, c2, pr2), 2 * width, width, cots)
+    places = unpack_places()
+    gather_rows((c1, qr1, c2, pr2), 1, places, rows)
+    gather_rows((c1, qr1, c2, pr2), 2, places, cots)
     back = []
     products = None
     sources = (
         (wg[...], wu[...], wd[...]),
-        (other[0:width, :], other[width : 2 * width, :], down_columns(other, 0, width)),
+        (other[0:width, :], other[width : 2 * width, :], vd[...]),
     )
     for gate_w, up_w, down_w in sources:
         gate, up = hidden(rows[...], gate_w, up_w)
@@ -251,13 +288,19 @@
     grad_ref[...] = jnp.where(pair == 0, grads[0], grads[1]).astype(BF16)
 
 
-def spread_rows(own, a, b, c):
+def spread_rows(own, a, b, c, other):
     got_a, got_b, got_c = hop(a, HOP_A), hop(b, HOP_B), hop(c, HOP_C)
     half1 = jnp.concatenate([got_b, got_c], axis=0)
     half2 = jnp.concatenate([own, got_a], axis=0)
     p1 = hop(half1, HOP_X1)
     q2 = hop(half2, HOP_X3)
-    c1 = jnp.concatenate([half1, p1], axis=0)
+    vmem = pl.BlockSpec(memory_space=pltpu.VMEM)
+    c1 = pl.pallas_call(
+        near_kernel,
+        out_shape=jax.ShapeDtypeStruct((2 * half1.shape[0], half1.shape[1]), BF16),
+        in_specs=[vmem, vmem, pl.BlockSpec(memory_space=pl.ANY)],
+        out_specs=vmem,
+    )(half1, p1, other)
     c2 = jnp.concatenate([half2, q2], axis=0)
     return c1, hop(c1, HOP_X3), c2, hop(c2, HOP_X1)
 
@@ -295,18 +338,20 @@
     info = jnp.stack([index >> 3, (index >> 2) & 1]).astype(jnp.int32)
     weights = (w_gate[0, 0], w_up[0, 0], w_down[0, 0])
     units = w_down.shape[2]
-    (merged,) = kernel_call(merge_kernel, [((3 * width, units), BF16)], 3, info=False)(*weights)
+    (merged,) = kernel_call(merge_kernel, [((2 * width, units), BF16)], 2, info=False)(*weights[:2])
     other = hop(merged, HOP_W)
-    wide = [((SLOT, 3 * width), BF16)] * 4
-    sent = kernel_call(pack_kernel, wide, 6)(
-        info, act_fwd[0], route_fwd[0], act_bwd[0], route_bwd[0], cot_bwd[0], norm_gain
-    )
-    rows = spread_rows(*sent)
+    other_down = hop(weights[2], HOP_W)
+    wide = [((4 * CAP, 3 * width // 4), BF16)] * 4
+    sent = kernel_call(pack_kernel, wide, 7)(
+        info, act_fwd[0], route_fwd[0], act_bwd[0], route_bwd[0], cot_bwd[0], norm_gain, merged
+    )
+    rows = spread_rows(*sent, other)
+    weights += (other, other_down)
     outs = [((64, width), F32), ((64, width), BF16)] * 2
     scratch = pltpu.VMEM((256, width), BF16)
-    part_a = kernel_call(fwd_kernel, outs, 8, [scratch], info=False)(*rows, *weights, other)
-    part_b = kernel_call(bwd_kernel, outs, 9, [scratch] * 2, info=False)(
-        *rows, *weights, other, part_a[1]
+    part_a = kernel_call(fwd_kernel, outs, 9, [scratch], info=False)(*rows, *weights)
+    part_b = kernel_call(bwd_kernel, outs, 10, [scratch] * 2, info=False)(
+        *rows, *weights, part_a[1]
     )
     halves = zip(return_x(*part_a), return_x(*part_b))
     back = return_z(*[jnp.concatenate(pair, axis=1) for pair in halves])

time: 177 us -> 201 us (1.14)
  waiting for transfers between devices: 67.9 us -> 81.9 us
  Pallas kernels: 9.69 us -> 20 us
  starting transfers between devices: 84.5 us -> 80 us
  local copies, waits for them, and re-layouts: 10.9 us -> 14.4 us
    ppermute x19 -> x20, waiting for transfers between devices: 63.7 us -> 77.7 us  [hop(): return lax.ppermute(value, 'expert', pairs)]
    pallas_call x4 -> x5, Pallas kernels: 6.73 us -> 17 us  [the longest x1 6.08 us: body(): kernel_call(bwd_kernel, outs, 10, [scratch] * 2, info=False)]
    ppermute x19 -> x20, starting transfers between devices: 76.9 us -> 69 us  [hop(): return lax.ppermute(value, 'expert', pairs)]
    unnamed x32 -> x41, local copies, waits for them, and re-layouts: 8.47 us -> 12.5 us
    ppermute x2, starting transfers between devices: 7.53 us -> 11 us  [shifted(): return lax.ppermute(value, axis, pairs)]
  transfers between devices with their start and end apart: 21 -> 22, of which waited for: 12 -> 9; matrix products, arithmetic and copies ran while one was open for 1% -> 2% of each run, Pallas kernels for 2% -> 6%
where the time goes in v8:
time: 201 us; the launch traced here: 198 us
  waiting for transfers between devices  81.9 us (41%)
  starting transfers between devices  80 us (40%)
  Pallas kernels  20 us (10%)
  local copies, waits for them, and re-layouts  14.4 us (7%)
    ppermute x20, waiting for transfers between devices, hop(): return lax.ppermute(value, 'expert', pairs)  77.7 us
    ppermute x20, starting transfers between devices, hop(): return lax.ppermute(value, 'expert', pairs)  69 us
    unnamed x41, local copies, waits for them, and re-layouts  12.5 us
    ppermute x2, starting transfers between devices, shifted(): return lax.ppermute(value, axis, pairs)  11 us
    pallas_call x1, Pallas kernels, body(): kernel_call(bwd_kernel, outs, 10, [scratch] * 2, info=False)  6.08 us
    ppermute x2, waiting for transfers between devices, shifted(): return lax.ppermute(value, axis, pairs)  4.2 us
  transfers between devices with their start and end apart: 22, of which 9 were waited for; matrix products, arithmetic and copies ran while one was open for 2% of the time, Pallas kernels for 6%

profile of v8, /device:TPU:1, one launch (start us, length us, event | category | flops | bytes accessed | tf_op | source)
XLA Modules:
  0.0 198.0 jit_solution(14388644335495115649)
XLA Ops:
  4.4 4.8 %collective-permute-start.3 = (bf16[7168,128]{1,0:T(8,128)(2,1)}, bf16[7168,128]{1,0:T(8,128)(2,1)S(1)}, u32[]{:S(2)}, u32[]{:S(2)}) collective-permute-start(bf16[7168,128]{1,0:T(8,128)(2,1)} %shard_map.130._), channel_id=1, source_target_pairs={{0,4},{1,5},{2,6},{3,7},{4,0},{5,1},{6,2},{7,3},{8,12},{9,13},{10,... | collective-permute-start | bytes 5505032 | tf_op jit(solution)/shard_map/ppermute | solution.py:42
  9.5 3.3 %shard_map.131 = (bf16[56,2688]{1,0:T(8,128)(2,1)S(1)}, bf16[56,2688]{1,0:T(8,128)(2,1)S(1)}, bf16[56,2688]{1,0:T(8,128)(2,1)S(1)}, bf16[56,2688]{1,0:T(8,128)(2,1)S(1)}) custom-call(s32[2]{0:T(128)S(1)} %pad_add_fusion.info_ref, bf16[24,3584]{1,0:T(8,128)(2,1)S(1)} %bitcast.24, s32[24,2]{1,0:T(8,128)S(1)} %copy.16.ra_ref, bf16[24,3584]{1,0:T(8,128)(2,1)S(1)} %bitcast.26, ...), custom_call_target="tpu_custom_call" | custom-call | tf_op jit(solution)/shard_map/pallas_call | solution.py:345
  12.8 5.8 %collective-permute-start = (bf16[56,2688]{1,0:T(8,128)(2,1)S(1)}, bf16[56,2688]{1,0:T(8,128)(2,1)S(1)}, u32[]{:S(2)}, u32[]{:S(2)}) collective-permute-start(bf16[56,2688]{1,0:T(8,128)(2,1)S(1)} %get-tuple-element.18), channel_id=1, source_target_pairs={{0,8},{1,9},{2,10},{3,11},{4,28},{5,29},{6,30},{7,31},{8,16},{9,17... | collective-permute-start | bytes 903176 | tf_op jit(solution)/shard_map/ppermute | solution.py:42
  18.7 4.9 %collective-permute-start.1 = (bf16[56,2688]{1,0:T(8,128)(2,1)S(1)}, bf16[56,2688]{1,0:T(8,128)(2,1)S(1)}, u32[]{:S(2)}, u32[]{:S(2)}) collective-permute-start(bf16[56,2688]{1,0:T(8,128)(2,1)S(1)} %get-tuple-element.19), channel_id=1, source_target_pairs={{0,20},{1,21},{2,22},{3,23},{4,16},{5,17},{6,18},{7,19},{8,28},{9,... | collective-permute-start | bytes 903176 | tf_op jit(solution)/shard_map/ppermute | solution.py:42
  23.6 5.5 %collective-permute-start.5 = (bf16[56,2688]{1,0:T(8,128)(2,1)S(1)}, bf16[56,2688]{1,0:T(8,128)(2,1)S(1)}, u32[]{:S(2)}, u32[]{:S(2)}) collective-permute-start(bf16[56,2688]{1,0:T(8,128)(2,1)S(1)} %get-tuple-element.21), channel_id=1, source_target_pairs={{0,28},{1,29},{2,30},{3,31},{4,8},{5,9},{6,10},{7,11},{8,4},{9,5},... | collective-permute-start | bytes 903176 | tf_op jit(solution)/shard_map/ppermute | solution.py:42
  29.8 15.8 %collective-permute-done.5 = bf16[56,2688]{1,0:T(8,128)(2,1)S(1)} collective-permute-done((bf16[56,2688]{1,0:T(8,128)(2,1)S(1)}, bf16[56,2688]{1,0:T(8,128)(2,1)S(1)}, u32[]{:S(2)}, u32[]{:S(2)}) %collective-permute-start.5) | collective-permute-done | bytes 301088 | tf_op jit(solution)/shard_map/ppermute | solution.py:42
  45.7 4.4 %collective-permute-start.6 = (bf16[112,2688]{1,0:T(8,128)(2,1)S(1)}, bf16[112,2688]{1,0:T(8,128)(2,1)S(1)}, u32[]{:S(2)}, u32[]{:S(2)}) collective-permute-start(bf16[112,2688]{1,0:T(8,128)(2,1)S(1)} %pad_maximum_fusion), channel_id=1, source_target_pairs={{0,3},{1,2},{2,1},{3,0},{4,7},{5,6},{6,5},{7,4},{8,11},{9,10},{10,... | collective-permute-start | bytes 1806344 | tf_op jit(solution)/shard_map/ppermute | solution.py:42
  50.1 19.5 %collective-permute-done = bf16[56,2688]{1,0:T(8,128)(2,1)S(1)} collective-permute-done((bf16[56,2688]{1,0:T(8,128)(2,1)S(1)}, bf16[56,2688]{1,0:T(8,128)(2,1)S(1)}, u32[]{:S(2)}, u32[]{:S(2)}) %collective-permute-start) | collective-permute-done | bytes 301088 | tf_op jit(solution)/shard_map/ppermute | solution.py:42
  69.7 3.1 %collective-permute-start.2 = (bf16[112,2688]{1,0:T(8,128)(2,1)S(1)}, bf16[112,2688]{1,0:T(8,128)(2,1)S(1)}, u32[]{:S(2)}, u32[]{:S(2)}) collective-permute-start(bf16[112,2688]{1,0:T(8,128)(2,1)S(1)} %constant_dynamic-update-slice_fusion.half), channel_id=1, source_target_pairs={{0,1},{1,0},{2,3},{3,2},{4,5},{5,4},{6,7},{7,6},{8,9},{9,8},{10,11... | collective-permute-start | bytes 1806344 | tf_op jit(solution)/shard_map/ppermute | solution.py:42
  76.7 8.4 %collective-permute-done.2.got = bf16[112,2688]{1,0:T(8,128)(2,1)S(1)} collective-permute-done((bf16[112,2688]{1,0:T(8,128)(2,1)S(1)}, bf16[112,2688]{1,0:T(8,128)(2,1)S(1)}, u32[]{:S(2)}, u32[]{:S(2)}) %collective-permute-start.2) | collective-permute-done | bytes 602144 | tf_op jit(solution)/shard_map/ppermute | solution.py:42
  89.5 4.4 %collective-permute-start.4 = (bf16[224,2688]{1,0:T(8,128)(2,1)}, bf16[224,2688]{1,0:T(8,128)(2,1)S(1)}, u32[]{:S(2)}, u32[]{:S(2)}) collective-permute-start(bf16[224,2688]{1,0:T(8,128)(2,1)} %shard_map.132.c1), channel_id=1, source_target_pairs={{0,3},{1,2},{2,1},{3,0},{4,7},{5,6},{6,5},{7,4},{8,11},{9,10},{10,... | collective-permute-start | bytes 3612680 | tf_op jit(solution)/shard_map/ppermute | solution.py:42
  95.9 17.2 %collective-permute-done.8.vd = bf16[128,3584]{1,0:T(8,128)(2,1)S(1)} collective-permute-done((bf16[128,3584]{1,0:T(8,128)(2,1)}, bf16[128,3584]{1,0:T(8,128)(2,1)S(1)}, u32[]{:S(2)}, u32[]{:S(2)}) %collective-permute-start.8) | collective-permute-done | bytes 917536 | tf_op jit(solution)/shard_map/ppermute | solution.py:42
  113.1 3.2 %collective-permute-done.4.qr1 = bf16[224,2688]{1,0:T(8,128)(2,1)S(1)} collective-permute-done((bf16[224,2688]{1,0:T(8,128)(2,1)}, bf16[224,2688]{1,0:T(8,128)(2,1)S(1)}, u32[]{:S(2)}, u32[]{:S(2)}) %collective-permute-start.4) | collective-permute-done | bytes 1204256 | tf_op jit(solution)/shard_map/ppermute | solution.py:42
  121.4 3.9 %shard_map.133 = (f32[64,3584]{1,0:T(8,128)S(1)}, bf16[64,3584]{1,0:T(8,128)(2,1)S(1)}, f32[64,3584]{1,0:T(8,128)S(1)}, bf16[64,3584]{1,0:T(8,128)(2,1)S(1)}) custom-call(bf16[224,2688]{1,0:T(8,128)(2,1)S(1)} %copy-done.2, bf16[224,2688]{1,0:T(8,128)(2,1)S(1)} %collective-permute-done.4.qr1, bf16[224,2688]{1,0:T(8,128)(2,1)} %constant_dynamic-update-slice_fusion.2.c2, ...), custom_call_target="tpu_custom_call" | custom-call | tf_op jit(solution)/shard_map/pallas_call | solution.py:352
  127.2 4.4 %collective-permute-start.9 = (bf16[64,3584]{1,0:T(8,128)(2,1)S(1)}, bf16[64,3584]{1,0:T(8,128)(2,1)S(1)}, u32[]{:S(2)}, u32[]{:S(2)}) collective-permute-start(bf16[64,3584]{1,0:T(8,128)(2,1)S(1)} %get-tuple-element.23._), channel_id=1, source_target_pairs={{0,3},{1,2},{2,1},{3,0},{4,7},{5,6},{6,5},{7,4},{8,11},{9,10},{10,... | collective-permute-start | bytes 1376264 | tf_op jit(solution)/shard_map/ppermute | solution.py:42
  131.6 6.1 %shard_map.134 = (f32[64,3584]{1,0:T(8,128)S(1)}, bf16[64,3584]{1,0:T(8,128)(2,1)S(1)}, f32[64,3584]{1,0:T(8,128)S(1)}, bf16[64,3584]{1,0:T(8,128)(2,1)S(1)}) custom-call(bf16[224,2688]{1,0:T(8,128)(2,1)S(1)} %copy-done.2, bf16[224,2688]{1,0:T(8,128)(2,1)S(1)} %collective-permute-done.4.qr1, bf16[224,2688]{1,0:T(8,128)(2,1)} %constant_dynamic-update-slice_fusion.2.c2, ...), custom_call_target="tpu_custom_call" | custom-call | tf_op jit(solution)/shard_map/pallas_call | solution.py:353
  143.1 4.0 %collective-permute-start.15 = (bf16[32,3584]{1,0:T(8,128)(2,1)S(1)}, bf16[32,3584]{1,0:T(8,128)(2,1)S(1)}, u32[]{:S(2)}, u32[]{:S(2)}) collective-permute-start(bf16[32,3584]{1,0:T(8,128)(2,1)S(1)} %slice.93), channel_id=1, source_target_pairs={{0,3},{1,2},{2,1},{3,0},{4,7},{5,6},{6,5},{7,4},{8,11},{9,10},{10,... | collective-permute-start | bytes 688136 | tf_op jit(solution)/shard_map/ppermute | solution.py:42
  152.1 3.4 %collective-permute-start.12 = (bf16[32,3584]{1,0:T(8,128)(2,1)S(1)}, bf16[32,3584]{1,0:T(8,128)(2,1)S(1)}, u32[]{:S(2)}, u32[]{:S(2)}) collective-permute-start(bf16[32,3584]{1,0:T(8,128)(2,1)S(1)} %slice.94), channel_id=1, source_target_pairs={{0,1},{1,0},{2,3},{3,2},{4,5},{5,4},{6,7},{7,6},{8,9},{9,8},{10,11... | collective-permute-start | bytes 688136 | tf_op jit(solution)/shard_map/ppermute | solution.py:42
  155.5 3.6 %collective-permute-done.17 = bf16[32,3584]{1,0:T(8,128)(2,1)S(1)} collective-permute-done((bf16[32,3584]{1,0:T(8,128)(2,1)S(1)}, bf16[32,3584]{1,0:T(8,128)(2,1)S(1)}, u32[]{:S(2)}, u32[]{:S(2)}) %collective-permute-start.17) | collective-permute-done | bytes 229408 | tf_op jit(solution)/shard_map/ppermute | solution.py:42
  159.2 3.1 %collective-permute-start.18 = (bf16[16,7168]{1,0:T(8,128)(2,1)S(1)}, bf16[16,7168]{1,0:T(8,128)(2,1)S(1)}, u32[]{:S(2)}, u32[]{:S(2)}) collective-permute-start(bf16[16,7168]{1,0:T(8,128)(2,1)S(1)} %get-tuple-element.34), channel_id=1, source_target_pairs={{0,20},{1,21},{2,22},{3,23},{4,16},{5,17},{6,18},{7,19},{8,28},{9,... | collective-permute-start | bytes 688136 | tf_op jit(solution)/shard_map/ppermute | solution.py:42
  162.3 3.4 %collective-permute-start.19 = (bf16[16,7168]{1,0:T(8,128)(2,1)S(1)}, bf16[16,7168]{1,0:T(8,128)(2,1)S(1)}, u32[]{:S(2)}, u32[]{:S(2)}) collective-permute-start(bf16[16,7168]{1,0:T(8,128)(2,1)S(1)} %get-tuple-element.33), channel_id=1, source_target_pairs={{0,24},{1,25},{2,26},{3,27},{4,12},{5,13},{6,14},{7,15},{8,0},{9,1... | collective-permute-start | bytes 688136 | tf_op jit(solution)/shard_map/ppermute | solution.py:42
  170.4 7.5 %collective-permute-done.13.rest_1_ = bf16[16,7168]{1,0:T(8,128)(2,1)S(1)} collective-permute-done((bf16[16,7168]{1,0:T(8,128)(2,1)S(1)}, bf16[16,7168]{1,0:T(8,128)(2,1)S(1)}, u32[]{:S(2)}, u32[]{:S(2)}) %collective-permute-start.13) | collective-permute-done | bytes 229408 | tf_op jit(solution)/shard_map/ppermute | solution.py:42
  180.9 9.1 %collective-permute-start.20 = (bf16[24,3584]{1,0:T(8,128)(2,1)S(1)}, bf16[24,3584]{1,0:T(8,128)(2,1)S(1)}, u32[]{:S(2)}, u32[]{:S(2)}) collective-permute-start(bf16[24,3584]{1,0:T(8,128)(2,1)S(1)} %get-tuple-element.30), channel_id=1, source_target_pairs={{0,32},{32,64},{64,96},{96,128},{128,160},{160,192},{192,224},{224... | collective-permute-start | bytes 516104 | tf_op jit(solution)/shard_map/ppermute | solution.py:48
  192.5 4.2 %collective-permute-done.21 = bf16[24,3584]{1,0:T(8,128)(2,1)S(1)} collective-permute-done((bf16[24,3584]{1,0:T(8,128)(2,1)S(1)}, bf16[24,3584]{1,0:T(8,128)(2,1)S(1)}, u32[]{:S(2)}, u32[]{:S(2)}) %collective-permute-start.21) | collective-permute-done | bytes 172064 | tf_op jit(solution)/shard_map/ppermute | solution.py:48
  (90 shorter events, 44.0 us)
Async XLA Ops:
  4.4 81.5 %collective-permute-start.3 = (bf16[7168,128]{1,0:T(8,128)(2,1)}, bf16[7168,128]{1,0:T(8,128)(2,1)S(1)}, u32[]{:S(2)}, u32[]{:S(2)}) collective-permute-start(bf16[7168,128]{1,0:T(8,128)(2,1)} %shard_map.130._), channel_id=1, source_target_pairs={{0,4},{1,5},{2,6},{3,7},{4,0},{5,1},{6,2},{7,3},{8,12},{9,13},{10,... | collective-permute-start | bytes 5505032 | tf_op jit(solution)/shard_map/ppermute | solution.py:42
  12.8 56.7 %collective-permute-start = (bf16[56,2688]{1,0:T(8,128)(2,1)S(1)}, bf16[56,2688]{1,0:T(8,128)(2,1)S(1)}, u32[]{:S(2)}, u32[]{:S(2)}) collective-permute-start(bf16[56,2688]{1,0:T(8,128)(2,1)S(1)} %get-tuple-element.18), channel_id=1, source_target_pairs={{0,8},{1,9},{2,10},{3,11},{4,28},{5,29},{6,30},{7,31},{8,16},{9,17... | collective-permute-start | bytes 903176 | tf_op jit(solution)/shard_map/ppermute | solution.py:42
  18.7 51.0 %collective-permute-start.1 = (bf16[56,2688]{1,0:T(8,128)(2,1)S(1)}, bf16[56,2688]{1,0:T(8,128)(2,1)S(1)}, u32[]{:S(2)}, u32[]{:S(2)}) collective-permute-start(bf16[56,2688]{1,0:T(8,128)(2,1)S(1)} %get-tuple-element.19), channel_id=1, source_target_pairs={{0,20},{1,21},{2,22},{3,23},{4,16},{5,17},{6,18},{7,19},{8,28},{9,... | collective-permute-start | bytes 903176 | tf_op jit(solution)/shard_map/ppermute | solution.py:42
  23.6 22.0 %collective-permute-start.5 = (bf16[56,2688]{1,0:T(8,128)(2,1)S(1)}, bf16[56,2688]{1,0:T(8,128)(2,1)S(1)}, u32[]{:S(2)}, u32[]{:S(2)}) collective-permute-start(bf16[56,2688]{1,0:T(8,128)(2,1)S(1)} %get-tuple-element.21), channel_id=1, source_target_pairs={{0,28},{1,29},{2,30},{3,31},{4,8},{5,9},{6,10},{7,11},{8,4},{9,5},... | collective-permute-start | bytes 903176 | tf_op jit(solution)/shard_map/ppermute | solution.py:42
  45.7 27.9 %collective-permute-start.6 = (bf16[112,2688]{1,0:T(8,128)(2,1)S(1)}, bf16[112,2688]{1,0:T(8,128)(2,1)S(1)}, u32[]{:S(2)}, u32[]{:S(2)}) collective-permute-start(bf16[112,2688]{1,0:T(8,128)(2,1)S(1)} %pad_maximum_fusion), channel_id=1, source_target_pairs={{0,3},{1,2},{2,1},{3,0},{4,7},{5,6},{6,5},{7,4},{8,11},{9,10},{10,... | collective-permute-start | bytes 1806344 | tf_op jit(solution)/shard_map/ppermute | solution.py:42
  69.6 7.1 %copy-start.12 = (bf16[112,2688]{1,0:T(8,128)(2,1)}, bf16[112,2688]{1,0:T(8,128)(2,1)S(1)}, u32[]{:S(2)}) copy-start(bf16[112,2688]{1,0:T(8,128)(2,1)S(1)} %constant_dynamic-update-slice_fusion.half) | copy-start | bytes 1806340
  69.7 15.4 %collective-permute-start.2 = (bf16[112,2688]{1,0:T(8,128)(2,1)S(1)}, bf16[112,2688]{1,0:T(8,128)(2,1)S(1)}, u32[]{:S(2)}, u32[]{:S(2)}) collective-permute-start(bf16[112,2688]{1,0:T(8,128)(2,1)S(1)} %constant_dynamic-update-slice_fusion.half), channel_id=1, source_target_pairs={{0,1},{1,0},{2,3},{3,2},{4,5},{5,4},{6,7},{7,6},{8,9},{9,8},{10,11... | collective-permute-start | bytes 1806344 | tf_op jit(solution)/shard_map/ppermute | solution.py:42
  74.4 41.9 %copy-start.4 = (bf16[1,1,3584,128]{3,2,1,0:T(8,128)(2,1)S(1)}, bf16[1,1,3584,128]{3,2,1,0:T(8,128)(2,1)}, u32[]{:S(2)}) copy-start(bf16[1,1,3584,128]{3,2,1,0:T(8,128)(2,1)} %param.19) | copy-start | bytes 2752516
  74.4 38.6 %collective-permute-start.7 = (bf16[224,2688]{1,0:T(8,128)(2,1)}, bf16[224,2688]{1,0:T(8,128)(2,1)}, u32[]{:S(2)}, u32[]{:S(2)}) collective-permute-start(bf16[224,2688]{1,0:T(8,128)(2,1)} %constant_dynamic-update-slice_fusion.2.c2), channel_id=1, source_target_pairs={{0,1},{1,0},{2,3},{3,2},{4,5},{5,4},{6,7},{7,6},{8,9},{9,8},{10,11... | collective-permute-start | bytes 3612680 | tf_op jit(solution)/shard_map/ppermute | solution.py:42
  89.5 26.8 %collective-permute-start.4 = (bf16[224,2688]{1,0:T(8,128)(2,1)}, bf16[224,2688]{1,0:T(8,128)(2,1)S(1)}, u32[]{:S(2)}, u32[]{:S(2)}) collective-permute-start(bf16[224,2688]{1,0:T(8,128)(2,1)} %shard_map.132.c1), channel_id=1, source_target_pairs={{0,3},{1,2},{2,1},{3,0},{4,7},{5,6},{6,5},{7,4},{8,11},{9,10},{10,... | collective-permute-start | bytes 3612680 | tf_op jit(solution)/shard_map/ppermute | solution.py:42
  93.9 19.1 %collective-permute-start.8 = (bf16[128,3584]{1,0:T(8,128)(2,1)}, bf16[128,3584]{1,0:T(8,128)(2,1)S(1)}, u32[]{:S(2)}, u32[]{:S(2)}) collective-permute-start(bf16[128,3584]{1,0:T(8,128)(2,1)} %bitcast.21), channel_id=1, source_target_pairs={{0,4},{1,5},{2,6},{3,7},{4,0},{5,1},{6,2},{7,3},{8,12},{9,13},{10,... | collective-permute-start | bytes 2752520 | tf_op jit(solution)/shard_map/ppermute | solution.py:42
  125.3 17.7 %collective-permute-start.14 = (bf16[64,3584]{1,0:T(8,128)(2,1)S(1)}, bf16[64,3584]{1,0:T(8,128)(2,1)S(1)}, u32[]{:S(2)}, u32[]{:S(2)}) collective-permute-start(bf16[64,3584]{1,0:T(8,128)(2,1)S(1)} %get-tuple-element.27), channel_id=1, source_target_pairs={{0,1},{1,0},{2,3},{3,2},{4,5},{5,4},{6,7},{7,6},{8,9},{9,8},{10,11... | collective-permute-start | bytes 1376264 | tf_op jit(solution)/shard_map/ppermute | solution.py:42
  127.2 22.6 %collective-permute-start.9 = (bf16[64,3584]{1,0:T(8,128)(2,1)S(1)}, bf16[64,3584]{1,0:T(8,128)(2,1)S(1)}, u32[]{:S(2)}, u32[]{:S(2)}) collective-permute-start(bf16[64,3584]{1,0:T(8,128)(2,1)S(1)} %get-tuple-element.23._), channel_id=1, source_target_pairs={{0,3},{1,2},{2,1},{3,0},{4,7},{5,6},{6,5},{7,4},{8,11},{9,10},{10,... | collective-permute-start | bytes 1376264 | tf_op jit(solution)/shard_map/ppermute | solution.py:42
  137.7 9.4 %collective-permute-start.16 = (bf16[64,3584]{1,0:T(8,128)(2,1)S(1)}, bf16[64,3584]{1,0:T(8,128)(2,1)S(1)}, u32[]{:S(2)}, u32[]{:S(2)}) collective-permute-start(bf16[64,3584]{1,0:T(8,128)(2,1)S(1)} %get-tuple-element.29), channel_id=1, source_target_pairs={{0,1},{1,0},{2,3},{3,2},{4,5},{5,4},{6,7},{7,6},{8,9},{9,8},{10,11... | collective-permute-start | bytes 1376264 | tf_op jit(solution)/shard_map/ppermute | solution.py:42
  140.5 11.5 %collective-permute-start.11 = (bf16[64,3584]{1,0:T(8,128)(2,1)S(1)}, bf16[64,3584]{1,0:T(8,128)(2,1)S(1)}, u32[]{:S(2)}, u32[]{:S(2)}) collective-permute-start(bf16[64,3584]{1,0:T(8,128)(2,1)S(1)} %get-tuple-element.25), channel_id=1, source_target_pairs={{0,3},{1,2},{2,1},{3,0},{4,7},{5,6},{6,5},{7,4},{8,11},{9,10},{10,... | collective-permute-start | bytes 1376264 | tf_op jit(solution)/shard_map/ppermute | solution.py:42
  143.1 12.3 %collective-permute-start.15 = (bf16[32,3584]{1,0:T(8,128)(2,1)S(1)}, bf16[32,3584]{1,0:T(8,128)(2,1)S(1)}, u32[]{:S(2)}, u32[]{:S(2)}) collective-permute-start(bf16[32,3584]{1,0:T(8,128)(2,1)S(1)} %slice.93), channel_id=1, source_target_pairs={{0,3},{1,2},{2,1},{3,0},{4,7},{5,6},{6,5},{7,4},{8,11},{9,10},{10,... | collective-permute-start | bytes 688136 | tf_op jit(solution)/shard_map/ppermute | solution.py:42
  147.2 11.9 %collective-permute-start.17 = (bf16[32,3584]{1,0:T(8,128)(2,1)S(1)}, bf16[32,3584]{1,0:T(8,128)(2,1)S(1)}, u32[]{:S(2)}, u32[]{:S(2)}) collective-permute-start(bf16[32,3584]{1,0:T(8,128)(2,1)S(1)} %slice.92), channel_id=1, source_target_pairs={{0,3},{1,2},{2,1},{3,0},{4,7},{5,6},{6,5},{7,4},{8,11},{9,10},{10,... | collective-permute-start | bytes 688136 | tf_op jit(solution)/shard_map/ppermute | solution.py:42
  150.0 15.7 %collective-permute-start.10 = (bf16[32,3584]{1,0:T(8,128)(2,1)S(1)}, bf16[32,3584]{1,0:T(8,128)(2,1)S(1)}, u32[]{:S(2)}, u32[]{:S(2)}) collective-permute-start(bf16[32,3584]{1,0:T(8,128)(2,1)S(1)} %slice.95), channel_id=1, source_target_pairs={{0,1},{1,0},{2,3},{3,2},{4,5},{5,4},{6,7},{7,6},{8,9},{9,8},{10,11... | collective-permute-start | bytes 688136 | tf_op jit(solution)/shard_map/ppermute | solution.py:42
  152.1 13.7 %collective-permute-start.12 = (bf16[32,3584]{1,0:T(8,128)(2,1)S(1)}, bf16[32,3584]{1,0:T(8,128)(2,1)S(1)}, u32[]{:S(2)}, u32[]{:S(2)}) collective-permute-start(bf16[32,3584]{1,0:T(8,128)(2,1)S(1)} %slice.94), channel_id=1, source_target_pairs={{0,1},{1,0},{2,3},{3,2},{4,5},{5,4},{6,7},{7,6},{8,9},{9,8},{10,11... | collective-permute-start | bytes 688136 | tf_op jit(solution)/shard_map/ppermute | solution.py:42
  159.2 11.2 %collective-permute-start.18 = (bf16[16,7168]{1,0:T(8,128)(2,1)S(1)}, bf16[16,7168]{1,0:T(8,128)(2,1)S(1)}, u32[]{:S(2)}, u32[]{:S(2)}) collective-permute-start(bf16[16,7168]{1,0:T(8,128)(2,1)S(1)} %get-tuple-element.34), channel_id=1, source_target_pairs={{0,20},{1,21},{2,22},{3,23},{4,16},{5,17},{6,18},{7,19},{8,28},{9,... | collective-permute-start | bytes 688136 | tf_op jit(solution)/shard_map/ppermute | solution.py:42
  162.3 8.1 %collective-permute-start.19 = (bf16[16,7168]{1,0:T(8,128)(2,1)S(1)}, bf16[16,7168]{1,0:T(8,128)(2,1)S(1)}, u32[]{:S(2)}, u32[]{:S(2)}) collective-permute-start(bf16[16,7168]{1,0:T(8,128)(2,1)S(1)} %get-tuple-element.33), channel_id=1, source_target_pairs={{0,24},{1,25},{2,26},{3,27},{4,12},{5,13},{6,14},{7,15},{8,0},{9,1... | collective-permute-start | bytes 688136 | tf_op jit(solution)/shard_map/ppermute | solution.py:42
  165.9 12.1 %collective-permute-start.13 = (bf16[16,7168]{1,0:T(8,128)(2,1)S(1)}, bf16[16,7168]{1,0:T(8,128)(2,1)S(1)}, u32[]{:S(2)}, u32[]{:S(2)}) collective-permute-start(bf16[16,7168]{1,0:T(8,128)(2,1)S(1)} %get-tuple-element.35), channel_id=1, source_target_pairs={{0,28},{1,29},{2,30},{3,31},{4,8},{5,9},{6,10},{7,11},{8,4},{9,5},... | collective-permute-start | bytes 688136 | tf_op jit(solution)/shard_map/ppermute | solution.py:42
  180.9 11.6 %collective-permute-start.20 = (bf16[24,3584]{1,0:T(8,128)(2,1)S(1)}, bf16[24,3584]{1,0:T(8,128)(2,1)S(1)}, u32[]{:S(2)}, u32[]{:S(2)}) collective-permute-start(bf16[24,3584]{1,0:T(8,128)(2,1)S(1)} %get-tuple-element.30), channel_id=1, source_target_pairs={{0,32},{32,64},{64,96},{96,128},{128,160},{160,192},{192,224},{224... | collective-permute-start | bytes 516104 | tf_op jit(solution)/shard_map/ppermute | solution.py:48
  190.0 6.7 %collective-permute-start.21 = (bf16[24,3584]{1,0:T(8,128)(2,1)S(1)}, bf16[24,3584]{1,0:T(8,128)(2,1)S(1)}, u32[]{:S(2)}, u32[]{:S(2)}) collective-permute-start(bf16[24,3584]{1,0:T(8,128)(2,1)S(1)} %get-tuple-element.31), channel_id=1, source_target_pairs={{32,0},{64,32},{96,64},{128,96},{160,128},{192,160},{224,192},{256... | collective-permute-start | bytes 516104 | tf_op jit(solution)/shard_map/ppermute | solution.py:48
  (16 other events, 59.2 us)

commit v9 on v7

--- a/solution.py
+++ b/solution.py
@@ -60,12 +60,38 @@
     )
 
 
+def local_copy_call(kernel, outs, n_near, scratch):
+    n_far = 4 if n_near else 3
+    smem = pl.BlockSpec(memory_space=pltpu.SMEM)
+    vmem = pl.BlockSpec(memory_space=pltpu.VMEM)
+    near = ([smem] + [vmem] * (n_near - 1)) if n_near else []
+    return pl.pallas_call(
+        kernel,
+        out_shape=[jax.ShapeDtypeStruct(s, d) for s, d in outs],
+        in_specs=near + [pl.BlockSpec(memory_space=pl.ANY)] * n_far,
+        out_specs=[vmem] * len(outs),
+        scratch_shapes=scratch,
+        compiler_params=pltpu.CompilerParams(vmem_limit_bytes=60 * 1024 * 1024),
+    )
+
+
+def columns(ref):
+    count = ref.shape[1]
+    row = lax.broadcasted_iota(jnp.int32, (count, count), 0)
+    col = lax.broadcasted_iota(jnp.int32, (count, count), 1)
+    values = ref[...].astype(F32)
+    return [
+        jnp.sum(jnp.where(row == col, values[k : k + 1, :], 0.0), axis=1, keepdims=True)
+        for k in range(2)
+    ]
+
+
 def slot_masks(info_ref, route_ref):
-    tokens = route_ref.shape[0]
+    tokens = route_ref.shape[1]
     own, odd = info_ref[0], info_ref[1]
     lanes = lax.broadcasted_iota(jnp.int32, (tokens, 128), 1)
-    route = route_ref[...]
-    named = [(route[:, k : k + 1] == lanes).astype(F32) for k in range(2)]
+    route = [column.astype(jnp.int32) for column in columns(route_ref)]
+    named = [(route[k] == lanes).astype(F32) for k in range(2)]
     row = lax.broadcasted_iota(jnp.int32, (tokens, tokens), 0)
     col = lax.broadcasted_iota(jnp.int32, (tokens, tokens), 1)
     earlier = (col < row).astype(BF16)
@@ -73,7 +99,7 @@
     out = []
     for k in range(2):
         rank = jnp.sum(named[k] * counts, axis=1, keepdims=True).astype(jnp.int32)
-        away = (route[:, k : k + 1] - own) & 3
+        away = (route[k] - own) & 3
         side = jnp.where((away == 3) == (odd == 0), 1, 2)
         rel = jnp.where(away == 0, 0, jnp.where(away == 2, 3, side))
         slots = lax.broadcasted_iota(jnp.int32, (tokens, 4 * SLOT), 1)
@@ -87,12 +113,19 @@
     return values * scale, scale
 
 
-def pack_kernel(info_ref, xa_ref, ra_ref, xb_ref, rb_ref, cot_ref, gain_ref, *outs):
-    width = xa_ref.shape[1]
+def pack_kernel(info_ref, ra_ref, rb_ref, xa, gain_in, xb, cot, *rest):
+    outs, (xa_ref, gain_ref, xb_ref, cot_ref, sems) = rest[:4], rest[4:]
+    width = xa.shape[1]
+    moves = ((xa, xa_ref), (gain_in, gain_ref), (xb, xb_ref), (cot, cot_ref))
+    copies = [pltpu.make_async_copy(*move, sems.at[i]) for i, move in enumerate(moves)]
+    for copy in copies:
+        copy.start()
     places = []
     for route_ref in (ra_ref, rb_ref):
         masks = slot_masks(info_ref, route_ref)
         places.append((masks[0][0] | masks[1][0]).astype(F32).astype(BF16))
+    for copy in copies:
+        copy.wait()
     gain = gain_ref[...]
     normed_a = (normalized(xa_ref[...])[0] * gain).astype(BF16)
     normed_b = (normalized(xb_ref[...])[0] * gain).astype(BF16)
@@ -103,12 +136,17 @@
             outs[j][:, i * width : (i + 1) * width] = packed[j * SLOT : (j + 1) * SLOT]
 
 
-def merge_kernel(wg, wu, wd, out):
+def merge_kernel(wg, wu, wd, out, down, sems):
     width, units = wg.shape
-    out[0:width, :] = wg[...]
-    out[width : 2 * width, :] = wu[...]
+    moves = ((wd, down), (wg, out.at[pl.ds(0, width)]), (wu, out.at[pl.ds(width, width)]))
+    copies = [pltpu.make_async_copy(*move, sems.at[i]) for i, move in enumerate(moves)]
+    for copy in copies:
+        copy.start()
+    copies[0].wait()
     for at in range(0, width, units):
-        out[2 * width + at : 2 * width + at + units, :] = wd[:, at : at + units]
+        out[2 * width + at : 2 * width + at + units, :] = down[:, at : at + units]
+    copies[1].wait()
+    copies[2].wait()
 
 
 def hidden(rows, wg, wu):
@@ -128,7 +166,7 @@
 
 
 def store_parts(part, cols, keep1, send1, keep2, send2):
-    for ref, starts in ((keep1, (128, 192)), (send1, (160, 224)), (keep2, (0, 64)), (send2, (32, 96))):
+    for ref, starts in ((keep1, (128, 160)), (send1, (192, 224)), (keep2, (0, 32)), (send2, (64, 96))):
         for i, start in enumerate(starts):
             ref[32 * i : 32 * (i + 1), cols] = part[start : start + 32].astype(ref.dtype)
 
@@ -204,21 +242,16 @@
 
 
 def mixed_rows(masks, weight_ref, parts):
-    weights = weight_ref[...]
-    spread = jnp.where(masks[0][0], weights[:, 0:1], 0.0) + jnp.where(
-        masks[1][0], weights[:, 1:2], 0.0
-    )
+    weights = columns(weight_ref)
+    spread = jnp.where(masks[0][0], weights[0], 0.0) + jnp.where(masks[1][0], weights[1], 0.0)
     high = spread.astype(BF16)
     rest = spread - high.astype(F32)
     middle = rest.astype(BF16)
     low = (rest - middle.astype(F32)).astype(BF16)
-    total = None
-    for j, part in enumerate(parts):
-        at = slice(j * SLOT, (j + 1) * SLOT)
-        for piece in (high, middle, low):
-            term = jnp.dot(piece[:, at], part, preferred_element_type=F32)
-            total = term if total is None else total + term
-    return total
+    tokens = spread.shape[0]
+    pieces = jnp.concatenate([high, middle, low], axis=0)
+    product = jnp.dot(pieces, jnp.concatenate(parts, axis=0), preferred_element_type=F32)
+    return product[:tokens] + product[tokens : 2 * tokens] + product[2 * tokens :]
 
 
 def last_kernel(
@@ -255,11 +288,11 @@
     got_a, got_b, got_c = hop(a, HOP_A), hop(b, HOP_B), hop(c, HOP_C)
     half1 = jnp.concatenate([got_b, got_c], axis=0)
     half2 = jnp.concatenate([own, got_a], axis=0)
-    p1 = hop(half1, HOP_X1)
-    q2 = hop(half2, HOP_X3)
-    c1 = jnp.concatenate([half1, p1], axis=0)
-    c2 = jnp.concatenate([half2, q2], axis=0)
-    return c1, hop(c1, HOP_X3), c2, hop(c2, HOP_X1)
+    q1 = hop(half1, HOP_X3)
+    p2 = hop(half2, HOP_X1)
+    c1 = jnp.concatenate([half1, q1], axis=0)
+    c2 = jnp.concatenate([half2, p2], axis=0)
+    return c1, hop(c1, HOP_X1), c2, hop(c2, HOP_X3)
 
 
 def return_x(keep1, send1, keep2, send2):
@@ -295,12 +328,22 @@
     info = jnp.stack([index >> 3, (index >> 2) & 1]).astype(jnp.int32)
     weights = (w_gate[0, 0], w_up[0, 0], w_down[0, 0])
     units = w_down.shape[2]
-    (merged,) = kernel_call(merge_kernel, [((3 * width, units), BF16)], 3, info=False)(*weights)
+    (merged,) = local_copy_call(
+        merge_kernel,
+        [((3 * width, units), BF16)],
+        0,
+        [pltpu.VMEM((units, width), BF16), pltpu.SemaphoreType.DMA((3,))],
+    )(*weights)
     other = hop(merged, HOP_W)
     wide = [((SLOT, 3 * width), BF16)] * 4
-    sent = kernel_call(pack_kernel, wide, 6)(
-        info, act_fwd[0], route_fwd[0], act_bwd[0], route_bwd[0], cot_bwd[0], norm_gain
-    )
+    sent = local_copy_call(
+        pack_kernel,
+        wide,
+        3,
+        [pltpu.VMEM((tokens, width), BF16), pltpu.VMEM((1, width), F32)]
+        + [pltpu.VMEM((tokens, width), BF16)] * 2
+        + [pltpu.SemaphoreType.DMA((4,))],
+    )(info, route_fwd[0].T, route_bwd[0].T, act_fwd[0], norm_gain, act_bwd[0], cot_bwd[0])
     rows = spread_rows(*sent)
     outs = [((64, width), F32), ((64, width), BF16)] * 2
     scratch = pltpu.VMEM((256, width), BF16)
@@ -315,11 +358,11 @@
     )(
         info,
         act_fwd[0],
-        route_fwd[0],
-        weight_fwd[0],
+        route_fwd[0].T,
+        weight_fwd[0].T,
         act_bwd[0],
-        route_bwd[0],
-        weight_bwd[0],
+        route_bwd[0].T,
+        weight_bwd[0].T,
         cot_bwd[0],
         norm_gain,
         *back,

time: 177 us -> 174 us (0.983)
  local copies, waits for them, and re-layouts: 10.9 us -> 2.31 us
  Pallas kernels: 9.69 us -> 13.5 us
    unnamed x32, local copies, waits for them, and re-layouts: 8.47 us -> 1.52 us
    pallas_call x2, Pallas kernels: 1.72 us -> 6.87 us  [the longest x1 3.54 us: body(): local_copy_call(pack_kernel, wide, 3, [pltpu.VMEM((tokens, width), BF16),...]
  transfers between devices with their start and end apart: 21 -> 21, of which waited for: 12 -> 11; matrix products, arithmetic and copies ran while one was open for 1% -> 1% of each run, Pallas kernels for 2% -> 4%
where the time goes in v9:
time: 174 us; the launch traced here: 172 us
  starting transfers between devices  84.7 us (49%)
  waiting for transfers between devices  68.5 us (39%)
  Pallas kernels  13.5 us (8%)
  local copies, waits for them, and re-layouts  2.31 us (1%)
    ppermute x19, starting transfers between devices, hop(): return lax.ppermute(value, 'expert', pairs)  77.3 us
    ppermute x19, waiting for transfers between devices, hop(): return lax.ppermute(value, 'expert', pairs)  64.3 us
    ppermute x2, starting transfers between devices, shifted(): return lax.ppermute(value, axis, pairs)  7.44 us
    ppermute x2, waiting for transfers between devices, shifted(): return lax.ppermute(value, axis, pairs)  4.2 us
    pallas_call x1, Pallas kernels, body(): local_copy_call(pack_kernel, wide, 3, [pltpu.VMEM((tokens, width), BF16),...  3.54 us
  transfers between devices with their start and end apart: 21, of which 11 were waited for; matrix products, arithmetic and copies ran while one was open for 1% of the time, Pallas kernels for 4%

profile of v9, /device:TPU:1, one launch (start us, length us, event | category | flops | bytes accessed | tf_op | source)
XLA Modules:
  0.0 171.5 jit_solution(466186993817464344)
XLA Ops:
  1.2 3.5 %shard_map.130 = (bf16[16,10752]{1,0:T(8,128)(2,1)}, bf16[16,10752]{1,0:T(8,128)(2,1)}, bf16[16,10752]{1,0:T(8,128)(2,1)}, bf16[16,10752]{1,0:T(8,128)(2,1)}) custom-call(s32[2]{0:T(128)} %pad_add_fusion.info_ref, s32[2,24]{1,0:T(2,128)} %bitcast.38, s32[2,24]{1,0:T(2,128)} %bitcast.40, bf16[24,3584]{1,0:T(8,128)(2,1)} %bitcast.32, f32[1,3584]{1,0:T(1,128)} %gain_ref.1, ...), custom_call_target="tpu_custom_call" | custom-call | tf_op jit(solution)/shard_map/pallas_call | solution.py:339
  4.8 11.5 %collective-permute-start.4 = (bf16[16,10752]{1,0:T(8,128)(2,1)}, bf16[16,10752]{1,0:T(8,128)(2,1)S(1)}, u32[]{:S(2)}, u32[]{:S(2)}) collective-permute-start(bf16[16,10752]{1,0:T(8,128)(2,1)} %get-tuple-element.21), channel_id=1, source_target_pairs={{0,28},{1,29},{2,30},{3,31},{4,8},{5,9},{6,10},{7,11},{8,4},{9,5},... | collective-permute-start | bytes 1032200 | tf_op jit(solution)/shard_map/ppermute | solution.py:41
  18.2 4.5 %collective-permute-start.1 = (bf16[16,10752]{1,0:T(8,128)(2,1)}, bf16[16,10752]{1,0:T(8,128)(2,1)S(1)}, u32[]{:S(2)}, u32[]{:S(2)}) collective-permute-start(bf16[16,10752]{1,0:T(8,128)(2,1)} %get-tuple-element.19), channel_id=1, source_target_pairs={{0,20},{1,21},{2,22},{3,23},{4,16},{5,17},{6,18},{7,19},{8,28},{9,... | collective-permute-start | bytes 1032200 | tf_op jit(solution)/shard_map/ppermute | solution.py:41
  22.8 3.3 %shard_map.131 = bf16[10752,128]{1,0:T(8,128)(2,1)} custom-call(bf16[3584,128]{1,0:T(8,128)(2,1)} %bitcast.23, bf16[3584,128]{1,0:T(8,128)(2,1)} %bitcast.26, bf16[128,3584]{1,0:T(8,128)(2,1)} %bitcast.29), custom_call_target="tpu_custom_call" | custom-call | tf_op jit(solution)/shard_map/pallas_call | solution.py:331
  28.1 10.0 %collective-permute-done.4 = bf16[16,10752]{1,0:T(8,128)(2,1)S(1)} collective-permute-done((bf16[16,10752]{1,0:T(8,128)(2,1)}, bf16[16,10752]{1,0:T(8,128)(2,1)S(1)}, u32[]{:S(2)}, u32[]{:S(2)}) %collective-permute-start.4) | collective-permute-done | bytes 344096 | tf_op jit(solution)/shard_map/ppermute | solution.py:41
  41.2 4.2 %collective-permute-done.1 = bf16[16,10752]{1,0:T(8,128)(2,1)S(1)} collective-permute-done((bf16[16,10752]{1,0:T(8,128)(2,1)}, bf16[16,10752]{1,0:T(8,128)(2,1)S(1)}, u32[]{:S(2)}, u32[]{:S(2)}) %collective-permute-start.1) | collective-permute-done | bytes 344096 | tf_op jit(solution)/shard_map/ppermute | solution.py:41
  45.5 4.4 %collective-permute-start.2 = (bf16[32,10752]{1,0:T(8,128)(2,1)S(1)}, bf16[32,10752]{1,0:T(8,128)(2,1)S(1)}, u32[]{:S(2)}, u32[]{:S(2)}) collective-permute-start(bf16[32,10752]{1,0:T(8,128)(2,1)S(1)} %pad_maximum_fusion), channel_id=1, source_target_pairs={{0,3},{1,2},{2,1},{3,0},{4,7},{5,6},{6,5},{7,4},{8,11},{9,10},{10,... | collective-permute-start | bytes 2064392 | tf_op jit(solution)/shard_map/ppermute | solution.py:41
  50.0 4.2 %collective-permute-done.5 = bf16[32,10752]{1,0:T(8,128)(2,1)S(1)} collective-permute-done((bf16[32,10752]{1,0:T(8,128)(2,1)S(1)}, bf16[32,10752]{1,0:T(8,128)(2,1)S(1)}, u32[]{:S(2)}, u32[]{:S(2)}) %collective-permute-start.5) | collective-permute-done | bytes 688160 | tf_op jit(solution)/shard_map/ppermute | solution.py:41
  54.3 4.4 %collective-permute-start.6 = (bf16[64,10752]{1,0:T(8,128)(2,1)S(1)}, bf16[64,10752]{1,0:T(8,128)(2,1)S(1)}, u32[]{:S(2)}, u32[]{:S(2)}) collective-permute-start(bf16[64,10752]{1,0:T(8,128)(2,1)S(1)} %constant_dynamic-update-slice_fusion.3.c2), channel_id=1, source_target_pairs={{0,3},{1,2},{2,1},{3,0},{4,7},{5,6},{6,5},{7,4},{8,11},{9,10},{10,... | collective-permute-start | bytes 4128776 | tf_op jit(solution)/shard_map/ppermute | solution.py:41
  58.7 5.3 %collective-permute-done.2 = bf16[32,10752]{1,0:T(8,128)(2,1)S(1)} collective-permute-done((bf16[32,10752]{1,0:T(8,128)(2,1)S(1)}, bf16[32,10752]{1,0:T(8,128)(2,1)S(1)}, u32[]{:S(2)}, u32[]{:S(2)}) %collective-permute-start.2) | collective-permute-done | bytes 688160 | tf_op jit(solution)/shard_map/ppermute | solution.py:41
  66.0 27.5 %collective-permute-done.6.pr2 = bf16[64,10752]{1,0:T(8,128)(2,1)S(1)} collective-permute-done((bf16[64,10752]{1,0:T(8,128)(2,1)S(1)}, bf16[64,10752]{1,0:T(8,128)(2,1)S(1)}, u32[]{:S(2)}, u32[]{:S(2)}) %collective-permute-start.6) | collective-permute-done | bytes 1376288 | tf_op jit(solution)/shard_map/ppermute | solution.py:41
  95.8 3.1 %collective-permute-start.13 = (bf16[64,3584]{1,0:T(8,128)(2,1)S(1)}, bf16[64,3584]{1,0:T(8,128)(2,1)S(1)}, u32[]{:S(2)}, u32[]{:S(2)}) collective-permute-start(bf16[64,3584]{1,0:T(8,128)(2,1)S(1)} %get-tuple-element.27), channel_id=1, source_target_pairs={{0,1},{1,0},{2,3},{3,2},{4,5},{5,4},{6,7},{7,6},{8,9},{9,8},{10,11... | collective-permute-start | bytes 1376264 | tf_op jit(solution)/shard_map/ppermute | solution.py:41
  99.0 3.7 %collective-permute-start.8 = (bf16[64,3584]{1,0:T(8,128)(2,1)S(1)}, bf16[64,3584]{1,0:T(8,128)(2,1)S(1)}, u32[]{:S(2)}, u32[]{:S(2)}) collective-permute-start(bf16[64,3584]{1,0:T(8,128)(2,1)S(1)} %get-tuple-element.23._), channel_id=1, source_target_pairs={{0,3},{1,2},{2,1},{3,0},{4,7},{5,6},{6,5},{7,4},{8,11},{9,10},{10,... | collective-permute-start | bytes 1376264 | tf_op jit(solution)/shard_map/ppermute | solution.py:41
  102.7 3.3 %shard_map.133 = (f32[64,3584]{1,0:T(8,128)S(1)}, bf16[64,3584]{1,0:T(8,128)(2,1)S(1)}, f32[64,3584]{1,0:T(8,128)S(1)}, bf16[64,3584]{1,0:T(8,128)(2,1)S(1)}) custom-call(bf16[64,10752]{1,0:T(8,128)(2,1)S(1)} %constant_dynamic-update-slice_fusion.c1, bf16[64,10752]{1,0:T(8,128)(2,1)S(1)} %collective-permute-done.3.qr1, ...), custom_call_target="tpu_custom_call" | custom-call | tf_op jit(solution)/shard_map/pallas_call | solution.py:351
  110.9 4.0 %collective-permute-start.14 = (bf16[32,3584]{1,0:T(8,128)(2,1)S(1)}, bf16[32,3584]{1,0:T(8,128)(2,1)S(1)}, u32[]{:S(2)}, u32[]{:S(2)}) collective-permute-start(bf16[32,3584]{1,0:T(8,128)(2,1)S(1)} %slice.93), channel_id=1, source_target_pairs={{0,3},{1,2},{2,1},{3,0},{4,7},{5,6},{6,5},{7,4},{8,11},{9,10},{10,... | collective-permute-start | bytes 688136 | tf_op jit(solution)/shard_map/ppermute | solution.py:41
  115.4 6.1 %collective-permute-start.16 = (bf16[32,3584]{1,0:T(8,128)(2,1)S(1)}, bf16[32,3584]{1,0:T(8,128)(2,1)S(1)}, u32[]{:S(2)}, u32[]{:S(2)}) collective-permute-start(bf16[32,3584]{1,0:T(8,128)(2,1)S(1)} %slice.92), channel_id=1, source_target_pairs={{0,3},{1,2},{2,1},{3,0},{4,7},{5,6},{6,5},{7,4},{8,11},{9,10},{10,... | collective-permute-start | bytes 688136 | tf_op jit(solution)/shard_map/ppermute | solution.py:41
  123.7 3.4 %collective-permute-start.11 = (bf16[32,3584]{1,0:T(8,128)(2,1)S(1)}, bf16[32,3584]{1,0:T(8,128)(2,1)S(1)}, u32[]{:S(2)}, u32[]{:S(2)}) collective-permute-start(bf16[32,3584]{1,0:T(8,128)(2,1)S(1)} %slice.94), channel_id=1, source_target_pairs={{0,1},{1,0},{2,3},{3,2},{4,5},{5,4},{6,7},{7,6},{8,9},{9,8},{10,11... | collective-permute-start | bytes 688136 | tf_op jit(solution)/shard_map/ppermute | solution.py:41
  129.1 6.2 %collective-permute-start.17 = (bf16[16,7168]{1,0:T(8,128)(2,1)S(1)}, bf16[16,7168]{1,0:T(8,128)(2,1)S(1)}, u32[]{:S(2)}, u32[]{:S(2)}) collective-permute-start(bf16[16,7168]{1,0:T(8,128)(2,1)S(1)} %get-tuple-element.34), channel_id=1, source_target_pairs={{0,20},{1,21},{2,22},{3,23},{4,16},{5,17},{6,18},{7,19},{8,28},{9,... | collective-permute-start | bytes 688136 | tf_op jit(solution)/shard_map/ppermute | solution.py:41
  135.4 5.4 %collective-permute-start.18 = (bf16[16,7168]{1,0:T(8,128)(2,1)S(1)}, bf16[16,7168]{1,0:T(8,128)(2,1)S(1)}, u32[]{:S(2)}, u32[]{:S(2)}) collective-permute-start(bf16[16,7168]{1,0:T(8,128)(2,1)S(1)} %get-tuple-element.33), channel_id=1, source_target_pairs={{0,24},{1,25},{2,26},{3,27},{4,12},{5,13},{6,14},{7,15},{8,0},{9,1... | collective-permute-start | bytes 688136 | tf_op jit(solution)/shard_map/ppermute | solution.py:41
  141.0 5.0 %collective-permute-start.12 = (bf16[16,7168]{1,0:T(8,128)(2,1)S(1)}, bf16[16,7168]{1,0:T(8,128)(2,1)S(1)}, u32[]{:S(2)}, u32[]{:S(2)}) collective-permute-start(bf16[16,7168]{1,0:T(8,128)(2,1)S(1)} %get-tuple-element.35), channel_id=1, source_target_pairs={{0,28},{1,29},{2,30},{3,31},{4,8},{5,9},{6,10},{7,11},{8,4},{9,5},... | collective-permute-start | bytes 688136 | tf_op jit(solution)/shard_map/ppermute | solution.py:41
  146.0 3.3 %collective-permute-done.18.rest_3_ = bf16[16,7168]{1,0:T(8,128)(2,1)S(1)} collective-permute-done((bf16[16,7168]{1,0:T(8,128)(2,1)S(1)}, bf16[16,7168]{1,0:T(8,128)(2,1)S(1)}, u32[]{:S(2)}, u32[]{:S(2)}) %collective-permute-start.18) | collective-permute-done | bytes 229408 | tf_op jit(solution)/shard_map/ppermute | solution.py:41
  149.3 6.9 %collective-permute-done.12.rest_1_ = bf16[16,7168]{1,0:T(8,128)(2,1)S(1)} collective-permute-done((bf16[16,7168]{1,0:T(8,128)(2,1)S(1)}, bf16[16,7168]{1,0:T(8,128)(2,1)S(1)}, u32[]{:S(2)}, u32[]{:S(2)}) %collective-permute-start.12) | collective-permute-done | bytes 229408 | tf_op jit(solution)/shard_map/ppermute | solution.py:41
  157.9 5.5 %collective-permute-start.19 = (bf16[24,3584]{1,0:T(8,128)(2,1)S(1)}, bf16[24,3584]{1,0:T(8,128)(2,1)S(1)}, u32[]{:S(2)}, u32[]{:S(2)}) collective-permute-start(bf16[24,3584]{1,0:T(8,128)(2,1)S(1)} %get-tuple-element.30), channel_id=1, source_target_pairs={{0,32},{32,64},{64,96},{96,128},{128,160},{160,192},{192,224},{224... | collective-permute-start | bytes 516104 | tf_op jit(solution)/shard_map/ppermute | solution.py:47
  166.0 4.2 %collective-permute-done.20 = bf16[24,3584]{1,0:T(8,128)(2,1)S(1)} collective-permute-done((bf16[24,3584]{1,0:T(8,128)(2,1)S(1)}, bf16[24,3584]{1,0:T(8,128)(2,1)S(1)}, u32[]{:S(2)}, u32[]{:S(2)}) %collective-permute-start.20) | collective-permute-done | bytes 172064 | tf_op jit(solution)/shard_map/ppermute | solution.py:47
  (75 shorter events, 27.2 us)
Async XLA Ops:
  4.8 33.3 %collective-permute-start.4 = (bf16[16,10752]{1,0:T(8,128)(2,1)}, bf16[16,10752]{1,0:T(8,128)(2,1)S(1)}, u32[]{:S(2)}, u32[]{:S(2)}) collective-permute-start(bf16[16,10752]{1,0:T(8,128)(2,1)} %get-tuple-element.21), channel_id=1, source_target_pairs={{0,28},{1,29},{2,30},{3,31},{4,8},{5,9},{6,10},{7,11},{8,4},{9,5},... | collective-permute-start | bytes 1032200 | tf_op jit(solution)/shard_map/ppermute | solution.py:41
  16.3 24.9 %collective-permute-start = (bf16[16,10752]{1,0:T(8,128)(2,1)}, bf16[16,10752]{1,0:T(8,128)(2,1)S(1)}, u32[]{:S(2)}, u32[]{:S(2)}) collective-permute-start(bf16[16,10752]{1,0:T(8,128)(2,1)} %get-tuple-element.18), channel_id=1, source_target_pairs={{0,8},{1,9},{2,10},{3,11},{4,28},{5,29},{6,30},{7,31},{8,16},{9,17... | collective-permute-start | bytes 1032200 | tf_op jit(solution)/shard_map/ppermute | solution.py:41
  18.2 27.3 %collective-permute-start.1 = (bf16[16,10752]{1,0:T(8,128)(2,1)}, bf16[16,10752]{1,0:T(8,128)(2,1)S(1)}, u32[]{:S(2)}, u32[]{:S(2)}) collective-permute-start(bf16[16,10752]{1,0:T(8,128)(2,1)} %get-tuple-element.19), channel_id=1, source_target_pairs={{0,20},{1,21},{2,22},{3,23},{4,16},{5,17},{6,18},{7,19},{8,28},{9,... | collective-permute-start | bytes 1032200 | tf_op jit(solution)/shard_map/ppermute | solution.py:41
  26.1 68.0 %collective-permute-start.7 = (bf16[10752,128]{1,0:T(8,128)(2,1)}, bf16[10752,128]{1,0:T(8,128)(2,1)S(1)}, u32[]{:S(2)}, u32[]{:S(2)}) collective-permute-start(bf16[10752,128]{1,0:T(8,128)(2,1)} %shard_map.131), channel_id=1, source_target_pairs={{0,4},{1,5},{2,6},{3,7},{4,0},{5,1},{6,2},{7,3},{8,12},{9,13},{10,... | collective-permute-start | bytes 8257544 | tf_op jit(solution)/shard_map/ppermute | solution.py:41
  38.1 16.1 %collective-permute-start.5 = (bf16[32,10752]{1,0:T(8,128)(2,1)S(1)}, bf16[32,10752]{1,0:T(8,128)(2,1)S(1)}, u32[]{:S(2)}, u32[]{:S(2)}) collective-permute-start(bf16[32,10752]{1,0:T(8,128)(2,1)S(1)} %pad_maximum_fusion.1), channel_id=1, source_target_pairs={{0,1},{1,0},{2,3},{3,2},{4,5},{5,4},{6,7},{7,6},{8,9},{9,8},{10,11... | collective-permute-start | bytes 2064392 | tf_op jit(solution)/shard_map/ppermute | solution.py:41
  45.5 18.5 %collective-permute-start.2 = (bf16[32,10752]{1,0:T(8,128)(2,1)S(1)}, bf16[32,10752]{1,0:T(8,128)(2,1)S(1)}, u32[]{:S(2)}, u32[]{:S(2)}) collective-permute-start(bf16[32,10752]{1,0:T(8,128)(2,1)S(1)} %pad_maximum_fusion), channel_id=1, source_target_pairs={{0,3},{1,2},{2,1},{3,0},{4,7},{5,6},{6,5},{7,4},{8,11},{9,10},{10,... | collective-permute-start | bytes 2064392 | tf_op jit(solution)/shard_map/ppermute | solution.py:41
  50.0 44.1 %copy-start = (bf16[1,1,3584,128]{3,2,1,0:T(8,128)(2,1)S(1)}, bf16[1,1,3584,128]{3,2,1,0:T(8,128)(2,1)}, u32[]{:S(2)}) copy-start(bf16[1,1,3584,128]{3,2,1,0:T(8,128)(2,1)} %param.19) | copy-start | bytes 2752516
  50.0 44.1 %copy-start.1 = (bf16[1,1,3584,128]{3,2,1,0:T(8,128)(2,1)S(1)}, bf16[1,1,3584,128]{3,2,1,0:T(8,128)(2,1)}, u32[]{:S(2)}) copy-start(bf16[1,1,3584,128]{3,2,1,0:T(8,128)(2,1)} %param.20) | copy-start | bytes 2752516
  50.0 44.1 %copy-start.2 = (bf16[1,1,128,3584]{3,2,1,0:T(8,128)(2,1)S(1)}, bf16[1,1,128,3584]{3,2,1,0:T(8,128)(2,1)}, u32[]{:S(2)}) copy-start(bf16[1,1,128,3584]{3,2,1,0:T(8,128)(2,1)} %param.21) | copy-start | bytes 2752516
  54.3 39.2 %collective-permute-start.6 = (bf16[64,10752]{1,0:T(8,128)(2,1)S(1)}, bf16[64,10752]{1,0:T(8,128)(2,1)S(1)}, u32[]{:S(2)}, u32[]{:S(2)}) collective-permute-start(bf16[64,10752]{1,0:T(8,128)(2,1)S(1)} %constant_dynamic-update-slice_fusion.3.c2), channel_id=1, source_target_pairs={{0,3},{1,2},{2,1},{3,0},{4,7},{5,6},{6,5},{7,4},{8,11},{9,10},{10,... | collective-permute-start | bytes 4128776 | tf_op jit(solution)/shard_map/ppermute | solution.py:41
  64.0 29.4 %collective-permute-start.3 = (bf16[64,10752]{1,0:T(8,128)(2,1)S(1)}, bf16[64,10752]{1,0:T(8,128)(2,1)S(1)}, u32[]{:S(2)}, u32[]{:S(2)}) collective-permute-start(bf16[64,10752]{1,0:T(8,128)(2,1)S(1)} %constant_dynamic-update-slice_fusion.c1), channel_id=1, source_target_pairs={{0,1},{1,0},{2,3},{3,2},{4,5},{5,4},{6,7},{7,6},{8,9},{9,8},{10,11... | collective-permute-start | bytes 4128776 | tf_op jit(solution)/shard_map/ppermute | solution.py:41
  95.8 15.0 %collective-permute-start.13 = (bf16[64,3584]{1,0:T(8,128)(2,1)S(1)}, bf16[64,3584]{1,0:T(8,128)(2,1)S(1)}, u32[]{:S(2)}, u32[]{:S(2)}) collective-permute-start(bf16[64,3584]{1,0:T(8,128)(2,1)S(1)} %get-tuple-element.27), channel_id=1, source_target_pairs={{0,1},{1,0},{2,3},{3,2},{4,5},{5,4},{6,7},{7,6},{8,9},{9,8},{10,11... | collective-permute-start | bytes 1376264 | tf_op jit(solution)/shard_map/ppermute | solution.py:41
  99.0 22.6 %collective-permute-start.8 = (bf16[64,3584]{1,0:T(8,128)(2,1)S(1)}, bf16[64,3584]{1,0:T(8,128)(2,1)S(1)}, u32[]{:S(2)}, u32[]{:S(2)}) collective-permute-start(bf16[64,3584]{1,0:T(8,128)(2,1)S(1)} %get-tuple-element.23._), channel_id=1, source_target_pairs={{0,3},{1,2},{2,1},{3,0},{4,7},{5,6},{6,5},{7,4},{8,11},{9,10},{10,... | collective-permute-start | bytes 1376264 | tf_op jit(solution)/shard_map/ppermute | solution.py:41
  106.0 9.2 %collective-permute-start.15 = (bf16[64,3584]{1,0:T(8,128)(2,1)S(1)}, bf16[64,3584]{1,0:T(8,128)(2,1)S(1)}, u32[]{:S(2)}, u32[]{:S(2)}) collective-permute-start(bf16[64,3584]{1,0:T(8,128)(2,1)S(1)} %get-tuple-element.29), channel_id=1, source_target_pairs={{0,1},{1,0},{2,3},{3,2},{4,5},{5,4},{6,7},{7,6},{8,9},{9,8},{10,11... | collective-permute-start | bytes 1376264 | tf_op jit(solution)/shard_map/ppermute | solution.py:41
  108.3 15.3 %collective-permute-start.10 = (bf16[64,3584]{1,0:T(8,128)(2,1)S(1)}, bf16[64,3584]{1,0:T(8,128)(2,1)S(1)}, u32[]{:S(2)}, u32[]{:S(2)}) collective-permute-start(bf16[64,3584]{1,0:T(8,128)(2,1)S(1)} %get-tuple-element.25), channel_id=1, source_target_pairs={{0,3},{1,2},{2,1},{3,0},{4,7},{5,6},{6,5},{7,4},{8,11},{9,10},{10,... | collective-permute-start | bytes 1376264 | tf_op jit(solution)/shard_map/ppermute | solution.py:41
  110.9 16.2 %collective-permute-start.14 = (bf16[32,3584]{1,0:T(8,128)(2,1)S(1)}, bf16[32,3584]{1,0:T(8,128)(2,1)S(1)}, u32[]{:S(2)}, u32[]{:S(2)}) collective-permute-start(bf16[32,3584]{1,0:T(8,128)(2,1)S(1)} %slice.93), channel_id=1, source_target_pairs={{0,3},{1,2},{2,1},{3,0},{4,7},{5,6},{6,5},{7,4},{8,11},{9,10},{10,... | collective-permute-start | bytes 688136 | tf_op jit(solution)/shard_map/ppermute | solution.py:41
  115.4 13.6 %collective-permute-start.16 = (bf16[32,3584]{1,0:T(8,128)(2,1)S(1)}, bf16[32,3584]{1,0:T(8,128)(2,1)S(1)}, u32[]{:S(2)}, u32[]{:S(2)}) collective-permute-start(bf16[32,3584]{1,0:T(8,128)(2,1)S(1)} %slice.92), channel_id=1, source_target_pairs={{0,3},{1,2},{2,1},{3,0},{4,7},{5,6},{6,5},{7,4},{8,11},{9,10},{10,... | collective-permute-start | bytes 688136 | tf_op jit(solution)/shard_map/ppermute | solution.py:41
  121.7 19.2 %collective-permute-start.9 = (bf16[32,3584]{1,0:T(8,128)(2,1)S(1)}, bf16[32,3584]{1,0:T(8,128)(2,1)S(1)}, u32[]{:S(2)}, u32[]{:S(2)}) collective-permute-start(bf16[32,3584]{1,0:T(8,128)(2,1)S(1)} %slice.95), channel_id=1, source_target_pairs={{0,1},{1,0},{2,3},{3,2},{4,5},{5,4},{6,7},{7,6},{8,9},{9,8},{10,11... | collective-permute-start | bytes 688136 | tf_op jit(solution)/shard_map/ppermute | solution.py:41
  123.7 17.2 %collective-permute-start.11 = (bf16[32,3584]{1,0:T(8,128)(2,1)S(1)}, bf16[32,3584]{1,0:T(8,128)(2,1)S(1)}, u32[]{:S(2)}, u32[]{:S(2)}) collective-permute-start(bf16[32,3584]{1,0:T(8,128)(2,1)S(1)} %slice.94), channel_id=1, source_target_pairs={{0,1},{1,0},{2,3},{3,2},{4,5},{5,4},{6,7},{7,6},{8,9},{9,8},{10,11... | collective-permute-start | bytes 688136 | tf_op jit(solution)/shard_map/ppermute | solution.py:41
  129.1 16.9 %collective-permute-start.17 = (bf16[16,7168]{1,0:T(8,128)(2,1)S(1)}, bf16[16,7168]{1,0:T(8,128)(2,1)S(1)}, u32[]{:S(2)}, u32[]{:S(2)}) collective-permute-start(bf16[16,7168]{1,0:T(8,128)(2,1)S(1)} %get-tuple-element.34), channel_id=1, source_target_pairs={{0,20},{1,21},{2,22},{3,23},{4,16},{5,17},{6,18},{7,19},{8,28},{9,... | collective-permute-start | bytes 688136 | tf_op jit(solution)/shard_map/ppermute | solution.py:41
  135.4 13.9 %collective-permute-start.18 = (bf16[16,7168]{1,0:T(8,128)(2,1)S(1)}, bf16[16,7168]{1,0:T(8,128)(2,1)S(1)}, u32[]{:S(2)}, u32[]{:S(2)}) collective-permute-start(bf16[16,7168]{1,0:T(8,128)(2,1)S(1)} %get-tuple-element.33), channel_id=1, source_target_pairs={{0,24},{1,25},{2,26},{3,27},{4,12},{5,13},{6,14},{7,15},{8,0},{9,1... | collective-permute-start | bytes 688136 | tf_op jit(solution)/shard_map/ppermute | solution.py:41
  141.0 15.2 %collective-permute-start.12 = (bf16[16,7168]{1,0:T(8,128)(2,1)S(1)}, bf16[16,7168]{1,0:T(8,128)(2,1)S(1)}, u32[]{:S(2)}, u32[]{:S(2)}) collective-permute-start(bf16[16,7168]{1,0:T(8,128)(2,1)S(1)} %get-tuple-element.35), channel_id=1, source_target_pairs={{0,28},{1,29},{2,30},{3,31},{4,8},{5,9},{6,10},{7,11},{8,4},{9,5},... | collective-permute-start | bytes 688136 | tf_op jit(solution)/shard_map/ppermute | solution.py:41
  157.9 8.1 %collective-permute-start.19 = (bf16[24,3584]{1,0:T(8,128)(2,1)S(1)}, bf16[24,3584]{1,0:T(8,128)(2,1)S(1)}, u32[]{:S(2)}, u32[]{:S(2)}) collective-permute-start(bf16[24,3584]{1,0:T(8,128)(2,1)S(1)} %get-tuple-element.30), channel_id=1, source_target_pairs={{0,32},{32,64},{64,96},{96,128},{128,160},{160,192},{192,224},{224... | collective-permute-start | bytes 516104 | tf_op jit(solution)/shard_map/ppermute | solution.py:47
  163.5 6.7 %collective-permute-start.20 = (bf16[24,3584]{1,0:T(8,128)(2,1)S(1)}, bf16[24,3584]{1,0:T(8,128)(2,1)S(1)}, u32[]{:S(2)}, u32[]{:S(2)}) collective-permute-start(bf16[24,3584]{1,0:T(8,128)(2,1)S(1)} %get-tuple-element.31), channel_id=1, source_target_pairs={{32,0},{64,32},{96,64},{128,96},{160,128},{192,160},{224,192},{256... | collective-permute-start | bytes 516104 | tf_op jit(solution)/shard_map/ppermute | solution.py:47
  (10 other events, 193.3 us)

commit v10 on v9

--- a/solution.py
+++ b/solution.py
@@ -166,9 +166,16 @@
 
 
 def store_parts(part, cols, keep1, send1, keep2, send2):
-    for ref, starts in ((keep1, (128, 160)), (send1, (192, 224)), (keep2, (0, 32)), (send2, (64, 96))):
+    places = (
+        (keep1, (128, 0, 160, 64)),
+        (send1, (192, 32, 224, 96)),
+        (keep2, (144, 16, 208, 48)),
+        (send2, (176, 80, 240, 112)),
+    )
+    for ref, starts in places:
         for i, start in enumerate(starts):
-            ref[32 * i : 32 * (i + 1), cols] = part[start : start + 32].astype(ref.dtype)
+            rows = slice(SLOT * i, SLOT * (i + 1))
+            ref[rows, cols] = part[start : start + SLOT].astype(ref.dtype)
 
 
 def fwd_kernel(c1, qr1, c2, pr2, wg, wu, wd, other, keep1, send1, keep2, send2, rows):
@@ -304,9 +311,9 @@
 
 
 def return_z(full1, full2):
+    back_a = hop(full2[:SLOT], HOP_A)
     back_c = hop(full2[SLOT:], HOP_C)
-    back_b = hop(full2[:SLOT], HOP_B_BACK)
-    back_a = hop(full1[SLOT:], HOP_A)
+    back_b = hop(full1[SLOT:], HOP_B_BACK)
     return full1[:SLOT], back_a, back_c, back_b
 
 

time: 174 us -> 173 us (level)
  the two profiles are of different devices: /device:TPU:1 before, /device:TPU:31 now
where the time goes in v10:
time: 173 us; the launch traced here: 172 us
  waiting for transfers between devices  79.4 us (46%)
  starting transfers between devices  74.3 us (43%)
  Pallas kernels  13.5 us (8%)
  local copies, waits for them, and re-layouts  2.31 us (1%)
    ppermute x19, waiting for transfers between devices, hop(): return lax.ppermute(value, 'expert', pairs)  74 us
    ppermute x19, starting transfers between devices, hop(): return lax.ppermute(value, 'expert', pairs)  64.2 us
    ppermute x2, starting transfers between devices, shifted(): return lax.ppermute(value, axis, pairs)  10.2 us
    ppermute x2, waiting for transfers between devices, shifted(): return lax.ppermute(value, axis, pairs)  5.41 us
    pallas_call x1, Pallas kernels, body(): local_copy_call(pack_kernel, wide, 3, [pltpu.VMEM((tokens, width), BF16),...  3.54 us
  transfers between devices with their start and end apart: 21, of which 12 were waited for; matrix products, arithmetic and copies ran while one was open for 1% of the time, Pallas kernels for 4%

profile of v10, /device:TPU:31, one launch (start us, length us, event | category | flops | bytes accessed | tf_op | source)
XLA Modules:
  0.0 172.0 jit_solution(15618859708529142499)
XLA Ops:
  1.2 3.5 %shard_map.130 = (bf16[16,10752]{1,0:T(8,128)(2,1)}, bf16[16,10752]{1,0:T(8,128)(2,1)}, bf16[16,10752]{1,0:T(8,128)(2,1)}, bf16[16,10752]{1,0:T(8,128)(2,1)}) custom-call(s32[2]{0:T(128)} %pad_add_fusion.info_ref, s32[2,24]{1,0:T(2,128)} %bitcast.38, s32[2,24]{1,0:T(2,128)} %bitcast.40, bf16[24,3584]{1,0:T(8,128)(2,1)} %bitcast.32, f32[1,3584]{1,0:T(1,128)} %gain_ref.1, ...), custom_call_target="tpu_custom_call" | custom-call | tf_op jit(solution)/shard_map/pallas_call | solution.py:346
  4.8 10.7 %collective-permute-start.4 = (bf16[16,10752]{1,0:T(8,128)(2,1)}, bf16[16,10752]{1,0:T(8,128)(2,1)S(1)}, u32[]{:S(2)}, u32[]{:S(2)}) collective-permute-start(bf16[16,10752]{1,0:T(8,128)(2,1)} %get-tuple-element.21), channel_id=1, source_target_pairs={{0,28},{1,29},{2,30},{3,31},{4,8},{5,9},{6,10},{7,11},{8,4},{9,5},... | collective-permute-start | bytes 1032200 | tf_op jit(solution)/shard_map/ppermute | solution.py:41
  17.4 4.5 %collective-permute-start.1 = (bf16[16,10752]{1,0:T(8,128)(2,1)}, bf16[16,10752]{1,0:T(8,128)(2,1)S(1)}, u32[]{:S(2)}, u32[]{:S(2)}) collective-permute-start(bf16[16,10752]{1,0:T(8,128)(2,1)} %get-tuple-element.19), channel_id=1, source_target_pairs={{0,20},{1,21},{2,22},{3,23},{4,16},{5,17},{6,18},{7,19},{8,28},{9,... | collective-permute-start | bytes 1032200 | tf_op jit(solution)/shard_map/ppermute | solution.py:41
  21.9 3.3 %shard_map.131 = bf16[10752,128]{1,0:T(8,128)(2,1)} custom-call(bf16[3584,128]{1,0:T(8,128)(2,1)} %bitcast.23, bf16[3584,128]{1,0:T(8,128)(2,1)} %bitcast.26, bf16[128,3584]{1,0:T(8,128)(2,1)} %bitcast.29), custom_call_target="tpu_custom_call" | custom-call | tf_op jit(solution)/shard_map/pallas_call | solution.py:338
  27.2 10.0 %collective-permute-done.4 = bf16[16,10752]{1,0:T(8,128)(2,1)S(1)} collective-permute-done((bf16[16,10752]{1,0:T(8,128)(2,1)}, bf16[16,10752]{1,0:T(8,128)(2,1)S(1)}, u32[]{:S(2)}, u32[]{:S(2)}) %collective-permute-start.4) | collective-permute-done | bytes 344096 | tf_op jit(solution)/shard_map/ppermute | solution.py:41
  37.2 2.5 %collective-permute-start.5 = (bf16[32,10752]{1,0:T(8,128)(2,1)S(1)}, bf16[32,10752]{1,0:T(8,128)(2,1)S(1)}, u32[]{:S(2)}, u32[]{:S(2)}) collective-permute-start(bf16[32,10752]{1,0:T(8,128)(2,1)S(1)} %pad_maximum_fusion.1), channel_id=1, source_target_pairs={{0,1},{1,0},{2,3},{3,2},{4,5},{5,4},{6,7},{7,6},{8,9},{9,8},{10,11... | collective-permute-start | bytes 2064392 | tf_op jit(solution)/shard_map/ppermute | solution.py:41
  39.7 4.9 %collective-permute-done.1 = bf16[16,10752]{1,0:T(8,128)(2,1)S(1)} collective-permute-done((bf16[16,10752]{1,0:T(8,128)(2,1)}, bf16[16,10752]{1,0:T(8,128)(2,1)S(1)}, u32[]{:S(2)}, u32[]{:S(2)}) %collective-permute-start.1) | collective-permute-done | bytes 344096 | tf_op jit(solution)/shard_map/ppermute | solution.py:41
  46.9 6.4 %collective-permute-done.5 = bf16[32,10752]{1,0:T(8,128)(2,1)S(1)} collective-permute-done((bf16[32,10752]{1,0:T(8,128)(2,1)S(1)}, bf16[32,10752]{1,0:T(8,128)(2,1)S(1)}, u32[]{:S(2)}, u32[]{:S(2)}) %collective-permute-start.5) | collective-permute-done | bytes 688160 | tf_op jit(solution)/shard_map/ppermute | solution.py:41
  55.5 7.6 %collective-permute-done.2 = bf16[32,10752]{1,0:T(8,128)(2,1)S(1)} collective-permute-done((bf16[32,10752]{1,0:T(8,128)(2,1)S(1)}, bf16[32,10752]{1,0:T(8,128)(2,1)S(1)}, u32[]{:S(2)}, u32[]{:S(2)}) %collective-permute-start.2) | collective-permute-done | bytes 688160 | tf_op jit(solution)/shard_map/ppermute | solution.py:41
  65.1 27.5 %collective-permute-done.6.pr2 = bf16[64,10752]{1,0:T(8,128)(2,1)S(1)} collective-permute-done((bf16[64,10752]{1,0:T(8,128)(2,1)S(1)}, bf16[64,10752]{1,0:T(8,128)(2,1)S(1)}, u32[]{:S(2)}, u32[]{:S(2)}) %collective-permute-start.6) | collective-permute-done | bytes 1376288 | tf_op jit(solution)/shard_map/ppermute | solution.py:41
  95.0 2.5 %collective-permute-start.12 = (bf16[64,3584]{1,0:T(8,128)(2,1)S(1)}, bf16[64,3584]{1,0:T(8,128)(2,1)S(1)}, u32[]{:S(2)}, u32[]{:S(2)}) collective-permute-start(bf16[64,3584]{1,0:T(8,128)(2,1)S(1)} %get-tuple-element.27), channel_id=1, source_target_pairs={{0,1},{1,0},{2,3},{3,2},{4,5},{5,4},{6,7},{7,6},{8,9},{9,8},{10,11... | collective-permute-start | bytes 1376264 | tf_op jit(solution)/shard_map/ppermute | solution.py:41
  97.5 2.8 %collective-permute-start.8 = (bf16[64,3584]{1,0:T(8,128)(2,1)S(1)}, bf16[64,3584]{1,0:T(8,128)(2,1)S(1)}, u32[]{:S(2)}, u32[]{:S(2)}) collective-permute-start(bf16[64,3584]{1,0:T(8,128)(2,1)S(1)} %get-tuple-element.23._), channel_id=1, source_target_pairs={{0,3},{1,2},{2,1},{3,0},{4,7},{5,6},{6,5},{7,4},{8,11},{9,10},{10,... | collective-permute-start | bytes 1376264 | tf_op jit(solution)/shard_map/ppermute | solution.py:41
  100.2 3.3 %shard_map.133 = (f32[64,3584]{1,0:T(8,128)S(1)}, bf16[64,3584]{1,0:T(8,128)(2,1)S(1)}, f32[64,3584]{1,0:T(8,128)S(1)}, bf16[64,3584]{1,0:T(8,128)(2,1)S(1)}) custom-call(bf16[64,10752]{1,0:T(8,128)(2,1)S(1)} %constant_dynamic-update-slice_fusion.c1, bf16[64,10752]{1,0:T(8,128)(2,1)S(1)} %collective-permute-done.3.qr1, ...), custom_call_target="tpu_custom_call" | custom-call | tf_op jit(solution)/shard_map/pallas_call | solution.py:358
  105.6 4.0 %collective-permute-start.10 = (bf16[64,3584]{1,0:T(8,128)(2,1)S(1)}, bf16[64,3584]{1,0:T(8,128)(2,1)S(1)}, u32[]{:S(2)}, u32[]{:S(2)}) collective-permute-start(bf16[64,3584]{1,0:T(8,128)(2,1)S(1)} %get-tuple-element.25), channel_id=1, source_target_pairs={{0,3},{1,2},{2,1},{3,0},{4,7},{5,6},{6,5},{7,4},{8,11},{9,10},{10,... | collective-permute-start | bytes 1376264 | tf_op jit(solution)/shard_map/ppermute | solution.py:41
  109.7 2.5 %collective-permute-start.13 = (bf16[32,3584]{1,0:T(8,128)(2,1)S(1)}, bf16[32,3584]{1,0:T(8,128)(2,1)S(1)}, u32[]{:S(2)}, u32[]{:S(2)}) collective-permute-start(bf16[32,3584]{1,0:T(8,128)(2,1)S(1)} %slice.93), channel_id=1, source_target_pairs={{0,3},{1,2},{2,1},{3,0},{4,7},{5,6},{6,5},{7,4},{8,11},{9,10},{10,... | collective-permute-start | bytes 688136 | tf_op jit(solution)/shard_map/ppermute | solution.py:41
  112.2 4.0 %collective-permute-done.14 = bf16[64,3584]{1,0:T(8,128)(2,1)S(1)} collective-permute-done((bf16[64,3584]{1,0:T(8,128)(2,1)S(1)}, bf16[64,3584]{1,0:T(8,128)(2,1)S(1)}, u32[]{:S(2)}, u32[]{:S(2)}) %collective-permute-start.14) | collective-permute-done | bytes 458784 | tf_op jit(solution)/shard_map/ppermute | solution.py:41
  120.5 3.3 %collective-permute-start.11 = (bf16[32,3584]{1,0:T(8,128)(2,1)S(1)}, bf16[32,3584]{1,0:T(8,128)(2,1)S(1)}, u32[]{:S(2)}, u32[]{:S(2)}) collective-permute-start(bf16[32,3584]{1,0:T(8,128)(2,1)S(1)} %slice.94), channel_id=1, source_target_pairs={{0,1},{1,0},{2,3},{3,2},{4,5},{5,4},{6,7},{7,6},{8,9},{9,8},{10,11... | collective-permute-start | bytes 688136 | tf_op jit(solution)/shard_map/ppermute | solution.py:41
  124.1 4.9 %collective-permute-done.15 = bf16[32,3584]{1,0:T(8,128)(2,1)S(1)} collective-permute-done((bf16[32,3584]{1,0:T(8,128)(2,1)S(1)}, bf16[32,3584]{1,0:T(8,128)(2,1)S(1)}, u32[]{:S(2)}, u32[]{:S(2)}) %collective-permute-start.15) | collective-permute-done | bytes 229408 | tf_op jit(solution)/shard_map/ppermute | solution.py:41
  129.1 4.0 %collective-permute-start.16 = (bf16[16,7168]{1,0:T(8,128)(2,1)S(1)}, bf16[16,7168]{1,0:T(8,128)(2,1)S(1)}, u32[]{:S(2)}, u32[]{:S(2)}) collective-permute-start(bf16[16,7168]{1,0:T(8,128)(2,1)S(1)} %get-tuple-element.36), channel_id=1, source_target_pairs={{0,28},{1,29},{2,30},{3,31},{4,8},{5,9},{6,10},{7,11},{8,4},{9,5},... | collective-permute-start | bytes 688136 | tf_op jit(solution)/shard_map/ppermute | solution.py:41
  133.2 4.3 %collective-permute-start.17 = (bf16[16,7168]{1,0:T(8,128)(2,1)S(1)}, bf16[16,7168]{1,0:T(8,128)(2,1)S(1)}, u32[]{:S(2)}, u32[]{:S(2)}) collective-permute-start(bf16[16,7168]{1,0:T(8,128)(2,1)S(1)} %get-tuple-element.35), channel_id=1, source_target_pairs={{0,20},{1,21},{2,22},{3,23},{4,16},{5,17},{6,18},{7,19},{8,28},{9,... | collective-permute-start | bytes 688136 | tf_op jit(solution)/shard_map/ppermute | solution.py:41
  137.7 7.2 %collective-permute-start.18 = (bf16[16,7168]{1,0:T(8,128)(2,1)S(1)}, bf16[16,7168]{1,0:T(8,128)(2,1)S(1)}, u32[]{:S(2)}, u32[]{:S(2)}) collective-permute-start(bf16[16,7168]{1,0:T(8,128)(2,1)S(1)} %get-tuple-element.33), channel_id=1, source_target_pairs={{0,24},{1,25},{2,26},{3,27},{4,12},{5,13},{6,14},{7,15},{8,0},{9,1... | collective-permute-start | bytes 688136 | tf_op jit(solution)/shard_map/ppermute | solution.py:41
  146.4 6.3 %collective-permute-done.18.rest_3_ = bf16[16,7168]{1,0:T(8,128)(2,1)S(1)} collective-permute-done((bf16[16,7168]{1,0:T(8,128)(2,1)S(1)}, bf16[16,7168]{1,0:T(8,128)(2,1)S(1)}, u32[]{:S(2)}, u32[]{:S(2)}) %collective-permute-start.18) | collective-permute-done | bytes 229408 | tf_op jit(solution)/shard_map/ppermute | solution.py:41
  154.5 8.3 %collective-permute-start.19 = (bf16[24,3584]{1,0:T(8,128)(2,1)S(1)}, bf16[24,3584]{1,0:T(8,128)(2,1)S(1)}, u32[]{:S(2)}, u32[]{:S(2)}) collective-permute-start(bf16[24,3584]{1,0:T(8,128)(2,1)S(1)} %get-tuple-element.30), channel_id=1, source_target_pairs={{0,32},{32,64},{64,96},{96,128},{128,160},{160,192},{192,224},{224... | collective-permute-start | bytes 516104 | tf_op jit(solution)/shard_map/ppermute | solution.py:47
  165.3 5.4 %collective-permute-done.20 = bf16[24,3584]{1,0:T(8,128)(2,1)S(1)} collective-permute-done((bf16[24,3584]{1,0:T(8,128)(2,1)S(1)}, bf16[24,3584]{1,0:T(8,128)(2,1)S(1)}, u32[]{:S(2)}, u32[]{:S(2)}) %collective-permute-start.20) | collective-permute-done | bytes 172064 | tf_op jit(solution)/shard_map/ppermute | solution.py:47
  (75 shorter events, 27.1 us)
Async XLA Ops:
  4.8 32.4 %collective-permute-start.4 = (bf16[16,10752]{1,0:T(8,128)(2,1)}, bf16[16,10752]{1,0:T(8,128)(2,1)S(1)}, u32[]{:S(2)}, u32[]{:S(2)}) collective-permute-start(bf16[16,10752]{1,0:T(8,128)(2,1)} %get-tuple-element.21), channel_id=1, source_target_pairs={{0,28},{1,29},{2,30},{3,31},{4,8},{5,9},{6,10},{7,11},{8,4},{9,5},... | collective-permute-start | bytes 1032200 | tf_op jit(solution)/shard_map/ppermute | solution.py:41
  15.4 24.3 %collective-permute-start = (bf16[16,10752]{1,0:T(8,128)(2,1)}, bf16[16,10752]{1,0:T(8,128)(2,1)S(1)}, u32[]{:S(2)}, u32[]{:S(2)}) collective-permute-start(bf16[16,10752]{1,0:T(8,128)(2,1)} %get-tuple-element.18), channel_id=1, source_target_pairs={{0,8},{1,9},{2,10},{3,11},{4,28},{5,29},{6,30},{7,31},{8,16},{9,17... | collective-permute-start | bytes 1032200 | tf_op jit(solution)/shard_map/ppermute | solution.py:41
  17.4 27.2 %collective-permute-start.1 = (bf16[16,10752]{1,0:T(8,128)(2,1)}, bf16[16,10752]{1,0:T(8,128)(2,1)S(1)}, u32[]{:S(2)}, u32[]{:S(2)}) collective-permute-start(bf16[16,10752]{1,0:T(8,128)(2,1)} %get-tuple-element.19), channel_id=1, source_target_pairs={{0,20},{1,21},{2,22},{3,23},{4,16},{5,17},{6,18},{7,19},{8,28},{9,... | collective-permute-start | bytes 1032200 | tf_op jit(solution)/shard_map/ppermute | solution.py:41
  25.3 68.0 %collective-permute-start.7 = (bf16[10752,128]{1,0:T(8,128)(2,1)}, bf16[10752,128]{1,0:T(8,128)(2,1)S(1)}, u32[]{:S(2)}, u32[]{:S(2)}) collective-permute-start(bf16[10752,128]{1,0:T(8,128)(2,1)} %shard_map.131), channel_id=1, source_target_pairs={{0,4},{1,5},{2,6},{3,7},{4,0},{5,1},{6,2},{7,3},{8,12},{9,13},{10,... | collective-permute-start | bytes 8257544 | tf_op jit(solution)/shard_map/ppermute | solution.py:41
  37.2 16.1 %collective-permute-start.5 = (bf16[32,10752]{1,0:T(8,128)(2,1)S(1)}, bf16[32,10752]{1,0:T(8,128)(2,1)S(1)}, u32[]{:S(2)}, u32[]{:S(2)}) collective-permute-start(bf16[32,10752]{1,0:T(8,128)(2,1)S(1)} %pad_maximum_fusion.1), channel_id=1, source_target_pairs={{0,1},{1,0},{2,3},{3,2},{4,5},{5,4},{6,7},{7,6},{8,9},{9,8},{10,11... | collective-permute-start | bytes 2064392 | tf_op jit(solution)/shard_map/ppermute | solution.py:41
  44.7 18.5 %collective-permute-start.2 = (bf16[32,10752]{1,0:T(8,128)(2,1)S(1)}, bf16[32,10752]{1,0:T(8,128)(2,1)S(1)}, u32[]{:S(2)}, u32[]{:S(2)}) collective-permute-start(bf16[32,10752]{1,0:T(8,128)(2,1)S(1)} %pad_maximum_fusion), channel_id=1, source_target_pairs={{0,3},{1,2},{2,1},{3,0},{4,7},{5,6},{6,5},{7,4},{8,11},{9,10},{10,... | collective-permute-start | bytes 2064392 | tf_op jit(solution)/shard_map/ppermute | solution.py:41
  46.9 46.4 %copy-start = (bf16[1,1,3584,128]{3,2,1,0:T(8,128)(2,1)S(1)}, bf16[1,1,3584,128]{3,2,1,0:T(8,128)(2,1)}, u32[]{:S(2)}) copy-start(bf16[1,1,3584,128]{3,2,1,0:T(8,128)(2,1)} %param.19) | copy-start | bytes 2752516
  46.9 46.4 %copy-start.1 = (bf16[1,1,3584,128]{3,2,1,0:T(8,128)(2,1)S(1)}, bf16[1,1,3584,128]{3,2,1,0:T(8,128)(2,1)}, u32[]{:S(2)}) copy-start(bf16[1,1,3584,128]{3,2,1,0:T(8,128)(2,1)} %param.20) | copy-start | bytes 2752516
  46.9 46.4 %copy-start.2 = (bf16[1,1,128,3584]{3,2,1,0:T(8,128)(2,1)S(1)}, bf16[1,1,128,3584]{3,2,1,0:T(8,128)(2,1)}, u32[]{:S(2)}) copy-start(bf16[1,1,128,3584]{3,2,1,0:T(8,128)(2,1)} %param.21) | copy-start | bytes 2752516
  53.4 39.2 %collective-permute-start.6 = (bf16[64,10752]{1,0:T(8,128)(2,1)S(1)}, bf16[64,10752]{1,0:T(8,128)(2,1)S(1)}, u32[]{:S(2)}, u32[]{:S(2)}) collective-permute-start(bf16[64,10752]{1,0:T(8,128)(2,1)S(1)} %constant_dynamic-update-slice_fusion.3.c2), channel_id=1, source_target_pairs={{0,3},{1,2},{2,1},{3,0},{4,7},{5,6},{6,5},{7,4},{8,11},{9,10},{10,... | collective-permute-start | bytes 4128776 | tf_op jit(solution)/shard_map/ppermute | solution.py:41
  63.2 29.4 %collective-permute-start.3 = (bf16[64,10752]{1,0:T(8,128)(2,1)S(1)}, bf16[64,10752]{1,0:T(8,128)(2,1)S(1)}, u32[]{:S(2)}, u32[]{:S(2)}) collective-permute-start(bf16[64,10752]{1,0:T(8,128)(2,1)S(1)} %constant_dynamic-update-slice_fusion.c1), channel_id=1, source_target_pairs={{0,1},{1,0},{2,3},{3,2},{4,5},{5,4},{6,7},{7,6},{8,9},{9,8},{10,11... | collective-permute-start | bytes 4128776 | tf_op jit(solution)/shard_map/ppermute | solution.py:41
  95.0 14.6 %collective-permute-start.12 = (bf16[64,3584]{1,0:T(8,128)(2,1)S(1)}, bf16[64,3584]{1,0:T(8,128)(2,1)S(1)}, u32[]{:S(2)}, u32[]{:S(2)}) collective-permute-start(bf16[64,3584]{1,0:T(8,128)(2,1)S(1)} %get-tuple-element.27), channel_id=1, source_target_pairs={{0,1},{1,0},{2,3},{3,2},{4,5},{5,4},{6,7},{7,6},{8,9},{9,8},{10,11... | collective-permute-start | bytes 1376264 | tf_op jit(solution)/shard_map/ppermute | solution.py:41
  97.5 20.8 %collective-permute-start.8 = (bf16[64,3584]{1,0:T(8,128)(2,1)S(1)}, bf16[64,3584]{1,0:T(8,128)(2,1)S(1)}, u32[]{:S(2)}, u32[]{:S(2)}) collective-permute-start(bf16[64,3584]{1,0:T(8,128)(2,1)S(1)} %get-tuple-element.23._), channel_id=1, source_target_pairs={{0,3},{1,2},{2,1},{3,0},{4,7},{5,6},{6,5},{7,4},{8,11},{9,10},{10,... | collective-permute-start | bytes 1376264 | tf_op jit(solution)/shard_map/ppermute | solution.py:41
  103.6 12.6 %collective-permute-start.14 = (bf16[64,3584]{1,0:T(8,128)(2,1)S(1)}, bf16[64,3584]{1,0:T(8,128)(2,1)S(1)}, u32[]{:S(2)}, u32[]{:S(2)}) collective-permute-start(bf16[64,3584]{1,0:T(8,128)(2,1)S(1)} %get-tuple-element.29), channel_id=1, source_target_pairs={{0,1},{1,0},{2,3},{3,2},{4,5},{5,4},{6,7},{7,6},{8,9},{9,8},{10,11... | collective-permute-start | bytes 1376264 | tf_op jit(solution)/shard_map/ppermute | solution.py:41
  105.6 14.8 %collective-permute-start.10 = (bf16[64,3584]{1,0:T(8,128)(2,1)S(1)}, bf16[64,3584]{1,0:T(8,128)(2,1)S(1)}, u32[]{:S(2)}, u32[]{:S(2)}) collective-permute-start(bf16[64,3584]{1,0:T(8,128)(2,1)S(1)} %get-tuple-element.25), channel_id=1, source_target_pairs={{0,3},{1,2},{2,1},{3,0},{4,7},{5,6},{6,5},{7,4},{8,11},{9,10},{10,... | collective-permute-start | bytes 1376264 | tf_op jit(solution)/shard_map/ppermute | solution.py:41
  109.7 14.4 %collective-permute-start.13 = (bf16[32,3584]{1,0:T(8,128)(2,1)S(1)}, bf16[32,3584]{1,0:T(8,128)(2,1)S(1)}, u32[]{:S(2)}, u32[]{:S(2)}) collective-permute-start(bf16[32,3584]{1,0:T(8,128)(2,1)S(1)} %slice.93), channel_id=1, source_target_pairs={{0,3},{1,2},{2,1},{3,0},{4,7},{5,6},{6,5},{7,4},{8,11},{9,10},{10,... | collective-permute-start | bytes 688136 | tf_op jit(solution)/shard_map/ppermute | solution.py:41
  116.3 12.7 %collective-permute-start.15 = (bf16[32,3584]{1,0:T(8,128)(2,1)S(1)}, bf16[32,3584]{1,0:T(8,128)(2,1)S(1)}, u32[]{:S(2)}, u32[]{:S(2)}) collective-permute-start(bf16[32,3584]{1,0:T(8,128)(2,1)S(1)} %slice.92), channel_id=1, source_target_pairs={{0,3},{1,2},{2,1},{3,0},{4,7},{5,6},{6,5},{7,4},{8,11},{9,10},{10,... | collective-permute-start | bytes 688136 | tf_op jit(solution)/shard_map/ppermute | solution.py:41
  118.4 19.2 %collective-permute-start.9 = (bf16[32,3584]{1,0:T(8,128)(2,1)S(1)}, bf16[32,3584]{1,0:T(8,128)(2,1)S(1)}, u32[]{:S(2)}, u32[]{:S(2)}) collective-permute-start(bf16[32,3584]{1,0:T(8,128)(2,1)S(1)} %slice.95), channel_id=1, source_target_pairs={{0,1},{1,0},{2,3},{3,2},{4,5},{5,4},{6,7},{7,6},{8,9},{9,8},{10,11... | collective-permute-start | bytes 688136 | tf_op jit(solution)/shard_map/ppermute | solution.py:41
  120.5 17.1 %collective-permute-start.11 = (bf16[32,3584]{1,0:T(8,128)(2,1)S(1)}, bf16[32,3584]{1,0:T(8,128)(2,1)S(1)}, u32[]{:S(2)}, u32[]{:S(2)}) collective-permute-start(bf16[32,3584]{1,0:T(8,128)(2,1)S(1)} %slice.94), channel_id=1, source_target_pairs={{0,1},{1,0},{2,3},{3,2},{4,5},{5,4},{6,7},{7,6},{8,9},{9,8},{10,11... | collective-permute-start | bytes 688136 | tf_op jit(solution)/shard_map/ppermute | solution.py:41
  129.1 15.9 %collective-permute-start.16 = (bf16[16,7168]{1,0:T(8,128)(2,1)S(1)}, bf16[16,7168]{1,0:T(8,128)(2,1)S(1)}, u32[]{:S(2)}, u32[]{:S(2)}) collective-permute-start(bf16[16,7168]{1,0:T(8,128)(2,1)S(1)} %get-tuple-element.36), channel_id=1, source_target_pairs={{0,28},{1,29},{2,30},{3,31},{4,8},{5,9},{6,10},{7,11},{8,4},{9,5},... | collective-permute-start | bytes 688136 | tf_op jit(solution)/shard_map/ppermute | solution.py:41
  133.2 13.2 %collective-permute-start.17 = (bf16[16,7168]{1,0:T(8,128)(2,1)S(1)}, bf16[16,7168]{1,0:T(8,128)(2,1)S(1)}, u32[]{:S(2)}, u32[]{:S(2)}) collective-permute-start(bf16[16,7168]{1,0:T(8,128)(2,1)S(1)} %get-tuple-element.35), channel_id=1, source_target_pairs={{0,20},{1,21},{2,22},{3,23},{4,16},{5,17},{6,18},{7,19},{8,28},{9,... | collective-permute-start | bytes 688136 | tf_op jit(solution)/shard_map/ppermute | solution.py:41
  137.7 15.0 %collective-permute-start.18 = (bf16[16,7168]{1,0:T(8,128)(2,1)S(1)}, bf16[16,7168]{1,0:T(8,128)(2,1)S(1)}, u32[]{:S(2)}, u32[]{:S(2)}) collective-permute-start(bf16[16,7168]{1,0:T(8,128)(2,1)S(1)} %get-tuple-element.33), channel_id=1, source_target_pairs={{0,24},{1,25},{2,26},{3,27},{4,12},{5,13},{6,14},{7,15},{8,0},{9,1... | collective-permute-start | bytes 688136 | tf_op jit(solution)/shard_map/ppermute | solution.py:41
  154.5 10.8 %collective-permute-start.19 = (bf16[24,3584]{1,0:T(8,128)(2,1)S(1)}, bf16[24,3584]{1,0:T(8,128)(2,1)S(1)}, u32[]{:S(2)}, u32[]{:S(2)}) collective-permute-start(bf16[24,3584]{1,0:T(8,128)(2,1)S(1)} %get-tuple-element.30), channel_id=1, source_target_pairs={{0,32},{32,64},{64,96},{96,128},{128,160},{160,192},{192,224},{224... | collective-permute-start | bytes 516104 | tf_op jit(solution)/shard_map/ppermute | solution.py:47
  162.7 7.9 %collective-permute-start.20 = (bf16[24,3584]{1,0:T(8,128)(2,1)S(1)}, bf16[24,3584]{1,0:T(8,128)(2,1)S(1)}, u32[]{:S(2)}, u32[]{:S(2)}) collective-permute-start(bf16[24,3584]{1,0:T(8,128)(2,1)S(1)} %get-tuple-element.31), channel_id=1, source_target_pairs={{32,0},{64,32},{96,64},{128,96},{160,128},{192,160},{224,192},{256... | collective-permute-start | bytes 516104 | tf_op jit(solution)/shard_map/ppermute | solution.py:47
  (10 other events, 181.9 us)

commit v11 on v10

--- a/solution.py
+++ b/solution.py
@@ -61,7 +61,7 @@
 
 
 def local_copy_call(kernel, outs, n_near, scratch):
-    n_far = 4 if n_near else 3
+    n_far = 4 if n_near else 2
     smem = pl.BlockSpec(memory_space=pltpu.SMEM)
     vmem = pl.BlockSpec(memory_space=pltpu.VMEM)
     near = ([smem] + [vmem] * (n_near - 1)) if n_near else []
@@ -136,17 +136,22 @@
             outs[j][:, i * width : (i + 1) * width] = packed[j * SLOT : (j + 1) * SLOT]
 
 
-def merge_kernel(wg, wu, wd, out, down, sems):
-    width, units = wg.shape
-    moves = ((wd, down), (wg, out.at[pl.ds(0, width)]), (wu, out.at[pl.ds(width, width)]))
-    copies = [pltpu.make_async_copy(*move, sems.at[i]) for i, move in enumerate(moves)]
+def merge_kernel(wg, wu, out, sems):
+    width = wg.shape[0]
+    copies = [
+        pltpu.make_async_copy(wg, out.at[pl.ds(0, width)], sems.at[0]),
+        pltpu.make_async_copy(wu, out.at[pl.ds(width, width)], sems.at[1]),
+    ]
     for copy in copies:
         copy.start()
-    copies[0].wait()
-    for at in range(0, width, units):
-        out[2 * width + at : 2 * width + at + units, :] = down[:, at : at + units]
-    copies[1].wait()
-    copies[2].wait()
+    for copy in copies:
+        copy.wait()
+
+
+def near_kernel(half, got, _, out):
+    count = half.shape[0]
+    out[0:count, :] = half[...]
+    out[count : 2 * count, :] = got[...]
 
 
 def hidden(rows, wg, wu):
@@ -154,23 +159,27 @@
     return both[:, :128], both[:, 128:]
 
 
-def down_columns(merged, at, count):
-    width = merged.shape[0] // 3
-    starts = range(2 * width + at, 2 * width + at + count, 128)
-    return jnp.concatenate([merged[start : start + 128, :] for start in starts], axis=1)
-
-
-def gather_rows(refs, at, width, scratch):
-    for i, ref in enumerate(refs):
-        scratch[64 * i : 64 * (i + 1), :] = ref[:, at : at + width]
+X1_FIRST = (0, 32, 64, 96)
+X3_FIRST = (0, 64, 32, 96)
+LEFT = (X3_FIRST, X1_FIRST)
+RIGHT = (X1_FIRST, X3_FIRST)
+
+
+def gather_rows(refs, orders, at, to, width, scratch):
+    cols, into = slice(at, at + width), slice(to, to + width)
+    for half in range(2):
+        for i, start in enumerate(orders[half]):
+            ref, row = refs[2 * half + i // 2], 32 * (i % 2)
+            base = 128 * half + start
+            scratch[base : base + 32, into] = ref[row : row + 32, cols]
 
 
 def store_parts(part, cols, keep1, send1, keep2, send2):
     places = (
-        (keep1, (128, 0, 160, 64)),
-        (send1, (192, 32, 224, 96)),
-        (keep2, (144, 16, 208, 48)),
-        (send2, (176, 80, 240, 112)),
+        (keep1, (128, 0, 160, 32)),
+        (send1, (192, 64, 224, 96)),
+        (keep2, (144, 16, 208, 80)),
+        (send2, (176, 48, 240, 112)),
     )
     for ref, starts in places:
         for i, start in enumerate(starts):
@@ -178,9 +187,9 @@
             ref[rows, cols] = part[start : start + SLOT].astype(ref.dtype)
 
 
-def fwd_kernel(c1, qr1, c2, pr2, wg, wu, wd, other, keep1, send1, keep2, send2, rows):
+def fwd_kernel(l1, l2, l3, l4, wg, wu, wd, other, vd, keep1, send1, keep2, send2, rows):
     width = rows.shape[1]
-    gather_rows((c1, qr1, c2, pr2), 0, width, rows)
+    gather_rows((l1, l2, l3, l4), LEFT, 0, 0, width, rows)
     inner = []
     for weights in ((wg[...], wu[...]), (other[0:width, :], other[width : 2 * width, :])):
         gate, up = hidden(rows[...], *weights)
@@ -189,22 +198,25 @@
     step = 512
     for at in range(0, width, step):
         cols = slice(at, at + step)
-        down = jnp.concatenate([wd[:, cols], down_columns(other, at, step)], axis=0)
+        down = jnp.concatenate([wd[:, cols], vd[:, cols]], axis=0)
         part = jnp.dot(inner, down, preferred_element_type=F32)
         store_parts(part, cols, keep1, send1, keep2, send2)
 
 
 def bwd_kernel(
-    c1, qr1, c2, pr2, wg, wu, wd, other, _, keep1, send1, keep2, send2, rows, cots
+    l1, l2, l3, l4, r1, r2, r3, r4, wg, wu, wd, other, vd, _, keep1, send1, keep2, send2, rows, cots
 ):
     width = rows.shape[1]
-    gather_rows((c1, qr1, c2, pr2), width, width, rows)
-    gather_rows((c1, qr1, c2, pr2), 2 * width, width, cots)
+    half = width // 2
+    lefts, rights = (l1, l2, l3, l4), (r1, r2, r3, r4)
+    gather_rows(lefts, LEFT, width, 0, half, rows)
+    gather_rows(rights, RIGHT, 0, half, half, rows)
+    gather_rows(rights, RIGHT, half, 0, width, cots)
     back = []
     products = None
     sources = (
         (wg[...], wu[...], wd[...]),
-        (other[0:width, :], other[width : 2 * width, :], down_columns(other, 0, width)),
+        (other[0:width, :], other[width : 2 * width, :], vd[...]),
     )
     for gate_w, up_w, down_w in sources:
         gate, up = hidden(rows[...], gate_w, up_w)
@@ -291,15 +303,31 @@
     grad_ref[...] = jnp.where(pair == 0, grads[0], grads[1]).astype(BF16)
 
 
-def spread_rows(own, a, b, c):
+def spread_x(value, first, second, ready=None):
+    got = hop(value, first)
+    if ready is None:
+        near = jnp.concatenate([value, got], axis=0)
+    else:
+        vmem = pl.BlockSpec(memory_space=pltpu.VMEM)
+        near = pl.pallas_call(
+            near_kernel,
+            out_shape=jax.ShapeDtypeStruct((2 * value.shape[0], value.shape[1]), BF16),
+            in_specs=[vmem, vmem, pl.BlockSpec(memory_space=pl.ANY)],
+            out_specs=vmem,
+        )(value, got, ready)
+    return near, hop(near, second)
+
+
+def spread_rows(own, a, b, c, other_down):
     got_a, got_b, got_c = hop(a, HOP_A), hop(b, HOP_B), hop(c, HOP_C)
-    half1 = jnp.concatenate([got_b, got_c], axis=0)
-    half2 = jnp.concatenate([own, got_a], axis=0)
-    q1 = hop(half1, HOP_X3)
-    p2 = hop(half2, HOP_X1)
-    c1 = jnp.concatenate([half1, q1], axis=0)
-    c2 = jnp.concatenate([half2, p2], axis=0)
-    return c1, hop(c1, HOP_X1), c2, hop(c2, HOP_X3)
+    early = jnp.concatenate([own, got_a], axis=0)
+    late = jnp.concatenate([got_b, got_c], axis=0)
+    middle = own.shape[1] // 2
+    late_left = spread_x(late[:, :middle], HOP_X3, HOP_X1, other_down)
+    late_right = spread_x(late[:, middle:], HOP_X1, HOP_X3)
+    early_left = spread_x(early[:, :middle], HOP_X1, HOP_X3)
+    early_right = spread_x(early[:, middle:], HOP_X3, HOP_X1)
+    return late_left + early_left, late_right + early_right
 
 
 def return_x(keep1, send1, keep2, send2):
@@ -337,10 +365,11 @@
     units = w_down.shape[2]
     (merged,) = local_copy_call(
         merge_kernel,
-        [((3 * width, units), BF16)],
+        [((2 * width, units), BF16)],
         0,
-        [pltpu.VMEM((units, width), BF16), pltpu.SemaphoreType.DMA((3,))],
-    )(*weights)
+        [pltpu.SemaphoreType.DMA((2,))],
+    )(*weights[:2])
+    other_down = hop(weights[2], HOP_W)
     other = hop(merged, HOP_W)
     wide = [((SLOT, 3 * width), BF16)] * 4
     sent = local_copy_call(
@@ -351,12 +380,13 @@
         + [pltpu.VMEM((tokens, width), BF16)] * 2
         + [pltpu.SemaphoreType.DMA((4,))],
     )(info, route_fwd[0].T, route_bwd[0].T, act_fwd[0], norm_gain, act_bwd[0], cot_bwd[0])
-    rows = spread_rows(*sent)
+    lefts, rights = spread_rows(*sent, other_down)
+    weights += (other, other_down)
     outs = [((64, width), F32), ((64, width), BF16)] * 2
     scratch = pltpu.VMEM((256, width), BF16)
-    part_a = kernel_call(fwd_kernel, outs, 8, [scratch], info=False)(*rows, *weights, other)
-    part_b = kernel_call(bwd_kernel, outs, 9, [scratch] * 2, info=False)(
-        *rows, *weights, other, part_a[1]
+    part_a = kernel_call(fwd_kernel, outs, 9, [scratch], info=False)(*lefts, *weights)
+    part_b = kernel_call(bwd_kernel, outs, 14, [scratch] * 2, info=False)(
+        *lefts, *rights, *weights, part_a[1]
     )
     halves = zip(return_x(*part_a), return_x(*part_b))
     back = return_z(*[jnp.concatenate(pair, axis=1) for pair in halves])

time: 173 us -> 189 us (1.092)
  the two profiles are of different devices: /device:TPU:31 before, /device:TPU:1 now
where the time goes in v11:
time: 189 us; the launch traced here: 187 us
  starting transfers between devices  91.4 us (48%)
  waiting for transfers between devices  65 us (34%)
  Pallas kernels  18.9 us (10%)
  local copies, waits for them, and re-layouts  7.03 us (4%)
  other arithmetic  3.22 us (2%)
    ppermute x24, starting transfers between devices, hop(): return lax.ppermute(value, 'expert', pairs)  81.1 us
    ppermute x24, waiting for transfers between devices, hop(): return lax.ppermute(value, 'expert', pairs)  60.8 us
    ppermute x2, starting transfers between devices, shifted(): return lax.ppermute(value, axis, pairs)  10.3 us
    pallas_call x1, Pallas kernels, body(): kernel_call(bwd_kernel, outs, 14, [scratch] * 2, info=False)  5.48 us
    unnamed x42, local copies, waits for them, and re-layouts  5.41 us
    ppermute x2, waiting for transfers between devices, shifted(): return lax.ppermute(value, axis, pairs)  4.2 us
  transfers between devices with their start and end apart: 26, of which 10 were waited for; matrix products, arithmetic and copies ran while one was open for 2% of the time, Pallas kernels for 7%

profile of v11, /device:TPU:1, one launch (start us, length us, event | category | flops | bytes accessed | tf_op | source)
XLA Modules:
  0.0 186.8 jit_solution(6796195990443974972)
XLA Ops:
  1.2 3.6 %shard_map.130 = (bf16[16,10752]{1,0:T(8,128)(2,1)}, bf16[16,10752]{1,0:T(8,128)(2,1)}, bf16[16,10752]{1,0:T(8,128)(2,1)}, bf16[16,10752]{1,0:T(8,128)(2,1)}) custom-call(s32[2]{0:T(128)} %pad_add_fusion.info_ref, s32[2,24]{1,0:T(2,128)} %bitcast.38, s32[2,24]{1,0:T(2,128)} %bitcast.40, bf16[24,3584]{1,0:T(8,128)(2,1)} %bitcast.32, f32[1,3584]{1,0:T(1,128)} %gain_ref.1, ...), custom_call_target="tpu_custom_call" | custom-call | tf_op jit(solution)/shard_map/pallas_call | solution.py:375
  4.8 6.6 %collective-permute-start = (bf16[16,10752]{1,0:T(8,128)(2,1)}, bf16[16,10752]{1,0:T(8,128)(2,1)S(1)}, u32[]{:S(2)}, u32[]{:S(2)}) collective-permute-start(bf16[16,10752]{1,0:T(8,128)(2,1)} %get-tuple-element.18), channel_id=1, source_target_pairs={{0,8},{1,9},{2,10},{3,11},{4,28},{5,29},{6,30},{7,31},{8,16},{9,17... | collective-permute-start | bytes 1032200 | tf_op jit(solution)/shard_map/ppermute | solution.py:41
  11.4 6.8 %collective-permute-start.1 = (bf16[16,10752]{1,0:T(8,128)(2,1)}, bf16[16,10752]{1,0:T(8,128)(2,1)S(1)}, u32[]{:S(2)}, u32[]{:S(2)}) collective-permute-start(bf16[16,10752]{1,0:T(8,128)(2,1)} %get-tuple-element.19), channel_id=1, source_target_pairs={{0,20},{1,21},{2,22},{3,23},{4,16},{5,17},{6,18},{7,19},{8,28},{9,... | collective-permute-start | bytes 1032200 | tf_op jit(solution)/shard_map/ppermute | solution.py:41
  18.2 4.3 %collective-permute-start.3 = (bf16[128,3584]{1,0:T(8,128)(2,1)}, bf16[128,3584]{1,0:T(8,128)(2,1)S(1)}, u32[]{:S(2)}, u32[]{:S(2)}) collective-permute-start(bf16[128,3584]{1,0:T(8,128)(2,1)} %bitcast.29), channel_id=1, source_target_pairs={{0,4},{1,5},{2,6},{3,7},{4,0},{5,1},{6,2},{7,3},{8,12},{9,13},{10,... | collective-permute-start | bytes 2752520 | tf_op jit(solution)/shard_map/ppermute | solution.py:41
  29.4 18.0 %collective-permute-done.5 = bf16[16,10752]{1,0:T(8,128)(2,1)S(1)} collective-permute-done((bf16[16,10752]{1,0:T(8,128)(2,1)}, bf16[16,10752]{1,0:T(8,128)(2,1)S(1)}, u32[]{:S(2)}, u32[]{:S(2)}) %collective-permute-start.5) | collective-permute-done | bytes 344096 | tf_op jit(solution)/shard_map/ppermute | solution.py:41
  47.5 3.1 %collective-permute-start.6 = (bf16[32,5376]{1,0:T(8,128)(2,1)S(1)}, bf16[32,5376]{1,0:T(8,128)(2,1)S(1)}, u32[]{:S(2)}, u32[]{:S(2)}) collective-permute-start(bf16[32,5376]{1,0:T(8,128)(2,1)S(1)} %get-tuple-element.34), channel_id=1, source_target_pairs={{0,1},{1,0},{2,3},{3,2},{4,5},{5,4},{6,7},{7,6},{8,9},{9,8},{10,11... | collective-permute-start | bytes 1032200 | tf_op jit(solution)/shard_map/ppermute | solution.py:41
  51.6 3.7 %collective-permute-start.2 = (bf16[32,5376]{1,0:T(8,128)(2,1)S(1)}, bf16[32,5376]{1,0:T(8,128)(2,1)S(1)}, u32[]{:S(2)}, u32[]{:S(2)}) collective-permute-start(bf16[32,5376]{1,0:T(8,128)(2,1)S(1)} %get-tuple-element.36.half), channel_id=1, source_target_pairs={{0,3},{1,2},{2,1},{3,0},{4,7},{5,6},{6,5},{7,4},{8,11},{9,10},{10,... | collective-permute-start | bytes 1032200 | tf_op jit(solution)/shard_map/ppermute | solution.py:41
  58.7 3.1 %collective-permute-start.11 = (bf16[32,5376]{1,0:T(8,128)(2,1)}, bf16[32,5376]{1,0:T(8,128)(2,1)}, u32[]{:S(2)}, u32[]{:S(2)}) collective-permute-start(bf16[32,5376]{1,0:T(8,128)(2,1)} %get-tuple-element.35), channel_id=1, source_target_pairs={{0,1},{1,0},{2,3},{3,2},{4,5},{5,4},{6,7},{7,6},{8,9},{9,8},{10,11... | collective-permute-start | bytes 1032200 | tf_op jit(solution)/shard_map/ppermute | solution.py:41
  61.8 9.0 %collective-permute-done.13 = bf16[32,5376]{1,0:T(8,128)(2,1)S(1)} collective-permute-done((bf16[32,5376]{1,0:T(8,128)(2,1)S(1)}, bf16[32,5376]{1,0:T(8,128)(2,1)S(1)}, u32[]{:S(2)}, u32[]{:S(2)}) %collective-permute-start.13) | collective-permute-done | bytes 344096 | tf_op jit(solution)/shard_map/ppermute | solution.py:41
  70.8 3.7 %collective-permute-start.7 = (bf16[64,5376]{1,0:T(8,128)(2,1)S(1)}, bf16[64,5376]{1,0:T(8,128)(2,1)}, u32[]{:S(2)}, u32[]{:S(2)}) collective-permute-start(bf16[64,5376]{1,0:T(8,128)(2,1)S(1)} %pad_maximum_fusion.l3), channel_id=1, source_target_pairs={{0,3},{1,2},{2,1},{3,0},{4,7},{5,6},{6,5},{7,4},{8,11},{9,10},{10,... | collective-permute-start | bytes 2064392 | tf_op jit(solution)/shard_map/ppermute | solution.py:41
  81.1 3.5 %collective-permute-start.4 = (bf16[64,5376]{1,0:T(8,128)(2,1)}, bf16[64,5376]{1,0:T(8,128)(2,1)S(1)}, u32[]{:S(2)}, u32[]{:S(2)}) collective-permute-start(bf16[64,5376]{1,0:T(8,128)(2,1)} %shard_map.131.l1), channel_id=1, source_target_pairs={{0,1},{1,0},{2,3},{3,2},{4,5},{5,4},{6,7},{7,6},{8,9},{9,8},{10,11... | collective-permute-start | bytes 2064392 | tf_op jit(solution)/shard_map/ppermute | solution.py:41
  89.3 18.8 %collective-permute-done.4.l2 = bf16[64,5376]{1,0:T(8,128)(2,1)S(1)} collective-permute-done((bf16[64,5376]{1,0:T(8,128)(2,1)}, bf16[64,5376]{1,0:T(8,128)(2,1)S(1)}, u32[]{:S(2)}, u32[]{:S(2)}) %collective-permute-start.4) | collective-permute-done | bytes 688160 | tf_op jit(solution)/shard_map/ppermute | solution.py:41
  110.4 3.4 %shard_map.133 = (f32[64,3584]{1,0:T(8,128)S(1)}, bf16[64,3584]{1,0:T(8,128)(2,1)S(1)}, f32[64,3584]{1,0:T(8,128)S(1)}, bf16[64,3584]{1,0:T(8,128)(2,1)S(1)}) custom-call(bf16[64,5376]{1,0:T(8,128)(2,1)S(1)} %copy-done.4, bf16[64,5376]{1,0:T(8,128)(2,1)S(1)} %collective-permute-done.4.l2, bf16[64,5376]{1,0:T(8,128)(2,1)S(1)} %pad_maximum_fusion.l3, ...), custom_call_target="tpu_custom_call" | custom-call | tf_op jit(solution)/shard_map/pallas_call | solution.py:387
  116.0 2.8 %collective-permute-start.9 = (bf16[64,3584]{1,0:T(8,128)(2,1)S(1)}, bf16[64,3584]{1,0:T(8,128)(2,1)S(1)}, u32[]{:S(2)}, u32[]{:S(2)}) collective-permute-start(bf16[64,3584]{1,0:T(8,128)(2,1)S(1)} %get-tuple-element.23._), channel_id=1, source_target_pairs={{0,3},{1,2},{2,1},{3,0},{4,7},{5,6},{6,5},{7,4},{8,11},{9,10},{10,... | collective-permute-start | bytes 1376264 | tf_op jit(solution)/shard_map/ppermute | solution.py:41
  118.8 5.5 %shard_map.134 = (f32[64,3584]{1,0:T(8,128)S(1)}, bf16[64,3584]{1,0:T(8,128)(2,1)S(1)}, f32[64,3584]{1,0:T(8,128)S(1)}, bf16[64,3584]{1,0:T(8,128)(2,1)S(1)}) custom-call(bf16[64,5376]{1,0:T(8,128)(2,1)S(1)} %copy-done.5, bf16[64,5376]{1,0:T(8,128)(2,1)S(1)} %collective-permute-done.4.l2, bf16[64,5376]{1,0:T(8,128)(2,1)S(1)} %pad_maximum_fusion.l3, ...), custom_call_target="tpu_custom_call" | custom-call | tf_op jit(solution)/shard_map/pallas_call | solution.py:388
  126.8 3.7 %collective-permute-start.15 = (bf16[64,3584]{1,0:T(8,128)(2,1)S(1)}, bf16[64,3584]{1,0:T(8,128)(2,1)S(1)}, u32[]{:S(2)}, u32[]{:S(2)}) collective-permute-start(bf16[64,3584]{1,0:T(8,128)(2,1)S(1)} %get-tuple-element.25), channel_id=1, source_target_pairs={{0,3},{1,2},{2,1},{3,0},{4,7},{5,6},{6,5},{7,4},{8,11},{9,10},{10,... | collective-permute-start | bytes 1376264 | tf_op jit(solution)/shard_map/ppermute | solution.py:41
  135.2 3.7 %collective-permute-start.20 = (bf16[32,3584]{1,0:T(8,128)(2,1)S(1)}, bf16[32,3584]{1,0:T(8,128)(2,1)S(1)}, u32[]{:S(2)}, u32[]{:S(2)}) collective-permute-start(bf16[32,3584]{1,0:T(8,128)(2,1)S(1)} %slice.112), channel_id=1, source_target_pairs={{0,3},{1,2},{2,1},{3,0},{4,7},{5,6},{6,5},{7,4},{8,11},{9,10},{10,... | collective-permute-start | bytes 688136 | tf_op jit(solution)/shard_map/ppermute | solution.py:41
  141.1 3.4 %collective-permute-start.16 = (bf16[32,3584]{1,0:T(8,128)(2,1)S(1)}, bf16[32,3584]{1,0:T(8,128)(2,1)S(1)}, u32[]{:S(2)}, u32[]{:S(2)}) collective-permute-start(bf16[32,3584]{1,0:T(8,128)(2,1)S(1)} %slice.114), channel_id=1, source_target_pairs={{0,1},{1,0},{2,3},{3,2},{4,5},{5,4},{6,7},{7,6},{8,9},{9,8},{10,11... | collective-permute-start | bytes 688136 | tf_op jit(solution)/shard_map/ppermute | solution.py:41
  144.6 3.5 %collective-permute-done.20 = bf16[32,3584]{1,0:T(8,128)(2,1)S(1)} collective-permute-done((bf16[32,3584]{1,0:T(8,128)(2,1)S(1)}, bf16[32,3584]{1,0:T(8,128)(2,1)S(1)}, u32[]{:S(2)}, u32[]{:S(2)}) %collective-permute-start.20) | collective-permute-done | bytes 229408 | tf_op jit(solution)/shard_map/ppermute | solution.py:41
  148.1 5.2 %collective-permute-start.21 = (bf16[16,7168]{1,0:T(8,128)(2,1)S(1)}, bf16[16,7168]{1,0:T(8,128)(2,1)S(1)}, u32[]{:S(2)}, u32[]{:S(2)}) collective-permute-start(bf16[16,7168]{1,0:T(8,128)(2,1)S(1)} %get-tuple-element.40), channel_id=1, source_target_pairs={{0,28},{1,29},{2,30},{3,31},{4,8},{5,9},{6,10},{7,11},{8,4},{9,5},... | collective-permute-start | bytes 688136 | tf_op jit(solution)/shard_map/ppermute | solution.py:41
  155.7 4.5 %collective-permute-start.23 = (bf16[16,7168]{1,0:T(8,128)(2,1)S(1)}, bf16[16,7168]{1,0:T(8,128)(2,1)S(1)}, u32[]{:S(2)}, u32[]{:S(2)}) collective-permute-start(bf16[16,7168]{1,0:T(8,128)(2,1)S(1)} %get-tuple-element.37), channel_id=1, source_target_pairs={{0,24},{1,25},{2,26},{3,27},{4,12},{5,13},{6,14},{7,15},{8,0},{9,1... | collective-permute-start | bytes 688136 | tf_op jit(solution)/shard_map/ppermute | solution.py:41
  160.2 5.7 %collective-permute-done.22.rest_2_ = bf16[16,7168]{1,0:T(8,128)(2,1)S(1)} collective-permute-done((bf16[16,7168]{1,0:T(8,128)(2,1)S(1)}, bf16[16,7168]{1,0:T(8,128)(2,1)S(1)}, u32[]{:S(2)}, u32[]{:S(2)}) %collective-permute-start.22) | collective-permute-done | bytes 229408 | tf_op jit(solution)/shard_map/ppermute | solution.py:41
  170.3 8.4 %collective-permute-start.24 = (bf16[24,3584]{1,0:T(8,128)(2,1)S(1)}, bf16[24,3584]{1,0:T(8,128)(2,1)S(1)}, u32[]{:S(2)}, u32[]{:S(2)}) collective-permute-start(bf16[24,3584]{1,0:T(8,128)(2,1)S(1)} %get-tuple-element.30), channel_id=1, source_target_pairs={{0,32},{32,64},{64,96},{96,128},{128,160},{160,192},{192,224},{224... | collective-permute-start | bytes 516104 | tf_op jit(solution)/shard_map/ppermute | solution.py:47
  181.2 4.2 %collective-permute-done.25 = bf16[24,3584]{1,0:T(8,128)(2,1)S(1)} collective-permute-done((bf16[24,3584]{1,0:T(8,128)(2,1)S(1)}, bf16[24,3584]{1,0:T(8,128)(2,1)S(1)}, u32[]{:S(2)}, u32[]{:S(2)}) %collective-permute-start.25) | collective-permute-done | bytes 172064 | tf_op jit(solution)/shard_map/ppermute | solution.py:47
  (99 shorter events, 47.4 us)
Async XLA Ops:
  4.8 45.9 %collective-permute-start = (bf16[16,10752]{1,0:T(8,128)(2,1)}, bf16[16,10752]{1,0:T(8,128)(2,1)S(1)}, u32[]{:S(2)}, u32[]{:S(2)}) collective-permute-start(bf16[16,10752]{1,0:T(8,128)(2,1)} %get-tuple-element.18), channel_id=1, source_target_pairs={{0,8},{1,9},{2,10},{3,11},{4,28},{5,29},{6,30},{7,31},{8,16},{9,17... | collective-permute-start | bytes 1032200 | tf_op jit(solution)/shard_map/ppermute | solution.py:41
  11.4 39.3 %collective-permute-start.1 = (bf16[16,10752]{1,0:T(8,128)(2,1)}, bf16[16,10752]{1,0:T(8,128)(2,1)S(1)}, u32[]{:S(2)}, u32[]{:S(2)}) collective-permute-start(bf16[16,10752]{1,0:T(8,128)(2,1)} %get-tuple-element.19), channel_id=1, source_target_pairs={{0,20},{1,21},{2,22},{3,23},{4,16},{5,17},{6,18},{7,19},{8,28},{9,... | collective-permute-start | bytes 1032200 | tf_op jit(solution)/shard_map/ppermute | solution.py:41
  18.2 60.0 %collective-permute-start.3 = (bf16[128,3584]{1,0:T(8,128)(2,1)}, bf16[128,3584]{1,0:T(8,128)(2,1)S(1)}, u32[]{:S(2)}, u32[]{:S(2)}) collective-permute-start(bf16[128,3584]{1,0:T(8,128)(2,1)} %bitcast.29), channel_id=1, source_target_pairs={{0,4},{1,5},{2,6},{3,7},{4,0},{5,1},{6,2},{7,3},{8,12},{9,13},{10,... | collective-permute-start | bytes 2752520 | tf_op jit(solution)/shard_map/ppermute | solution.py:41
  22.5 25.0 %collective-permute-start.5 = (bf16[16,10752]{1,0:T(8,128)(2,1)}, bf16[16,10752]{1,0:T(8,128)(2,1)S(1)}, u32[]{:S(2)}, u32[]{:S(2)}) collective-permute-start(bf16[16,10752]{1,0:T(8,128)(2,1)} %get-tuple-element.21), channel_id=1, source_target_pairs={{0,28},{1,29},{2,30},{3,31},{4,8},{5,9},{6,10},{7,11},{8,4},{9,5},... | collective-permute-start | bytes 1032200 | tf_op jit(solution)/shard_map/ppermute | solution.py:41
  27.5 80.6 %collective-permute-start.8 = (bf16[7168,128]{1,0:T(8,128)(2,1)}, bf16[7168,128]{1,0:T(8,128)(2,1)}, u32[]{:S(2)}, u32[]{:S(2)}) collective-permute-start(bf16[7168,128]{1,0:T(8,128)(2,1)} %shard_map.132), channel_id=1, source_target_pairs={{0,4},{1,5},{2,6},{3,7},{4,0},{5,1},{6,2},{7,3},{8,12},{9,13},{10,... | collective-permute-start | bytes 5505032 | tf_op jit(solution)/shard_map/ppermute | solution.py:41
  47.5 11.1 %collective-permute-start.6 = (bf16[32,5376]{1,0:T(8,128)(2,1)S(1)}, bf16[32,5376]{1,0:T(8,128)(2,1)S(1)}, u32[]{:S(2)}, u32[]{:S(2)}) collective-permute-start(bf16[32,5376]{1,0:T(8,128)(2,1)S(1)} %get-tuple-element.34), channel_id=1, source_target_pairs={{0,1},{1,0},{2,3},{3,2},{4,5},{5,4},{6,7},{7,6},{8,9},{9,8},{10,11... | collective-permute-start | bytes 1032200 | tf_op jit(solution)/shard_map/ppermute | solution.py:41
  51.6 23.9 %collective-permute-start.2 = (bf16[32,5376]{1,0:T(8,128)(2,1)S(1)}, bf16[32,5376]{1,0:T(8,128)(2,1)S(1)}, u32[]{:S(2)}, u32[]{:S(2)}) collective-permute-start(bf16[32,5376]{1,0:T(8,128)(2,1)S(1)} %get-tuple-element.36.half), channel_id=1, source_target_pairs={{0,3},{1,2},{2,1},{3,0},{4,7},{5,6},{6,5},{7,4},{8,11},{9,10},{10,... | collective-permute-start | bytes 1032200 | tf_op jit(solution)/shard_map/ppermute | solution.py:41
  55.3 15.6 %collective-permute-start.13 = (bf16[32,5376]{1,0:T(8,128)(2,1)S(1)}, bf16[32,5376]{1,0:T(8,128)(2,1)S(1)}, u32[]{:S(2)}, u32[]{:S(2)}) collective-permute-start(bf16[32,5376]{1,0:T(8,128)(2,1)S(1)} %get-tuple-element.33), channel_id=1, source_target_pairs={{0,3},{1,2},{2,1},{3,0},{4,7},{5,6},{6,5},{7,4},{8,11},{9,10},{10,... | collective-permute-start | bytes 1032200 | tf_op jit(solution)/shard_map/ppermute | solution.py:41
  58.7 25.9 %collective-permute-start.11 = (bf16[32,5376]{1,0:T(8,128)(2,1)}, bf16[32,5376]{1,0:T(8,128)(2,1)}, u32[]{:S(2)}, u32[]{:S(2)}) collective-permute-start(bf16[32,5376]{1,0:T(8,128)(2,1)} %get-tuple-element.35), channel_id=1, source_target_pairs={{0,1},{1,0},{2,3},{3,2},{4,5},{5,4},{6,7},{7,6},{8,9},{9,8},{10,11... | collective-permute-start | bytes 1032200 | tf_op jit(solution)/shard_map/ppermute | solution.py:41
  70.8 18.5 %collective-permute-start.7 = (bf16[64,5376]{1,0:T(8,128)(2,1)S(1)}, bf16[64,5376]{1,0:T(8,128)(2,1)}, u32[]{:S(2)}, u32[]{:S(2)}) collective-permute-start(bf16[64,5376]{1,0:T(8,128)(2,1)S(1)} %pad_maximum_fusion.l3), channel_id=1, source_target_pairs={{0,3},{1,2},{2,1},{3,0},{4,7},{5,6},{6,5},{7,4},{8,11},{9,10},{10,... | collective-permute-start | bytes 2064392 | tf_op jit(solution)/shard_map/ppermute | solution.py:41
  76.2 42.6 %collective-permute-start.14 = (bf16[64,5376]{1,0:T(8,128)(2,1)}, bf16[64,5376]{1,0:T(8,128)(2,1)}, u32[]{:S(2)}, u32[]{:S(2)}) collective-permute-start(bf16[64,5376]{1,0:T(8,128)(2,1)} %pad_maximum_fusion.2.r3), channel_id=1, source_target_pairs={{0,1},{1,0},{2,3},{3,2},{4,5},{5,4},{6,7},{7,6},{8,9},{9,8},{10,11... | collective-permute-start | bytes 2064392 | tf_op jit(solution)/shard_map/ppermute | solution.py:41
  81.1 27.0 %collective-permute-start.4 = (bf16[64,5376]{1,0:T(8,128)(2,1)}, bf16[64,5376]{1,0:T(8,128)(2,1)S(1)}, u32[]{:S(2)}, u32[]{:S(2)}) collective-permute-start(bf16[64,5376]{1,0:T(8,128)(2,1)} %shard_map.131.l1), channel_id=1, source_target_pairs={{0,1},{1,0},{2,3},{3,2},{4,5},{5,4},{6,7},{7,6},{8,9},{9,8},{10,11... | collective-permute-start | bytes 2064392 | tf_op jit(solution)/shard_map/ppermute | solution.py:41
  85.7 33.1 %collective-permute-start.12 = (bf16[64,5376]{1,0:T(8,128)(2,1)S(1)}, bf16[64,5376]{1,0:T(8,128)(2,1)S(1)}, u32[]{:S(2)}, u32[]{:S(2)}) collective-permute-start(bf16[64,5376]{1,0:T(8,128)(2,1)S(1)} %pad_maximum_fusion.1.r1), channel_id=1, source_target_pairs={{0,3},{1,2},{2,1},{3,0},{4,7},{5,6},{6,5},{7,4},{8,11},{9,10},{10,... | collective-permute-start | bytes 2064392 | tf_op jit(solution)/shard_map/ppermute | solution.py:41
  113.8 16.7 %collective-permute-start.17 = (bf16[64,3584]{1,0:T(8,128)(2,1)S(1)}, bf16[64,3584]{1,0:T(8,128)(2,1)S(1)}, u32[]{:S(2)}, u32[]{:S(2)}) collective-permute-start(bf16[64,3584]{1,0:T(8,128)(2,1)S(1)} %get-tuple-element.27), channel_id=1, source_target_pairs={{0,1},{1,0},{2,3},{3,2},{4,5},{5,4},{6,7},{7,6},{8,9},{9,8},{10,11... | collective-permute-start | bytes 1376264 | tf_op jit(solution)/shard_map/ppermute | solution.py:41
  116.0 22.9 %collective-permute-start.9 = (bf16[64,3584]{1,0:T(8,128)(2,1)S(1)}, bf16[64,3584]{1,0:T(8,128)(2,1)S(1)}, u32[]{:S(2)}, u32[]{:S(2)}) collective-permute-start(bf16[64,3584]{1,0:T(8,128)(2,1)S(1)} %get-tuple-element.23._), channel_id=1, source_target_pairs={{0,3},{1,2},{2,1},{3,0},{4,7},{5,6},{6,5},{7,4},{8,11},{9,10},{10,... | collective-permute-start | bytes 1376264 | tf_op jit(solution)/shard_map/ppermute | solution.py:41
  126.8 14.2 %collective-permute-start.15 = (bf16[64,3584]{1,0:T(8,128)(2,1)S(1)}, bf16[64,3584]{1,0:T(8,128)(2,1)S(1)}, u32[]{:S(2)}, u32[]{:S(2)}) collective-permute-start(bf16[64,3584]{1,0:T(8,128)(2,1)S(1)} %get-tuple-element.25), channel_id=1, source_target_pairs={{0,3},{1,2},{2,1},{3,0},{4,7},{5,6},{6,5},{7,4},{8,11},{9,10},{10,... | collective-permute-start | bytes 1376264 | tf_op jit(solution)/shard_map/ppermute | solution.py:41
  130.7 13.8 %collective-permute-start.18 = (bf16[32,3584]{1,0:T(8,128)(2,1)S(1)}, bf16[32,3584]{1,0:T(8,128)(2,1)S(1)}, u32[]{:S(2)}, u32[]{:S(2)}) collective-permute-start(bf16[32,3584]{1,0:T(8,128)(2,1)S(1)} %slice.113), channel_id=1, source_target_pairs={{0,3},{1,2},{2,1},{3,0},{4,7},{5,6},{6,5},{7,4},{8,11},{9,10},{10,... | collective-permute-start | bytes 688136 | tf_op jit(solution)/shard_map/ppermute | solution.py:41
  135.2 12.8 %collective-permute-start.20 = (bf16[32,3584]{1,0:T(8,128)(2,1)S(1)}, bf16[32,3584]{1,0:T(8,128)(2,1)S(1)}, u32[]{:S(2)}, u32[]{:S(2)}) collective-permute-start(bf16[32,3584]{1,0:T(8,128)(2,1)S(1)} %slice.112), channel_id=1, source_target_pairs={{0,3},{1,2},{2,1},{3,0},{4,7},{5,6},{6,5},{7,4},{8,11},{9,10},{10,... | collective-permute-start | bytes 688136 | tf_op jit(solution)/shard_map/ppermute | solution.py:41
  139.1 16.5 %collective-permute-start.10 = (bf16[32,3584]{1,0:T(8,128)(2,1)S(1)}, bf16[32,3584]{1,0:T(8,128)(2,1)S(1)}, u32[]{:S(2)}, u32[]{:S(2)}) collective-permute-start(bf16[32,3584]{1,0:T(8,128)(2,1)S(1)} %slice.115), channel_id=1, source_target_pairs={{0,1},{1,0},{2,3},{3,2},{4,5},{5,4},{6,7},{7,6},{8,9},{9,8},{10,11... | collective-permute-start | bytes 688136 | tf_op jit(solution)/shard_map/ppermute | solution.py:41
  141.1 14.5 %collective-permute-start.16 = (bf16[32,3584]{1,0:T(8,128)(2,1)S(1)}, bf16[32,3584]{1,0:T(8,128)(2,1)S(1)}, u32[]{:S(2)}, u32[]{:S(2)}) collective-permute-start(bf16[32,3584]{1,0:T(8,128)(2,1)S(1)} %slice.114), channel_id=1, source_target_pairs={{0,1},{1,0},{2,3},{3,2},{4,5},{5,4},{6,7},{7,6},{8,9},{9,8},{10,11... | collective-permute-start | bytes 688136 | tf_op jit(solution)/shard_map/ppermute | solution.py:41
  148.1 12.1 %collective-permute-start.21 = (bf16[16,7168]{1,0:T(8,128)(2,1)S(1)}, bf16[16,7168]{1,0:T(8,128)(2,1)S(1)}, u32[]{:S(2)}, u32[]{:S(2)}) collective-permute-start(bf16[16,7168]{1,0:T(8,128)(2,1)S(1)} %get-tuple-element.40), channel_id=1, source_target_pairs={{0,28},{1,29},{2,30},{3,31},{4,8},{5,9},{6,10},{7,11},{8,4},{9,5},... | collective-permute-start | bytes 688136 | tf_op jit(solution)/shard_map/ppermute | solution.py:41
  153.5 12.4 %collective-permute-start.22 = (bf16[16,7168]{1,0:T(8,128)(2,1)S(1)}, bf16[16,7168]{1,0:T(8,128)(2,1)S(1)}, u32[]{:S(2)}, u32[]{:S(2)}) collective-permute-start(bf16[16,7168]{1,0:T(8,128)(2,1)S(1)} %get-tuple-element.39), channel_id=1, source_target_pairs={{0,20},{1,21},{2,22},{3,23},{4,16},{5,17},{6,18},{7,19},{8,28},{9,... | collective-permute-start | bytes 688136 | tf_op jit(solution)/shard_map/ppermute | solution.py:41
  155.7 12.9 %collective-permute-start.23 = (bf16[16,7168]{1,0:T(8,128)(2,1)S(1)}, bf16[16,7168]{1,0:T(8,128)(2,1)S(1)}, u32[]{:S(2)}, u32[]{:S(2)}) collective-permute-start(bf16[16,7168]{1,0:T(8,128)(2,1)S(1)} %get-tuple-element.37), channel_id=1, source_target_pairs={{0,24},{1,25},{2,26},{3,27},{4,12},{5,13},{6,14},{7,15},{8,0},{9,1... | collective-permute-start | bytes 688136 | tf_op jit(solution)/shard_map/ppermute | solution.py:41
  170.3 10.9 %collective-permute-start.24 = (bf16[24,3584]{1,0:T(8,128)(2,1)S(1)}, bf16[24,3584]{1,0:T(8,128)(2,1)S(1)}, u32[]{:S(2)}, u32[]{:S(2)}) collective-permute-start(bf16[24,3584]{1,0:T(8,128)(2,1)S(1)} %get-tuple-element.30), channel_id=1, source_target_pairs={{0,32},{32,64},{64,96},{96,128},{128,160},{160,192},{192,224},{224... | collective-permute-start | bytes 516104 | tf_op jit(solution)/shard_map/ppermute | solution.py:47
  (21 other events, 287.9 us)

commit v12 on v10

--- a/solution.py
+++ b/solution.py
@@ -60,19 +60,17 @@
     )
 
 
-def local_copy_call(kernel, outs, n_near, scratch):
-    n_far = 4 if n_near else 3
-    smem = pl.BlockSpec(memory_space=pltpu.SMEM)
-    vmem = pl.BlockSpec(memory_space=pltpu.VMEM)
-    near = ([smem] + [vmem] * (n_near - 1)) if n_near else []
+def local_copy_call(kernel, scalars, arrays, outs, scratch):
+    arrays = [pltpu.with_memory_space_constraint(array, pltpu.HBM) for array in arrays]
     return pl.pallas_call(
         kernel,
         out_shape=[jax.ShapeDtypeStruct(s, d) for s, d in outs],
-        in_specs=near + [pl.BlockSpec(memory_space=pl.ANY)] * n_far,
-        out_specs=[vmem] * len(outs),
-        scratch_shapes=scratch,
-        compiler_params=pltpu.CompilerParams(vmem_limit_bytes=60 * 1024 * 1024),
-    )
+        in_specs=[pl.BlockSpec(memory_space=pltpu.SMEM)] * len(scalars)
+        + [pl.BlockSpec(memory_space=pltpu.HBM)] * len(arrays),
+        out_specs=[pl.BlockSpec(memory_space=pltpu.VMEM)] * len(outs),
+        scratch_shapes=scratch + [pltpu.SemaphoreType.DMA((len(arrays),))],
+        compiler_params=pltpu.CompilerParams(vmem_limit_bytes=16 * 1024 * 1024),
+    )(*scalars, *arrays)
 
 
 def columns(ref):
@@ -113,18 +111,27 @@
     return values * scale, scale
 
 
-def pack_kernel(info_ref, ra_ref, rb_ref, xa, gain_in, xb, cot, *rest):
-    outs, (xa_ref, gain_ref, xb_ref, cot_ref, sems) = rest[:4], rest[4:]
+def pack_kernel(info_ref, ra, rb, xa, gain_in, xb, cot, *rest):
+    outs, (ra_ref, rb_ref, xa_ref, gain_ref, xb_ref, cot_ref, sems) = rest[:4], rest[4:]
     width = xa.shape[1]
-    moves = ((xa, xa_ref), (gain_in, gain_ref), (xb, xb_ref), (cot, cot_ref))
+    moves = (
+        (ra, ra_ref),
+        (rb, rb_ref),
+        (xa, xa_ref),
+        (gain_in, gain_ref),
+        (xb, xb_ref),
+        (cot, cot_ref),
+    )
     copies = [pltpu.make_async_copy(*move, sems.at[i]) for i, move in enumerate(moves)]
     for copy in copies:
         copy.start()
+    for copy in copies[:2]:
+        copy.wait()
     places = []
     for route_ref in (ra_ref, rb_ref):
         masks = slot_masks(info_ref, route_ref)
         places.append((masks[0][0] | masks[1][0]).astype(F32).astype(BF16))
-    for copy in copies:
+    for copy in copies[2:]:
         copy.wait()
     gain = gain_ref[...]
     normed_a = (normalized(xa_ref[...])[0] * gain).astype(BF16)
@@ -336,21 +343,21 @@
     weights = (w_gate[0, 0], w_up[0, 0], w_down[0, 0])
     units = w_down.shape[2]
     (merged,) = local_copy_call(
-        merge_kernel,
-        [((3 * width, units), BF16)],
-        0,
-        [pltpu.VMEM((units, width), BF16), pltpu.SemaphoreType.DMA((3,))],
-    )(*weights)
+        merge_kernel, (), weights, [((3 * width, units), BF16)], [pltpu.VMEM((units, width), BF16)]
+    )
     other = hop(merged, HOP_W)
     wide = [((SLOT, 3 * width), BF16)] * 4
+    sources = (
+        route_fwd[0].T,
+        route_bwd[0].T,
+        act_fwd[0],
+        norm_gain,
+        act_bwd[0],
+        cot_bwd[0],
+    )
     sent = local_copy_call(
-        pack_kernel,
-        wide,
-        3,
-        [pltpu.VMEM((tokens, width), BF16), pltpu.VMEM((1, width), F32)]
-        + [pltpu.VMEM((tokens, width), BF16)] * 2
-        + [pltpu.SemaphoreType.DMA((4,))],
-    )(info, route_fwd[0].T, route_bwd[0].T, act_fwd[0], norm_gain, act_bwd[0], cot_bwd[0])
+        pack_kernel, (info,), sources, wide, [pltpu.VMEM(v.shape, v.dtype) for v in sources]
+    )
     rows = spread_rows(*sent)
     outs = [((64, width), F32), ((64, width), BF16)] * 2
     scratch = pltpu.VMEM((256, width), BF16)

time: 173 us -> 171 us (0.988)
  the two profiles are of different devices: /device:TPU:31 before, /device:TPU:1 now
where the time goes in v12:
time: 171 us; the launch traced here: 168 us
  starting transfers between devices  83.4 us (49%)
  waiting for transfers between devices  69.4 us (41%)
  Pallas kernels  10.8 us (6%)
  local copies, waits for them, and re-layouts  2.3 us (1%)
    ppermute x19, starting transfers between devices, hop(): return lax.ppermute(value, 'expert', pairs)  73.6 us
    ppermute x19, waiting for transfers between devices, hop(): return lax.ppermute(value, 'expert', pairs)  65.2 us
    ppermute x2, starting transfers between devices, shifted(): return lax.ppermute(value, axis, pairs)  9.75 us
    ppermute x2, waiting for transfers between devices, shifted(): return lax.ppermute(value, axis, pairs)  4.2 us
    pallas_call x2, Pallas kernels, local_copy_call(): pl.pallas_call(kernel, out_shape=[jax.ShapeDtypeStruct(s, d) for s, d in...  4.11 us
  transfers between devices with their start and end apart: 21, of which 11 were waited for; matrix products, arithmetic and copies ran while one was open for 1% of the time, Pallas kernels for 3%

profile of v12, /device:TPU:1, one launch (start us, length us, event | category | flops | bytes accessed | tf_op | source)
XLA Modules:
  0.0 167.8 jit_solution(16947790363151306256)
XLA Ops:
  3.1 11.5 %collective-permute-start.4 = (bf16[16,10752]{1,0:T(8,128)(2,1)S(1)}, bf16[16,10752]{1,0:T(8,128)(2,1)S(1)}, u32[]{:S(2)}, u32[]{:S(2)}) collective-permute-start(bf16[16,10752]{1,0:T(8,128)(2,1)S(1)} %get-tuple-element.21), channel_id=1, source_target_pairs={{0,28},{1,29},{2,30},{3,31},{4,8},{5,9},{6,10},{7,11},{8,4},{9,5},... | collective-permute-start | bytes 1032200 | tf_op jit(solution)/shard_map/ppermute | solution.py:41
  16.5 4.5 %collective-permute-start.1 = (bf16[16,10752]{1,0:T(8,128)(2,1)S(1)}, bf16[16,10752]{1,0:T(8,128)(2,1)S(1)}, u32[]{:S(2)}, u32[]{:S(2)}) collective-permute-start(bf16[16,10752]{1,0:T(8,128)(2,1)S(1)} %get-tuple-element.19), channel_id=1, source_target_pairs={{0,20},{1,21},{2,22},{3,23},{4,16},{5,17},{6,18},{7,19},{8,28},{9,... | collective-permute-start | bytes 1032200 | tf_op jit(solution)/shard_map/ppermute | solution.py:41
  24.8 11.3 %collective-permute-done.4 = bf16[16,10752]{1,0:T(8,128)(2,1)S(1)} collective-permute-done((bf16[16,10752]{1,0:T(8,128)(2,1)S(1)}, bf16[16,10752]{1,0:T(8,128)(2,1)S(1)}, u32[]{:S(2)}, u32[]{:S(2)}) %collective-permute-start.4) | collective-permute-done | bytes 344096 | tf_op jit(solution)/shard_map/ppermute | solution.py:41
  36.1 3.1 %collective-permute-start.5 = (bf16[32,10752]{1,0:T(8,128)(2,1)S(1)}, bf16[32,10752]{1,0:T(8,128)(2,1)S(1)}, u32[]{:S(2)}, u32[]{:S(2)}) collective-permute-start(bf16[32,10752]{1,0:T(8,128)(2,1)S(1)} %pad_maximum_fusion.1), channel_id=1, source_target_pairs={{0,1},{1,0},{2,3},{3,2},{4,5},{5,4},{6,7},{7,6},{8,9},{9,8},{10,11... | collective-permute-start | bytes 2064392 | tf_op jit(solution)/shard_map/ppermute | solution.py:41
  39.2 4.2 %collective-permute-done.1 = bf16[16,10752]{1,0:T(8,128)(2,1)S(1)} collective-permute-done((bf16[16,10752]{1,0:T(8,128)(2,1)S(1)}, bf16[16,10752]{1,0:T(8,128)(2,1)S(1)}, u32[]{:S(2)}, u32[]{:S(2)}) %collective-permute-start.1) | collective-permute-done | bytes 344096 | tf_op jit(solution)/shard_map/ppermute | solution.py:41
  43.5 4.4 %collective-permute-start.2 = (bf16[32,10752]{1,0:T(8,128)(2,1)S(1)}, bf16[32,10752]{1,0:T(8,128)(2,1)S(1)}, u32[]{:S(2)}, u32[]{:S(2)}) collective-permute-start(bf16[32,10752]{1,0:T(8,128)(2,1)S(1)} %pad_maximum_fusion), channel_id=1, source_target_pairs={{0,3},{1,2},{2,1},{3,0},{4,7},{5,6},{6,5},{7,4},{8,11},{9,10},{10,... | collective-permute-start | bytes 2064392 | tf_op jit(solution)/shard_map/ppermute | solution.py:41
  48.0 4.2 %collective-permute-done.5 = bf16[32,10752]{1,0:T(8,128)(2,1)S(1)} collective-permute-done((bf16[32,10752]{1,0:T(8,128)(2,1)S(1)}, bf16[32,10752]{1,0:T(8,128)(2,1)S(1)}, u32[]{:S(2)}, u32[]{:S(2)}) %collective-permute-start.5) | collective-permute-done | bytes 688160 | tf_op jit(solution)/shard_map/ppermute | solution.py:41
  52.3 4.4 %collective-permute-start.6 = (bf16[64,10752]{1,0:T(8,128)(2,1)S(1)}, bf16[64,10752]{1,0:T(8,128)(2,1)S(1)}, u32[]{:S(2)}, u32[]{:S(2)}) collective-permute-start(bf16[64,10752]{1,0:T(8,128)(2,1)S(1)} %constant_dynamic-update-slice_fusion.3.c2), channel_id=1, source_target_pairs={{0,3},{1,2},{2,1},{3,0},{4,7},{5,6},{6,5},{7,4},{8,11},{9,10},{10,... | collective-permute-start | bytes 4128776 | tf_op jit(solution)/shard_map/ppermute | solution.py:41
  56.7 5.3 %collective-permute-done.2 = bf16[32,10752]{1,0:T(8,128)(2,1)S(1)} collective-permute-done((bf16[32,10752]{1,0:T(8,128)(2,1)S(1)}, bf16[32,10752]{1,0:T(8,128)(2,1)S(1)}, u32[]{:S(2)}, u32[]{:S(2)}) %collective-permute-start.2) | collective-permute-done | bytes 688160 | tf_op jit(solution)/shard_map/ppermute | solution.py:41
  64.0 27.5 %collective-permute-done.6.pr2 = bf16[64,10752]{1,0:T(8,128)(2,1)S(1)} collective-permute-done((bf16[64,10752]{1,0:T(8,128)(2,1)S(1)}, bf16[64,10752]{1,0:T(8,128)(2,1)S(1)}, u32[]{:S(2)}, u32[]{:S(2)}) %collective-permute-start.6) | collective-permute-done | bytes 1376288 | tf_op jit(solution)/shard_map/ppermute | solution.py:41
  93.9 3.1 %collective-permute-start.12 = (bf16[64,3584]{1,0:T(8,128)(2,1)S(1)}, bf16[64,3584]{1,0:T(8,128)(2,1)S(1)}, u32[]{:S(2)}, u32[]{:S(2)}) collective-permute-start(bf16[64,3584]{1,0:T(8,128)(2,1)S(1)} %get-tuple-element.27), channel_id=1, source_target_pairs={{0,1},{1,0},{2,3},{3,2},{4,5},{5,4},{6,7},{7,6},{8,9},{9,8},{10,11... | collective-permute-start | bytes 1376264 | tf_op jit(solution)/shard_map/ppermute | solution.py:41
  97.0 3.7 %collective-permute-start.8 = (bf16[64,3584]{1,0:T(8,128)(2,1)S(1)}, bf16[64,3584]{1,0:T(8,128)(2,1)S(1)}, u32[]{:S(2)}, u32[]{:S(2)}) collective-permute-start(bf16[64,3584]{1,0:T(8,128)(2,1)S(1)} %get-tuple-element.23._), channel_id=1, source_target_pairs={{0,3},{1,2},{2,1},{3,0},{4,7},{5,6},{6,5},{7,4},{8,11},{9,10},{10,... | collective-permute-start | bytes 1376264 | tf_op jit(solution)/shard_map/ppermute | solution.py:41
  100.8 3.3 %shard_map.133 = (f32[64,3584]{1,0:T(8,128)S(1)}, bf16[64,3584]{1,0:T(8,128)(2,1)S(1)}, f32[64,3584]{1,0:T(8,128)S(1)}, bf16[64,3584]{1,0:T(8,128)(2,1)S(1)}) custom-call(bf16[64,10752]{1,0:T(8,128)(2,1)S(1)} %constant_dynamic-update-slice_fusion.c1, bf16[64,10752]{1,0:T(8,128)(2,1)S(1)} %collective-permute-done.3.qr1, ...), custom_call_target="tpu_custom_call" | custom-call | tf_op jit(solution)/shard_map/pallas_call | solution.py:365
  106.3 2.5 %collective-permute-start.10 = (bf16[64,3584]{1,0:T(8,128)(2,1)S(1)}, bf16[64,3584]{1,0:T(8,128)(2,1)S(1)}, u32[]{:S(2)}, u32[]{:S(2)}) collective-permute-start(bf16[64,3584]{1,0:T(8,128)(2,1)S(1)} %get-tuple-element.25), channel_id=1, source_target_pairs={{0,3},{1,2},{2,1},{3,0},{4,7},{5,6},{6,5},{7,4},{8,11},{9,10},{10,... | collective-permute-start | bytes 1376264 | tf_op jit(solution)/shard_map/ppermute | solution.py:41
  109.0 4.0 %collective-permute-start.13 = (bf16[32,3584]{1,0:T(8,128)(2,1)S(1)}, bf16[32,3584]{1,0:T(8,128)(2,1)S(1)}, u32[]{:S(2)}, u32[]{:S(2)}) collective-permute-start(bf16[32,3584]{1,0:T(8,128)(2,1)S(1)} %slice.93), channel_id=1, source_target_pairs={{0,3},{1,2},{2,1},{3,0},{4,7},{5,6},{6,5},{7,4},{8,11},{9,10},{10,... | collective-permute-start | bytes 688136 | tf_op jit(solution)/shard_map/ppermute | solution.py:41
  113.8 5.9 %collective-permute-start.15 = (bf16[32,3584]{1,0:T(8,128)(2,1)S(1)}, bf16[32,3584]{1,0:T(8,128)(2,1)S(1)}, u32[]{:S(2)}, u32[]{:S(2)}) collective-permute-start(bf16[32,3584]{1,0:T(8,128)(2,1)S(1)} %slice.92), channel_id=1, source_target_pairs={{0,3},{1,2},{2,1},{3,0},{4,7},{5,6},{6,5},{7,4},{8,11},{9,10},{10,... | collective-permute-start | bytes 688136 | tf_op jit(solution)/shard_map/ppermute | solution.py:41
  121.9 3.4 %collective-permute-start.11 = (bf16[32,3584]{1,0:T(8,128)(2,1)S(1)}, bf16[32,3584]{1,0:T(8,128)(2,1)S(1)}, u32[]{:S(2)}, u32[]{:S(2)}) collective-permute-start(bf16[32,3584]{1,0:T(8,128)(2,1)S(1)} %slice.94), channel_id=1, source_target_pairs={{0,1},{1,0},{2,3},{3,2},{4,5},{5,4},{6,7},{7,6},{8,9},{9,8},{10,11... | collective-permute-start | bytes 688136 | tf_op jit(solution)/shard_map/ppermute | solution.py:41
  127.3 4.7 %collective-permute-start.16 = (bf16[16,7168]{1,0:T(8,128)(2,1)S(1)}, bf16[16,7168]{1,0:T(8,128)(2,1)S(1)}, u32[]{:S(2)}, u32[]{:S(2)}) collective-permute-start(bf16[16,7168]{1,0:T(8,128)(2,1)S(1)} %get-tuple-element.36), channel_id=1, source_target_pairs={{0,28},{1,29},{2,30},{3,31},{4,8},{5,9},{6,10},{7,11},{8,4},{9,5},... | collective-permute-start | bytes 688136 | tf_op jit(solution)/shard_map/ppermute | solution.py:41
  132.0 3.5 %collective-permute-start.17 = (bf16[16,7168]{1,0:T(8,128)(2,1)S(1)}, bf16[16,7168]{1,0:T(8,128)(2,1)S(1)}, u32[]{:S(2)}, u32[]{:S(2)}) collective-permute-start(bf16[16,7168]{1,0:T(8,128)(2,1)S(1)} %get-tuple-element.35), channel_id=1, source_target_pairs={{0,20},{1,21},{2,22},{3,23},{4,16},{5,17},{6,18},{7,19},{8,28},{9,... | collective-permute-start | bytes 688136 | tf_op jit(solution)/shard_map/ppermute | solution.py:41
  135.8 4.9 %collective-permute-start.18 = (bf16[16,7168]{1,0:T(8,128)(2,1)S(1)}, bf16[16,7168]{1,0:T(8,128)(2,1)S(1)}, u32[]{:S(2)}, u32[]{:S(2)}) collective-permute-start(bf16[16,7168]{1,0:T(8,128)(2,1)S(1)} %get-tuple-element.33), channel_id=1, source_target_pairs={{0,24},{1,25},{2,26},{3,27},{4,12},{5,13},{6,14},{7,15},{8,0},{9,1... | collective-permute-start | bytes 688136 | tf_op jit(solution)/shard_map/ppermute | solution.py:41
  140.7 5.6 %collective-permute-done.17.rest_2_ = bf16[16,7168]{1,0:T(8,128)(2,1)S(1)} collective-permute-done((bf16[16,7168]{1,0:T(8,128)(2,1)S(1)}, bf16[16,7168]{1,0:T(8,128)(2,1)S(1)}, u32[]{:S(2)}, u32[]{:S(2)}) %collective-permute-start.17) | collective-permute-done | bytes 229408 | tf_op jit(solution)/shard_map/ppermute | solution.py:41
  146.3 3.9 %collective-permute-done.18.rest_3_ = bf16[16,7168]{1,0:T(8,128)(2,1)S(1)} collective-permute-done((bf16[16,7168]{1,0:T(8,128)(2,1)S(1)}, bf16[16,7168]{1,0:T(8,128)(2,1)S(1)}, u32[]{:S(2)}, u32[]{:S(2)}) %collective-permute-start.18) | collective-permute-done | bytes 229408 | tf_op jit(solution)/shard_map/ppermute | solution.py:41
  151.9 7.8 %collective-permute-start.19 = (bf16[24,3584]{1,0:T(8,128)(2,1)S(1)}, bf16[24,3584]{1,0:T(8,128)(2,1)S(1)}, u32[]{:S(2)}, u32[]{:S(2)}) collective-permute-start(bf16[24,3584]{1,0:T(8,128)(2,1)S(1)} %get-tuple-element.30), channel_id=1, source_target_pairs={{0,32},{32,64},{64,96},{96,128},{128,160},{160,192},{192,224},{224... | collective-permute-start | bytes 516104 | tf_op jit(solution)/shard_map/ppermute | solution.py:47
  162.3 4.2 %collective-permute-done.20 = bf16[24,3584]{1,0:T(8,128)(2,1)S(1)} collective-permute-done((bf16[24,3584]{1,0:T(8,128)(2,1)S(1)}, bf16[24,3584]{1,0:T(8,128)(2,1)S(1)}, u32[]{:S(2)}, u32[]{:S(2)}) %collective-permute-start.20) | collective-permute-done | bytes 172064 | tf_op jit(solution)/shard_map/ppermute | solution.py:47
  (71 shorter events, 25.6 us)
Async XLA Ops:
  3.1 33.0 %collective-permute-start.4 = (bf16[16,10752]{1,0:T(8,128)(2,1)S(1)}, bf16[16,10752]{1,0:T(8,128)(2,1)S(1)}, u32[]{:S(2)}, u32[]{:S(2)}) collective-permute-start(bf16[16,10752]{1,0:T(8,128)(2,1)S(1)} %get-tuple-element.21), channel_id=1, source_target_pairs={{0,28},{1,29},{2,30},{3,31},{4,8},{5,9},{6,10},{7,11},{8,4},{9,5},... | collective-permute-start | bytes 1032200 | tf_op jit(solution)/shard_map/ppermute | solution.py:41
  14.6 24.7 %collective-permute-start = (bf16[16,10752]{1,0:T(8,128)(2,1)S(1)}, bf16[16,10752]{1,0:T(8,128)(2,1)S(1)}, u32[]{:S(2)}, u32[]{:S(2)}) collective-permute-start(bf16[16,10752]{1,0:T(8,128)(2,1)S(1)} %get-tuple-element.18), channel_id=1, source_target_pairs={{0,8},{1,9},{2,10},{3,11},{4,28},{5,29},{6,30},{7,31},{8,16},{9,17... | collective-permute-start | bytes 1032200 | tf_op jit(solution)/shard_map/ppermute | solution.py:41
  16.5 26.9 %collective-permute-start.1 = (bf16[16,10752]{1,0:T(8,128)(2,1)S(1)}, bf16[16,10752]{1,0:T(8,128)(2,1)S(1)}, u32[]{:S(2)}, u32[]{:S(2)}) collective-permute-start(bf16[16,10752]{1,0:T(8,128)(2,1)S(1)} %get-tuple-element.19), channel_id=1, source_target_pairs={{0,20},{1,21},{2,22},{3,23},{4,16},{5,17},{6,18},{7,19},{8,28},{9,... | collective-permute-start | bytes 1032200 | tf_op jit(solution)/shard_map/ppermute | solution.py:41
  22.8 69.4 %collective-permute-start.7 = (bf16[10752,128]{1,0:T(8,128)(2,1)S(1)}, bf16[10752,128]{1,0:T(8,128)(2,1)S(1)}, u32[]{:S(2)}, u32[]{:S(2)}) collective-permute-start(bf16[10752,128]{1,0:T(8,128)(2,1)S(1)} %shard_map.131), channel_id=1, source_target_pairs={{0,4},{1,5},{2,6},{3,7},{4,0},{5,1},{6,2},{7,3},{8,12},{9,13},{10,... | collective-permute-start | bytes 8257544 | tf_op jit(solution)/shard_map/ppermute | solution.py:41
  36.1 16.1 %collective-permute-start.5 = (bf16[32,10752]{1,0:T(8,128)(2,1)S(1)}, bf16[32,10752]{1,0:T(8,128)(2,1)S(1)}, u32[]{:S(2)}, u32[]{:S(2)}) collective-permute-start(bf16[32,10752]{1,0:T(8,128)(2,1)S(1)} %pad_maximum_fusion.1), channel_id=1, source_target_pairs={{0,1},{1,0},{2,3},{3,2},{4,5},{5,4},{6,7},{7,6},{8,9},{9,8},{10,11... | collective-permute-start | bytes 2064392 | tf_op jit(solution)/shard_map/ppermute | solution.py:41
  43.5 18.5 %collective-permute-start.2 = (bf16[32,10752]{1,0:T(8,128)(2,1)S(1)}, bf16[32,10752]{1,0:T(8,128)(2,1)S(1)}, u32[]{:S(2)}, u32[]{:S(2)}) collective-permute-start(bf16[32,10752]{1,0:T(8,128)(2,1)S(1)} %pad_maximum_fusion), channel_id=1, source_target_pairs={{0,3},{1,2},{2,1},{3,0},{4,7},{5,6},{6,5},{7,4},{8,11},{9,10},{10,... | collective-permute-start | bytes 2064392 | tf_op jit(solution)/shard_map/ppermute | solution.py:41
  48.0 44.2 %copy-start = (bf16[1,1,3584,128]{3,2,1,0:T(8,128)(2,1)S(1)}, bf16[1,1,3584,128]{3,2,1,0:T(8,128)(2,1)}, u32[]{:S(2)}) copy-start(bf16[1,1,3584,128]{3,2,1,0:T(8,128)(2,1)} %param.19) | copy-start | bytes 2752516
  48.0 44.2 %copy-start.1 = (bf16[1,1,3584,128]{3,2,1,0:T(8,128)(2,1)S(1)}, bf16[1,1,3584,128]{3,2,1,0:T(8,128)(2,1)}, u32[]{:S(2)}) copy-start(bf16[1,1,3584,128]{3,2,1,0:T(8,128)(2,1)} %param.20) | copy-start | bytes 2752516
  48.0 44.2 %copy-start.2 = (bf16[1,1,128,3584]{3,2,1,0:T(8,128)(2,1)S(1)}, bf16[1,1,128,3584]{3,2,1,0:T(8,128)(2,1)}, u32[]{:S(2)}) copy-start(bf16[1,1,128,3584]{3,2,1,0:T(8,128)(2,1)} %param.21) | copy-start | bytes 2752516
  52.3 39.2 %collective-permute-start.6 = (bf16[64,10752]{1,0:T(8,128)(2,1)S(1)}, bf16[64,10752]{1,0:T(8,128)(2,1)S(1)}, u32[]{:S(2)}, u32[]{:S(2)}) collective-permute-start(bf16[64,10752]{1,0:T(8,128)(2,1)S(1)} %constant_dynamic-update-slice_fusion.3.c2), channel_id=1, source_target_pairs={{0,3},{1,2},{2,1},{3,0},{4,7},{5,6},{6,5},{7,4},{8,11},{9,10},{10,... | collective-permute-start | bytes 4128776 | tf_op jit(solution)/shard_map/ppermute | solution.py:41
  62.0 29.4 %collective-permute-start.3 = (bf16[64,10752]{1,0:T(8,128)(2,1)S(1)}, bf16[64,10752]{1,0:T(8,128)(2,1)S(1)}, u32[]{:S(2)}, u32[]{:S(2)}) collective-permute-start(bf16[64,10752]{1,0:T(8,128)(2,1)S(1)} %constant_dynamic-update-slice_fusion.c1), channel_id=1, source_target_pairs={{0,1},{1,0},{2,3},{3,2},{4,5},{5,4},{6,7},{7,6},{8,9},{9,8},{10,11... | collective-permute-start | bytes 4128776 | tf_op jit(solution)/shard_map/ppermute | solution.py:41
  93.9 15.0 %collective-permute-start.12 = (bf16[64,3584]{1,0:T(8,128)(2,1)S(1)}, bf16[64,3584]{1,0:T(8,128)(2,1)S(1)}, u32[]{:S(2)}, u32[]{:S(2)}) collective-permute-start(bf16[64,3584]{1,0:T(8,128)(2,1)S(1)} %get-tuple-element.27), channel_id=1, source_target_pairs={{0,1},{1,0},{2,3},{3,2},{4,5},{5,4},{6,7},{7,6},{8,9},{9,8},{10,11... | collective-permute-start | bytes 1376264 | tf_op jit(solution)/shard_map/ppermute | solution.py:41
  97.0 22.7 %collective-permute-start.8 = (bf16[64,3584]{1,0:T(8,128)(2,1)S(1)}, bf16[64,3584]{1,0:T(8,128)(2,1)S(1)}, u32[]{:S(2)}, u32[]{:S(2)}) collective-permute-start(bf16[64,3584]{1,0:T(8,128)(2,1)S(1)} %get-tuple-element.23._), channel_id=1, source_target_pairs={{0,3},{1,2},{2,1},{3,0},{4,7},{5,6},{6,5},{7,4},{8,11},{9,10},{10,... | collective-permute-start | bytes 1376264 | tf_op jit(solution)/shard_map/ppermute | solution.py:41
  104.1 9.6 %collective-permute-start.14 = (bf16[64,3584]{1,0:T(8,128)(2,1)S(1)}, bf16[64,3584]{1,0:T(8,128)(2,1)S(1)}, u32[]{:S(2)}, u32[]{:S(2)}) collective-permute-start(bf16[64,3584]{1,0:T(8,128)(2,1)S(1)} %get-tuple-element.29), channel_id=1, source_target_pairs={{0,1},{1,0},{2,3},{3,2},{4,5},{5,4},{6,7},{7,6},{8,9},{9,8},{10,11... | collective-permute-start | bytes 1376264 | tf_op jit(solution)/shard_map/ppermute | solution.py:41
  106.3 15.5 %collective-permute-start.10 = (bf16[64,3584]{1,0:T(8,128)(2,1)S(1)}, bf16[64,3584]{1,0:T(8,128)(2,1)S(1)}, u32[]{:S(2)}, u32[]{:S(2)}) collective-permute-start(bf16[64,3584]{1,0:T(8,128)(2,1)S(1)} %get-tuple-element.25), channel_id=1, source_target_pairs={{0,3},{1,2},{2,1},{3,0},{4,7},{5,6},{6,5},{7,4},{8,11},{9,10},{10,... | collective-permute-start | bytes 1376264 | tf_op jit(solution)/shard_map/ppermute | solution.py:41
  109.0 16.3 %collective-permute-start.13 = (bf16[32,3584]{1,0:T(8,128)(2,1)S(1)}, bf16[32,3584]{1,0:T(8,128)(2,1)S(1)}, u32[]{:S(2)}, u32[]{:S(2)}) collective-permute-start(bf16[32,3584]{1,0:T(8,128)(2,1)S(1)} %slice.93), channel_id=1, source_target_pairs={{0,3},{1,2},{2,1},{3,0},{4,7},{5,6},{6,5},{7,4},{8,11},{9,10},{10,... | collective-permute-start | bytes 688136 | tf_op jit(solution)/shard_map/ppermute | solution.py:41
  113.8 13.4 %collective-permute-start.15 = (bf16[32,3584]{1,0:T(8,128)(2,1)S(1)}, bf16[32,3584]{1,0:T(8,128)(2,1)S(1)}, u32[]{:S(2)}, u32[]{:S(2)}) collective-permute-start(bf16[32,3584]{1,0:T(8,128)(2,1)S(1)} %slice.92), channel_id=1, source_target_pairs={{0,3},{1,2},{2,1},{3,0},{4,7},{5,6},{6,5},{7,4},{8,11},{9,10},{10,... | collective-permute-start | bytes 688136 | tf_op jit(solution)/shard_map/ppermute | solution.py:41
  119.9 15.7 %collective-permute-start.9 = (bf16[32,3584]{1,0:T(8,128)(2,1)S(1)}, bf16[32,3584]{1,0:T(8,128)(2,1)S(1)}, u32[]{:S(2)}, u32[]{:S(2)}) collective-permute-start(bf16[32,3584]{1,0:T(8,128)(2,1)S(1)} %slice.95), channel_id=1, source_target_pairs={{0,1},{1,0},{2,3},{3,2},{4,5},{5,4},{6,7},{7,6},{8,9},{9,8},{10,11... | collective-permute-start | bytes 688136 | tf_op jit(solution)/shard_map/ppermute | solution.py:41
  121.9 13.7 %collective-permute-start.11 = (bf16[32,3584]{1,0:T(8,128)(2,1)S(1)}, bf16[32,3584]{1,0:T(8,128)(2,1)S(1)}, u32[]{:S(2)}, u32[]{:S(2)}) collective-permute-start(bf16[32,3584]{1,0:T(8,128)(2,1)S(1)} %slice.94), channel_id=1, source_target_pairs={{0,1},{1,0},{2,3},{3,2},{4,5},{5,4},{6,7},{7,6},{8,9},{9,8},{10,11... | collective-permute-start | bytes 688136 | tf_op jit(solution)/shard_map/ppermute | solution.py:41
  127.3 13.4 %collective-permute-start.16 = (bf16[16,7168]{1,0:T(8,128)(2,1)S(1)}, bf16[16,7168]{1,0:T(8,128)(2,1)S(1)}, u32[]{:S(2)}, u32[]{:S(2)}) collective-permute-start(bf16[16,7168]{1,0:T(8,128)(2,1)S(1)} %get-tuple-element.36), channel_id=1, source_target_pairs={{0,28},{1,29},{2,30},{3,31},{4,8},{5,9},{6,10},{7,11},{8,4},{9,5},... | collective-permute-start | bytes 688136 | tf_op jit(solution)/shard_map/ppermute | solution.py:41
  132.0 14.3 %collective-permute-start.17 = (bf16[16,7168]{1,0:T(8,128)(2,1)S(1)}, bf16[16,7168]{1,0:T(8,128)(2,1)S(1)}, u32[]{:S(2)}, u32[]{:S(2)}) collective-permute-start(bf16[16,7168]{1,0:T(8,128)(2,1)S(1)} %get-tuple-element.35), channel_id=1, source_target_pairs={{0,20},{1,21},{2,22},{3,23},{4,16},{5,17},{6,18},{7,19},{8,28},{9,... | collective-permute-start | bytes 688136 | tf_op jit(solution)/shard_map/ppermute | solution.py:41
  135.8 14.5 %collective-permute-start.18 = (bf16[16,7168]{1,0:T(8,128)(2,1)S(1)}, bf16[16,7168]{1,0:T(8,128)(2,1)S(1)}, u32[]{:S(2)}, u32[]{:S(2)}) collective-permute-start(bf16[16,7168]{1,0:T(8,128)(2,1)S(1)} %get-tuple-element.33), channel_id=1, source_target_pairs={{0,24},{1,25},{2,26},{3,27},{4,12},{5,13},{6,14},{7,15},{8,0},{9,1... | collective-permute-start | bytes 688136 | tf_op jit(solution)/shard_map/ppermute | solution.py:41
  151.9 10.4 %collective-permute-start.19 = (bf16[24,3584]{1,0:T(8,128)(2,1)S(1)}, bf16[24,3584]{1,0:T(8,128)(2,1)S(1)}, u32[]{:S(2)}, u32[]{:S(2)}) collective-permute-start(bf16[24,3584]{1,0:T(8,128)(2,1)S(1)} %get-tuple-element.30), channel_id=1, source_target_pairs={{0,32},{32,64},{64,96},{96,128},{128,160},{160,192},{192,224},{224... | collective-permute-start | bytes 516104 | tf_op jit(solution)/shard_map/ppermute | solution.py:47
  159.8 6.7 %collective-permute-start.20 = (bf16[24,3584]{1,0:T(8,128)(2,1)S(1)}, bf16[24,3584]{1,0:T(8,128)(2,1)S(1)}, u32[]{:S(2)}, u32[]{:S(2)}) collective-permute-start(bf16[24,3584]{1,0:T(8,128)(2,1)S(1)} %get-tuple-element.31), channel_id=1, source_target_pairs={{32,0},{64,32},{96,64},{128,96},{160,128},{192,160},{224,192},{256... | collective-permute-start | bytes 516104 | tf_op jit(solution)/shard_map/ppermute | solution.py:47
  (8 other events, 146.0 us)

commit v13 on v12

--- a/solution.py
+++ b/solution.py
@@ -111,9 +111,10 @@
     return values * scale, scale
 
 
-def pack_kernel(info_ref, ra, rb, xa, gain_in, xb, cot, *rest):
-    outs, (ra_ref, rb_ref, xa_ref, gain_ref, xb_ref, cot_ref, sems) = rest[:4], rest[4:]
-    width = xa.shape[1]
+def first_kernel(info_ref, ra, rb, xa, gain_in, xb, cot, wg, wu, wd, *rest):
+    outs, merged, scratch = rest[:4], rest[4], rest[5:]
+    ra_ref, rb_ref, xa_ref, gain_ref, xb_ref, cot_ref, down, sems = scratch
+    width, units = wg.shape
     moves = (
         (ra, ra_ref),
         (rb, rb_ref),
@@ -121,6 +122,9 @@
         (gain_in, gain_ref),
         (xb, xb_ref),
         (cot, cot_ref),
+        (wd, down),
+        (wg, merged.at[pl.ds(0, width)]),
+        (wu, merged.at[pl.ds(width, width)]),
     )
     copies = [pltpu.make_async_copy(*move, sems.at[i]) for i, move in enumerate(moves)]
     for copy in copies:
@@ -131,7 +135,7 @@
     for route_ref in (ra_ref, rb_ref):
         masks = slot_masks(info_ref, route_ref)
         places.append((masks[0][0] | masks[1][0]).astype(F32).astype(BF16))
-    for copy in copies[2:]:
+    for copy in copies[2:6]:
         copy.wait()
     gain = gain_ref[...]
     normed_a = (normalized(xa_ref[...])[0] * gain).astype(BF16)
@@ -141,19 +145,11 @@
         packed = lax.dot_general(place, rows, TN, preferred_element_type=F32).astype(BF16)
         for j in range(4):
             outs[j][:, i * width : (i + 1) * width] = packed[j * SLOT : (j + 1) * SLOT]
-
-
-def merge_kernel(wg, wu, wd, out, down, sems):
-    width, units = wg.shape
-    moves = ((wd, down), (wg, out.at[pl.ds(0, width)]), (wu, out.at[pl.ds(width, width)]))
-    copies = [pltpu.make_async_copy(*move, sems.at[i]) for i, move in enumerate(moves)]
-    for copy in copies:
-        copy.start()
-    copies[0].wait()
+    copies[6].wait()
     for at in range(0, width, units):
-        out[2 * width + at : 2 * width + at + units, :] = down[:, at : at + units]
-    copies[1].wait()
-    copies[2].wait()
+        merged[2 * width + at : 2 * width + at + units, :] = down[:, at : at + units]
+    copies[7].wait()
+    copies[8].wait()
 
 
 def hidden(rows, wg, wu):
@@ -342,11 +338,7 @@
     info = jnp.stack([index >> 3, (index >> 2) & 1]).astype(jnp.int32)
     weights = (w_gate[0, 0], w_up[0, 0], w_down[0, 0])
     units = w_down.shape[2]
-    (merged,) = local_copy_call(
-        merge_kernel, (), weights, [((3 * width, units), BF16)], [pltpu.VMEM((units, width), BF16)]
-    )
-    other = hop(merged, HOP_W)
-    wide = [((SLOT, 3 * width), BF16)] * 4
+    wide = [((SLOT, 3 * width), BF16)] * 4 + [((3 * width, units), BF16)]
     sources = (
         route_fwd[0].T,
         route_bwd[0].T,
@@ -355,9 +347,9 @@
         act_bwd[0],
         cot_bwd[0],
     )
-    sent = local_copy_call(
-        pack_kernel, (info,), sources, wide, [pltpu.VMEM(v.shape, v.dtype) for v in sources]
-    )
+    scratch = [pltpu.VMEM(v.shape, v.dtype) for v in (*sources, weights[2])]
+    *sent, merged = local_copy_call(first_kernel, (info,), (*sources, *weights), wide, scratch)
+    other = hop(merged, HOP_W)
     rows = spread_rows(*sent)
     outs = [((64, width), F32), ((64, width), BF16)] * 2
     scratch = pltpu.VMEM((256, width), BF16)

time: 171 us -> 171 us (level)
  waiting for transfers between devices: 69.4 us -> 71.6 us
    ppermute x19, waiting for transfers between devices: 65.2 us -> 67.4 us  [hop(): return lax.ppermute(value, 'expert', pairs)]
    pallas_call x2 -> x1, Pallas kernels: 4.11 us -> 2.66 us  [local_copy_call(): pl.pallas_call(kernel, out_shape=[jax.ShapeDtypeStruct(s, d) for s, d in...]
  transfers between devices with their start and end apart: 21 -> 21, of which waited for: 11 -> 11; matrix products, arithmetic and copies ran while one was open for 1% -> 1% of each run, Pallas kernels for 3% -> 2%
where the time goes in v13:
time: 171 us; the launch traced here: 168 us
  starting transfers between devices  83 us (49%)
  waiting for transfers between devices  71.6 us (42%)
  Pallas kernels  9.3 us (5%)
  local copies, waits for them, and re-layouts  2.3 us (1%)
    ppermute x19, starting transfers between devices, hop(): return lax.ppermute(value, 'expert', pairs)  72.8 us
    ppermute x19, waiting for transfers between devices, hop(): return lax.ppermute(value, 'expert', pairs)  67.4 us
    ppermute x2, starting transfers between devices, shifted(): return lax.ppermute(value, axis, pairs)  10.2 us
    ppermute x2, waiting for transfers between devices, shifted(): return lax.ppermute(value, axis, pairs)  4.2 us
  transfers between devices with their start and end apart: 21, of which 11 were waited for; matrix products, arithmetic and copies ran while one was open for 1% of the time, Pallas kernels for 2%

profile of v13, /device:TPU:1, one launch (start us, length us, event | category | flops | bytes accessed | tf_op | source)
XLA Modules:
  0.0 168.2 jit_solution(12857440819305077195)
XLA Ops:
  0.7 2.7 %shard_map.130 = (bf16[16,10752]{1,0:T(8,128)(2,1)S(1)}, bf16[16,10752]{1,0:T(8,128)(2,1)S(1)}, bf16[16,10752]{1,0:T(8,128)(2,1)S(1)}, bf16[16,10752]{1,0:T(8,128)(2,1)S(1)}, bf16[10752,128]{1,0:T(8,128)(2,1)S(1)}) custom-call(s32[2]{0:T(128)S(1)} %pad_add_fusion.info_ref, s32[2,24]{1,0:T(2,128)} %bitcast.38, s32[2,24]{1,0:T(2,128)} %bitcast.40, ...), custom_call_target="tpu_custom_call" | custom-call | tf_op jit(solution)/shard_map/pallas_call | solution.py:65
  3.4 11.5 %collective-permute-start.4 = (bf16[16,10752]{1,0:T(8,128)(2,1)S(1)}, bf16[16,10752]{1,0:T(8,128)(2,1)S(1)}, u32[]{:S(2)}, u32[]{:S(2)}) collective-permute-start(bf16[16,10752]{1,0:T(8,128)(2,1)S(1)} %get-tuple-element.22), channel_id=1, source_target_pairs={{0,28},{1,29},{2,30},{3,31},{4,8},{5,9},{6,10},{7,11},{8,4},{9,5},... | collective-permute-start | bytes 1032200 | tf_op jit(solution)/shard_map/ppermute | solution.py:41
  16.8 4.5 %collective-permute-start.1 = (bf16[16,10752]{1,0:T(8,128)(2,1)S(1)}, bf16[16,10752]{1,0:T(8,128)(2,1)S(1)}, u32[]{:S(2)}, u32[]{:S(2)}) collective-permute-start(bf16[16,10752]{1,0:T(8,128)(2,1)S(1)} %get-tuple-element.20), channel_id=1, source_target_pairs={{0,20},{1,21},{2,22},{3,23},{4,16},{5,17},{6,18},{7,19},{8,28},{9,... | collective-permute-start | bytes 1032200 | tf_op jit(solution)/shard_map/ppermute | solution.py:41
  23.3 13.0 %collective-permute-done.4 = bf16[16,10752]{1,0:T(8,128)(2,1)S(1)} collective-permute-done((bf16[16,10752]{1,0:T(8,128)(2,1)S(1)}, bf16[16,10752]{1,0:T(8,128)(2,1)S(1)}, u32[]{:S(2)}, u32[]{:S(2)}) %collective-permute-start.4) | collective-permute-done | bytes 344096 | tf_op jit(solution)/shard_map/ppermute | solution.py:41
  36.4 3.1 %collective-permute-start.5 = (bf16[32,10752]{1,0:T(8,128)(2,1)S(1)}, bf16[32,10752]{1,0:T(8,128)(2,1)S(1)}, u32[]{:S(2)}, u32[]{:S(2)}) collective-permute-start(bf16[32,10752]{1,0:T(8,128)(2,1)S(1)} %pad_maximum_fusion.1), channel_id=1, source_target_pairs={{0,1},{1,0},{2,3},{3,2},{4,5},{5,4},{6,7},{7,6},{8,9},{9,8},{10,11... | collective-permute-start | bytes 2064392 | tf_op jit(solution)/shard_map/ppermute | solution.py:41
  39.5 4.2 %collective-permute-done.1 = bf16[16,10752]{1,0:T(8,128)(2,1)S(1)} collective-permute-done((bf16[16,10752]{1,0:T(8,128)(2,1)S(1)}, bf16[16,10752]{1,0:T(8,128)(2,1)S(1)}, u32[]{:S(2)}, u32[]{:S(2)}) %collective-permute-start.1) | collective-permute-done | bytes 344096 | tf_op jit(solution)/shard_map/ppermute | solution.py:41
  43.8 4.4 %collective-permute-start.2 = (bf16[32,10752]{1,0:T(8,128)(2,1)S(1)}, bf16[32,10752]{1,0:T(8,128)(2,1)S(1)}, u32[]{:S(2)}, u32[]{:S(2)}) collective-permute-start(bf16[32,10752]{1,0:T(8,128)(2,1)S(1)} %pad_maximum_fusion), channel_id=1, source_target_pairs={{0,3},{1,2},{2,1},{3,0},{4,7},{5,6},{6,5},{7,4},{8,11},{9,10},{10,... | collective-permute-start | bytes 2064392 | tf_op jit(solution)/shard_map/ppermute | solution.py:41
  48.3 4.2 %collective-permute-done.5 = bf16[32,10752]{1,0:T(8,128)(2,1)S(1)} collective-permute-done((bf16[32,10752]{1,0:T(8,128)(2,1)S(1)}, bf16[32,10752]{1,0:T(8,128)(2,1)S(1)}, u32[]{:S(2)}, u32[]{:S(2)}) %collective-permute-start.5) | collective-permute-done | bytes 688160 | tf_op jit(solution)/shard_map/ppermute | solution.py:41
  52.6 4.4 %collective-permute-start.6 = (bf16[64,10752]{1,0:T(8,128)(2,1)S(1)}, bf16[64,10752]{1,0:T(8,128)(2,1)S(1)}, u32[]{:S(2)}, u32[]{:S(2)}) collective-permute-start(bf16[64,10752]{1,0:T(8,128)(2,1)S(1)} %constant_dynamic-update-slice_fusion.3.c2), channel_id=1, source_target_pairs={{0,3},{1,2},{2,1},{3,0},{4,7},{5,6},{6,5},{7,4},{8,11},{9,10},{10,... | collective-permute-start | bytes 4128776 | tf_op jit(solution)/shard_map/ppermute | solution.py:41
  57.0 5.3 %collective-permute-done.2 = bf16[32,10752]{1,0:T(8,128)(2,1)S(1)} collective-permute-done((bf16[32,10752]{1,0:T(8,128)(2,1)S(1)}, bf16[32,10752]{1,0:T(8,128)(2,1)S(1)}, u32[]{:S(2)}, u32[]{:S(2)}) %collective-permute-start.2) | collective-permute-done | bytes 688160 | tf_op jit(solution)/shard_map/ppermute | solution.py:41
  64.3 27.5 %collective-permute-done.6.pr2 = bf16[64,10752]{1,0:T(8,128)(2,1)S(1)} collective-permute-done((bf16[64,10752]{1,0:T(8,128)(2,1)S(1)}, bf16[64,10752]{1,0:T(8,128)(2,1)S(1)}, u32[]{:S(2)}, u32[]{:S(2)}) %collective-permute-start.6) | collective-permute-done | bytes 1376288 | tf_op jit(solution)/shard_map/ppermute | solution.py:41
  94.0 3.1 %collective-permute-start.12 = (bf16[64,3584]{1,0:T(8,128)(2,1)S(1)}, bf16[64,3584]{1,0:T(8,128)(2,1)S(1)}, u32[]{:S(2)}, u32[]{:S(2)}) collective-permute-start(bf16[64,3584]{1,0:T(8,128)(2,1)S(1)} %get-tuple-element.29), channel_id=1, source_target_pairs={{0,1},{1,0},{2,3},{3,2},{4,5},{5,4},{6,7},{7,6},{8,9},{9,8},{10,11... | collective-permute-start | bytes 1376264 | tf_op jit(solution)/shard_map/ppermute | solution.py:41
  97.1 3.7 %collective-permute-start.8 = (bf16[64,3584]{1,0:T(8,128)(2,1)S(1)}, bf16[64,3584]{1,0:T(8,128)(2,1)S(1)}, u32[]{:S(2)}, u32[]{:S(2)}) collective-permute-start(bf16[64,3584]{1,0:T(8,128)(2,1)S(1)} %get-tuple-element.25._), channel_id=1, source_target_pairs={{0,3},{1,2},{2,1},{3,0},{4,7},{5,6},{6,5},{7,4},{8,11},{9,10},{10,... | collective-permute-start | bytes 1376264 | tf_op jit(solution)/shard_map/ppermute | solution.py:41
  100.9 3.3 %shard_map.132 = (f32[64,3584]{1,0:T(8,128)S(1)}, bf16[64,3584]{1,0:T(8,128)(2,1)S(1)}, f32[64,3584]{1,0:T(8,128)S(1)}, bf16[64,3584]{1,0:T(8,128)(2,1)S(1)}) custom-call(bf16[64,10752]{1,0:T(8,128)(2,1)S(1)} %constant_dynamic-update-slice_fusion.c1, bf16[64,10752]{1,0:T(8,128)(2,1)S(1)} %collective-permute-done.3.qr1, ...), custom_call_target="tpu_custom_call" | custom-call | tf_op jit(solution)/shard_map/pallas_call | solution.py:357
  109.1 4.0 %collective-permute-start.13 = (bf16[32,3584]{1,0:T(8,128)(2,1)S(1)}, bf16[32,3584]{1,0:T(8,128)(2,1)S(1)}, u32[]{:S(2)}, u32[]{:S(2)}) collective-permute-start(bf16[32,3584]{1,0:T(8,128)(2,1)S(1)} %slice.93), channel_id=1, source_target_pairs={{0,3},{1,2},{2,1},{3,0},{4,7},{5,6},{6,5},{7,4},{8,11},{9,10},{10,... | collective-permute-start | bytes 688136 | tf_op jit(solution)/shard_map/ppermute | solution.py:41
  113.6 6.2 %collective-permute-start.15 = (bf16[32,3584]{1,0:T(8,128)(2,1)S(1)}, bf16[32,3584]{1,0:T(8,128)(2,1)S(1)}, u32[]{:S(2)}, u32[]{:S(2)}) collective-permute-start(bf16[32,3584]{1,0:T(8,128)(2,1)S(1)} %slice.92), channel_id=1, source_target_pairs={{0,3},{1,2},{2,1},{3,0},{4,7},{5,6},{6,5},{7,4},{8,11},{9,10},{10,... | collective-permute-start | bytes 688136 | tf_op jit(solution)/shard_map/ppermute | solution.py:41
  121.9 3.4 %collective-permute-start.11 = (bf16[32,3584]{1,0:T(8,128)(2,1)S(1)}, bf16[32,3584]{1,0:T(8,128)(2,1)S(1)}, u32[]{:S(2)}, u32[]{:S(2)}) collective-permute-start(bf16[32,3584]{1,0:T(8,128)(2,1)S(1)} %slice.94), channel_id=1, source_target_pairs={{0,1},{1,0},{2,3},{3,2},{4,5},{5,4},{6,7},{7,6},{8,9},{9,8},{10,11... | collective-permute-start | bytes 688136 | tf_op jit(solution)/shard_map/ppermute | solution.py:41
  127.2 5.1 %collective-permute-start.16 = (bf16[16,7168]{1,0:T(8,128)(2,1)S(1)}, bf16[16,7168]{1,0:T(8,128)(2,1)S(1)}, u32[]{:S(2)}, u32[]{:S(2)}) collective-permute-start(bf16[16,7168]{1,0:T(8,128)(2,1)S(1)} %get-tuple-element.38), channel_id=1, source_target_pairs={{0,28},{1,29},{2,30},{3,31},{4,8},{5,9},{6,10},{7,11},{8,4},{9,5},... | collective-permute-start | bytes 688136 | tf_op jit(solution)/shard_map/ppermute | solution.py:41
  132.4 3.5 %collective-permute-start.17 = (bf16[16,7168]{1,0:T(8,128)(2,1)S(1)}, bf16[16,7168]{1,0:T(8,128)(2,1)S(1)}, u32[]{:S(2)}, u32[]{:S(2)}) collective-permute-start(bf16[16,7168]{1,0:T(8,128)(2,1)S(1)} %get-tuple-element.37), channel_id=1, source_target_pairs={{0,20},{1,21},{2,22},{3,23},{4,16},{5,17},{6,18},{7,19},{8,28},{9,... | collective-permute-start | bytes 688136 | tf_op jit(solution)/shard_map/ppermute | solution.py:41
  136.1 3.5 %collective-permute-start.18 = (bf16[16,7168]{1,0:T(8,128)(2,1)S(1)}, bf16[16,7168]{1,0:T(8,128)(2,1)S(1)}, u32[]{:S(2)}, u32[]{:S(2)}) collective-permute-start(bf16[16,7168]{1,0:T(8,128)(2,1)S(1)} %get-tuple-element.35), channel_id=1, source_target_pairs={{0,24},{1,25},{2,26},{3,27},{4,12},{5,13},{6,14},{7,15},{8,0},{9,1... | collective-permute-start | bytes 688136 | tf_op jit(solution)/shard_map/ppermute | solution.py:41
  139.6 7.2 %collective-permute-done.17.rest_2_ = bf16[16,7168]{1,0:T(8,128)(2,1)S(1)} collective-permute-done((bf16[16,7168]{1,0:T(8,128)(2,1)S(1)}, bf16[16,7168]{1,0:T(8,128)(2,1)S(1)}, u32[]{:S(2)}, u32[]{:S(2)}) %collective-permute-start.17) | collective-permute-done | bytes 229408 | tf_op jit(solution)/shard_map/ppermute | solution.py:41
  146.8 3.4 %collective-permute-done.18.rest_3_ = bf16[16,7168]{1,0:T(8,128)(2,1)S(1)} collective-permute-done((bf16[16,7168]{1,0:T(8,128)(2,1)S(1)}, bf16[16,7168]{1,0:T(8,128)(2,1)S(1)}, u32[]{:S(2)}, u32[]{:S(2)}) %collective-permute-start.18) | collective-permute-done | bytes 229408 | tf_op jit(solution)/shard_map/ppermute | solution.py:41
  151.9 8.2 %collective-permute-start.19 = (bf16[24,3584]{1,0:T(8,128)(2,1)S(1)}, bf16[24,3584]{1,0:T(8,128)(2,1)S(1)}, u32[]{:S(2)}, u32[]{:S(2)}) collective-permute-start(bf16[24,3584]{1,0:T(8,128)(2,1)S(1)} %get-tuple-element.32), channel_id=1, source_target_pairs={{0,32},{32,64},{64,96},{96,128},{128,160},{160,192},{192,224},{224... | collective-permute-start | bytes 516104 | tf_op jit(solution)/shard_map/ppermute | solution.py:47
  162.6 4.2 %collective-permute-done.20 = bf16[24,3584]{1,0:T(8,128)(2,1)S(1)} collective-permute-done((bf16[24,3584]{1,0:T(8,128)(2,1)S(1)}, bf16[24,3584]{1,0:T(8,128)(2,1)S(1)}, u32[]{:S(2)}, u32[]{:S(2)}) %collective-permute-start.20) | collective-permute-done | bytes 172064 | tf_op jit(solution)/shard_map/ppermute | solution.py:47
  (70 shorter events, 23.3 us)
Async XLA Ops:
  3.4 33.0 %collective-permute-start.4 = (bf16[16,10752]{1,0:T(8,128)(2,1)S(1)}, bf16[16,10752]{1,0:T(8,128)(2,1)S(1)}, u32[]{:S(2)}, u32[]{:S(2)}) collective-permute-start(bf16[16,10752]{1,0:T(8,128)(2,1)S(1)} %get-tuple-element.22), channel_id=1, source_target_pairs={{0,28},{1,29},{2,30},{3,31},{4,8},{5,9},{6,10},{7,11},{8,4},{9,5},... | collective-permute-start | bytes 1032200 | tf_op jit(solution)/shard_map/ppermute | solution.py:41
  14.9 24.6 %collective-permute-start = (bf16[16,10752]{1,0:T(8,128)(2,1)S(1)}, bf16[16,10752]{1,0:T(8,128)(2,1)S(1)}, u32[]{:S(2)}, u32[]{:S(2)}) collective-permute-start(bf16[16,10752]{1,0:T(8,128)(2,1)S(1)} %get-tuple-element.19), channel_id=1, source_target_pairs={{0,8},{1,9},{2,10},{3,11},{4,28},{5,29},{6,30},{7,31},{8,16},{9,17... | collective-permute-start | bytes 1032200 | tf_op jit(solution)/shard_map/ppermute | solution.py:41
  16.8 26.9 %collective-permute-start.1 = (bf16[16,10752]{1,0:T(8,128)(2,1)S(1)}, bf16[16,10752]{1,0:T(8,128)(2,1)S(1)}, u32[]{:S(2)}, u32[]{:S(2)}) collective-permute-start(bf16[16,10752]{1,0:T(8,128)(2,1)S(1)} %get-tuple-element.20), channel_id=1, source_target_pairs={{0,20},{1,21},{2,22},{3,23},{4,16},{5,17},{6,18},{7,19},{8,28},{9,... | collective-permute-start | bytes 1032200 | tf_op jit(solution)/shard_map/ppermute | solution.py:41
  21.4 71.0 %collective-permute-start.7 = (bf16[10752,128]{1,0:T(8,128)(2,1)S(1)}, bf16[10752,128]{1,0:T(8,128)(2,1)S(1)}, u32[]{:S(2)}, u32[]{:S(2)}) collective-permute-start(bf16[10752,128]{1,0:T(8,128)(2,1)S(1)} %get-tuple-element.23), channel_id=1, source_target_pairs={{0,4},{1,5},{2,6},{3,7},{4,0},{5,1},{6,2},{7,3},{8,12},{9,13},{10,... | collective-permute-start | bytes 8257544 | tf_op jit(solution)/shard_map/ppermute | solution.py:41
  36.4 16.1 %collective-permute-start.5 = (bf16[32,10752]{1,0:T(8,128)(2,1)S(1)}, bf16[32,10752]{1,0:T(8,128)(2,1)S(1)}, u32[]{:S(2)}, u32[]{:S(2)}) collective-permute-start(bf16[32,10752]{1,0:T(8,128)(2,1)S(1)} %pad_maximum_fusion.1), channel_id=1, source_target_pairs={{0,1},{1,0},{2,3},{3,2},{4,5},{5,4},{6,7},{7,6},{8,9},{9,8},{10,11... | collective-permute-start | bytes 2064392 | tf_op jit(solution)/shard_map/ppermute | solution.py:41
  43.8 18.5 %collective-permute-start.2 = (bf16[32,10752]{1,0:T(8,128)(2,1)S(1)}, bf16[32,10752]{1,0:T(8,128)(2,1)S(1)}, u32[]{:S(2)}, u32[]{:S(2)}) collective-permute-start(bf16[32,10752]{1,0:T(8,128)(2,1)S(1)} %pad_maximum_fusion), channel_id=1, source_target_pairs={{0,3},{1,2},{2,1},{3,0},{4,7},{5,6},{6,5},{7,4},{8,11},{9,10},{10,... | collective-permute-start | bytes 2064392 | tf_op jit(solution)/shard_map/ppermute | solution.py:41
  48.3 44.0 %copy-start = (bf16[1,1,3584,128]{3,2,1,0:T(8,128)(2,1)S(1)}, bf16[1,1,3584,128]{3,2,1,0:T(8,128)(2,1)}, u32[]{:S(2)}) copy-start(bf16[1,1,3584,128]{3,2,1,0:T(8,128)(2,1)} %param.19) | copy-start | bytes 2752516
  48.3 44.0 %copy-start.1 = (bf16[1,1,3584,128]{3,2,1,0:T(8,128)(2,1)S(1)}, bf16[1,1,3584,128]{3,2,1,0:T(8,128)(2,1)}, u32[]{:S(2)}) copy-start(bf16[1,1,3584,128]{3,2,1,0:T(8,128)(2,1)} %param.20) | copy-start | bytes 2752516
  48.3 44.0 %copy-start.2 = (bf16[1,1,128,3584]{3,2,1,0:T(8,128)(2,1)S(1)}, bf16[1,1,128,3584]{3,2,1,0:T(8,128)(2,1)}, u32[]{:S(2)}) copy-start(bf16[1,1,128,3584]{3,2,1,0:T(8,128)(2,1)} %param.21) | copy-start | bytes 2752516
  52.6 39.2 %collective-permute-start.6 = (bf16[64,10752]{1,0:T(8,128)(2,1)S(1)}, bf16[64,10752]{1,0:T(8,128)(2,1)S(1)}, u32[]{:S(2)}, u32[]{:S(2)}) collective-permute-start(bf16[64,10752]{1,0:T(8,128)(2,1)S(1)} %constant_dynamic-update-slice_fusion.3.c2), channel_id=1, source_target_pairs={{0,3},{1,2},{2,1},{3,0},{4,7},{5,6},{6,5},{7,4},{8,11},{9,10},{10,... | collective-permute-start | bytes 4128776 | tf_op jit(solution)/shard_map/ppermute | solution.py:41
  62.3 29.4 %collective-permute-start.3 = (bf16[64,10752]{1,0:T(8,128)(2,1)S(1)}, bf16[64,10752]{1,0:T(8,128)(2,1)S(1)}, u32[]{:S(2)}, u32[]{:S(2)}) collective-permute-start(bf16[64,10752]{1,0:T(8,128)(2,1)S(1)} %constant_dynamic-update-slice_fusion.c1), channel_id=1, source_target_pairs={{0,1},{1,0},{2,3},{3,2},{4,5},{5,4},{6,7},{7,6},{8,9},{9,8},{10,11... | collective-permute-start | bytes 4128776 | tf_op jit(solution)/shard_map/ppermute | solution.py:41
  94.0 15.0 %collective-permute-start.12 = (bf16[64,3584]{1,0:T(8,128)(2,1)S(1)}, bf16[64,3584]{1,0:T(8,128)(2,1)S(1)}, u32[]{:S(2)}, u32[]{:S(2)}) collective-permute-start(bf16[64,3584]{1,0:T(8,128)(2,1)S(1)} %get-tuple-element.29), channel_id=1, source_target_pairs={{0,1},{1,0},{2,3},{3,2},{4,5},{5,4},{6,7},{7,6},{8,9},{9,8},{10,11... | collective-permute-start | bytes 1376264 | tf_op jit(solution)/shard_map/ppermute | solution.py:41
  97.1 22.6 %collective-permute-start.8 = (bf16[64,3584]{1,0:T(8,128)(2,1)S(1)}, bf16[64,3584]{1,0:T(8,128)(2,1)S(1)}, u32[]{:S(2)}, u32[]{:S(2)}) collective-permute-start(bf16[64,3584]{1,0:T(8,128)(2,1)S(1)} %get-tuple-element.25._), channel_id=1, source_target_pairs={{0,3},{1,2},{2,1},{3,0},{4,7},{5,6},{6,5},{7,4},{8,11},{9,10},{10,... | collective-permute-start | bytes 1376264 | tf_op jit(solution)/shard_map/ppermute | solution.py:41
  104.2 9.2 %collective-permute-start.14 = (bf16[64,3584]{1,0:T(8,128)(2,1)S(1)}, bf16[64,3584]{1,0:T(8,128)(2,1)S(1)}, u32[]{:S(2)}, u32[]{:S(2)}) collective-permute-start(bf16[64,3584]{1,0:T(8,128)(2,1)S(1)} %get-tuple-element.31), channel_id=1, source_target_pairs={{0,1},{1,0},{2,3},{3,2},{4,5},{5,4},{6,7},{7,6},{8,9},{9,8},{10,11... | collective-permute-start | bytes 1376264 | tf_op jit(solution)/shard_map/ppermute | solution.py:41
  106.4 15.4 %collective-permute-start.10 = (bf16[64,3584]{1,0:T(8,128)(2,1)S(1)}, bf16[64,3584]{1,0:T(8,128)(2,1)S(1)}, u32[]{:S(2)}, u32[]{:S(2)}) collective-permute-start(bf16[64,3584]{1,0:T(8,128)(2,1)S(1)} %get-tuple-element.27), channel_id=1, source_target_pairs={{0,3},{1,2},{2,1},{3,0},{4,7},{5,6},{6,5},{7,4},{8,11},{9,10},{10,... | collective-permute-start | bytes 1376264 | tf_op jit(solution)/shard_map/ppermute | solution.py:41
  109.1 16.2 %collective-permute-start.13 = (bf16[32,3584]{1,0:T(8,128)(2,1)S(1)}, bf16[32,3584]{1,0:T(8,128)(2,1)S(1)}, u32[]{:S(2)}, u32[]{:S(2)}) collective-permute-start(bf16[32,3584]{1,0:T(8,128)(2,1)S(1)} %slice.93), channel_id=1, source_target_pairs={{0,3},{1,2},{2,1},{3,0},{4,7},{5,6},{6,5},{7,4},{8,11},{9,10},{10,... | collective-permute-start | bytes 688136 | tf_op jit(solution)/shard_map/ppermute | solution.py:41
  113.6 13.5 %collective-permute-start.15 = (bf16[32,3584]{1,0:T(8,128)(2,1)S(1)}, bf16[32,3584]{1,0:T(8,128)(2,1)S(1)}, u32[]{:S(2)}, u32[]{:S(2)}) collective-permute-start(bf16[32,3584]{1,0:T(8,128)(2,1)S(1)} %slice.92), channel_id=1, source_target_pairs={{0,3},{1,2},{2,1},{3,0},{4,7},{5,6},{6,5},{7,4},{8,11},{9,10},{10,... | collective-permute-start | bytes 688136 | tf_op jit(solution)/shard_map/ppermute | solution.py:41
  119.9 16.0 %collective-permute-start.9 = (bf16[32,3584]{1,0:T(8,128)(2,1)S(1)}, bf16[32,3584]{1,0:T(8,128)(2,1)S(1)}, u32[]{:S(2)}, u32[]{:S(2)}) collective-permute-start(bf16[32,3584]{1,0:T(8,128)(2,1)S(1)} %slice.95), channel_id=1, source_target_pairs={{0,1},{1,0},{2,3},{3,2},{4,5},{5,4},{6,7},{7,6},{8,9},{9,8},{10,11... | collective-permute-start | bytes 688136 | tf_op jit(solution)/shard_map/ppermute | solution.py:41
  121.9 14.0 %collective-permute-start.11 = (bf16[32,3584]{1,0:T(8,128)(2,1)S(1)}, bf16[32,3584]{1,0:T(8,128)(2,1)S(1)}, u32[]{:S(2)}, u32[]{:S(2)}) collective-permute-start(bf16[32,3584]{1,0:T(8,128)(2,1)S(1)} %slice.94), channel_id=1, source_target_pairs={{0,1},{1,0},{2,3},{3,2},{4,5},{5,4},{6,7},{7,6},{8,9},{9,8},{10,11... | collective-permute-start | bytes 688136 | tf_op jit(solution)/shard_map/ppermute | solution.py:41
  127.2 12.4 %collective-permute-start.16 = (bf16[16,7168]{1,0:T(8,128)(2,1)S(1)}, bf16[16,7168]{1,0:T(8,128)(2,1)S(1)}, u32[]{:S(2)}, u32[]{:S(2)}) collective-permute-start(bf16[16,7168]{1,0:T(8,128)(2,1)S(1)} %get-tuple-element.38), channel_id=1, source_target_pairs={{0,28},{1,29},{2,30},{3,31},{4,8},{5,9},{6,10},{7,11},{8,4},{9,5},... | collective-permute-start | bytes 688136 | tf_op jit(solution)/shard_map/ppermute | solution.py:41
  132.4 14.4 %collective-permute-start.17 = (bf16[16,7168]{1,0:T(8,128)(2,1)S(1)}, bf16[16,7168]{1,0:T(8,128)(2,1)S(1)}, u32[]{:S(2)}, u32[]{:S(2)}) collective-permute-start(bf16[16,7168]{1,0:T(8,128)(2,1)S(1)} %get-tuple-element.37), channel_id=1, source_target_pairs={{0,20},{1,21},{2,22},{3,23},{4,16},{5,17},{6,18},{7,19},{8,28},{9,... | collective-permute-start | bytes 688136 | tf_op jit(solution)/shard_map/ppermute | solution.py:41
  136.1 14.1 %collective-permute-start.18 = (bf16[16,7168]{1,0:T(8,128)(2,1)S(1)}, bf16[16,7168]{1,0:T(8,128)(2,1)S(1)}, u32[]{:S(2)}, u32[]{:S(2)}) collective-permute-start(bf16[16,7168]{1,0:T(8,128)(2,1)S(1)} %get-tuple-element.35), channel_id=1, source_target_pairs={{0,24},{1,25},{2,26},{3,27},{4,12},{5,13},{6,14},{7,15},{8,0},{9,1... | collective-permute-start | bytes 688136 | tf_op jit(solution)/shard_map/ppermute | solution.py:41
  151.9 10.8 %collective-permute-start.19 = (bf16[24,3584]{1,0:T(8,128)(2,1)S(1)}, bf16[24,3584]{1,0:T(8,128)(2,1)S(1)}, u32[]{:S(2)}, u32[]{:S(2)}) collective-permute-start(bf16[24,3584]{1,0:T(8,128)(2,1)S(1)} %get-tuple-element.32), channel_id=1, source_target_pairs={{0,32},{32,64},{64,96},{96,128},{128,160},{160,192},{192,224},{224... | collective-permute-start | bytes 516104 | tf_op jit(solution)/shard_map/ppermute | solution.py:47
  160.1 6.7 %collective-permute-start.20 = (bf16[24,3584]{1,0:T(8,128)(2,1)S(1)}, bf16[24,3584]{1,0:T(8,128)(2,1)S(1)}, u32[]{:S(2)}, u32[]{:S(2)}) collective-permute-start(bf16[24,3584]{1,0:T(8,128)(2,1)S(1)} %get-tuple-element.33), channel_id=1, source_target_pairs={{32,0},{64,32},{96,64},{128,96},{160,128},{192,160},{224,192},{256... | collective-permute-start | bytes 516104 | tf_op jit(solution)/shard_map/ppermute | solution.py:47
  (8 other events, 143.2 us)

commit v14 on v13

--- a/solution.py
+++ b/solution.py
@@ -296,12 +296,8 @@
 
 def spread_rows(own, a, b, c):
     got_a, got_b, got_c = hop(a, HOP_A), hop(b, HOP_B), hop(c, HOP_C)
-    half1 = jnp.concatenate([got_b, got_c], axis=0)
-    half2 = jnp.concatenate([own, got_a], axis=0)
-    q1 = hop(half1, HOP_X3)
-    p2 = hop(half2, HOP_X1)
-    c1 = jnp.concatenate([half1, q1], axis=0)
-    c2 = jnp.concatenate([half2, p2], axis=0)
+    c1 = jnp.concatenate([got_b, got_c, hop(got_b, HOP_X3), hop(got_c, HOP_X3)], axis=0)
+    c2 = jnp.concatenate([own, got_a, hop(own, HOP_X1), hop(got_a, HOP_X1)], axis=0)
     return c1, hop(c1, HOP_X1), c2, hop(c2, HOP_X3)
 
 

time: 171 us -> 173 us (1.012)
  waiting for transfers between devices: 71.6 us -> 74.9 us
    ppermute x19 -> x21, waiting for transfers between devices: 67.4 us -> 70.7 us  [hop(): return lax.ppermute(value, 'expert', pairs)]
    ppermute x19 -> x21, starting transfers between devices: 72.8 us -> 73 us  [hop(): return lax.ppermute(value, 'expert', pairs)]
  transfers between devices with their start and end apart: 21 -> 23, of which waited for: 11 -> 10; matrix products, arithmetic and copies ran while one was open for 1% -> 1% of each run, Pallas kernels for 2% -> 2%
where the time goes in v14:
time: 173 us; the launch traced here: 170 us
  starting transfers between devices  81.6 us (47%)
  waiting for transfers between devices  74.9 us (43%)
  Pallas kernels  9.3 us (5%)
  local copies, waits for them, and re-layouts  2.3 us (1%)
    ppermute x21, starting transfers between devices, hop(): return lax.ppermute(value, 'expert', pairs)  73 us
    ppermute x21, waiting for transfers between devices, hop(): return lax.ppermute(value, 'expert', pairs)  70.7 us
    ppermute x2, starting transfers between devices, shifted(): return lax.ppermute(value, axis, pairs)  8.67 us
    ppermute x2, waiting for transfers between devices, shifted(): return lax.ppermute(value, axis, pairs)  4.2 us
  transfers between devices with their start and end apart: 23, of which 10 were waited for; matrix products, arithmetic and copies ran while one was open for 1% of the time, Pallas kernels for 2%

profile of v14, /device:TPU:1, one launch (start us, length us, event | category | flops | bytes accessed | tf_op | source)
XLA Modules:
  0.0 170.0 jit_solution(17477618573476538433)
XLA Ops:
  3.4 11.5 %collective-permute-start.5 = (bf16[16,10752]{1,0:T(8,128)(2,1)S(1)}, bf16[16,10752]{1,0:T(8,128)(2,1)S(1)}, u32[]{:S(2)}, u32[]{:S(2)}) collective-permute-start(bf16[16,10752]{1,0:T(8,128)(2,1)S(1)} %get-tuple-element.22), channel_id=1, source_target_pairs={{0,28},{1,29},{2,30},{3,31},{4,8},{5,9},{6,10},{7,11},{8,4},{9,5},... | collective-permute-start | bytes 1032200 | tf_op jit(solution)/shard_map/ppermute | solution.py:41
  14.9 3.1 %collective-permute-start.6 = (bf16[16,10752]{1,0:T(8,128)(2,1)S(1)}, bf16[16,10752]{1,0:T(8,128)(2,1)S(1)}, u32[]{:S(2)}, u32[]{:S(2)}) collective-permute-start(bf16[16,10752]{1,0:T(8,128)(2,1)S(1)} %get-tuple-element.21), channel_id=1, source_target_pairs={{0,1},{1,0},{2,3},{3,2},{4,5},{5,4},{6,7},{7,6},{8,9},{9,8},{10,11... | collective-permute-start | bytes 1032200 | tf_op jit(solution)/shard_map/ppermute | solution.py:41
  19.9 4.5 %collective-permute-start.1 = (bf16[16,10752]{1,0:T(8,128)(2,1)S(1)}, bf16[16,10752]{1,0:T(8,128)(2,1)S(1)}, u32[]{:S(2)}, u32[]{:S(2)}) collective-permute-start(bf16[16,10752]{1,0:T(8,128)(2,1)S(1)} %get-tuple-element.20), channel_id=1, source_target_pairs={{0,20},{1,21},{2,22},{3,23},{4,16},{5,17},{6,18},{7,19},{8,28},{9,... | collective-permute-start | bytes 1032200 | tf_op jit(solution)/shard_map/ppermute | solution.py:41
  26.4 3.9 %collective-permute-done = bf16[16,10752]{1,0:T(8,128)(2,1)S(1)} collective-permute-done((bf16[16,10752]{1,0:T(8,128)(2,1)S(1)}, bf16[16,10752]{1,0:T(8,128)(2,1)S(1)}, u32[]{:S(2)}, u32[]{:S(2)}) %collective-permute-start) | collective-permute-done | bytes 344096 | tf_op jit(solution)/shard_map/ppermute | solution.py:41
  30.4 3.7 %collective-permute-start.2 = (bf16[16,10752]{1,0:T(8,128)(2,1)S(1)}, bf16[16,10752]{1,0:T(8,128)(2,1)S(1)}, u32[]{:S(2)}, u32[]{:S(2)}) collective-permute-start(bf16[16,10752]{1,0:T(8,128)(2,1)S(1)} %collective-permute-done), channel_id=1, source_target_pairs={{0,3},{1,2},{2,1},{3,0},{4,7},{5,6},{6,5},{7,4},{8,11},{9,10},{10,... | collective-permute-start | bytes 1032200 | tf_op jit(solution)/shard_map/ppermute | solution.py:41
  36.4 7.4 %collective-permute-done.1 = bf16[16,10752]{1,0:T(8,128)(2,1)S(1)} collective-permute-done((bf16[16,10752]{1,0:T(8,128)(2,1)S(1)}, bf16[16,10752]{1,0:T(8,128)(2,1)S(1)}, u32[]{:S(2)}, u32[]{:S(2)}) %collective-permute-start.1) | collective-permute-done | bytes 344096 | tf_op jit(solution)/shard_map/ppermute | solution.py:41
  43.8 4.4 %collective-permute-start.3 = (bf16[16,10752]{1,0:T(8,128)(2,1)S(1)}, bf16[16,10752]{1,0:T(8,128)(2,1)S(1)}, u32[]{:S(2)}, u32[]{:S(2)}) collective-permute-start(bf16[16,10752]{1,0:T(8,128)(2,1)S(1)} %collective-permute-done.1), channel_id=1, source_target_pairs={{0,3},{1,2},{2,1},{3,0},{4,7},{5,6},{6,5},{7,4},{8,11},{9,10},{10,... | collective-permute-start | bytes 1032200 | tf_op jit(solution)/shard_map/ppermute | solution.py:41
  50.6 6.2 %collective-permute-done.3 = bf16[16,10752]{1,0:T(8,128)(2,1)S(1)} collective-permute-done((bf16[16,10752]{1,0:T(8,128)(2,1)S(1)}, bf16[16,10752]{1,0:T(8,128)(2,1)S(1)}, u32[]{:S(2)}, u32[]{:S(2)}) %collective-permute-start.3) | collective-permute-done | bytes 344096 | tf_op jit(solution)/shard_map/ppermute | solution.py:41
  58.8 27.5 %collective-permute-done.8.pr2 = bf16[64,10752]{1,0:T(8,128)(2,1)S(1)} collective-permute-done((bf16[64,10752]{1,0:T(8,128)(2,1)S(1)}, bf16[64,10752]{1,0:T(8,128)(2,1)S(1)}, u32[]{:S(2)}, u32[]{:S(2)}) %collective-permute-start.8) | collective-permute-done | bytes 1376288 | tf_op jit(solution)/shard_map/ppermute | solution.py:41
  86.3 9.0 %collective-permute-done.9.other = bf16[10752,128]{1,0:T(8,128)(2,1)S(1)} collective-permute-done((bf16[10752,128]{1,0:T(8,128)(2,1)S(1)}, bf16[10752,128]{1,0:T(8,128)(2,1)S(1)}, u32[]{:S(2)}, u32[]{:S(2)}) %collective-permute-start.9) | collective-permute-done | bytes 2752544 | tf_op jit(solution)/shard_map/ppermute | solution.py:41
  99.2 4.4 %collective-permute-start.10 = (bf16[64,3584]{1,0:T(8,128)(2,1)S(1)}, bf16[64,3584]{1,0:T(8,128)(2,1)S(1)}, u32[]{:S(2)}, u32[]{:S(2)}) collective-permute-start(bf16[64,3584]{1,0:T(8,128)(2,1)S(1)} %get-tuple-element.25._), channel_id=1, source_target_pairs={{0,3},{1,2},{2,1},{3,0},{4,7},{5,6},{6,5},{7,4},{8,11},{9,10},{10,... | collective-permute-start | bytes 1376264 | tf_op jit(solution)/shard_map/ppermute | solution.py:41
  103.6 3.3 %shard_map.132 = (f32[64,3584]{1,0:T(8,128)S(1)}, bf16[64,3584]{1,0:T(8,128)(2,1)S(1)}, f32[64,3584]{1,0:T(8,128)S(1)}, bf16[64,3584]{1,0:T(8,128)(2,1)S(1)}) custom-call(bf16[64,10752]{1,0:T(8,128)(2,1)S(1)} %constant_dynamic-update-slice_fusion.c1, bf16[64,10752]{1,0:T(8,128)(2,1)S(1)} %collective-permute-done.4.qr1, ...), custom_call_target="tpu_custom_call" | custom-call | tf_op jit(solution)/shard_map/pallas_call | solution.py:353
  108.9 2.7 %collective-permute-start.12 = (bf16[64,3584]{1,0:T(8,128)(2,1)S(1)}, bf16[64,3584]{1,0:T(8,128)(2,1)S(1)}, u32[]{:S(2)}, u32[]{:S(2)}) collective-permute-start(bf16[64,3584]{1,0:T(8,128)(2,1)S(1)} %get-tuple-element.27), channel_id=1, source_target_pairs={{0,3},{1,2},{2,1},{3,0},{4,7},{5,6},{6,5},{7,4},{8,11},{9,10},{10,... | collective-permute-start | bytes 1376264 | tf_op jit(solution)/shard_map/ppermute | solution.py:41
  111.7 3.8 %collective-permute-start.15 = (bf16[32,3584]{1,0:T(8,128)(2,1)S(1)}, bf16[32,3584]{1,0:T(8,128)(2,1)S(1)}, u32[]{:S(2)}, u32[]{:S(2)}) collective-permute-start(bf16[32,3584]{1,0:T(8,128)(2,1)S(1)} %slice.93), channel_id=1, source_target_pairs={{0,3},{1,2},{2,1},{3,0},{4,7},{5,6},{6,5},{7,4},{8,11},{9,10},{10,... | collective-permute-start | bytes 688136 | tf_op jit(solution)/shard_map/ppermute | solution.py:41
  115.5 3.6 %collective-permute-done.16 = bf16[64,3584]{1,0:T(8,128)(2,1)S(1)} collective-permute-done((bf16[64,3584]{1,0:T(8,128)(2,1)S(1)}, bf16[64,3584]{1,0:T(8,128)(2,1)S(1)}, u32[]{:S(2)}, u32[]{:S(2)}) %collective-permute-start.16) | collective-permute-done | bytes 458784 | tf_op jit(solution)/shard_map/ppermute | solution.py:41
  119.3 4.4 %collective-permute-start.17 = (bf16[32,3584]{1,0:T(8,128)(2,1)S(1)}, bf16[32,3584]{1,0:T(8,128)(2,1)S(1)}, u32[]{:S(2)}, u32[]{:S(2)}) collective-permute-start(bf16[32,3584]{1,0:T(8,128)(2,1)S(1)} %slice.92), channel_id=1, source_target_pairs={{0,3},{1,2},{2,1},{3,0},{4,7},{5,6},{6,5},{7,4},{8,11},{9,10},{10,... | collective-permute-start | bytes 688136 | tf_op jit(solution)/shard_map/ppermute | solution.py:41
  126.0 3.3 %collective-permute-start.13 = (bf16[32,3584]{1,0:T(8,128)(2,1)S(1)}, bf16[32,3584]{1,0:T(8,128)(2,1)S(1)}, u32[]{:S(2)}, u32[]{:S(2)}) collective-permute-start(bf16[32,3584]{1,0:T(8,128)(2,1)S(1)} %slice.94), channel_id=1, source_target_pairs={{0,1},{1,0},{2,3},{3,2},{4,5},{5,4},{6,7},{7,6},{8,9},{9,8},{10,11... | collective-permute-start | bytes 688136 | tf_op jit(solution)/shard_map/ppermute | solution.py:41
  129.3 2.9 %collective-permute-done.17 = bf16[32,3584]{1,0:T(8,128)(2,1)S(1)} collective-permute-done((bf16[32,3584]{1,0:T(8,128)(2,1)S(1)}, bf16[32,3584]{1,0:T(8,128)(2,1)S(1)}, u32[]{:S(2)}, u32[]{:S(2)}) %collective-permute-start.17) | collective-permute-done | bytes 229408 | tf_op jit(solution)/shard_map/ppermute | solution.py:41
  132.3 3.2 %collective-permute-start.18 = (bf16[16,7168]{1,0:T(8,128)(2,1)S(1)}, bf16[16,7168]{1,0:T(8,128)(2,1)S(1)}, u32[]{:S(2)}, u32[]{:S(2)}) collective-permute-start(bf16[16,7168]{1,0:T(8,128)(2,1)S(1)} %get-tuple-element.38), channel_id=1, source_target_pairs={{0,28},{1,29},{2,30},{3,31},{4,8},{5,9},{6,10},{7,11},{8,4},{9,5},... | collective-permute-start | bytes 688136 | tf_op jit(solution)/shard_map/ppermute | solution.py:41
  138.4 5.0 %collective-permute-start.20 = (bf16[16,7168]{1,0:T(8,128)(2,1)S(1)}, bf16[16,7168]{1,0:T(8,128)(2,1)S(1)}, u32[]{:S(2)}, u32[]{:S(2)}) collective-permute-start(bf16[16,7168]{1,0:T(8,128)(2,1)S(1)} %get-tuple-element.35), channel_id=1, source_target_pairs={{0,24},{1,25},{2,26},{3,27},{4,12},{5,13},{6,14},{7,15},{8,0},{9,1... | collective-permute-start | bytes 688136 | tf_op jit(solution)/shard_map/ppermute | solution.py:41
  143.4 6.0 %collective-permute-done.19.rest_2_ = bf16[16,7168]{1,0:T(8,128)(2,1)S(1)} collective-permute-done((bf16[16,7168]{1,0:T(8,128)(2,1)S(1)}, bf16[16,7168]{1,0:T(8,128)(2,1)S(1)}, u32[]{:S(2)}, u32[]{:S(2)}) %collective-permute-start.19) | collective-permute-done | bytes 229408 | tf_op jit(solution)/shard_map/ppermute | solution.py:41
  149.4 4.1 %collective-permute-done.20.rest_3_ = bf16[16,7168]{1,0:T(8,128)(2,1)S(1)} collective-permute-done((bf16[16,7168]{1,0:T(8,128)(2,1)S(1)}, bf16[16,7168]{1,0:T(8,128)(2,1)S(1)}, u32[]{:S(2)}, u32[]{:S(2)}) %collective-permute-start.20) | collective-permute-done | bytes 229408 | tf_op jit(solution)/shard_map/ppermute | solution.py:41
  155.2 6.8 %collective-permute-start.21 = (bf16[24,3584]{1,0:T(8,128)(2,1)S(1)}, bf16[24,3584]{1,0:T(8,128)(2,1)S(1)}, u32[]{:S(2)}, u32[]{:S(2)}) collective-permute-start(bf16[24,3584]{1,0:T(8,128)(2,1)S(1)} %get-tuple-element.32), channel_id=1, source_target_pairs={{0,32},{32,64},{64,96},{96,128},{128,160},{160,192},{192,224},{224... | collective-permute-start | bytes 516104 | tf_op jit(solution)/shard_map/ppermute | solution.py:47
  164.5 4.2 %collective-permute-done.22 = bf16[24,3584]{1,0:T(8,128)(2,1)S(1)} collective-permute-done((bf16[24,3584]{1,0:T(8,128)(2,1)S(1)}, bf16[24,3584]{1,0:T(8,128)(2,1)S(1)}, u32[]{:S(2)}, u32[]{:S(2)}) %collective-permute-start.22) | collective-permute-done | bytes 172064 | tf_op jit(solution)/shard_map/ppermute | solution.py:47
  (74 shorter events, 29.9 us)
Async XLA Ops:
  3.4 30.8 %collective-permute-start.5 = (bf16[16,10752]{1,0:T(8,128)(2,1)S(1)}, bf16[16,10752]{1,0:T(8,128)(2,1)S(1)}, u32[]{:S(2)}, u32[]{:S(2)}) collective-permute-start(bf16[16,10752]{1,0:T(8,128)(2,1)S(1)} %get-tuple-element.22), channel_id=1, source_target_pairs={{0,28},{1,29},{2,30},{3,31},{4,8},{5,9},{6,10},{7,11},{8,4},{9,5},... | collective-permute-start | bytes 1032200 | tf_op jit(solution)/shard_map/ppermute | solution.py:41
  14.9 33.3 %collective-permute-start.6 = (bf16[16,10752]{1,0:T(8,128)(2,1)S(1)}, bf16[16,10752]{1,0:T(8,128)(2,1)S(1)}, u32[]{:S(2)}, u32[]{:S(2)}) collective-permute-start(bf16[16,10752]{1,0:T(8,128)(2,1)S(1)} %get-tuple-element.21), channel_id=1, source_target_pairs={{0,1},{1,0},{2,3},{3,2},{4,5},{5,4},{6,7},{7,6},{8,9},{9,8},{10,11... | collective-permute-start | bytes 1032200 | tf_op jit(solution)/shard_map/ppermute | solution.py:41
  18.0 12.4 %collective-permute-start = (bf16[16,10752]{1,0:T(8,128)(2,1)S(1)}, bf16[16,10752]{1,0:T(8,128)(2,1)S(1)}, u32[]{:S(2)}, u32[]{:S(2)}) collective-permute-start(bf16[16,10752]{1,0:T(8,128)(2,1)S(1)} %get-tuple-element.19), channel_id=1, source_target_pairs={{0,8},{1,9},{2,10},{3,11},{4,28},{5,29},{6,30},{7,31},{8,16},{9,17... | collective-permute-start | bytes 1032200 | tf_op jit(solution)/shard_map/ppermute | solution.py:41
  19.9 23.8 %collective-permute-start.1 = (bf16[16,10752]{1,0:T(8,128)(2,1)S(1)}, bf16[16,10752]{1,0:T(8,128)(2,1)S(1)}, u32[]{:S(2)}, u32[]{:S(2)}) collective-permute-start(bf16[16,10752]{1,0:T(8,128)(2,1)S(1)} %get-tuple-element.20), channel_id=1, source_target_pairs={{0,20},{1,21},{2,22},{3,23},{4,16},{5,17},{6,18},{7,19},{8,28},{9,... | collective-permute-start | bytes 1032200 | tf_op jit(solution)/shard_map/ppermute | solution.py:41
  24.5 70.9 %collective-permute-start.9 = (bf16[10752,128]{1,0:T(8,128)(2,1)S(1)}, bf16[10752,128]{1,0:T(8,128)(2,1)S(1)}, u32[]{:S(2)}, u32[]{:S(2)}) collective-permute-start(bf16[10752,128]{1,0:T(8,128)(2,1)S(1)} %get-tuple-element.23), channel_id=1, source_target_pairs={{0,4},{1,5},{2,6},{3,7},{4,0},{5,1},{6,2},{7,3},{8,12},{9,13},{10,... | collective-permute-start | bytes 8257544 | tf_op jit(solution)/shard_map/ppermute | solution.py:41
  30.4 20.1 %collective-permute-start.2 = (bf16[16,10752]{1,0:T(8,128)(2,1)S(1)}, bf16[16,10752]{1,0:T(8,128)(2,1)S(1)}, u32[]{:S(2)}, u32[]{:S(2)}) collective-permute-start(bf16[16,10752]{1,0:T(8,128)(2,1)S(1)} %collective-permute-done), channel_id=1, source_target_pairs={{0,3},{1,2},{2,1},{3,0},{4,7},{5,6},{6,5},{7,4},{8,11},{9,10},{10,... | collective-permute-start | bytes 1032200 | tf_op jit(solution)/shard_map/ppermute | solution.py:41
  34.1 14.1 %collective-permute-start.7 = (bf16[16,10752]{1,0:T(8,128)(2,1)S(1)}, bf16[16,10752]{1,0:T(8,128)(2,1)S(1)}, u32[]{:S(2)}, u32[]{:S(2)}) collective-permute-start(bf16[16,10752]{1,0:T(8,128)(2,1)S(1)} %collective-permute-done.5), channel_id=1, source_target_pairs={{0,1},{1,0},{2,3},{3,2},{4,5},{5,4},{6,7},{7,6},{8,9},{9,8},{10,11... | collective-permute-start | bytes 1032200 | tf_op jit(solution)/shard_map/ppermute | solution.py:41
  43.8 13.1 %collective-permute-start.3 = (bf16[16,10752]{1,0:T(8,128)(2,1)S(1)}, bf16[16,10752]{1,0:T(8,128)(2,1)S(1)}, u32[]{:S(2)}, u32[]{:S(2)}) collective-permute-start(bf16[16,10752]{1,0:T(8,128)(2,1)S(1)} %collective-permute-done.1), channel_id=1, source_target_pairs={{0,3},{1,2},{2,1},{3,0},{4,7},{5,6},{6,5},{7,4},{8,11},{9,10},{10,... | collective-permute-start | bytes 1032200 | tf_op jit(solution)/shard_map/ppermute | solution.py:41
  48.2 47.2 %copy-start = (bf16[1,1,3584,128]{3,2,1,0:T(8,128)(2,1)S(1)}, bf16[1,1,3584,128]{3,2,1,0:T(8,128)(2,1)}, u32[]{:S(2)}) copy-start(bf16[1,1,3584,128]{3,2,1,0:T(8,128)(2,1)} %param.19) | copy-start | bytes 2752516
  48.3 38.0 %collective-permute-start.8 = (bf16[64,10752]{1,0:T(8,128)(2,1)S(1)}, bf16[64,10752]{1,0:T(8,128)(2,1)S(1)}, u32[]{:S(2)}, u32[]{:S(2)}) collective-permute-start(bf16[64,10752]{1,0:T(8,128)(2,1)S(1)} %constant_dynamic-update-slice_fusion.4.c2), channel_id=1, source_target_pairs={{0,3},{1,2},{2,1},{3,0},{4,7},{5,6},{6,5},{7,4},{8,11},{9,10},{10,... | collective-permute-start | bytes 4128776 | tf_op jit(solution)/shard_map/ppermute | solution.py:41
  56.8 29.5 %collective-permute-start.4 = (bf16[64,10752]{1,0:T(8,128)(2,1)S(1)}, bf16[64,10752]{1,0:T(8,128)(2,1)S(1)}, u32[]{:S(2)}, u32[]{:S(2)}) collective-permute-start(bf16[64,10752]{1,0:T(8,128)(2,1)S(1)} %constant_dynamic-update-slice_fusion.c1), channel_id=1, source_target_pairs={{0,1},{1,0},{2,3},{3,2},{4,5},{5,4},{6,7},{7,6},{8,9},{9,8},{10,11... | collective-permute-start | bytes 4128776 | tf_op jit(solution)/shard_map/ppermute | solution.py:41
  97.0 14.6 %collective-permute-start.14 = (bf16[64,3584]{1,0:T(8,128)(2,1)S(1)}, bf16[64,3584]{1,0:T(8,128)(2,1)S(1)}, u32[]{:S(2)}, u32[]{:S(2)}) collective-permute-start(bf16[64,3584]{1,0:T(8,128)(2,1)S(1)} %get-tuple-element.29), channel_id=1, source_target_pairs={{0,1},{1,0},{2,3},{3,2},{4,5},{5,4},{6,7},{7,6},{8,9},{9,8},{10,11... | collective-permute-start | bytes 1376264 | tf_op jit(solution)/shard_map/ppermute | solution.py:41
  99.2 24.5 %collective-permute-start.10 = (bf16[64,3584]{1,0:T(8,128)(2,1)S(1)}, bf16[64,3584]{1,0:T(8,128)(2,1)S(1)}, u32[]{:S(2)}, u32[]{:S(2)}) collective-permute-start(bf16[64,3584]{1,0:T(8,128)(2,1)S(1)} %get-tuple-element.25._), channel_id=1, source_target_pairs={{0,3},{1,2},{2,1},{3,0},{4,7},{5,6},{6,5},{7,4},{8,11},{9,10},{10,... | collective-permute-start | bytes 1376264 | tf_op jit(solution)/shard_map/ppermute | solution.py:41
  107.0 12.2 %collective-permute-start.16 = (bf16[64,3584]{1,0:T(8,128)(2,1)S(1)}, bf16[64,3584]{1,0:T(8,128)(2,1)S(1)}, u32[]{:S(2)}, u32[]{:S(2)}) collective-permute-start(bf16[64,3584]{1,0:T(8,128)(2,1)S(1)} %get-tuple-element.31), channel_id=1, source_target_pairs={{0,1},{1,0},{2,3},{3,2},{4,5},{5,4},{6,7},{7,6},{8,9},{9,8},{10,11... | collective-permute-start | bytes 1376264 | tf_op jit(solution)/shard_map/ppermute | solution.py:41
  108.9 16.9 %collective-permute-start.12 = (bf16[64,3584]{1,0:T(8,128)(2,1)S(1)}, bf16[64,3584]{1,0:T(8,128)(2,1)S(1)}, u32[]{:S(2)}, u32[]{:S(2)}) collective-permute-start(bf16[64,3584]{1,0:T(8,128)(2,1)S(1)} %get-tuple-element.27), channel_id=1, source_target_pairs={{0,3},{1,2},{2,1},{3,0},{4,7},{5,6},{6,5},{7,4},{8,11},{9,10},{10,... | collective-permute-start | bytes 1376264 | tf_op jit(solution)/shard_map/ppermute | solution.py:41
  111.7 17.5 %collective-permute-start.15 = (bf16[32,3584]{1,0:T(8,128)(2,1)S(1)}, bf16[32,3584]{1,0:T(8,128)(2,1)S(1)}, u32[]{:S(2)}, u32[]{:S(2)}) collective-permute-start(bf16[32,3584]{1,0:T(8,128)(2,1)S(1)} %slice.93), channel_id=1, source_target_pairs={{0,3},{1,2},{2,1},{3,0},{4,7},{5,6},{6,5},{7,4},{8,11},{9,10},{10,... | collective-permute-start | bytes 688136 | tf_op jit(solution)/shard_map/ppermute | solution.py:41
  119.3 12.9 %collective-permute-start.17 = (bf16[32,3584]{1,0:T(8,128)(2,1)S(1)}, bf16[32,3584]{1,0:T(8,128)(2,1)S(1)}, u32[]{:S(2)}, u32[]{:S(2)}) collective-permute-start(bf16[32,3584]{1,0:T(8,128)(2,1)S(1)} %slice.92), channel_id=1, source_target_pairs={{0,3},{1,2},{2,1},{3,0},{4,7},{5,6},{6,5},{7,4},{8,11},{9,10},{10,... | collective-permute-start | bytes 688136 | tf_op jit(solution)/shard_map/ppermute | solution.py:41
  123.8 14.4 %collective-permute-start.11 = (bf16[32,3584]{1,0:T(8,128)(2,1)S(1)}, bf16[32,3584]{1,0:T(8,128)(2,1)S(1)}, u32[]{:S(2)}, u32[]{:S(2)}) collective-permute-start(bf16[32,3584]{1,0:T(8,128)(2,1)S(1)} %slice.95), channel_id=1, source_target_pairs={{0,1},{1,0},{2,3},{3,2},{4,5},{5,4},{6,7},{7,6},{8,9},{9,8},{10,11... | collective-permute-start | bytes 688136 | tf_op jit(solution)/shard_map/ppermute | solution.py:41
  126.0 12.4 %collective-permute-start.13 = (bf16[32,3584]{1,0:T(8,128)(2,1)S(1)}, bf16[32,3584]{1,0:T(8,128)(2,1)S(1)}, u32[]{:S(2)}, u32[]{:S(2)}) collective-permute-start(bf16[32,3584]{1,0:T(8,128)(2,1)S(1)} %slice.94), channel_id=1, source_target_pairs={{0,1},{1,0},{2,3},{3,2},{4,5},{5,4},{6,7},{7,6},{8,9},{9,8},{10,11... | collective-permute-start | bytes 688136 | tf_op jit(solution)/shard_map/ppermute | solution.py:41
  132.3 11.1 %collective-permute-start.18 = (bf16[16,7168]{1,0:T(8,128)(2,1)S(1)}, bf16[16,7168]{1,0:T(8,128)(2,1)S(1)}, u32[]{:S(2)}, u32[]{:S(2)}) collective-permute-start(bf16[16,7168]{1,0:T(8,128)(2,1)S(1)} %get-tuple-element.38), channel_id=1, source_target_pairs={{0,28},{1,29},{2,30},{3,31},{4,8},{5,9},{6,10},{7,11},{8,4},{9,5},... | collective-permute-start | bytes 688136 | tf_op jit(solution)/shard_map/ppermute | solution.py:41
  135.6 13.9 %collective-permute-start.19 = (bf16[16,7168]{1,0:T(8,128)(2,1)S(1)}, bf16[16,7168]{1,0:T(8,128)(2,1)S(1)}, u32[]{:S(2)}, u32[]{:S(2)}) collective-permute-start(bf16[16,7168]{1,0:T(8,128)(2,1)S(1)} %get-tuple-element.37), channel_id=1, source_target_pairs={{0,20},{1,21},{2,22},{3,23},{4,16},{5,17},{6,18},{7,19},{8,28},{9,... | collective-permute-start | bytes 688136 | tf_op jit(solution)/shard_map/ppermute | solution.py:41
  138.4 15.1 %collective-permute-start.20 = (bf16[16,7168]{1,0:T(8,128)(2,1)S(1)}, bf16[16,7168]{1,0:T(8,128)(2,1)S(1)}, u32[]{:S(2)}, u32[]{:S(2)}) collective-permute-start(bf16[16,7168]{1,0:T(8,128)(2,1)S(1)} %get-tuple-element.35), channel_id=1, source_target_pairs={{0,24},{1,25},{2,26},{3,27},{4,12},{5,13},{6,14},{7,15},{8,0},{9,1... | collective-permute-start | bytes 688136 | tf_op jit(solution)/shard_map/ppermute | solution.py:41
  155.2 9.3 %collective-permute-start.21 = (bf16[24,3584]{1,0:T(8,128)(2,1)S(1)}, bf16[24,3584]{1,0:T(8,128)(2,1)S(1)}, u32[]{:S(2)}, u32[]{:S(2)}) collective-permute-start(bf16[24,3584]{1,0:T(8,128)(2,1)S(1)} %get-tuple-element.32), channel_id=1, source_target_pairs={{0,32},{32,64},{64,96},{96,128},{128,160},{160,192},{192,224},{224... | collective-permute-start | bytes 516104 | tf_op jit(solution)/shard_map/ppermute | solution.py:47
  162.0 6.7 %collective-permute-start.22 = (bf16[24,3584]{1,0:T(8,128)(2,1)S(1)}, bf16[24,3584]{1,0:T(8,128)(2,1)S(1)}, u32[]{:S(2)}, u32[]{:S(2)}) collective-permute-start(bf16[24,3584]{1,0:T(8,128)(2,1)S(1)} %get-tuple-element.33), channel_id=1, source_target_pairs={{32,0},{64,32},{96,64},{128,96},{160,128},{192,160},{224,192},{256... | collective-permute-start | bytes 516104 | tf_op jit(solution)/shard_map/ppermute | solution.py:47
  (10 other events, 238.4 us)
